TPU v7x, 32 devices: a whole 2x2x4 slice. The times are simulated.
32 devices in a mesh: row: 4 (over x, core), col: 8 (over z, y).
Axes of the slice: x: 2, y: 2, z: 4, core: 2. Of those that a mesh axis runs over, the one named last changes fastest.
Arguments:
- node_feats: bfloat16 [4096, 2048], P(('col', 'row')), may hold values from -6 to 6
- block_vals: bfloat16 [4096, 2048], P('row', 'col'), may hold values from -0.125 to 0.125
- block_cols: int32 [16, 32], P('col', 'row'), may hold values from 0 to 3, as said below
- block_counts: int32 [8, 32], P('col', 'row'), may hold values from 1 to 2, as said below
- self_weight: float32 [4096], P('row'), may hold values from 0.25 to 1
- weight: bfloat16 [2048, 2048], P(('row', 'col')), may hold values from -0.125 to 0.125
- bias: float32 [2048], replicated, may hold values from -3 to 3
- out_grad: bfloat16 [4096, 2048], P(('row', 'col')), may hold values from -6 to 6
Outputs:
- activations: bfloat16 [4096, 2048], P(('row', 'col'))
- feat_grad: float32 [4096, 2048], P(('col', 'row'))
- weight_grad: float32 [2048, 2048], P(('row', 'col'))
- bias_grad: float32 [2048], P(('row', 'col'))
Inputs may be any that keep to these rules, and one draw needn't show every extreme that they name: `block_cols`: for each column tile and row block, the 2 slots name distinct blocks among the tile's 4. `block_counts`: slots at or past the count are ignored; tiles differ in load.
All inputs are finite; a program needn't handle non-finite values.
Results may differ from a plain program's by a relative error of at most 0.0095.
Values may be sent and summed in bfloat16 or wider, within the bound.
No kernel may reach another device: no remote copies, remote signals or barrier semaphores. Data moves between devices by JAX's collectives and lax.ppermute only.
A program may use at most 256 MiB of HBM per device.

v0:
```python
import jax
import jax.numpy as jnp
from jax import lax
from jax.sharding import PartitionSpec as P

boost = 2.0


def group_width():
    return 4


def live_values(block_vals, block_cols, block_counts, block_size):
    tile_rows, wide = block_vals.shape
    slot_count, block_total = block_cols.shape
    slot_ids = jnp.arange(slot_count, dtype=jnp.int32)
    live = slot_ids[None, :] < block_counts[0][:, None]
    values = block_vals.reshape(block_total, block_size, slot_count, block_size)
    masked = jnp.where(live[:, None, :, None], values, jnp.zeros_like(values))
    return masked.reshape(tile_rows, wide)


def rows_apply(values, columns, source_blocks, block_size):
    slot_count, block_total = columns.shape
    width = source_blocks.shape[2]
    group = group_width()
    grouped_vals = values.reshape(block_total // group, group, block_size, slot_count, block_size)
    grouped_cols = columns.T.reshape(block_total // group, group, slot_count)

    def rows_step(item):
        vals_part, cols_part = item
        picked = jnp.take(source_blocks, cols_part, axis=0)
        product = jnp.einsum(
            "gisj,gsjf->gif", vals_part, picked, preferred_element_type=jnp.float32
        )
        return product.reshape(group * block_size, width)

    return lax.map(rows_step, (grouped_vals, grouped_cols)).reshape(block_total * block_size, width)


def transpose_apply(values, columns, grads, tile_blocks, block_size):
    slot_count, block_total = columns.shape
    width = grads.shape[1]
    group = group_width()
    grouped_vals = values.reshape(block_total // group, group, block_size, slot_count, block_size)
    grouped_cols = columns.T.reshape(block_total // group, group * slot_count)
    grouped_grads = grads.reshape(block_total // group, group, block_size, width)

    def transpose_step(total, item):
        vals_part, cols_part, grad_part = item
        contrib = jnp.einsum(
            "gisj,gif->gsjf", vals_part, grad_part, preferred_element_type=jnp.float32
        )
        total = total.at[cols_part].add(contrib.reshape(group * slot_count, block_size, width))
        return (total, None)

    empty = jnp.zeros((tile_blocks, block_size, width), jnp.float32)
    total, _ = lax.scan(transpose_step, empty, (grouped_vals, grouped_cols, grouped_grads))
    return total.reshape(tile_blocks * block_size, width)


def shards(node_feats, block_vals, block_cols, block_counts, self_weight, weight, bias, out_grad):
    rows_count = lax.axis_size("row")
    cols_count = lax.axis_size("col")
    row_index = lax.axis_index("row")
    col_index = lax.axis_index("col")
    node_dev, width = node_feats.shape
    tile_rows = block_vals.shape[0]
    tile_cols = node_dev * rows_count
    slot_count, block_total = block_cols.shape
    block_size = tile_rows // block_total
    tile_blocks = tile_cols // block_size
    masked = live_values(block_vals, block_cols, block_counts, block_size)
    ratio = cols_count // rows_count
    offset = (col_index - row_index * ratio) * tile_cols
    tile_pos = jnp.arange(tile_rows, dtype=jnp.int32)
    inside = (tile_pos >= offset) & (tile_pos < offset + tile_cols)
    self_coef = jnp.where(inside, boost * self_weight, 0.0)
    self_index = jnp.clip(tile_pos - offset, 0, tile_cols - 1)
    offset_clip = jnp.clip(offset, 0, tile_rows - tile_cols)
    gathered = lax.all_gather(node_feats, "row", axis=0, tiled=True)
    source_blocks = gathered.reshape(tile_blocks, block_size, width)
    product = rows_apply(masked, block_cols, source_blocks, block_size)
    own_rows = jnp.take(gathered, self_index, axis=0)
    aggregated = lax.psum_scatter(
        product + self_coef[:, None] * own_rows.astype(jnp.float32),
        "col",
        scatter_dimension=0,
        tiled=True,
    )
    aggregated_low = aggregated.astype(jnp.bfloat16)
    whole_weight = lax.all_gather(weight, ("row", "col"), axis=0, tiled=True)
    pre_mat = jnp.dot(aggregated_low, whole_weight, preferred_element_type=jnp.float32)
    pre = pre_mat + bias[None, :]

    def smooth(value):
        return jax.nn.gelu(value, approximate=False)

    result, pull = jax.vjp(smooth, pre)
    activations = result.astype(jnp.bfloat16)
    (pre_grad,) = pull(out_grad.astype(jnp.float32))
    pre_low = pre_grad.astype(jnp.bfloat16)
    bias_part = jnp.sum(pre_low.astype(jnp.float32), axis=0)
    weight_part = lax.dot_general(
        aggregated_low, pre_low, (((0,), (0,)), ((), ())), preferred_element_type=jnp.float32
    )
    weight_grad, bias_grad = (
        lax.psum_scatter(weight_part, ("row", "col"), scatter_dimension=0, tiled=True),
        lax.psum_scatter(bias_part, ("row", "col"), scatter_dimension=0, tiled=True),
    )
    back_rows = lax.dot_general(
        pre_low, whole_weight, (((1,), (1,)), ((), ())), preferred_element_type=jnp.float32
    )
    back_low = back_rows.astype(jnp.bfloat16)
    row_grad = lax.all_gather(back_low, "col", axis=0, tiled=True)
    source_part = transpose_apply(masked, block_cols, row_grad, tile_blocks, block_size)
    coef_slice = lax.dynamic_slice_in_dim(self_coef, offset_clip, tile_cols, 0)
    own_grad = lax.dynamic_slice_in_dim(row_grad, offset_clip, tile_cols, 0)
    source_part = source_part + coef_slice[:, None] * own_grad.astype(jnp.float32)
    feat_grad = lax.psum_scatter(
        source_part.astype(jnp.bfloat16), "row", scatter_dimension=0, tiled=True
    ).astype(jnp.float32)
    return (activations, feat_grad, weight_grad, bias_grad)


def solution(mesh):
    placed = (
        P(("col", "row"), None),
        P("row", "col"),
        P("col", "row"),
        P("col", "row"),
        P("row"),
        P(("row", "col"), None),
        P(),
        P(("row", "col"), None),
    )
    return jax.shard_map(
        shards,
        mesh=mesh,
        in_specs=placed,
        out_specs=(
            P(("row", "col"), None),
            P(("col", "row"), None),
            P(("row", "col"), None),
            P(("row", "col")),
        ),
        check_vma=False,
    )
```

profile of v0, /device:TPU:0, one launch (start us, length us, event | category | flops | bytes accessed | tf_op | source)
XLA Modules:
  0.0 805.7 jit_solution(14173158343851946936)
XLA Ops:
  7.2 0.7 all-gather.4.cloned.1.call-update
  7.9 0.7 all-gather.6.cloned.1.call-update
  8.7 1.2 reshape.149
  9.9 0.5 broadcast.150
  10.4 1.3 reduce.3
  11.8 0.8 reshape.150
  12.7 0.7 multiply_select_fusion
  13.4 0.5 broadcast_select_fusion
  13.9 21.0 %all-gather.4.cloned.1.call-done = bf16[512,2048]{1,0:T(8,128)(2,1)} async-done(((bf16[128,2048]{1,0:T(8,128)(2,1)}), bf16[512,2048]{1,0:T(8,128)(2,1)}) %all-gather.4.cloned.1.call-update) | async-done | bytes 2097168 | tf_op jit(solution)/shard_map/all_gather | solution.py:81
  34.9 10.8 %gather_fusion.1 = bf16[1024,2048]{1,0:T(8,128)(2,1)} fusion(bf16[512,2048]{1,0:T(8,128)(2,1)} %all-gather.4.cloned.1.call-done, s32[1024]{0:T(1024)S(1)} %broadcast_clamp_fusion), kind=kCustom, calls=%fused_computation.1 | custom fusion | bytes 8392704 | tf_op jit(solution)/shard_map/jit(_take)/gather | solution.py:84
  45.7 17.0 %while.20 = (s32[]{:T(128)}, f32[2,512,2048]{2,1,0:T(8,128)}, bf16[2,4,128,2,128]{4,3,2,1,0:T(2,128)(2,1)S(1)}, s32[2,4,2]{1,0,2:T(2,128)S(1)}, bf16[4,128,2048]{2,1,0:T(8,128)(2,1)S(1)}, /*index=5*/s32[]{:T(128)}) while((s32[]{:T(128)}, f32[2,512,2048]{2,1,0:T(8,128)}, bf16[2,4,128,2,128]{4,3,2,1,0:T(2,128)(2,1)S(1)}, ...), condition=%wide.region_1.2_spmd, body=%wide.region_0.1_spmd.sunk | while | flops 538969152 | bytes 25957324 | solution.py:38
  45.7 0.1 copy.41
  45.9 2.8 gather_fusion
  48.7 0.1 copy.42
  48.8 0.2 constant_dynamic-slice_fusion.8
  49.0 3.0 fusion.46
  52.0 2.2 constant_dynamic-update-slice_fusion.2
  54.2 0.1 copy.41
  54.3 0.1 reshape.199
  54.4 2.7 gather_fusion
  57.2 0.1 copy.42
  57.3 0.2 constant_dynamic-slice_fusion.8
  57.5 3.0 fusion.46
  60.5 2.2 constant_dynamic-update-slice_fusion.2
  62.7 7.7 bitcast_add_fusion
  70.5 44.8 %all-gather.6.cloned.1.call-done = bf16[2048,2048]{1,0:T(8,128)(2,1)} async-done(((bf16[64,2048]{1,0:T(8,128)(2,1)}), bf16[2048,2048]{1,0:T(8,128)(2,1)}) %all-gather.6.cloned.1.call-update) | async-done | bytes 8388624 | tf_op jit(solution)/shard_map/all_gather | solution.py:92
  115.3 151.2 %reduce-scatter.4.cloned.1.call-done = f32[128,2048]{1,0:T(8,128)} async-done(((f32[1024,2048]{1,0:T(8,128)}), f32[128,2048]{1,0:T(8,128)}) %reduce-scatter.4.cloned.1.call-update) | async-done | bytes 1048592 | tf_op jit(solution)/shard_map/reduce_scatter | solution.py:85
  266.5 9.0 %convert_reduce_fusion = (f32[2048]{0:T(1024)S(1)}, bf16[128,2048]{1,0:T(8,128)(2,1)S(1)}, f32[128,2048]{1,0:T(8,128)}, f32[128,2048]{1,0:T(8,128)}) fusion(bf16[128,2048]{1,0:T(8,128)(2,1)S(1)} %copy-done.6, f32[2048]{0:T(1024)S(1)} %copy-done.7, bf16[2048,2048]{1,0:T(8,128)(2,1)} %all-gather.6.cloned.1.call-done, ...), kind=kOutput, calls=%fused_computation.42 | convolution fusion | flops 1093924864 | bytes 12599296 | tf_op jit(solution)/shard_map/dot_general | solution.py:93
  275.5 3.7 convolution_convert_fusion
  279.2 0.2 reduce-scatter.6.cloned.1.call-start
  279.7 72.1 %all-gather.8.cloned.1.call-done = bf16[1024,2048]{1,0:T(8,128)(2,1)} async-done(((bf16[128,2048]{1,0:T(8,128)(2,1)}), bf16[1024,2048]{1,0:T(8,128)(2,1)}) %all-gather.8.cloned.1.call-update) | async-done | bytes 4194320 | tf_op jit(solution)/shard_map/all_gather | solution.py:115
  351.8 2.4 broadcast_in_dim.57
  354.3 47.6 %while.21 = (s32[]{:T(128)}, f32[4,128,2048]{2,1,0:T(8,128)}, s32[2,8]{1,0:T(2,128)S(1)}, bf16[2,4,128,2,128]{4,3,2,1,0:T(2,128)(2,1)S(1)}, bf16[2,4,128,2048]{3,2,1,0:T(8,128)(2,1)}, /*index=5*/s32[]{:T(128)}) while((s32[]{:T(128)}, f32[4,128,2048]{2,1,0:T(8,128)}, s32[2,8]{1,0:T(2,128)S(1)}, bf16[2,4,128,2,128]{4,3,2,1,0:T(2,128)(2,1)S(1)}, ...), condition=%wide.region_5.6_spmd, body=%wide.region_3.5_spmd.sunk | while | flops 538968064 | bytes 36962988 | solution.py:58
  354.3 0.2 constant_dynamic-slice_fusion.9
  354.4 0.2 copy.43
  354.6 6.1 fusion.50
  360.7 17.3 %scatter_fusion = f32[4,128,2048]{2,1,0:T(8,128)} fusion(f32[4,128,2048]{2,1,0:T(8,128)} %get-tuple-element.196, s32[8]{0:T(128)S(1)} %fusion.49, f32[8,128,2048]{2,1,0:T(8,128)} %bitcast.70), kind=kCustom, calls=%fused_computation.2.clone.1 | custom fusion | flops 2097152 | bytes 25165856 | tf_op jit(solution)/shard_map/while/body/eval_jaxpr/scatter-add | solution.py:54
  378.0 0.2 constant_dynamic-slice_fusion.9
  378.2 0.2 copy.43
  378.4 6.1 fusion.50
  384.5 17.4 %scatter_fusion = f32[4,128,2048]{2,1,0:T(8,128)} fusion(f32[4,128,2048]{2,1,0:T(8,128)} %get-tuple-element.196, s32[8]{0:T(128)S(1)} %fusion.49, f32[8,128,2048]{2,1,0:T(8,128)} %bitcast.70), kind=kCustom, calls=%fused_computation.2.clone.1 | custom fusion | flops 2097152 | bytes 25165856 | tf_op jit(solution)/shard_map/while/body/eval_jaxpr/scatter-add | solution.py:54
  401.8 5.3 fusion.12
  407.2 9.0 %fusion.26 = f32[2048,2048]{1,0:T(8,128)} fusion(bf16[128,2048]{1,0:T(8,128)(2,1)S(1)} %get-tuple-element.106, f32[128,2048]{1,0:T(8,128)S(1)} %copy-done.2), kind=kOutput, calls=%fused_computation.58 | convolution fusion | flops 1074003968 | bytes 18350080 | tf_op jit(solution)/shard_map/dot_general | solution.py:104
  416.2 44.2 %all-reduce = f32[2048]{0:T(1024)S(1)} all-reduce(f32[2048]{0:T(1024)S(1)} %get-tuple-element.105), channel_id=5, replica_groups=mesh['row'=4,'col'=8] {'row','col'}, use_global_device_ids=true, to_apply=%region_9.10.clone | all-reduce | flops 2048 | bytes 16384
  460.4 0.6 dynamic-slice
  461.0 0.9 multiply_convert_fusion
  461.9 2.1 convert_element_type.38
  464.0 334.8 %reduce-scatter.8.cloned.1.call-done = f32[64,2048]{1,0:T(8,128)} async-done(((f32[2048,2048]{1,0:T(8,128)}), f32[64,2048]{1,0:T(8,128)}) %reduce-scatter.8.cloned.1.call-update) | async-done | bytes 524304 | tf_op jit(solution)/shard_map/reduce_scatter | solution.py:108
  (46 shorter events, 0.9 us)
Async XLA Ops:
  7.2 27.7 %all-gather.4.cloned.1.call-start = ((), (), s32[]{:S(2)}) async-start(), calls=%async_computation.3 | async-start | bytes 2621440 | tf_op jit(solution)/shard_map/all_gather | solution.py:81
  7.9 107.4 %all-gather.6.cloned.1.call-start = ((), (), s32[]{:S(2)}) async-start(), calls=%async_computation.5 | async-start | bytes 8650752 | tf_op jit(solution)/shard_map/all_gather | solution.py:92
  8.6 257.9 %reduce-scatter.4.cloned.1.call-start = ((), (), s32[]{:S(2)}) async-start(), calls=%async_computation.4 | async-start | bytes 9437184 | tf_op jit(solution)/shard_map/reduce_scatter | solution.py:85
  34.9 10.8 %copy-start = (bf16[512,2048]{1,0:T(8,128)(2,1)S(1)}, bf16[512,2048]{1,0:T(8,128)(2,1)}, u32[]{:S(2)}) copy-start(bf16[512,2048]{1,0:T(8,128)(2,1)} %all-gather.4.cloned.1.call-done) | copy-start | bytes 6291460
  70.4 196.1 %copy-start.6 = (bf16[128,2048]{1,0:T(8,128)(2,1)S(1)}, bf16[128,2048]{1,0:T(8,128)(2,1)}, u32[]{:S(2)}) copy-start(bf16[128,2048]{1,0:T(8,128)(2,1)} %param.19) | copy-start | bytes 1572868
  70.4 196.1 %copy-start.7 = (f32[2048]{0:T(1024)S(1)}, f32[2048]{0:T(1024)}, u32[]{:S(2)}) copy-start(f32[2048]{0:T(1024)} %param.18) | copy-start | bytes 24580
  70.5 281.3 %all-gather.8.cloned.1.call-start = ((), (), s32[]{:S(2)}) async-start(), calls=%async_computation.6 | async-start | bytes 4718592 | tf_op jit(solution)/shard_map/all_gather | solution.py:115
  266.5 9.0 %copy-start.1 = (bf16[2048,2048]{1,0:T(8,128)(2,1)S(1)}, bf16[2048,2048]{1,0:T(8,128)(2,1)}, u32[]{:S(2)}) copy-start(bf16[2048,2048]{1,0:T(8,128)(2,1)} %all-gather.6.cloned.1.call-done) | copy-start | bytes 25165828
  275.5 3.9 copy-start.5
  279.2 182.7 %reduce-scatter.6.cloned.1.call-start = ((), (), s32[]{:S(2)}) async-start(), calls=%async_computation.7 | async-start | bytes 2621440 | tf_op jit(solution)/shard_map/reduce_scatter | solution.py:120
  401.8 5.4 copy-start.2
  407.1 391.7 %reduce-scatter.8.cloned.1.call-start = ((), (), s32[]{:S(2)}) async-start(), calls=%async_computation.8 | async-start | bytes 17301504 | tf_op jit(solution)/shard_map/reduce_scatter | solution.py:108
  416.2 44.8 %copy-start.3 = (f32[128,2048]{1,0:T(8,128)S(1)}, f32[128,2048]{1,0:T(8,128)}, u32[]{:S(2)}) copy-start(f32[128,2048]{1,0:T(8,128)} %get-tuple-element.107) | copy-start | bytes 3145732
  416.2 44.8 %copy-start.4 = (f32[128,2048]{1,0:T(8,128)S(1)}, f32[128,2048]{1,0:T(8,128)}, u32[]{:S(2)}) copy-start(f32[128,2048]{1,0:T(8,128)} %get-tuple-element.108) | copy-start | bytes 3145732
Sparse Core Ops, SparseCore 0:
  9.6 25.2 all-gather.3
  37.9 77.3 all-gather.5
  118.9 147.5 reduce-scatter.3
  279.4 72.3 all-gather.7
  407.3 30.0 reduce-scatter.5
  440.1 358.6 reduce-scatter.7
where the time goes:
time: 806 us
  waiting for transfers between devices  625 us (78%)
  other arithmetic  53.4 us (7%)
  blocking collectives  44.2 us (5%)
  matrix products  39.8 us (5%)
  local copies, waits for them, and re-layouts  28.3 us (4%)
  between operations  14.2 us (2%)
    reduce_scatter x1, waiting for transfers between devices, shards(): lax.psum_scatter(weight_part, ('row', 'col'), scatter_dimension=0, tiled=...  335 us
    reduce_scatter x1, waiting for transfers between devices, shards(): lax.psum_scatter(product + self_coef[:, None] * own_rows.astype(jnp.float...  151 us
    all_gather x1, waiting for transfers between devices, shards(): row_grad = lax.all_gather(back_low, 'col', axis=0, tiled=True)  72.1 us
    all_gather x1, waiting for transfers between devices, shards(): whole_weight = lax.all_gather(weight, ('row', 'col'), axis=0, tiled=True)  44.8 us
    unnamed x1, blocking collectives  44.2 us
    scatter-add x2, other arithmetic, transpose_step(): total.at[cols_part]  34.7 us
    all_gather x1, waiting for transfers between devices, shards(): gathered = lax.all_gather(node_feats, 'row', axis=0, tiled=True)  21 us
  transfers between devices with their start and end apart: 6, of which 5 were waited for; matrix products, arithmetic and copies ran while one was open for 7% of the time, Pallas kernels for 0%

commit v1 on v0

v1 whole, which is shorter than its diff:
```python
import jax
import jax.numpy as jnp
from jax import lax
from jax.sharding import PartitionSpec as P

boost = 2.0
AXES = ("row", "col")
CORES = 2
LINE = 4
CHUNKS = 2


def dot(left, right, dims):
    return lax.dot_general(left, right, ((dims[0], dims[1]), ((), ())), preferred_element_type=jnp.float32)


class Place:
    def __init__(self):
        self.rows = lax.axis_size("row")
        self.cols = lax.axis_size("col")
        self.xs = self.rows // CORES
        self.bs = self.cols // LINE
        self.row = lax.axis_index("row")
        self.col = lax.axis_index("col")
        self.x = self.row // CORES
        self.core = self.row % CORES
        self.a = self.col // self.bs
        self.b = self.col % self.bs
        self.chips = [(dx, db) for db in range(self.bs) for dx in range(self.xs)]

    def index(self, x, core, a, b):
        return ((x % self.xs) * CORES + core % CORES) * self.cols + (a % LINE) * self.bs + b % self.bs

    def send(self, value, dx=0, dcore=0, da=0, db=0):
        pairs = [
            (self.index(x, core, a, b), self.index(x + dx, core + dcore, a + da, b + db))
            for x in range(self.xs)
            for core in range(CORES)
            for a in range(LINE)
            for b in range(self.bs)
        ]
        return lax.ppermute(value, AXES, pairs)


def rolled(value, start, axis):
    size = value.shape[axis]
    return lax.dynamic_slice_in_dim(jnp.concatenate([value, value], axis), start, size, axis)


def one_of(value, index, axis):
    return lax.dynamic_index_in_dim(value, index, axis, keepdims=False)


def operator(at, block_vals, block_cols, block_counts, self_weight, size):
    slots = block_cols.shape[0]
    live = jnp.arange(slots, dtype=jnp.int32)[:, None] < block_counts
    values = block_vals.reshape(LINE, at.bs, size, slots, size)
    live = live.reshape(slots, LINE, at.bs).transpose(1, 2, 0)
    values = jnp.where(live[:, :, None, :, None], values, jnp.zeros_like(values))
    values = rolled(values, at.a, 0)
    columns = rolled(block_cols.reshape(slots, LINE, at.bs), at.a, 1)
    tiles = []
    for db in range(at.bs):
        dest = (at.b + db) % at.bs
        part = one_of(values, dest, 1).reshape(LINE * size, slots * size)
        cols = one_of(columns, dest, 2)
        if db:
            head = jnp.pad(cols.reshape(1, -1).astype(part.dtype), ((0, 15), (0, slots * size - slots * LINE)))
            got = at.send(jnp.concatenate([part, head]), db=db)
            part = got[: LINE * size]
            cols = got[LINE * size, : slots * LINE].astype(jnp.int32).reshape(slots, LINE)
        tiles.append((part.reshape(LINE, size, slots, size), cols))
    weights = rolled(one_of(self_weight.reshape(LINE, at.bs, size), at.b, 1), at.a, 0)
    row_block = at.row * at.cols + ((at.a + jnp.arange(LINE, dtype=jnp.int32)) % LINE) * at.bs + at.b
    per_plane = at.bs * at.rows
    diagonal = jnp.eye(size, dtype=jnp.float32)[None] * (boost * weights)[:, :, None]
    result = []
    for dcore in range(CORES):
        blocks = []
        for dx, db in at.chips:
            part, cols = tiles[db]
            block = ((at.x - dx) % at.xs) * CORES + (at.core + dcore) % CORES
            total = jnp.zeros((LINE, size, size), jnp.float32)
            for slot in range(slots):
                hit = (cols[slot] == block)[:, None, None]
                total = total + jnp.where(hit, part[:, :, slot, :].astype(jnp.float32), 0.0)
            node_block = at.a * per_plane + ((at.b - db) % at.bs) * at.rows + block
            total = total + jnp.where((row_block == node_block)[:, None, None], diagonal, 0.0)
            blocks.append(total.astype(jnp.bfloat16))
        result.append(jnp.concatenate(blocks, 2).reshape(LINE * size, len(at.chips) * size))
    return result


def shards(node_feats, block_vals, block_cols, block_counts, self_weight, weight, bias, out_grad):
    at = Place()
    size, width = node_feats.shape
    chunk = width // CHUNKS
    own_rows = weight.shape[0]
    low = jnp.bfloat16
    whole_weight = lax.all_gather(weight, AXES, axis=0, tiled=True)
    own_op, other_op = operator(at, block_vals, block_cols, block_counts, self_weight, size)

    aggregated = []
    for k in range(CHUNKS):
        mine = node_feats[:, k * chunk : (k + 1) * chunk]
        own = jnp.concatenate([mine] + [at.send(mine, dx=dx, db=db) for dx, db in at.chips[1:]])
        other = at.send(own, dcore=1)
        part = dot(own_op, own, ((1,), (0,))) + dot(other_op, other, ((1,), (0,)))
        part_low = part.astype(low)
        total = part[:size]
        for da in range(1, LINE):
            total = total + at.send(part_low[da * size : (da + 1) * size], da=da).astype(jnp.float32)
        aggregated.append(total.astype(low))
    agg = jnp.concatenate(aggregated, 1)

    pre = dot(agg, whole_weight, ((1,), (0,))) + bias[None, :]
    phi = 0.5 * (1.0 + lax.erf(pre * (0.5**0.5)))
    activations = (pre * phi).astype(low)
    slope = phi + pre * (jnp.exp(-0.5 * pre * pre) * 0.3989422804014327)
    pre_low = (out_grad.astype(jnp.float32) * slope).astype(low)

    feat = []
    for k in range(CHUNKS):
        back = dot(pre_low, whole_weight[k * chunk : (k + 1) * chunk], ((1,), (1,))).astype(low)
        backs = jnp.concatenate([back] + [at.send(back, da=LINE - da) for da in range(1, LINE)])
        other = at.send(dot(other_op, backs, ((0,), (0,))).astype(low), dcore=1)
        both = dot(own_op, backs, ((0,), (0,))) + other.astype(jnp.float32)
        both_low = both.astype(low)
        total = both[:size]
        for i, (dx, db) in enumerate(at.chips):
            if i:
                total = total + at.send(both_low[i * size : (i + 1) * size], dx=-dx, db=-db).astype(jnp.float32)
        feat.append(total)
    feat_grad = jnp.concatenate(feat, 1)

    lanes = LINE * own_rows
    groups = rolled(agg.reshape(size, at.rows, LINE, at.bs, own_rows), at.a, 2)
    messages = []
    for dx, db in at.chips:
        dest_x = (at.x + dx) % at.xs
        wide = one_of(groups, (at.b + db) % at.bs, 3)
        picked = [
            one_of(wide, dest_x * CORES + (at.core + dcore) % CORES, 1).reshape(size, lanes) for dcore in range(CORES)
        ]
        message = jnp.concatenate([pre_low] + picked, 1)
        messages.append(at.send(message, dx=dx, db=db) if dx or db else message)
    own = jnp.concatenate(messages)
    other = at.send(own, dcore=1)
    weight_part = dot(own[:, width : width + lanes], own[:, :width], ((0,), (0,)))
    weight_part = weight_part + dot(other[:, width + lanes :], other[:, :width], ((0,), (0,)))
    bias_part = jnp.sum(own[:, :width].astype(jnp.float32), 0) + jnp.sum(other[:, :width].astype(jnp.float32), 0)
    bias_part = one_of(one_of(bias_part.reshape(at.rows, LINE, at.bs, own_rows), at.row, 0), at.b, 1)
    bias_part = rolled(bias_part, at.a, 0).reshape(lanes, 1)
    bias_high = bias_part.astype(low)
    bias_rest = (bias_part - bias_high.astype(jnp.float32)).astype(low)
    tail = jnp.pad(jnp.concatenate([bias_high, bias_rest], 1), ((0, 0), (0, 126)))
    sent = jnp.concatenate([weight_part.astype(low), tail], 1)
    weight_grad = weight_part[:own_rows]
    bias_grad = bias_part[:own_rows, 0]
    for da in range(1, LINE):
        got = at.send(sent[da * own_rows : (da + 1) * own_rows], da=da).astype(jnp.float32)
        weight_grad = weight_grad + got[:, :width]
        bias_grad = bias_grad + got[:, width] + got[:, width + 1]
    return activations, feat_grad, weight_grad, bias_grad


def solution(mesh):
    placed = (
        P(("col", "row"), None),
        P("row", "col"),
        P("col", "row"),
        P("col", "row"),
        P("row"),
        P(("row", "col"), None),
        P(),
        P(("row", "col"), None),
    )
    return jax.shard_map(
        shards,
        mesh=mesh,
        in_specs=placed,
        out_specs=(
            P(("row", "col"), None),
            P(("col", "row"), None),
            P(("row", "col"), None),
            P(("row", "col")),
        ),
        check_vma=False,
    )
```

time: 806 us -> 270 us (0.33)
  waiting for transfers between devices: 625 us -> 128 us
  starting transfers between devices: 0.42 us -> 58.2 us
  blocking collectives: 44.2 us -> 0 us
  other arithmetic: 53.4 us -> 22.6 us
  local copies, waits for them, and re-layouts: 28.3 us -> 11.1 us
    reduce_scatter x3 -> x0, waiting for transfers between devices: 486 us -> none  [the longest x1 335 us: shards(): lax.psum_scatter(weight_part, ('row', 'col'), scatter_dimension=0, tiled=...]
    all_gather x3 -> x1, waiting for transfers between devices: 138 us -> 0.02 us  [shards(): whole_weight = lax.all_gather(weight, AXES, axis=0, tiled=True)]
    ppermute x0 -> x36, waiting for transfers between devices: none -> 128 us  [send(): return lax.ppermute(value, AXES, pairs)]
    ppermute x0 -> x36, starting transfers between devices: none -> 58.2 us  [send(): return lax.ppermute(value, AXES, pairs)]
    unnamed x1 -> x0, blocking collectives: 44.2 us -> none
    scatter-add x2 -> x0, other arithmetic: 34.7 us -> none  [transpose_step(): total.at[cols_part]]
    gather x3 -> x0, local copies, waits for them, and re-layouts: 16.3 us -> none  [the longest x1 10.8 us: shards(): own_rows = jnp.take(gathered, self_index, axis=0)]
    dot_general x7 -> x13, matrix products: 39.8 us -> 34.5 us  [dot(): lax.dot_general(left, right, ((dims[0], dims[1]), ((), ())), preferred_el...]
  transfers between devices with their start and end apart: 6 -> 37, of which waited for: 5 -> 20; matrix products, arithmetic and copies ran while one was open for 7% -> 20% of each run, Pallas kernels for 0% -> 0%
where the time goes in v1:
time: 270 us
  waiting for transfers between devices  128 us (47%)
  starting transfers between devices  58.2 us (22%)
  matrix products  34.5 us (13%)
  other arithmetic  22.6 us (8%)
  between operations  14.9 us (6%)
  local copies, waits for them, and re-layouts  11.1 us (4%)
    ppermute x36, waiting for transfers between devices, send(): return lax.ppermute(value, AXES, pairs)  128 us
    ppermute x36, starting transfers between devices, send(): return lax.ppermute(value, AXES, pairs)  58.2 us
    dot_general x13, matrix products, dot(): lax.dot_general(left, right, ((dims[0], dims[1]), ((), ())), preferred_el...  34.5 us
  transfers between devices with their start and end apart: 37, of which 20 were waited for; matrix products, arithmetic and copies ran while one was open for 20% of the time, Pallas kernels for 0%

profile of v1, /device:TPU:0, one launch (start us, length us, event | category | flops | bytes accessed | tf_op | source)
XLA Modules:
  0.0 269.7 jit_solution(2882773253144127295)
XLA Ops:
  9.0 4.0 %collective-permute-start.3 = (bf16[128,1024]{1,0:T(8,128)(2,1)S(1)}, bf16[128,1024]{1,0:T(8,128)(2,1)S(1)}, u32[]{:S(2)}, u32[]{:S(2)}) collective-permute-start(bf16[128,1024]{1,0:T(8,128)(2,1)S(1)} %get-tuple-element.48), channel_id=1, source_target_pairs={{0,17},{1,16},{2,19},{3,18},{4,21},{5,20},{6,23},{7,22},{8,25},{9,... | collective-permute-start | bytes 786440 | tf_op jit(solution)/shard_map/ppermute | solution.py:42
  13.6 2.8 %collective-permute-start.10 = (bf16[128,1024]{1,0:T(8,128)(2,1)S(1)}, bf16[128,1024]{1,0:T(8,128)(2,1)S(1)}, u32[]{:S(2)}, u32[]{:S(2)}) collective-permute-start(bf16[128,1024]{1,0:T(8,128)(2,1)S(1)} %get-tuple-element.49), channel_id=1, source_target_pairs={{0,17},{1,16},{2,19},{3,18},{4,21},{5,20},{6,23},{7,22},{8,25},{9,... | collective-permute-start | bytes 786440 | tf_op jit(solution)/shard_map/ppermute | solution.py:42
  24.4 2.2 fusion.46
  26.8 2.3 collective-permute-start
  30.3 2.9 %collective-permute-done.10 = bf16[128,1024]{1,0:T(8,128)(2,1)S(1)} collective-permute-done((bf16[128,1024]{1,0:T(8,128)(2,1)S(1)}, bf16[128,1024]{1,0:T(8,128)(2,1)S(1)}, u32[]{:S(2)}, u32[]{:S(2)}) %collective-permute-start.10) | collective-permute-done | bytes 262176 | tf_op jit(solution)/shard_map/ppermute | solution.py:42
  33.2 4.8 %collective-permute-done.9 = bf16[128,1024]{1,0:T(8,128)(2,1)S(1)} collective-permute-done((bf16[128,1024]{1,0:T(8,128)(2,1)S(1)}, bf16[128,1024]{1,0:T(8,128)(2,1)S(1)}, u32[]{:S(2)}, u32[]{:S(2)}) %collective-permute-start.9) | collective-permute-done | bytes 262176 | tf_op jit(solution)/shard_map/ppermute | solution.py:42
  39.5 4.4 %collective-permute-done = bf16[528,256]{1,0:T(8,128)(2,1)} collective-permute-done((bf16[528,256]{1,0:T(8,128)(2,1)S(1)}, bf16[528,256]{1,0:T(8,128)(2,1)}, u32[]{:S(2)}, u32[]{:S(2)}) %collective-permute-start) | collective-permute-done | bytes 270368 | tf_op jit(solution)/shard_map/ppermute | solution.py:42
  47.5 2.2 fusion.87
  49.7 1.8 fusion.97
  51.6 1.8 collective-permute-start.5
  53.4 2.1 collective-permute-start.7
  56.4 2.0 fusion.86
  58.4 1.7 fusion.96
  60.2 1.6 collective-permute-start.12
  61.8 2.2 collective-permute-start.14
  64.1 4.2 %collective-permute-done.5 = bf16[128,1024]{1,0:T(8,128)(2,1)S(1)} collective-permute-done((bf16[128,1024]{1,0:T(8,128)(2,1)S(1)}, bf16[128,1024]{1,0:T(8,128)(2,1)S(1)}, u32[]{:S(2)}, u32[]{:S(2)}) %collective-permute-start.5) | collective-permute-done | bytes 262176 | tf_op jit(solution)/shard_map/ppermute | solution.py:42
  68.2 13.1 %collective-permute-start.13 = (bf16[128,1024]{1,0:T(8,128)(2,1)S(1)}, bf16[128,1024]{1,0:T(8,128)(2,1)S(1)}, u32[]{:S(2)}, u32[]{:S(2)}) collective-permute-start(bf16[128,1024]{1,0:T(8,128)(2,1)S(1)} %get-tuple-element.28), channel_id=1, source_target_pairs={{0,4},{1,5},{2,6},{3,7},{4,0},{5,1},{6,2},{7,3},{8,12},{9,13},{10,... | collective-permute-start | bytes 786440 | tf_op jit(solution)/shard_map/ppermute | solution.py:42
  81.3 19.8 %collective-permute-done.6 = bf16[128,1024]{1,0:T(8,128)(2,1)S(1)} collective-permute-done((bf16[128,1024]{1,0:T(8,128)(2,1)S(1)}, bf16[128,1024]{1,0:T(8,128)(2,1)S(1)}, u32[]{:S(2)}, u32[]{:S(2)}) %collective-permute-start.6) | collective-permute-done | bytes 262176 | tf_op jit(solution)/shard_map/ppermute | solution.py:42
  101.3 28.5 %collective-permute-done.13 = bf16[128,1024]{1,0:T(8,128)(2,1)S(1)} collective-permute-done((bf16[128,1024]{1,0:T(8,128)(2,1)S(1)}, bf16[128,1024]{1,0:T(8,128)(2,1)S(1)}, u32[]{:S(2)}, u32[]{:S(2)}) %collective-permute-start.13) | collective-permute-done | bytes 262176 | tf_op jit(solution)/shard_map/ppermute | solution.py:42
  131.3 6.2 %fusion.20 = (bf16[128,2048]{1,0:T(8,128)(2,1)S(1)}, bf16[128,2048]{1,0:T(8,128)(2,1)}) fusion(bf16[128,2048]{1,0:T(8,128)(2,1)} %param.15, f32[2048]{0:T(1024)S(1)} %copy-done.38, bf16[2048,2048]{1,0:T(8,128)(2,1)} %all-gather.2.cloned.1.call-done, bf16[128,1024]{1,0:T(8,128)(2,1)S(1)} %fusion.28, bf16[128,1024]{1,0:T(8,128)(2,1)S(1)} %fusion.31), kind=kOutput, calls=%fused_computation.45 | convolution fusion | flops 1078460416 | bytes 10493952 | tf_op jit(solution)/shard_map/dot_general | solution.py:14
  137.5 2.2 fusion.8
  143.4 1.8 collective-permute-start.16
  145.2 5.7 %collective-permute-done.17 = bf16[128,1024]{1,0:T(8,128)(2,1)S(1)} collective-permute-done((bf16[128,1024]{1,0:T(8,128)(2,1)}, bf16[128,1024]{1,0:T(8,128)(2,1)S(1)}, u32[]{:S(2)}, u32[]{:S(2)}) %collective-permute-start.17) | collective-permute-done | bytes 262176 | tf_op jit(solution)/shard_map/ppermute | solution.py:42
  151.9 9.5 %collective-permute-done.16 = bf16[128,1024]{1,0:T(8,128)(2,1)S(1)} collective-permute-done((bf16[128,1024]{1,0:T(8,128)(2,1)}, bf16[128,1024]{1,0:T(8,128)(2,1)S(1)}, u32[]{:S(2)}, u32[]{:S(2)}) %collective-permute-start.16) | collective-permute-done | bytes 262176 | tf_op jit(solution)/shard_map/ppermute | solution.py:42
  161.4 2.0 collective-permute-done.15
  163.4 2.9 %convolution_convert_fusion.1 = bf16[512,1024]{1,0:T(8,128)(2,1)} fusion(bf16[128,1024]{1,0:T(8,128)(2,1)} %copy-done.26, bf16[128,1024]{1,0:T(8,128)(2,1)S(1)} %collective-permute-done.16, bf16[128,1024]{1,0:T(8,128)(2,1)} %collective-permute-done.15, bf16[128,1024]{1,0:T(8,128)(2,1)} %fusion.8, bf16[512,128]{1,0:T(8,128)(2,1)S(1)} %copy-done.21, ...), kind=kOutput, calls=%fused_computation.36 | convolution fusion | flops 543686656 | bytes 2621440 | tf_op jit(solution)/shard_map/dot_general | solution.py:14
  166.3 4.0 %collective-permute-done.30 = bf16[128,2560]{1,0:T(8,128)(2,1)} collective-permute-done((bf16[128,2560]{1,0:T(8,128)(2,1)S(1)}, bf16[128,2560]{1,0:T(8,128)(2,1)}, u32[]{:S(2)}, u32[]{:S(2)}) %collective-permute-start.30) | collective-permute-done | bytes 655392 | tf_op jit(solution)/shard_map/ppermute | solution.py:42
  170.2 1.5 collective-permute-done.31
  171.8 3.9 %pad_maximum_fusion = bf16[512,2560]{1,0:T(8,128)(2,1)S(1)} fusion(bf16[128,2560]{1,0:T(8,128)(2,1)} %collective-permute-done.31, bf16[128,2560]{1,0:T(8,128)(2,1)} %collective-permute-done.30, bf16[128,2560]{1,0:T(8,128)(2,1)} %collective-permute-done.29, bf16[128,256]{1,0:T(8,128)(2,1)S(1)} %copy.27, bf16[128,256]{1,0:T(8,128)(2,1)S(1)} %copy.26, ...), kind=kLoop, calls=%fused_computation.7 | loop fusion | flops 15728640 | bytes 5242880 | tf_op jit(solution)/shard_map/concatenate | solution.py:147
  175.8 3.7 %fusion.11 = bf16[128,1024]{1,0:T(8,128)(2,1)S(1)} fusion(bf16[128,2048]{1,0:T(8,128)(2,1)S(1)} %get-tuple-element.21, bf16[2048,2048]{1,0:T(8,128)(2,1)} %all-gather.2.cloned.1.call-done), kind=kOutput, calls=%fused_computation.38 | convolution fusion | flops 537001984 | bytes 4980736 | tf_op jit(solution)/shard_map/dot_general | solution.py:14
  179.6 4.1 %collective-permute-start.23 = (bf16[128,1024]{1,0:T(8,128)(2,1)S(1)}, bf16[128,1024]{1,0:T(8,128)(2,1)S(1)}, u32[]{:S(2)}, u32[]{:S(2)}) collective-permute-start(bf16[128,1024]{1,0:T(8,128)(2,1)S(1)} %fusion.11), channel_id=1, source_target_pairs={{0,4},{1,5},{2,6},{3,7},{4,0},{5,1},{6,2},{7,3},{8,12},{9,13},{10,... | collective-permute-start | bytes 786440 | tf_op jit(solution)/shard_map/ppermute | solution.py:42
  183.7 6.9 %collective-permute-done.24 = bf16[128,1024]{1,0:T(8,128)(2,1)S(1)} collective-permute-done((bf16[128,1024]{1,0:T(8,128)(2,1)S(1)}, bf16[128,1024]{1,0:T(8,128)(2,1)S(1)}, u32[]{:S(2)}, u32[]{:S(2)}) %collective-permute-start.24) | collective-permute-done | bytes 262176 | tf_op jit(solution)/shard_map/ppermute | solution.py:42
  190.6 10.7 %collective-permute-done.23 = bf16[128,1024]{1,0:T(8,128)(2,1)S(1)} collective-permute-done((bf16[128,1024]{1,0:T(8,128)(2,1)S(1)}, bf16[128,1024]{1,0:T(8,128)(2,1)S(1)}, u32[]{:S(2)}, u32[]{:S(2)}) %collective-permute-start.23) | collective-permute-done | bytes 262176 | tf_op jit(solution)/shard_map/ppermute | solution.py:42
  202.1 1.7 convolution_convert_fusion
  205.1 2.1 fusion.99
  208.2 1.7 collective-permute-start.21
  210.9 3.3 %fusion.98 = (bf16[512,1024]{1,0:T(8,128)(2,1)S(1)}, f32[512,1024]{1,0:T(8,128)}) fusion(bf16[512,1024]{1,0:T(8,128)(2,1)} %collective-permute-done.25, bf16[128,1024]{1,0:T(8,128)(2,1)S(1)} %copy-done.33, bf16[128,1024]{1,0:T(8,128)(2,1)S(1)} %copy-done.35, bf16[128,1024]{1,0:T(8,128)(2,1)S(1)} %copy-done.37, bf16[128,1024]{1,0:T(8,128)(2,1)S(1)} %copy-done.31, ...), kind=kOutput, calls=%fused_computation.229 | convolution fusion | flops 544735232 | bytes 5767168 | tf_op jit(solution)/shard_map/dot_general | solution.py:14
  216.5 1.7 collective-permute-start.28
  218.2 4.4 %collective-permute-done.21 = bf16[128,1024]{1,0:T(8,128)(2,1)S(1)} collective-permute-done((bf16[128,1024]{1,0:T(8,128)(2,1)S(1)}, bf16[128,1024]{1,0:T(8,128)(2,1)S(1)}, u32[]{:S(2)}, u32[]{:S(2)}) %collective-permute-start.21) | collective-permute-done | bytes 262176 | tf_op jit(solution)/shard_map/ppermute | solution.py:42
  223.8 2.4 fusion.5
  226.2 2.4 fusion.100
  228.6 2.0 convert_reduce_fusion
  231.2 5.5 %collective-permute-start.33 = (bf16[64,2176]{1,0:T(8,128)(2,1)S(1)}, bf16[64,2176]{1,0:T(8,128)(2,1)S(1)}, u32[]{:S(2)}, u32[]{:S(2)}) collective-permute-start(bf16[64,2176]{1,0:T(8,128)(2,1)S(1)} %get-tuple-element.12), channel_id=1, source_target_pairs={{0,2},{1,3},{2,4},{3,5},{4,6},{5,7},{6,0},{7,1},{8,10},{9,11},{10,... | collective-permute-start | bytes 835592 | tf_op jit(solution)/shard_map/ppermute | solution.py:42
  238.3 3.2 %collective-permute-start.34 = (bf16[64,2176]{1,0:T(8,128)(2,1)S(1)}, bf16[64,2176]{1,0:T(8,128)(2,1)S(1)}, u32[]{:S(2)}, u32[]{:S(2)}) collective-permute-start(bf16[64,2176]{1,0:T(8,128)(2,1)S(1)} %get-tuple-element.14), channel_id=1, source_target_pairs={{0,4},{1,5},{2,6},{3,7},{4,0},{5,1},{6,2},{7,3},{8,12},{9,13},{10,... | collective-permute-start | bytes 835592 | tf_op jit(solution)/shard_map/ppermute | solution.py:42
  242.6 1.9 collective-permute-done.33
  244.5 5.3 %collective-permute-done.35 = bf16[64,2176]{1,0:T(8,128)(2,1)S(1)} collective-permute-done((bf16[64,2176]{1,0:T(8,128)(2,1)S(1)}, bf16[64,2176]{1,0:T(8,128)(2,1)S(1)}, u32[]{:S(2)}, u32[]{:S(2)}) %collective-permute-start.35) | collective-permute-done | bytes 278560 | tf_op jit(solution)/shard_map/ppermute | solution.py:42
  250.2 10.0 %collective-permute-done.34 = bf16[64,2176]{1,0:T(8,128)(2,1)S(1)} collective-permute-done((bf16[64,2176]{1,0:T(8,128)(2,1)S(1)}, bf16[64,2176]{1,0:T(8,128)(2,1)S(1)}, u32[]{:S(2)}, u32[]{:S(2)}) %collective-permute-start.34) | collective-permute-done | bytes 278560 | tf_op jit(solution)/shard_map/ppermute | solution.py:42
  260.4 1.9 slice_add_fusion
  (206 shorter events, 35.6 us)
Async XLA Ops:
  7.2 16.7 %copy-start = (f32[1024]{0:T(1024)S(1)}, f32[1024]{0:T(1024)}, u32[]{:S(2)}) copy-start(f32[1024]{0:T(1024)} %param.12) | copy-start | bytes 12292
  7.2 124.1 %all-gather.2.cloned.1.call-start = ((), (), s32[]{:S(2)}) async-start(), calls=%async_computation | async-start | bytes 8650752 | tf_op jit(solution)/shard_map/all_gather | solution.py:100
  9.0 15.0 %collective-permute-start.3 = (bf16[128,1024]{1,0:T(8,128)(2,1)S(1)}, bf16[128,1024]{1,0:T(8,128)(2,1)S(1)}, u32[]{:S(2)}, u32[]{:S(2)}) collective-permute-start(bf16[128,1024]{1,0:T(8,128)(2,1)S(1)} %get-tuple-element.48), channel_id=1, source_target_pairs={{0,17},{1,16},{2,19},{3,18},{4,21},{5,20},{6,23},{7,22},{8,25},{9,... | collective-permute-start | bytes 786440 | tf_op jit(solution)/shard_map/ppermute | solution.py:42
  12.9 13.8 %collective-permute-start.2 = (bf16[128,1024]{1,0:T(8,128)(2,1)S(1)}, bf16[128,1024]{1,0:T(8,128)(2,1)}, u32[]{:S(2)}, u32[]{:S(2)}) collective-permute-start(bf16[128,1024]{1,0:T(8,128)(2,1)S(1)} %get-tuple-element.48), channel_id=1, source_target_pairs={{0,1},{1,0},{2,3},{3,2},{4,5},{5,4},{6,7},{7,6},{8,9},{9,8},{10,11... | collective-permute-start | bytes 786440 | tf_op jit(solution)/shard_map/ppermute | solution.py:42
  13.5 15.7 %collective-permute-start.1 = (bf16[128,1024]{1,0:T(8,128)(2,1)S(1)}, bf16[128,1024]{1,0:T(8,128)(2,1)}, u32[]{:S(2)}, u32[]{:S(2)}) collective-permute-start(bf16[128,1024]{1,0:T(8,128)(2,1)S(1)} %get-tuple-element.48), channel_id=1, source_target_pairs={{0,16},{1,17},{2,18},{3,19},{4,20},{5,21},{6,22},{7,23},{8,24},{9,... | collective-permute-start | bytes 786440 | tf_op jit(solution)/shard_map/ppermute | solution.py:42
  13.6 19.7 %collective-permute-start.10 = (bf16[128,1024]{1,0:T(8,128)(2,1)S(1)}, bf16[128,1024]{1,0:T(8,128)(2,1)S(1)}, u32[]{:S(2)}, u32[]{:S(2)}) collective-permute-start(bf16[128,1024]{1,0:T(8,128)(2,1)S(1)} %get-tuple-element.49), channel_id=1, source_target_pairs={{0,17},{1,16},{2,19},{3,18},{4,21},{5,20},{6,23},{7,22},{8,25},{9,... | collective-permute-start | bytes 786440 | tf_op jit(solution)/shard_map/ppermute | solution.py:42
  16.4 21.6 %collective-permute-start.9 = (bf16[128,1024]{1,0:T(8,128)(2,1)S(1)}, bf16[128,1024]{1,0:T(8,128)(2,1)S(1)}, u32[]{:S(2)}, u32[]{:S(2)}) collective-permute-start(bf16[128,1024]{1,0:T(8,128)(2,1)S(1)} %get-tuple-element.49), channel_id=1, source_target_pairs={{0,1},{1,0},{2,3},{3,2},{4,5},{5,4},{6,7},{7,6},{8,9},{9,8},{10,11... | collective-permute-start | bytes 786440 | tf_op jit(solution)/shard_map/ppermute | solution.py:42
  24.0 14.4 %collective-permute-start.8 = (bf16[128,1024]{1,0:T(8,128)(2,1)S(1)}, bf16[128,1024]{1,0:T(8,128)(2,1)}, u32[]{:S(2)}, u32[]{:S(2)}) collective-permute-start(bf16[128,1024]{1,0:T(8,128)(2,1)S(1)} %get-tuple-element.49), channel_id=1, source_target_pairs={{0,16},{1,17},{2,18},{3,19},{4,20},{5,21},{6,22},{7,23},{8,24},{9,... | collective-permute-start | bytes 786440 | tf_op jit(solution)/shard_map/ppermute | solution.py:42
  26.8 17.1 %collective-permute-start = (bf16[528,256]{1,0:T(8,128)(2,1)S(1)}, bf16[528,256]{1,0:T(8,128)(2,1)}, u32[]{:S(2)}, u32[]{:S(2)}) collective-permute-start(bf16[528,256]{1,0:T(8,128)(2,1)S(1)} %fusion.32), channel_id=1, source_target_pairs={{0,1},{1,0},{2,3},{3,2},{4,5},{5,4},{6,7},{7,6},{8,9},{9,8},{10,11... | collective-permute-start | bytes 811016 | tf_op jit(solution)/shard_map/ppermute | solution.py:42
  30.2 17.2 %collective-permute-start.4 = (bf16[512,1024]{1,0:T(8,128)(2,1)S(1)}, bf16[512,1024]{1,0:T(8,128)(2,1)}, u32[]{:S(2)}, u32[]{:S(2)}) collective-permute-start(bf16[512,1024]{1,0:T(8,128)(2,1)S(1)} %pad_maximum_fusion.1), channel_id=1, source_target_pairs={{0,8},{1,9},{2,10},{3,11},{4,12},{5,13},{6,14},{7,15},{8,0},{9,1},... | collective-permute-start | bytes 3145736 | tf_op jit(solution)/shard_map/ppermute | solution.py:42
  39.4 17.0 %collective-permute-start.11 = (bf16[512,1024]{1,0:T(8,128)(2,1)S(1)}, bf16[512,1024]{1,0:T(8,128)(2,1)}, u32[]{:S(2)}, u32[]{:S(2)}) collective-permute-start(bf16[512,1024]{1,0:T(8,128)(2,1)S(1)} %pad_maximum_fusion.2), channel_id=1, source_target_pairs={{0,8},{1,9},{2,10},{3,11},{4,12},{5,13},{6,14},{7,15},{8,0},{9,1},... | collective-permute-start | bytes 3145736 | tf_op jit(solution)/shard_map/ppermute | solution.py:42
  47.4 11.0 %copy-start.15 = (bf16[512,128]{1,0:T(8,128)(2,1)}, bf16[512,128]{1,0:T(8,128)(2,1)S(1)}, u32[]{:S(2)}) copy-start(bf16[512,128]{1,0:T(8,128)(2,1)S(1)} %get-tuple-element.33) | copy-start | bytes 393220
  47.4 11.0 %copy-start.17 = (bf16[512,128]{1,0:T(8,128)(2,1)}, bf16[512,128]{1,0:T(8,128)(2,1)S(1)}, u32[]{:S(2)}) copy-start(bf16[512,128]{1,0:T(8,128)(2,1)S(1)} %get-tuple-element.36) | copy-start | bytes 393220
  51.6 16.7 %collective-permute-start.5 = (bf16[128,1024]{1,0:T(8,128)(2,1)S(1)}, bf16[128,1024]{1,0:T(8,128)(2,1)S(1)}, u32[]{:S(2)}, u32[]{:S(2)}) collective-permute-start(bf16[128,1024]{1,0:T(8,128)(2,1)S(1)} %get-tuple-element.23), channel_id=1, source_target_pairs={{0,2},{1,3},{2,4},{3,5},{4,6},{5,7},{6,0},{7,1},{8,10},{9,11},{10,... | collective-permute-start | bytes 786440 | tf_op jit(solution)/shard_map/ppermute | solution.py:42
  53.4 27.9 %collective-permute-start.7 = (bf16[128,1024]{1,0:T(8,128)(2,1)S(1)}, bf16[128,1024]{1,0:T(8,128)(2,1)S(1)}, u32[]{:S(2)}, u32[]{:S(2)}) collective-permute-start(bf16[128,1024]{1,0:T(8,128)(2,1)S(1)} %get-tuple-element.24), channel_id=1, source_target_pairs={{0,6},{1,7},{2,0},{3,1},{4,2},{5,3},{6,4},{7,5},{8,14},{9,15},{10,... | collective-permute-start | bytes 786440 | tf_op jit(solution)/shard_map/ppermute | solution.py:42
  55.5 45.6 %collective-permute-start.6 = (bf16[128,1024]{1,0:T(8,128)(2,1)S(1)}, bf16[128,1024]{1,0:T(8,128)(2,1)S(1)}, u32[]{:S(2)}, u32[]{:S(2)}) collective-permute-start(bf16[128,1024]{1,0:T(8,128)(2,1)S(1)} %get-tuple-element.25), channel_id=1, source_target_pairs={{0,4},{1,5},{2,6},{3,7},{4,0},{5,1},{6,2},{7,3},{8,12},{9,13},{10,... | collective-permute-start | bytes 786440 | tf_op jit(solution)/shard_map/ppermute | solution.py:42
  60.2 41.1 %collective-permute-start.12 = (bf16[128,1024]{1,0:T(8,128)(2,1)S(1)}, bf16[128,1024]{1,0:T(8,128)(2,1)S(1)}, u32[]{:S(2)}, u32[]{:S(2)}) collective-permute-start(bf16[128,1024]{1,0:T(8,128)(2,1)S(1)} %get-tuple-element.26), channel_id=1, source_target_pairs={{0,2},{1,3},{2,4},{3,5},{4,6},{5,7},{6,0},{7,1},{8,10},{9,11},{10,... | collective-permute-start | bytes 786440 | tf_op jit(solution)/shard_map/ppermute | solution.py:42
  61.8 39.4 %collective-permute-start.14 = (bf16[128,1024]{1,0:T(8,128)(2,1)S(1)}, bf16[128,1024]{1,0:T(8,128)(2,1)S(1)}, u32[]{:S(2)}, u32[]{:S(2)}) collective-permute-start(bf16[128,1024]{1,0:T(8,128)(2,1)S(1)} %get-tuple-element.27), channel_id=1, source_target_pairs={{0,6},{1,7},{2,0},{3,1},{4,2},{5,3},{6,4},{7,5},{8,14},{9,15},{10,... | collective-permute-start | bytes 786440 | tf_op jit(solution)/shard_map/ppermute | solution.py:42
  68.2 61.5 %collective-permute-start.13 = (bf16[128,1024]{1,0:T(8,128)(2,1)S(1)}, bf16[128,1024]{1,0:T(8,128)(2,1)S(1)}, u32[]{:S(2)}, u32[]{:S(2)}) collective-permute-start(bf16[128,1024]{1,0:T(8,128)(2,1)S(1)} %get-tuple-element.28), channel_id=1, source_target_pairs={{0,4},{1,5},{2,6},{3,7},{4,0},{5,1},{6,2},{7,3},{8,12},{9,13},{10,... | collective-permute-start | bytes 786440 | tf_op jit(solution)/shard_map/ppermute | solution.py:42
  139.7 23.7 %copy-start.12 = (bf16[512,128]{1,0:T(8,128)(2,1)S(1)}, bf16[512,128]{1,0:T(8,128)(2,1)}, u32[]{:S(2)}) copy-start(bf16[512,128]{1,0:T(8,128)(2,1)} %get-tuple-element.30) | copy-start | bytes 393220
  139.7 23.7 %copy-start.14 = (bf16[512,128]{1,0:T(8,128)(2,1)S(1)}, bf16[512,128]{1,0:T(8,128)(2,1)}, u32[]{:S(2)}) copy-start(bf16[512,128]{1,0:T(8,128)(2,1)} %get-tuple-element.31) | copy-start | bytes 393220
  139.7 23.7 %copy-start.21 = (bf16[512,128]{1,0:T(8,128)(2,1)S(1)}, bf16[512,128]{1,0:T(8,128)(2,1)}, u32[]{:S(2)}) copy-start(bf16[512,128]{1,0:T(8,128)(2,1)} %copy-done.20) | copy-start | bytes 393220
  139.7 11.3 %collective-permute-start.17 = (bf16[128,1024]{1,0:T(8,128)(2,1)}, bf16[128,1024]{1,0:T(8,128)(2,1)S(1)}, u32[]{:S(2)}, u32[]{:S(2)}) collective-permute-start(bf16[128,1024]{1,0:T(8,128)(2,1)} %fusion.8), channel_id=1, source_target_pairs={{0,2},{1,3},{2,4},{3,5},{4,6},{5,7},{6,0},{7,1},{8,10},{9,11},{10,... | collective-permute-start | bytes 786440 | tf_op jit(solution)/shard_map/ppermute | solution.py:42
  139.9 26.4 %collective-permute-start.29 = (bf16[128,2560]{1,0:T(8,128)(2,1)S(1)}, bf16[128,2560]{1,0:T(8,128)(2,1)}, u32[]{:S(2)}, u32[]{:S(2)}) collective-permute-start(bf16[128,2560]{1,0:T(8,128)(2,1)S(1)} %get-tuple-element.43), channel_id=1, source_target_pairs={{0,16},{1,17},{2,18},{3,19},{4,20},{5,21},{6,22},{7,23},{8,24},{9,... | collective-permute-start | bytes 1966088 | tf_op jit(solution)/shard_map/ppermute | solution.py:42
  141.1 29.1 %collective-permute-start.30 = (bf16[128,2560]{1,0:T(8,128)(2,1)S(1)}, bf16[128,2560]{1,0:T(8,128)(2,1)}, u32[]{:S(2)}, u32[]{:S(2)}) collective-permute-start(bf16[128,2560]{1,0:T(8,128)(2,1)S(1)} %get-tuple-element.44), channel_id=1, source_target_pairs={{0,1},{1,0},{2,3},{3,2},{4,5},{5,4},{6,7},{7,6},{8,9},{9,8},{10,11... | collective-permute-start | bytes 1966088 | tf_op jit(solution)/shard_map/ppermute | solution.py:42
  142.4 29.4 %collective-permute-start.31 = (bf16[128,2560]{1,0:T(8,128)(2,1)S(1)}, bf16[128,2560]{1,0:T(8,128)(2,1)}, u32[]{:S(2)}, u32[]{:S(2)}) collective-permute-start(bf16[128,2560]{1,0:T(8,128)(2,1)S(1)} %get-tuple-element.45), channel_id=1, source_target_pairs={{0,17},{1,16},{2,19},{3,18},{4,21},{5,20},{6,23},{7,22},{8,25},{9,... | collective-permute-start | bytes 1966088 | tf_op jit(solution)/shard_map/ppermute | solution.py:42
  143.4 18.0 %collective-permute-start.16 = (bf16[128,1024]{1,0:T(8,128)(2,1)}, bf16[128,1024]{1,0:T(8,128)(2,1)S(1)}, u32[]{:S(2)}, u32[]{:S(2)}) collective-permute-start(bf16[128,1024]{1,0:T(8,128)(2,1)} %fusion.8), channel_id=1, source_target_pairs={{0,4},{1,5},{2,6},{3,7},{4,0},{5,1},{6,2},{7,3},{8,12},{9,13},{10,... | collective-permute-start | bytes 786440 | tf_op jit(solution)/shard_map/ppermute | solution.py:42
  151.0 12.4 %collective-permute-start.15 = (bf16[128,1024]{1,0:T(8,128)(2,1)}, bf16[128,1024]{1,0:T(8,128)(2,1)}, u32[]{:S(2)}, u32[]{:S(2)}) collective-permute-start(bf16[128,1024]{1,0:T(8,128)(2,1)} %fusion.8), channel_id=1, source_target_pairs={{0,6},{1,7},{2,0},{3,1},{4,2},{5,3},{6,4},{7,5},{8,14},{9,15},{10,... | collective-permute-start | bytes 786440 | tf_op jit(solution)/shard_map/ppermute | solution.py:42
  166.3 38.0 %collective-permute-start.18 = (bf16[512,1024]{1,0:T(8,128)(2,1)}, bf16[512,1024]{1,0:T(8,128)(2,1)}, u32[]{:S(2)}, u32[]{:S(2)}) collective-permute-start(bf16[512,1024]{1,0:T(8,128)(2,1)} %convolution_convert_fusion.1), channel_id=1, source_target_pairs={{0,8},{1,9},{2,10},{3,11},{4,12},{5,13},{6,14},{7,15},{8,0},{9,1},... | collective-permute-start | bytes 3145736 | tf_op jit(solution)/shard_map/ppermute | solution.py:42
  175.7 26.4 %copy-start.22 = (bf16[512,128]{1,0:T(8,128)(2,1)S(1)}, bf16[512,128]{1,0:T(8,128)(2,1)}, u32[]{:S(2)}) copy-start(bf16[512,128]{1,0:T(8,128)(2,1)} %copy-done.20) | copy-start | bytes 393220
  175.7 26.4 %copy-start.24 = (bf16[512,128]{1,0:T(8,128)(2,1)S(1)}, bf16[512,128]{1,0:T(8,128)(2,1)}, u32[]{:S(2)}) copy-start(bf16[512,128]{1,0:T(8,128)(2,1)} %copy-done.23) | copy-start | bytes 393220
  175.7 48.1 %collective-permute-start.32 = (bf16[512,2560]{1,0:T(8,128)(2,1)S(1)}, bf16[512,2560]{1,0:T(8,128)(2,1)}, u32[]{:S(2)}, u32[]{:S(2)}) collective-permute-start(bf16[512,2560]{1,0:T(8,128)(2,1)S(1)} %pad_maximum_fusion), channel_id=1, source_target_pairs={{0,8},{1,9},{2,10},{3,11},{4,12},{5,13},{6,14},{7,15},{8,0},{9,1},... | collective-permute-start | bytes 7864328 | tf_op jit(solution)/shard_map/ppermute | solution.py:42
  179.5 24.3 %copy-start.30 = (bf16[128,1024]{1,0:T(8,128)(2,1)}, bf16[128,1024]{1,0:T(8,128)(2,1)S(1)}, u32[]{:S(2)}) copy-start(bf16[128,1024]{1,0:T(8,128)(2,1)S(1)} %fusion.11) | copy-start | bytes 786436
  179.5 11.1 %collective-permute-start.24 = (bf16[128,1024]{1,0:T(8,128)(2,1)S(1)}, bf16[128,1024]{1,0:T(8,128)(2,1)S(1)}, u32[]{:S(2)}, u32[]{:S(2)}) collective-permute-start(bf16[128,1024]{1,0:T(8,128)(2,1)S(1)} %fusion.11), channel_id=1, source_target_pairs={{0,2},{1,3},{2,4},{3,5},{4,6},{5,7},{6,0},{7,1},{8,10},{9,11},{10,... | collective-permute-start | bytes 786440 | tf_op jit(solution)/shard_map/ppermute | solution.py:42
  179.6 21.8 %collective-permute-start.23 = (bf16[128,1024]{1,0:T(8,128)(2,1)S(1)}, bf16[128,1024]{1,0:T(8,128)(2,1)S(1)}, u32[]{:S(2)}, u32[]{:S(2)}) collective-permute-start(bf16[128,1024]{1,0:T(8,128)(2,1)S(1)} %fusion.11), channel_id=1, source_target_pairs={{0,4},{1,5},{2,6},{3,7},{4,0},{5,1},{6,2},{7,3},{8,12},{9,13},{10,... | collective-permute-start | bytes 786440 | tf_op jit(solution)/shard_map/ppermute | solution.py:42
  183.7 17.7 %collective-permute-start.22 = (bf16[128,1024]{1,0:T(8,128)(2,1)S(1)}, bf16[128,1024]{1,0:T(8,128)(2,1)S(1)}, u32[]{:S(2)}, u32[]{:S(2)}) collective-permute-start(bf16[128,1024]{1,0:T(8,128)(2,1)S(1)} %fusion.11), channel_id=1, source_target_pairs={{0,6},{1,7},{2,0},{3,1},{4,2},{5,3},{6,4},{7,5},{8,14},{9,15},{10,... | collective-permute-start | bytes 786440 | tf_op jit(solution)/shard_map/ppermute | solution.py:42
  190.6 10.8 %copy-start.32 = (bf16[128,1024]{1,0:T(8,128)(2,1)}, bf16[128,1024]{1,0:T(8,128)(2,1)S(1)}, u32[]{:S(2)}) copy-start(bf16[128,1024]{1,0:T(8,128)(2,1)S(1)} %collective-permute-done.24) | copy-start | bytes 786436
  203.8 7.0 %collective-permute-start.25 = (bf16[512,1024]{1,0:T(8,128)(2,1)}, bf16[512,1024]{1,0:T(8,128)(2,1)}, u32[]{:S(2)}, u32[]{:S(2)}) collective-permute-start(bf16[512,1024]{1,0:T(8,128)(2,1)} %convolution_convert_fusion), channel_id=1, source_target_pairs={{0,8},{1,9},{2,10},{3,11},{4,12},{5,13},{6,14},{7,15},{8,0},{9,1},... | collective-permute-start | bytes 3145736 | tf_op jit(solution)/shard_map/ppermute | solution.py:42
  207.3 9.2 %collective-permute-start.19 = (bf16[128,1024]{1,0:T(8,128)(2,1)S(1)}, bf16[128,1024]{1,0:T(8,128)(2,1)S(1)}, u32[]{:S(2)}, u32[]{:S(2)}) collective-permute-start(bf16[128,1024]{1,0:T(8,128)(2,1)S(1)} %get-tuple-element.15), channel_id=1, source_target_pairs={{0,16},{1,17},{2,18},{3,19},{4,20},{5,21},{6,22},{7,23},{8,24},{9,... | collective-permute-start | bytes 786440 | tf_op jit(solution)/shard_map/ppermute | solution.py:42
  208.2 14.5 %collective-permute-start.21 = (bf16[128,1024]{1,0:T(8,128)(2,1)S(1)}, bf16[128,1024]{1,0:T(8,128)(2,1)S(1)}, u32[]{:S(2)}, u32[]{:S(2)}) collective-permute-start(bf16[128,1024]{1,0:T(8,128)(2,1)S(1)} %get-tuple-element.16), channel_id=1, source_target_pairs={{0,17},{1,16},{2,19},{3,18},{4,21},{5,20},{6,23},{7,22},{8,25},{9,... | collective-permute-start | bytes 786440 | tf_op jit(solution)/shard_map/ppermute | solution.py:42
  209.9 13.8 %collective-permute-start.20 = (bf16[128,1024]{1,0:T(8,128)(2,1)S(1)}, bf16[128,1024]{1,0:T(8,128)(2,1)S(1)}, u32[]{:S(2)}, u32[]{:S(2)}) collective-permute-start(bf16[128,1024]{1,0:T(8,128)(2,1)S(1)} %get-tuple-element.17), channel_id=1, source_target_pairs={{0,1},{1,0},{2,3},{3,2},{4,5},{5,4},{6,7},{7,6},{8,9},{9,8},{10,11... | collective-permute-start | bytes 786440 | tf_op jit(solution)/shard_map/ppermute | solution.py:42
  215.1 21.9 %collective-permute-start.26 = (bf16[128,1024]{1,0:T(8,128)(2,1)}, bf16[128,1024]{1,0:T(8,128)(2,1)S(1)}, u32[]{:S(2)}, u32[]{:S(2)}) collective-permute-start(bf16[128,1024]{1,0:T(8,128)(2,1)} %get-tuple-element.18), channel_id=1, source_target_pairs={{0,16},{1,17},{2,18},{3,19},{4,20},{5,21},{6,22},{7,23},{8,24},{9,... | collective-permute-start | bytes 786440 | tf_op jit(solution)/shard_map/ppermute | solution.py:42
  216.5 20.5 %collective-permute-start.28 = (bf16[128,1024]{1,0:T(8,128)(2,1)}, bf16[128,1024]{1,0:T(8,128)(2,1)}, u32[]{:S(2)}, u32[]{:S(2)}) collective-permute-start(bf16[128,1024]{1,0:T(8,128)(2,1)} %get-tuple-element.19), channel_id=1, source_target_pairs={{0,17},{1,16},{2,19},{3,18},{4,21},{5,20},{6,23},{7,22},{8,25},{9,... | collective-permute-start | bytes 786440 | tf_op jit(solution)/shard_map/ppermute | solution.py:42
  222.6 14.3 %collective-permute-start.27 = (bf16[128,1024]{1,0:T(8,128)(2,1)}, bf16[128,1024]{1,0:T(8,128)(2,1)}, u32[]{:S(2)}, u32[]{:S(2)}) collective-permute-start(bf16[128,1024]{1,0:T(8,128)(2,1)} %get-tuple-element.20), channel_id=1, source_target_pairs={{0,1},{1,0},{2,3},{3,2},{4,5},{5,4},{6,7},{7,6},{8,9},{9,8},{10,11... | collective-permute-start | bytes 786440 | tf_op jit(solution)/shard_map/ppermute | solution.py:42
  231.2 13.3 %collective-permute-start.33 = (bf16[64,2176]{1,0:T(8,128)(2,1)S(1)}, bf16[64,2176]{1,0:T(8,128)(2,1)S(1)}, u32[]{:S(2)}, u32[]{:S(2)}) collective-permute-start(bf16[64,2176]{1,0:T(8,128)(2,1)S(1)} %get-tuple-element.12), channel_id=1, source_target_pairs={{0,2},{1,3},{2,4},{3,5},{4,6},{5,7},{6,0},{7,1},{8,10},{9,11},{10,... | collective-permute-start | bytes 835592 | tf_op jit(solution)/shard_map/ppermute | solution.py:42
  236.7 13.1 %collective-permute-start.35 = (bf16[64,2176]{1,0:T(8,128)(2,1)S(1)}, bf16[64,2176]{1,0:T(8,128)(2,1)S(1)}, u32[]{:S(2)}, u32[]{:S(2)}) collective-permute-start(bf16[64,2176]{1,0:T(8,128)(2,1)S(1)} %get-tuple-element.13), channel_id=1, source_target_pairs={{0,6},{1,7},{2,0},{3,1},{4,2},{5,3},{6,4},{7,5},{8,14},{9,15},{10,... | collective-permute-start | bytes 835592 | tf_op jit(solution)/shard_map/ppermute | solution.py:42
  238.3 21.9 %collective-permute-start.34 = (bf16[64,2176]{1,0:T(8,128)(2,1)S(1)}, bf16[64,2176]{1,0:T(8,128)(2,1)S(1)}, u32[]{:S(2)}, u32[]{:S(2)}) collective-permute-start(bf16[64,2176]{1,0:T(8,128)(2,1)S(1)} %get-tuple-element.14), channel_id=1, source_target_pairs={{0,4},{1,5},{2,6},{3,7},{4,0},{5,1},{6,2},{7,3},{8,12},{9,13},{10,... | collective-permute-start | bytes 835592 | tf_op jit(solution)/shard_map/ppermute | solution.py:42
  244.5 18.4 %copy-start.1 = (f32[1024]{0:T(1024)S(1)}, f32[1024]{0:T(1024)}, u32[]{:S(2)}) copy-start(f32[1024]{0:T(1024)} %param.12) | copy-start | bytes 12292
  (28 other events, 101.6 us)
Sparse Core Ops, SparseCore 0:
  11.0 115.7 all-gather.1

commit v2 on v1

v2 whole, which is shorter than its diff:
```python
import functools

import jax
import jax.numpy as jnp
from jax import lax
from jax.experimental import pallas as pl
from jax.experimental.pallas import tpu as pltpu
from jax.sharding import PartitionSpec as P

boost = 2.0
AXES = ("row", "col")
CORES = 2
LINE = 4
ORDER = (0, 2, 1, 3)
CHUNKS = 2
LOW = jnp.bfloat16
F32 = jnp.float32


def dot(left, right, dims):
    return lax.dot_general(left, right, ((dims[0], dims[1]), ((), ())), preferred_element_type=F32)


def after(value, *others):
    return lax.optimization_barrier((value, *others))[0]


def one_of(value, index, axis):
    return lax.dynamic_index_in_dim(value, index, axis, keepdims=False)


def lookup(table, index):
    found = 0
    for k, entry in enumerate(table):
        found = found + entry * (index == k).astype(jnp.int32)
    return found


def call(kernel, outs, scratch, *operands, numbers=0):
    whole = pl.BlockSpec(memory_space=pltpu.VMEM)
    return pl.pallas_call(
        kernel,
        out_shape=outs,
        in_specs=[pl.BlockSpec(memory_space=pltpu.SMEM)] * numbers + [whole] * (len(operands) - numbers),
        out_specs=[whole] * len(outs),
        scratch_shapes=scratch,
        compiler_params=pltpu.CompilerParams(vmem_limit_bytes=56 * 2**20),
    )(*operands)


def like(*shape, kind=LOW):
    return jax.ShapeDtypeStruct(shape, kind)


class Place:
    def __init__(self):
        self.rows = lax.axis_size("row")
        self.cols = lax.axis_size("col")
        self.xs = self.rows // CORES
        self.bs = self.cols // LINE
        self.row = lax.axis_index("row")
        self.col = lax.axis_index("col")
        self.x = self.row // CORES
        self.core = self.row % CORES
        self.a = self.col // self.bs
        self.b = self.col % self.bs
        self.chips = [(dx, db) for db in range(self.bs) for dx in range(self.xs)]
        self.numbers = jnp.stack([self.a, self.b, self.x, self.core]).astype(jnp.int32)

    def index(self, x, core, a, b):
        return ((x % self.xs) * CORES + core % CORES) * self.cols + (a % LINE) * self.bs + b % self.bs

    def send(self, value, dx=0, dcore=0, db=0, flip=0):
        pairs = [
            (self.index(x, core, a, b), self.index(x + dx, core + dcore, a ^ flip, b + db))
            for x in range(self.xs)
            for core in range(CORES)
            for a in range(LINE)
            for b in range(self.bs)
        ]
        return lax.ppermute(value, AXES, pairs)


def put_blocks(xs, bs, place, weights, part, mask, db, outs):
    a, b, x, core = (place[i] for i in range(4))
    size = weights.shape[1]
    rows = xs * CORES
    eye = (
        lax.broadcasted_iota(jnp.int32, (size, size), 0) == lax.broadcasted_iota(jnp.int32, (size, size), 1)
    ).astype(F32)
    tile = lax.rem(b + db, bs)
    for k, flip in enumerate(ORDER):
        line = (a ^ flip) * bs + b
        row_block = (x * CORES + core) * (LINE * bs) + line
        diagonal = eye * (boost * weights[pl.ds(line, 1), :])
        values = part(k)
        for dcore in range(CORES):
            for dx in range(xs):
                block = lax.rem(x + dx, xs) * CORES + lax.rem(core + dcore, CORES)
                node_block = a * (bs * rows) + tile * rows + block
                total = diagonal * (row_block == node_block).astype(F32)
                for slot in range(values.shape[1] // size):
                    total = total + values[:, slot * size : (slot + 1) * size] * mask(k, slot, block)
                outs[dcore][k * size : (k + 1) * size, dx * size : (dx + 1) * size] = total.astype(LOW)


def own_blocks_kernel(xs, bs, slots, place, cols, counts, block_vals, weights, *outs):
    a, b = place[0], place[1]
    size = weights.shape[1]

    def line(k, dest):
        return (a ^ ORDER[k]) * bs + dest

    def rows(k, dest):
        return block_vals[pl.ds(pl.multiple_of(line(k, dest) * size, size), size), :]

    def column(k, slot, dest):
        at = line(k, dest)
        return jnp.where(slot < counts[0, at], cols[slot, at], -1)

    for db in range(1, bs):
        out = outs[CORES + db - 1]
        dest = lax.rem(b - db + bs, bs)
        for k in range(LINE):
            out[k * size : (k + 1) * size, :] = rows(k, dest)
        at_row = lax.broadcasted_iota(jnp.int32, (16, slots * size), 0)
        head = jnp.zeros((16, slots * size), jnp.int32)
        for k in range(LINE):
            for slot in range(slots):
                head = jnp.where(at_row == k * slots + slot, column(k, slot, dest), head)
        out[LINE * size :, :] = head.astype(F32).astype(LOW)
    put_blocks(
        xs,
        bs,
        place,
        weights,
        lambda k: rows(k, b).astype(F32),
        lambda k, slot, block: (column(k, slot, b) == block).astype(F32),
        0,
        outs[:CORES],
    )


def sent_blocks_kernel(xs, bs, slots, db, place, got, weights, *outs):
    size = weights.shape[1]
    head = got[LINE * size :, :].astype(F32)

    def mask(k, slot, block):
        at = k * slots + slot
        return (head[at : at + 1, :size] == block.astype(F32)).astype(F32)

    put_blocks(
        xs, bs, place, weights, lambda k: got[k * size : (k + 1) * size, :].astype(F32), mask, db, outs
    )


def operator(at, block_vals, block_cols, block_counts, self_weight, size):
    slots = block_cols.shape[0]
    weights = self_weight.reshape(-1, size)
    dense = like(LINE * size, at.xs * size)
    own, other, *sent = call(
        functools.partial(own_blocks_kernel, at.xs, at.bs, slots),
        [dense] * CORES + [like(LINE * size + 16, slots * size)] * (at.bs - 1),
        [],
        at.numbers,
        block_cols,
        block_counts,
        block_vals,
        weights,
        numbers=3,
    )
    result = [[own, other]]
    arrived = [at.send(value, db=-db) for db, value in enumerate(sent, 1)]
    for db, got in enumerate(arrived, 1):
        kernel = functools.partial(sent_blocks_kernel, at.xs, at.bs, slots, db)
        result.append(call(kernel, [dense] * CORES, [], at.numbers, got, weights, numbers=1))
    return result, arrived


def sums_kernel(xs, bs, *refs):
    per = CORES * xs
    ops, pieces = refs[: CORES * bs], refs[CORES * bs : CORES * bs + per * bs]
    keep, send, left, right = refs[CORES * bs + per * bs :]
    size, wide = pieces[0].shape[0], ops[0].shape[1]
    for i, op in enumerate(ops):
        left[:, i * wide : (i + 1) * wide] = op[...]
    for i, piece in enumerate(pieces):
        right[i * size : (i + 1) * size, :] = piece[...]
    half = left.shape[0] // 2
    keep[...] = dot(left[:half], right[...], ((1,), (0,)))
    send[...] = dot(left[half:], right[...], ((1,), (0,))).astype(LOW)


def sums(at, ops, own, other):
    size, chunk = own[0, 0].shape
    pieces = [held[dx, db] for db in range(at.bs) for held in (own, other) for dx in range(at.xs)]
    rows, depth = LINE * size, len(pieces) * size
    return call(
        functools.partial(sums_kernel, at.xs, at.bs),
        [like(rows // 2, chunk, kind=F32), like(rows // 2, chunk)],
        [pltpu.VMEM((rows, depth), LOW), pltpu.VMEM((depth, chunk), LOW)],
        *[op for pair in ops for op in pair],
        *pieces,
    )


def back_kernel(n_ops, *refs):
    ops, lines, rest = refs[:n_ops], refs[n_ops : n_ops + 3], refs[n_ops + 3 :]
    right = jnp.concatenate([line[...] for line in lines], 0)
    parts = [dot(op[...], right, ((0,), (0,))) for op in ops]
    if len(rest) == 1:
        rows = parts[0].shape[0]
        for i, part in enumerate(parts):
            rest[0][i * rows : (i + 1) * rows, :] = part.astype(LOW)
        return
    got, outs = rest[0], rest[1:]
    size = outs[0].shape[0]
    per = parts[0].shape[0] // size
    for i, out in enumerate(outs):
        k = i % per * size
        total = parts[i // per][k : k + size] + got[i * size : (i + 1) * size, :].astype(F32)
        out[...] = total.astype(out.dtype)


def add_up_kernel(n_keeps, *refs):
    *parts, out = refs
    wide = parts[0].shape[1]
    per = len(parts) // n_keeps
    for k in range(n_keeps):
        total = parts[k * per][...]
        for part in parts[k * per + 1 : (k + 1) * per]:
            total = total + part[...].astype(F32)
        out[:, k * wide : (k + 1) * wide] = total


def along_x(at, value):
    return [value] + [at.send(value, dx=-dx) for dx in range(1, at.xs)]


def along_b(at, value):
    return [value] + [at.send(value, db=-db) for db in range(1, at.bs)]


def gathered_halves(at, halves, gate, last_gate=None):
    arrays = list(halves)
    held = {(0, 0, 0, 0): (0, 0), (0, 0, 0, 1): (1, 0)}

    def keep(value, places, half):
        arrays.append(value)
        for i, (dx, db) in enumerate(places):
            held[0, dx, db, half] = (len(arrays) - 1, i)

    left = along_x(at, halves[0])
    right = along_b(at, halves[1])
    steps = [left[1:] + right[1:], []]
    for dx in range(1, at.xs):
        keep(left[dx], [(dx, 0)], 0)
    for db in range(1, at.bs):
        keep(right[db], [(0, db)], 1)
    left, right = after(jnp.concatenate(left), gate), after(jnp.concatenate(right), gate)
    for db in range(1, at.bs):
        keep(at.send(left, db=-db), [(dx, db) for dx in range(at.xs)], 0)
        steps[1].append(arrays[-1])
    for dx in range(1, at.xs):
        keep(at.send(right, dx=-dx), [(dx, db) for db in range(at.bs)], 1)
        steps[1].append(arrays[-1])
    count, early = len(arrays), 2 + len(steps[0])
    gates = [] if last_gate is None else [last_gate]
    across = arrays[:early] + [after(value, *gates) for value in arrays[early:]]
    arrays = arrays + [at.send(value, dcore=1) for value in across]
    for (_, dx, db, half), (k, i) in list(held.items()):
        held[1, dx, db, half] = (k + count, i)
    return arrays, held, steps


def line_weight(at, weight):
    count, width = weight.shape
    far = at.send(weight, flip=2)
    near = at.send(jnp.concatenate([weight, far]), flip=1)
    pieces = jnp.concatenate([weight, far, near]).reshape(LINE, count, width)
    places = [ORDER.index(k) for k in range(LINE)]
    return jnp.concatenate([one_of(pieces, lookup(places, at.a ^ k), 0) for k in range(LINE)])


def dense_kernel(held, xs, bs, lanes, n_held, place, *refs):
    totals, lasts, refs = refs[:CHUNKS], refs[CHUNKS : 2 * CHUNKS], refs[2 * CHUNKS :]
    arrays, refs = refs[:n_held], refs[n_held:]
    bias, out_grad, act_ref, left_ref, right_ref, mine_ref, other_ref = refs[:7]
    backs, (agg_ref, turned, acc, back) = refs[7 : 7 + CHUNKS], refs[7 + CHUNKS :]
    b, x, core = place[1], place[2], place[3]
    width = bias.shape[1]
    half = width // 2
    group = bs * lanes
    wide = width // CHUNKS

    for k in range(CHUNKS):
        agg_ref[:, k * wide : (k + 1) * wide] = (totals[k][...] + lasts[k][...].astype(F32)).astype(LOW)
    count = lanes // LINE
    at_in = lax.broadcasted_iota(jnp.int32, (group, group), 0)
    at_out = lax.broadcasted_iota(jnp.int32, (group, group), 1)
    db, inner = at_out // lanes, at_out % lanes
    source = (inner // count) * (bs * count) + lax.rem(b + db, bs) * count + inner % count
    turn = (at_in == source).astype(F32).astype(LOW)
    for r in range(width // group):
        at_r = slice(r * group, (r + 1) * group)
        turned[:, at_r] = dot(agg_ref[:, at_r], turn, ((1,), (0,))).astype(LOW)

    places = [(dcore, dx, db) for dcore in range(CORES) for db in range(bs) for dx in range(xs)]

    def columns(dcore, dx, db):
        row = lax.rem(x + dx, xs) * CORES + lax.rem(core + dcore, CORES)
        return pl.ds(pl.multiple_of(row * group + db * lanes, lanes), lanes)

    acc[...] = jnp.broadcast_to(bias[...], acc.shape)
    for at in places:
        left = turned[:, columns(*at)]
        for h in range(2):
            k, i = held[*at, h]
            acc[:, h * half : (h + 1) * half] += dot(left, arrays[k][i], ((1,), (0,)))
    for out, dcore in ((mine_ref, 0), (other_ref, 1)):
        for db in range(bs):
            for dx in range(xs):
                out[db, dx] = turned[:, columns(dcore, dx, db)]
    pre = acc[...]
    phi = 0.5 * (1.0 + lax.erf(pre * (0.5**0.5)))
    act_ref[...] = (pre * phi).astype(LOW)
    slope = phi + pre * (jnp.exp(-0.5 * pre * pre) * 0.3989422804014327)
    pre_low = (out_grad[...].astype(F32) * slope).astype(LOW)
    left_ref[0] = pre_low[:, :half]
    right_ref[0] = pre_low[:, half:]
    for at in places:
        total = 0.0
        for h, ref in enumerate((left_ref, right_ref)):
            k, i = held[*at, h]
            total = total + dot(ref[0], arrays[k][i], ((1,), (1,)))
        back[:, columns(*at)] = total.astype(LOW)
    for r in range(width // group):
        k, i = divmod(r * group, wide)
        backs[k][:, i : i + group] = dot(back[:, r * group : (r + 1) * group], turn, ((1,), (1,))).astype(LOW)


def grad_kernel(held, rows_held, xs, bs, lanes, n_arrays, n_rows, place, *refs):
    arrays, row_arrays = refs[:n_arrays], refs[n_arrays : n_arrays + n_rows]
    keep, send, left, right, product, sums_ref = refs[n_arrays + n_rows :]
    a, b, x, core = (place[i] for i in range(4))
    size, width = left.shape[0] // (xs * bs * CORES), right.shape[1]
    half, count, group = width // 2, lanes // LINE, bs * lanes
    places = [(dcore, dx, db) for dcore in range(CORES) for db in range(bs) for dx in range(xs)]
    total = jnp.zeros((1, width), F32)
    for n, at in enumerate(places):
        rows = slice(n * size, (n + 1) * size)
        k, i = rows_held[at]
        left[rows, :] = row_arrays[k][i]
        for h in range(2):
            k, i = held[*at, h]
            right[rows, h * half : (h + 1) * half] = arrays[k][i]
    product[...] = dot(left[...], right[...], ((0,), (0,)))
    total = jnp.sum(right[...].astype(F32), 0, keepdims=True)
    sums_ref[...] = jnp.broadcast_to(total, sums_ref.shape)
    own = sums_ref[0:1, pl.ds(pl.multiple_of((x * CORES + core) * group, group), group)]
    at_row = lax.broadcasted_iota(jnp.int32, (lanes, group), 0)
    at_lane = lax.broadcasted_iota(jnp.int32, (lanes, group), 1)
    source = (at_row // count) * (bs * count) + b * count + at_row % count
    column = jnp.sum(jnp.where(at_lane == source, own, 0.0), 1, keepdims=True)
    product_bias = jnp.broadcast_to(column, (lanes, 128))
    left_bias = keep.shape[1] - 128
    for k, flip in enumerate(ORDER):
        rows = pl.ds(pl.multiple_of((a ^ flip) * count, count), count)
        part = product[rows, :]
        picked = jnp.zeros((count, 128), F32)
        for line in range(LINE):
            mine = ((a ^ flip) == line).astype(F32)
            picked = picked + product_bias[line * count : (line + 1) * count] * mine
        if k < 2:
            keep[k * count : (k + 1) * count, :left_bias] = part
            keep[k * count : (k + 1) * count, left_bias:] = picked
        else:
            at_out = slice((k - 2) * count, (k - 1) * count)
            send[at_out, :left_bias] = part.astype(LOW)
            send[at_out, left_bias:] = two_parts(picked)


def two_parts(value):
    high = value.astype(LOW)
    rest = (value - high.astype(F32)).astype(LOW)
    lane = lax.broadcasted_iota(jnp.int32, value.shape, 1)
    return jnp.where(lane == 0, high.astype(F32), jnp.where(lane == 1, rest.astype(F32), 0.0)).astype(LOW)


def folded(kept, got):
    width = kept.shape[1] - 128
    tail = got[:, width:].astype(F32)
    return kept[:, :width] + got[:, :width].astype(F32), kept[:, width:] + (tail[:, 0:1] + tail[:, 1:2])


def fold_kernel(kept, got, total, far):
    count = total.shape[0]
    width = total.shape[1] - 128
    part, bias = folded(kept[:count, :], got[:count, :])
    total[:, :width] = part
    total[:, width:] = bias
    part, bias = folded(kept[count:, :], got[count:, :])
    far[:, :width] = part.astype(LOW)
    far[:, width:] = two_parts(bias)


def last_fold_kernel(kept, got, weight_out, bias_out):
    part, bias = folded(kept[...], got[...])
    weight_out[...] = part
    bias_out[...] = bias


def exchanged_rows(at, mine, other):
    got = at.send(other, dcore=1)
    both = jnp.stack([mine, got])
    arrays = [both]
    held = {(dcore, 0, 0): (0, (dcore, 0, 0)) for dcore in range(CORES)}
    sources = [both[:, :, 0]]
    for dx in range(1, at.xs):
        sources.append(at.send(both[:, :, dx], dx=dx))
        arrays.append(sources[-1])
        for dcore in range(CORES):
            held[dcore, at.xs - dx, 0] = (len(arrays) - 1, (dcore, 0))
    for db in range(1, at.bs):
        arrays.append(at.send(jnp.stack([source[:, db] for source in sources]), db=db))
        for dx in range(at.xs):
            for dcore in range(CORES):
                held[dcore, -dx % at.xs, at.bs - db] = (len(arrays) - 1, (dx, dcore))
    return arrays, held


def shards(node_feats, block_vals, block_cols, block_counts, self_weight, weight, bias, out_grad):
    at = Place()
    size, width = node_feats.shape
    chunk = width // CHUNKS
    own_rows = weight.shape[0]
    lanes = LINE * own_rows
    aligned = lanes % 128 == 0
    if aligned:
        weight_line = line_weight(at, weight)
    ops, arrived = operator(at, block_vals, block_cols, block_counts, self_weight, size)

    keeps, sends = [], []
    for k in range(CHUNKS):
        mine = node_feats[:, k * chunk : (k + 1) * chunk]
        if k:
            mine = after(mine, *[own[chip] for chip in at.chips[1:2]])
        own = {(dx, db): at.send(mine, dx=-dx, db=-db) if dx or db else mine for dx, db in at.chips}
        other = {chip: at.send(value, dcore=1) for chip, value in own.items()}
        keep, send = sums(at, ops, own, other)
        keeps.append(keep)
        sends.append(send)
    totals, lasts, nears = [], [], []
    for k in range(CHUNKS):
        nears.append(at.send(sends[k], flip=1))
        near = nears[k].astype(F32)
        far = (keeps[k][size:] + near[size:]).astype(LOW)
        if lasts:
            far = after(far, lasts[-1])
        totals.append(keeps[k][:size] + near[:size])
        lasts.append(at.send(far, flip=2))

    if not aligned:
        return plain_rest(at, ops, totals, lasts, weight, bias, out_grad)
    weight_line = after(weight_line, sends[0], *own.values())
    halves = [weight_line[None, :, : width // 2], weight_line[None, :, width // 2 :]]
    arrays, held, _ = gathered_halves(at, halves, nears[0], lasts[0])
    activations, left, right, mine, other, *backs = call(
        functools.partial(dense_kernel, held, at.xs, at.bs, lanes, len(arrays)),
        [like(size, width)]
        + [like(1, size, width // 2)] * 2
        + [like(at.bs, at.xs, size, lanes)] * 2
        + [like(size, chunk)] * CHUNKS,
        [pltpu.VMEM((size, width), kind) for kind in (LOW, LOW, F32, LOW)],
        at.numbers,
        *totals,
        *lasts,
        *arrays,
        bias[None, :],
        out_grad,
        numbers=1,
    )

    fars = [at.send(backs[0], flip=2)]
    arrays, held, steps = gathered_halves(at, [left, right], left)
    row_arrays, rows_held = exchanged_rows(at, mine, other)
    nears = []
    for k in range(CHUNKS):
        if k:
            fars.append(at.send(after(backs[k], fars[-1]), flip=2))
        nears.append(at.send(after(jnp.concatenate([backs[k], fars[k]]), *steps[0]), flip=1))
    feat, parts = feat_sums(at, ops, after(nears[0], fars[1], *steps[1], *row_arrays), backs[0], fars[0])
    gates = feat[1:]
    keep, send = call(
        functools.partial(
            grad_kernel, held, rows_held, at.xs, at.bs, lanes, len(arrays), len(row_arrays)
        ),
        [like(2 * own_rows, width + 128, kind=F32), like(2 * own_rows, width + 128)],
        [
            pltpu.VMEM((size * len(at.chips) * CORES, lanes), LOW),
            pltpu.VMEM((size * len(at.chips) * CORES, width), LOW),
            pltpu.VMEM((lanes, width), F32),
            pltpu.VMEM((8, width), F32),
        ],
        at.numbers,
        *[after(arrays[0], *parts)],
        *arrays[1:],
        *row_arrays,
        numbers=1,
    )
    for k in range(1, CHUNKS):
        more, parts = feat_sums(at, ops, after(nears[k], send), backs[k], fars[k])
        feat = feat + more
    near = after(at.send(after(send, nears[-1]), flip=1), *parts, *gates)
    total, far = call(fold_kernel, [like(own_rows, width + 128, kind=F32), like(own_rows, width + 128)], [], keep, near)
    far = at.send(far, flip=2)
    [feat_grad] = call(functools.partial(add_up_kernel, CHUNKS), [like(size, width, kind=F32)], [], *feat)
    weight_grad, bias_grad = call(
        last_fold_kernel, [like(own_rows, width, kind=F32), like(own_rows, 128, kind=F32)], [], total, far
    )
    return activations, feat_grad, weight_grad, bias_grad[:, 0]


def feat_sums(at, ops, near, back, far):
    size, chunk = back.shape
    rows = len(at.chips) * size
    lines = [back, far, near]
    n_ops = len(ops)
    kernel = functools.partial(back_kernel, n_ops)
    [across] = call(kernel, [like(rows, chunk)], [], *[pair[1] for pair in ops], *lines)
    got = at.send(across, dcore=1)
    outs = [like(size, chunk, kind=F32)] + [like(size, chunk)] * (len(at.chips) - 1)
    parts = call(kernel, outs, [], *[pair[0] for pair in ops], *lines, got)
    sent = [at.send(part, dx=dx, db=db) for part, (dx, db) in zip(parts[1:], at.chips[1:])]
    return [parts[0]] + sent, parts


def plain_rest(at, ops, totals, lasts, weight, bias, out_grad):
    size, width = out_grad.shape
    chunk = width // CHUNKS
    own_rows = weight.shape[0]
    lanes = LINE * own_rows
    agg = jnp.concatenate([t + got.astype(F32) for t, got in zip(totals, lasts)], 1).astype(LOW)
    whole_weight = lax.all_gather(weight, AXES, axis=0, tiled=True)
    pre = dot(agg, whole_weight, ((1,), (0,))) + bias[None, :]
    phi = 0.5 * (1.0 + lax.erf(pre * (0.5**0.5)))
    activations = (pre * phi).astype(LOW)
    slope = phi + pre * (jnp.exp(-0.5 * pre * pre) * 0.3989422804014327)
    pre_low = (out_grad.astype(F32) * slope).astype(LOW)
    feat = []
    for k in range(CHUNKS):
        back = dot(pre_low, whole_weight[k * chunk : (k + 1) * chunk], ((1,), (1,))).astype(LOW)
        far = at.send(back, flip=2)
        near = at.send(jnp.concatenate([back, far]), flip=1)
        feat = feat + feat_sums(at, ops, near, back, far)[0]
    [feat_grad] = call(functools.partial(add_up_kernel, CHUNKS), [like(size, width, kind=F32)], [], *feat)

    groups = agg.reshape(size, at.rows, LINE, at.bs, own_rows)
    groups = jnp.concatenate([lax.dynamic_slice_in_dim(groups, at.a ^ flip, 1, 2) for flip in ORDER], 2)
    messages = []
    for dx, db in at.chips:
        dest_x = (at.x + dx) % at.xs
        wide = one_of(groups, (at.b + db) % at.bs, 3)
        picked = [
            one_of(wide, dest_x * CORES + (at.core + dcore) % CORES, 1).reshape(size, lanes) for dcore in range(CORES)
        ]
        message = jnp.concatenate([pre_low] + picked, 1)
        messages.append(at.send(message, dx=dx, db=db) if dx or db else message)
    own = jnp.concatenate(messages)
    other = at.send(own, dcore=1)
    weight_part = dot(own[:, width : width + lanes], own[:, :width], ((0,), (0,)))
    weight_part = weight_part + dot(other[:, width + lanes :], other[:, :width], ((0,), (0,)))
    bias_part = jnp.sum(own[:, :width].astype(F32), 0) + jnp.sum(other[:, :width].astype(F32), 0)
    bias_part = one_of(one_of(bias_part.reshape(at.rows, LINE, at.bs, own_rows), at.row, 0), at.b, 1)
    bias_part = jnp.concatenate([one_of(bias_part, at.a ^ flip, 0) for flip in ORDER])
    near = at.send(weight_part[2 * own_rows :].astype(LOW), flip=1).astype(F32)
    kept = weight_part[: 2 * own_rows] + near
    far = at.send(kept[own_rows:].astype(LOW), flip=2).astype(F32)
    near_bias = at.send(bias_part[2 * own_rows :], flip=1)
    kept_bias = bias_part[: 2 * own_rows] + near_bias
    bias_grad = kept_bias[:own_rows] + at.send(kept_bias[own_rows:], flip=2)
    return activations, feat_grad, kept[:own_rows] + far, bias_grad


def solution(mesh):
    placed = (
        P(("col", "row"), None),
        P("row", "col"),
        P("col", "row"),
        P("col", "row"),
        P("row"),
        P(("row", "col"), None),
        P(),
        P(("row", "col"), None),
    )
    return jax.shard_map(
        shards,
        mesh=mesh,
        in_specs=placed,
        out_specs=(
            P(("row", "col"), None),
            P(("col", "row"), None),
            P(("row", "col"), None),
            P(("row", "col")),
        ),
        check_vma=False,
    )
```

time: 270 us -> 222 us (0.82)
  Pallas kernels: 0 us -> 47.4 us
  matrix products: 34.5 us -> 0 us
  waiting for transfers between devices: 128 us -> 106 us
  other arithmetic: 22.6 us -> 3.5 us
  between operations: 14.9 us -> 1.28 us
  starting transfers between devices: 58.2 us -> 46.2 us
  local copies, waits for them, and re-layouts: 11.1 us -> 17.4 us
    pallas_call x0 -> x13, Pallas kernels: none -> 47.4 us  [call(): pl.pallas_call(kernel, out_shape=outs, in_specs=[pl.BlockSpec(memory_spac...]
    dot_general x13 -> x0, matrix products: 34.5 us -> none  [dot(): lax.dot_general(left, right, ((dims[0], dims[1]), ((), ())), preferred_el...]
    ppermute x36 -> x58, waiting for transfers between devices: 128 us -> 106 us  [send(): return lax.ppermute(value, AXES, pairs)]
    ppermute x36 -> x58, starting transfers between devices: 58.2 us -> 46.2 us  [send(): return lax.ppermute(value, AXES, pairs)]
    unnamed x80 -> x138, local copies, waits for them, and re-layouts: 2.86 us -> 11 us
    concatenate x14 -> x9, other arithmetic: 7.74 us -> 0.6 us  [the longest x2 0.15 us: gathered_halves(): jnp.concatenate(right)]
    add x5 -> x0, other arithmetic: 3.92 us -> none  [the longest x1 1.94 us: shards(): weight_grad = weight_grad + got[:, :width]]
    convert_element_type x13 -> x4, other arithmetic: 5.21 us -> 2.18 us  [the longest x2 1.97 us: shards(): far = (keeps[k][size:] + near[size:]).astype(LOW)]
  transfers between devices with their start and end apart: 37 -> 58, of which waited for: 20 -> 27; matrix products, arithmetic and copies ran while one was open for 20% -> 4% of each run, Pallas kernels for 0% -> 12%
where the time goes in v2:
time: 222 us
  waiting for transfers between devices  106 us (48%)
  Pallas kernels  47.4 us (21%)
  starting transfers between devices  46.2 us (21%)
  local copies, waits for them, and re-layouts  17.4 us (8%)
  other arithmetic  3.5 us (2%)
    ppermute x58, waiting for transfers between devices, send(): return lax.ppermute(value, AXES, pairs)  106 us
    pallas_call x13, Pallas kernels, call(): pl.pallas_call(kernel, out_shape=outs, in_specs=[pl.BlockSpec(memory_spac...  47.4 us
    ppermute x58, starting transfers between devices, send(): return lax.ppermute(value, AXES, pairs)  46.2 us
    unnamed x138, local copies, waits for them, and re-layouts  11 us
  transfers between devices with their start and end apart: 58, of which 27 were waited for; matrix products, arithmetic and copies ran while one was open for 4% of the time, Pallas kernels for 12%

profile of v2, /device:TPU:0, one launch (start us, length us, event | category | flops | bytes accessed | tf_op | source)
XLA Modules:
  0.0 221.7 jit_solution(12570375872000814552)
XLA Ops:
  0.6 4.1 %collective-permute-start.19 = (bf16[64,2048]{1,0:T(8,128)(2,1)}, bf16[64,2048]{1,0:T(8,128)(2,1)S(1)}, u32[]{:S(2)}, u32[]{:S(2)}) collective-permute-start(bf16[64,2048]{1,0:T(8,128)(2,1)} %param.13), channel_id=1, source_target_pairs={{0,4},{1,5},{2,6},{3,7},{4,0},{5,1},{6,2},{7,3},{8,12},{9,13},{10,... | collective-permute-start | bytes 786440 | tf_op jit(solution)/shard_map/ppermute | solution.py:81
  5.8 2.5 %collective-permute-start.5 = (bf16[128,1024]{1,0:T(8,128)(2,1)S(1)}, bf16[128,1024]{1,0:T(8,128)(2,1)S(1)}, u32[]{:S(2)}, u32[]{:S(2)}) collective-permute-start(bf16[128,1024]{1,0:T(8,128)(2,1)S(1)} %get-tuple-element.111.refs_4_), channel_id=1, source_target_pairs={{0,17},{1,16},{2,19},{3,18},{4,21},{5,20},{6,23},{7,22},{8,25},{9,... | collective-permute-start | bytes 786440 | tf_op jit(solution)/shard_map/ppermute | solution.py:81
  10.0 2.1 shard_map.111
  12.1 1.5 collective-permute-start
  13.6 3.3 %collective-permute-done.19 = bf16[64,2048]{1,0:T(8,128)(2,1)S(1)} collective-permute-done((bf16[64,2048]{1,0:T(8,128)(2,1)}, bf16[64,2048]{1,0:T(8,128)(2,1)S(1)}, u32[]{:S(2)}, u32[]{:S(2)}) %collective-permute-start.19) | collective-permute-done | bytes 262176 | tf_op jit(solution)/shard_map/ppermute | solution.py:81
  17.8 2.4 %collective-permute-done.4.refs_8_ = bf16[128,1024]{1,0:T(8,128)(2,1)S(1)} collective-permute-done((bf16[128,1024]{1,0:T(8,128)(2,1)S(1)}, bf16[128,1024]{1,0:T(8,128)(2,1)S(1)}, u32[]{:S(2)}, u32[]{:S(2)}) %collective-permute-start.4) | collective-permute-done | bytes 262176 | tf_op jit(solution)/shard_map/ppermute | solution.py:81
  20.8 5.2 %collective-permute-done.got = bf16[528,256]{1,0:T(8,128)(2,1)S(1)} collective-permute-done((bf16[528,256]{1,0:T(8,128)(2,1)}, bf16[528,256]{1,0:T(8,128)(2,1)S(1)}, u32[]{:S(2)}, u32[]{:S(2)}) %collective-permute-start) | collective-permute-done | bytes 270368 | tf_op jit(solution)/shard_map/ppermute | solution.py:81
  26.7 2.0 shard_map.112
  28.7 1.7 collective-permute-start.13
  32.2 3.9 %shard_map.113 = (f32[256,1024]{1,0:T(8,128)}, bf16[256,1024]{1,0:T(8,128)(2,1)}) custom-call(bf16[512,256]{1,0:T(8,128)(2,1)} %get-tuple-element.51.refs_0_, bf16[512,256]{1,0:T(8,128)(2,1)} %get-tuple-element.52.refs_1_.refs_0_, bf16[512,256]{1,0:T(8,128)(2,1)} %get-tuple-element.54.refs_2_.refs_1_, bf16[512,256]{1,0:T(8,128)(2,1)} %get-tuple-element.55.refs_3_.refs_1_, ...), custom_call_target="tpu_custom_call" | custom-call | tf_op jit(solution)/shard_map/pallas_call | solution.py:41
  36.4 2.4 %collective-permute-done.13.refs_9_ = bf16[128,1024]{1,0:T(8,128)(2,1)S(1)} collective-permute-done((bf16[128,1024]{1,0:T(8,128)(2,1)S(1)}, bf16[128,1024]{1,0:T(8,128)(2,1)S(1)}, u32[]{:S(2)}, u32[]{:S(2)}) %collective-permute-start.13) | collective-permute-done | bytes 262176 | tf_op jit(solution)/shard_map/ppermute | solution.py:81
  38.8 4.6 %collective-permute-done.12.refs_8_ = bf16[128,1024]{1,0:T(8,128)(2,1)S(1)} collective-permute-done((bf16[128,1024]{1,0:T(8,128)(2,1)S(1)}, bf16[128,1024]{1,0:T(8,128)(2,1)S(1)}, u32[]{:S(2)}, u32[]{:S(2)}) %collective-permute-start.12) | collective-permute-done | bytes 262176 | tf_op jit(solution)/shard_map/ppermute | solution.py:81
  44.3 1.5 collective-permute-start.22
  45.8 1.6 collective-permute-start.8
  47.9 10.2 %collective-permute-done.22.refs_7_ = bf16[1,256,1024]{2,1,0:T(8,128)(2,1)S(1)} collective-permute-done((bf16[1,256,1024]{2,1,0:T(8,128)(2,1)S(1)}, bf16[1,256,1024]{2,1,0:T(8,128)(2,1)S(1)}, u32[]{:S(2)}, u32[]{:S(2)}) %collective-permute-start.22) | collective-permute-done | bytes 524320 | tf_op jit(solution)/shard_map/ppermute | solution.py:81
  66.1 3.9 %shard_map.114 = (f32[256,1024]{1,0:T(8,128)}, bf16[256,1024]{1,0:T(8,128)(2,1)}) custom-call(bf16[512,256]{1,0:T(8,128)(2,1)} %get-tuple-element.51.refs_0_, bf16[512,256]{1,0:T(8,128)(2,1)} %get-tuple-element.52.refs_1_.refs_0_, bf16[512,256]{1,0:T(8,128)(2,1)} %get-tuple-element.54.refs_2_.refs_1_, bf16[512,256]{1,0:T(8,128)(2,1)} %get-tuple-element.55.refs_3_.refs_1_, ...), custom_call_target="tpu_custom_call" | custom-call | tf_op jit(solution)/shard_map/pallas_call | solution.py:41
  70.0 1.6 collective-permute-start.16
  71.6 8.2 %collective-permute-done.17.refs_2_ = bf16[128,1024]{1,0:T(8,128)(2,1)S(1)} collective-permute-done((bf16[128,1024]{1,0:T(8,128)(2,1)}, bf16[128,1024]{1,0:T(8,128)(2,1)S(1)}, u32[]{:S(2)}, u32[]{:S(2)}) %collective-permute-start.17) | collective-permute-done | bytes 262176 | tf_op jit(solution)/shard_map/ppermute | solution.py:81
  79.8 3.5 %collective-permute-done.24.refs_9_ = bf16[2,256,1024]{2,1,0:T(8,128)(2,1)S(1)} collective-permute-done((bf16[2,256,1024]{2,1,0:T(8,128)(2,1)S(1)}, bf16[2,256,1024]{2,1,0:T(8,128)(2,1)S(1)}, u32[]{:S(2)}, u32[]{:S(2)}) %collective-permute-start.24) | collective-permute-done | bytes 1048608 | tf_op jit(solution)/shard_map/ppermute | solution.py:81
  84.9 3.7 %collective-permute-done.16 = bf16[256,1024]{1,0:T(8,128)(2,1)S(1)} collective-permute-done((bf16[256,1024]{1,0:T(8,128)(2,1)}, bf16[256,1024]{1,0:T(8,128)(2,1)S(1)}, u32[]{:S(2)}, u32[]{:S(2)}) %collective-permute-start.16) | collective-permute-done | bytes 524320 | tf_op jit(solution)/shard_map/ppermute | solution.py:81
  90.3 1.8 collective-permute-start.18
  92.1 13.1 %collective-permute-done.18.refs_3_ = bf16[128,1024]{1,0:T(8,128)(2,1)S(1)} collective-permute-done((bf16[128,1024]{1,0:T(8,128)(2,1)S(1)}, bf16[128,1024]{1,0:T(8,128)(2,1)S(1)}, u32[]{:S(2)}, u32[]{:S(2)}) %collective-permute-start.18) | collective-permute-done | bytes 262176 | tf_op jit(solution)/shard_map/ppermute | solution.py:81
  106.9 10.3 %shard_map.115 = (bf16[128,2048]{1,0:T(8,128)(2,1)}, bf16[1,128,1024]{2,1,0:T(8,128)(2,1)}, bf16[1,128,1024]{2,1,0:T(8,128)(2,1)}, bf16[2,2,128,256]{3,2,1,0:T(8...) custom-call(s32[4]{0:T(128)} %pad_add_fusion.place, ...), custom_call_target="tpu_custom_call" | custom-call | tf_op jit(solution)/shard_map/pallas_call | solution.py:41
  118.3 1.6 collective-permute-start.32
  121.4 9.9 %collective-permute-done.31.refs_3_ = bf16[128,1024]{1,0:T(8,128)(2,1)S(1)} collective-permute-done((bf16[128,1024]{1,0:T(8,128)(2,1)}, bf16[128,1024]{1,0:T(8,128)(2,1)S(1)}, u32[]{:S(2)}, u32[]{:S(2)}) %collective-permute-start.31) | collective-permute-done | bytes 262176 | tf_op jit(solution)/shard_map/ppermute | solution.py:81
  131.4 1.5 collective-permute-start.39
  133.2 2.7 %collective-permute-start.34 = (bf16[256,1024]{1,0:T(8,128)(2,1)S(1)}, bf16[256,1024]{1,0:T(8,128)(2,1)S(1)}, u32[]{:S(2)}, u32[]{:S(2)}) collective-permute-start(bf16[256,1024]{1,0:T(8,128)(2,1)S(1)} %pad_maximum_fusion.6), channel_id=1, source_target_pairs={{0,2},{1,3},{2,0},{3,1},{4,6},{5,7},{6,4},{7,5},{8,10},{9,11},{10,... | collective-permute-start | bytes 1572872 | tf_op jit(solution)/shard_map/ppermute | solution.py:81
  136.6 1.4 collective-permute-start.36
  138.0 2.7 %collective-permute-done.39 = bf16[2,2,128,256]{3,2,0,1:T(8,128)(2,1)S(1)} collective-permute-done((bf16[2,2,128,256]{3,2,0,1:T(8,128)(2,1)S(1)}, bf16[2,2,128,256]{3,2,0,1:T(8,128)(2,1)S(1)}, u32[]{:S(2)}, u32[]{:S(2)}) %collective-permute-start.39) | collective-permute-done | bytes 262176 | tf_op jit(solution)/shard_map/ppermute | solution.py:81
  140.7 1.5 collective-permute-start.40
  142.3 2.6 %collective-permute-done.35.refs_3_ = bf16[128,1024]{1,0:T(8,128)(2,1)S(1)} collective-permute-done((bf16[128,1024]{1,0:T(8,128)(2,1)}, bf16[128,1024]{1,0:T(8,128)(2,1)S(1)}, u32[]{:S(2)}, u32[]{:S(2)}) %collective-permute-start.35) | collective-permute-done | bytes 262176 | tf_op jit(solution)/shard_map/ppermute | solution.py:81
  145.0 8.0 %collective-permute-done.34.refs_4_ = bf16[256,1024]{1,0:T(8,128)(2,1)S(1)} collective-permute-done((bf16[256,1024]{1,0:T(8,128)(2,1)S(1)}, bf16[256,1024]{1,0:T(8,128)(2,1)S(1)}, u32[]{:S(2)}, u32[]{:S(2)}) %collective-permute-start.34) | collective-permute-done | bytes 524320 | tf_op jit(solution)/shard_map/ppermute | solution.py:81
  153.0 2.2 %collective-permute-done.40.refs_14_ = bf16[2,2,128,256]{3,2,1,0:T(8,128)(2,1)S(1)} collective-permute-done((bf16[2,2,128,256]{3,2,1,0:T(8,128)(2,1)S(1)}, bf16[2,2,128,256]{3,2,1,0:T(8,128)(2,1)S(1)}, u32[]{:S(2)}, u32[]{:S(2)}) %collective-permute-start.40) | collective-permute-done | bytes 262176 | tf_op jit(solution)/shard_map/ppermute | solution.py:81
  155.2 3.4 %shard_map.116 = bf16[512,1024]{1,0:T(8,128)(2,1)} custom-call(bf16[512,256]{1,0:T(8,128)(2,1)} %get-tuple-element.52.refs_1_.refs_0_, bf16[512,256]{1,0:T(8,128)(2,1)} %get-tuple-element.55.refs_3_.refs_1_, bf16[128,1024]{1,0:T(8,128)(2,1)} %get-tuple-element.68.refs_2_, bf16[128,1024]{1,0:T(8,128)(2,1)} %copy-done.5, bf16[256,1024]{1,0:T(8,128)(2,1)} %copy-done.6), custom_call_target="tpu_custom_call" | custom-call | tf_op jit(solution)/shard_map/pallas_call | solution.py:41
  159.8 1.4 collective-permute-done.47.refs_7_
  164.8 3.2 %shard_map.117 = (f32[128,1024]{1,0:T(8,128)}, bf16[128,1024]{1,0:T(8,128)(2,1)}, bf16[128,1024]{1,0:T(8,128)(2,1)}, bf16[128,1024]{1,0:T(8,128)(2,1)}) custom-call(bf16[512,256]{1,0:T(8,128)(2,1)} %get-tuple-element.51.refs_0_, bf16[512,256]{1,0:T(8,128)(2,1)} %get-tuple-element.54.refs_2_.refs_1_, bf16[128,1024]{1,0:T(8,128)(2,1)} %get-tuple-element.68.refs_2_, ...), custom_call_target="tpu_custom_call" | custom-call | tf_op jit(solution)/shard_map/pallas_call | solution.py:41
  169.8 5.0 %shard_map.118 = (f32[128,2176]{1,0:T(8,128)}, bf16[128,2176]{1,0:T(8,128)(2,1)}) custom-call(s32[4]{0:T(128)} %pad_add_fusion.place, bf16[1,128,1024]{2,1,0:T(8,128)(2,1)} %get-tuple-element.84.refs_0_, bf16[1,128,1024]{2,1,0:T(8,128)(2,1)} %get-tuple-element.70.refs_1_, bf16[1,128,1024]{2,1,0:T(8,128)(2,1)} %copy-done.23, ...), custom_call_target="tpu_custom_call" | custom-call | tf_op jit(solution)/shard_map/pallas_call | solution.py:41
  176.2 3.2 %shard_map.119 = bf16[512,1024]{1,0:T(8,128)(2,1)} custom-call(bf16[512,256]{1,0:T(8,128)(2,1)} %get-tuple-element.52.refs_1_.refs_0_, bf16[512,256]{1,0:T(8,128)(2,1)} %get-tuple-element.55.refs_3_.refs_1_, bf16[128,1024]{1,0:T(8,128)(2,1)} %get-tuple-element.73.refs_2_, bf16[128,1024]{1,0:T(8,128)(2,1)} %copy-done.3, bf16[256,1024]{1,0:T(8,128)(2,1)} %copy-done.7), custom_call_target="tpu_custom_call" | custom-call | tf_op jit(solution)/shard_map/pallas_call | solution.py:41
  184.2 3.2 %shard_map.120 = (f32[128,1024]{1,0:T(8,128)}, bf16[128,1024]{1,0:T(8,128)(2,1)}, bf16[128,1024]{1,0:T(8,128)(2,1)}, bf16[128,1024]{1,0:T(8,128)(2,1)}) custom-call(bf16[512,256]{1,0:T(8,128)(2,1)} %get-tuple-element.51.refs_0_, bf16[512,256]{1,0:T(8,128)(2,1)} %get-tuple-element.54.refs_2_.refs_1_, bf16[128,1024]{1,0:T(8,128)(2,1)} %get-tuple-element.73.refs_2_, ...), custom_call_target="tpu_custom_call" | custom-call | tf_op jit(solution)/shard_map/pallas_call | solution.py:41
  187.5 1.5 collective-permute-done.42.refs_1_
  188.9 5.7 %collective-permute-done.43.refs_2_ = bf16[128,1024]{1,0:T(8,128)(2,1)S(1)} collective-permute-done((bf16[128,1024]{1,0:T(8,128)(2,1)S(1)}, bf16[128,1024]{1,0:T(8,128)(2,1)S(1)}, u32[]{:S(2)}, u32[]{:S(2)}) %collective-permute-start.43) | collective-permute-done | bytes 262176 | tf_op jit(solution)/shard_map/ppermute | solution.py:81
  195.5 2.4 %shard_map.122 = (f32[64,2176]{1,0:T(8,128)}, bf16[64,2176]{1,0:T(8,128)(2,1)}) custom-call(f32[128,2176]{1,0:T(8,128)} %get-tuple-element.91.kept, bf16[128,2176]{1,0:T(8,128)(2,1)} %copy-done.25), custom_call_target="tpu_custom_call" | custom-call | tf_op jit(solution)/shard_map/pallas_call | solution.py:41
  197.9 1.9 collective-permute-start.57
  201.9 1.4 collective-permute-start.55
  203.3 5.8 %collective-permute-done.53.refs_5_ = bf16[128,1024]{1,0:T(8,128)(2,1)S(1)} collective-permute-done((bf16[128,1024]{1,0:T(8,128)(2,1)S(1)}, bf16[128,1024]{1,0:T(8,128)(2,1)S(1)}, u32[]{:S(2)}, u32[]{:S(2)}) %collective-permute-start.53) | collective-permute-done | bytes 262176 | tf_op jit(solution)/shard_map/ppermute | solution.py:81
  209.1 4.2 %collective-permute-done.54.refs_6_ = bf16[128,1024]{1,0:T(8,128)(2,1)S(1)} collective-permute-done((bf16[128,1024]{1,0:T(8,128)(2,1)S(1)}, bf16[128,1024]{1,0:T(8,128)(2,1)S(1)}, u32[]{:S(2)}, u32[]{:S(2)}) %collective-permute-start.54) | collective-permute-done | bytes 262176 | tf_op jit(solution)/shard_map/ppermute | solution.py:81
  214.7 2.8 %shard_map.121 = f32[128,2048]{1,0:T(8,128)} custom-call(f32[128,1024]{1,0:T(8,128)} %get-tuple-element.79.refs_0_, bf16[128,1024]{1,0:T(8,128)(2,1)} %copy-done.36, bf16[128,1024]{1,0:T(8,128)(2,1)} %copy-done.37, bf16[128,1024]{1,0:T(8,128)(2,1)} %copy-done.38, f32[128,1024]{1,0:T(8,128)} %get-tuple-element.87.refs_4_, bf16[128,1024]{1,0:T(8,128)(2,1)} %copy-done.39, ...), custom_call_target="tpu_custom_call" | custom-call | tf_op jit(solution)/shard_map/pallas_call | solution.py:41
  218.3 2.0 shard_map.123
  (246 shorter events, 44.2 us)
Async XLA Ops:
  0.6 16.2 %collective-permute-start.19 = (bf16[64,2048]{1,0:T(8,128)(2,1)}, bf16[64,2048]{1,0:T(8,128)(2,1)S(1)}, u32[]{:S(2)}, u32[]{:S(2)}) collective-permute-start(bf16[64,2048]{1,0:T(8,128)(2,1)} %param.13), channel_id=1, source_target_pairs={{0,4},{1,5},{2,6},{3,7},{4,0},{5,1},{6,2},{7,3},{8,12},{9,13},{10,... | collective-permute-start | bytes 786440 | tf_op jit(solution)/shard_map/ppermute | solution.py:81
  5.8 12.0 %collective-permute-start.5 = (bf16[128,1024]{1,0:T(8,128)(2,1)S(1)}, bf16[128,1024]{1,0:T(8,128)(2,1)S(1)}, u32[]{:S(2)}, u32[]{:S(2)}) collective-permute-start(bf16[128,1024]{1,0:T(8,128)(2,1)S(1)} %get-tuple-element.111.refs_4_), channel_id=1, source_target_pairs={{0,17},{1,16},{2,19},{3,18},{4,21},{5,20},{6,23},{7,22},{8,25},{9,... | collective-permute-start | bytes 786440 | tf_op jit(solution)/shard_map/ppermute | solution.py:81
  8.3 11.9 %collective-permute-start.4 = (bf16[128,1024]{1,0:T(8,128)(2,1)S(1)}, bf16[128,1024]{1,0:T(8,128)(2,1)S(1)}, u32[]{:S(2)}, u32[]{:S(2)}) collective-permute-start(bf16[128,1024]{1,0:T(8,128)(2,1)S(1)} %get-tuple-element.111.refs_4_), channel_id=1, source_target_pairs={{0,1},{1,0},{2,3},{3,2},{4,5},{5,4},{6,7},{7,6},{8,9},{9,8},{10,11... | collective-permute-start | bytes 786440 | tf_op jit(solution)/shard_map/ppermute | solution.py:81
  8.8 11.4 %collective-permute-start.1 = (bf16[128,1024]{1,0:T(8,128)(2,1)S(1)}, bf16[128,1024]{1,0:T(8,128)(2,1)S(1)}, u32[]{:S(2)}, u32[]{:S(2)}) collective-permute-start(bf16[128,1024]{1,0:T(8,128)(2,1)S(1)} %get-tuple-element.111.refs_4_), channel_id=1, source_target_pairs={{0,16},{1,17},{2,18},{3,19},{4,20},{5,21},{6,22},{7,23},{8,24},{9,... | collective-permute-start | bytes 786440 | tf_op jit(solution)/shard_map/ppermute | solution.py:81
  12.1 13.9 %collective-permute-start = (bf16[528,256]{1,0:T(8,128)(2,1)}, bf16[528,256]{1,0:T(8,128)(2,1)S(1)}, u32[]{:S(2)}, u32[]{:S(2)}) collective-permute-start(bf16[528,256]{1,0:T(8,128)(2,1)} %get-tuple-element.53), channel_id=1, source_target_pairs={{0,1},{1,0},{2,3},{3,2},{4,5},{5,4},{6,7},{7,6},{8,9},{9,8},{10,11... | collective-permute-start | bytes 811016 | tf_op jit(solution)/shard_map/ppermute | solution.py:81
  16.9 19.2 %collective-permute-start.20 = (bf16[128,2048]{1,0:T(8,128)(2,1)S(1)}, bf16[128,2048]{1,0:T(8,128)(2,1)S(1)}, u32[]{:S(2)}, u32[]{:S(2)}) collective-permute-start(bf16[128,2048]{1,0:T(8,128)(2,1)S(1)} %pad_maximum_fusion.5), channel_id=1, source_target_pairs={{0,2},{1,3},{2,0},{3,1},{4,6},{5,7},{6,4},{7,5},{8,10},{9,11},{10,... | collective-permute-start | bytes 1572872 | tf_op jit(solution)/shard_map/ppermute | solution.py:81
  17.8 10.9 %collective-permute-start.2 = (bf16[128,1024]{1,0:T(8,128)(2,1)S(1)}, bf16[128,1024]{1,0:T(8,128)(2,1)}, u32[]{:S(2)}, u32[]{:S(2)}) collective-permute-start(bf16[128,1024]{1,0:T(8,128)(2,1)S(1)} %get-tuple-element.111.refs_4_), channel_id=1, source_target_pairs={{0,8},{1,9},{2,10},{3,11},{4,12},{5,13},{6,14},{7,15},{8,0},{9,1},... | collective-permute-start | bytes 786440 | tf_op jit(solution)/shard_map/ppermute | solution.py:81
  20.3 10.2 %collective-permute-start.7 = (bf16[128,1024]{1,0:T(8,128)(2,1)S(1)}, bf16[128,1024]{1,0:T(8,128)(2,1)}, u32[]{:S(2)}, u32[]{:S(2)}) collective-permute-start(bf16[128,1024]{1,0:T(8,128)(2,1)S(1)} %collective-permute-done.5.refs_9_), channel_id=1, source_target_pairs={{0,8},{1,9},{2,10},{3,11},{4,12},{5,13},{6,14},{7,15},{8,0},{9,1},... | collective-permute-start | bytes 786440 | tf_op jit(solution)/shard_map/ppermute | solution.py:81
  20.3 11.3 %collective-permute-start.6 = (bf16[128,1024]{1,0:T(8,128)(2,1)S(1)}, bf16[128,1024]{1,0:T(8,128)(2,1)}, u32[]{:S(2)}, u32[]{:S(2)}) collective-permute-start(bf16[128,1024]{1,0:T(8,128)(2,1)S(1)} %collective-permute-done.4.refs_8_), channel_id=1, source_target_pairs={{0,8},{1,9},{2,10},{3,11},{4,12},{5,13},{6,14},{7,15},{8,0},{9,1},... | collective-permute-start | bytes 786440 | tf_op jit(solution)/shard_map/ppermute | solution.py:81
  26.0 6.2 %collective-permute-start.3 = (bf16[128,1024]{1,0:T(8,128)(2,1)S(1)}, bf16[128,1024]{1,0:T(8,128)(2,1)}, u32[]{:S(2)}, u32[]{:S(2)}) collective-permute-start(bf16[128,1024]{1,0:T(8,128)(2,1)S(1)} %collective-permute-done.1.refs_5_), channel_id=1, source_target_pairs={{0,8},{1,9},{2,10},{3,11},{4,12},{5,13},{6,14},{7,15},{8,0},{9,1},... | collective-permute-start | bytes 786440 | tf_op jit(solution)/shard_map/ppermute | solution.py:81
  28.7 10.1 %collective-permute-start.13 = (bf16[128,1024]{1,0:T(8,128)(2,1)S(1)}, bf16[128,1024]{1,0:T(8,128)(2,1)S(1)}, u32[]{:S(2)}, u32[]{:S(2)}) collective-permute-start(bf16[128,1024]{1,0:T(8,128)(2,1)S(1)} %get-tuple-element.58.refs_4_), channel_id=1, source_target_pairs={{0,17},{1,16},{2,19},{3,18},{4,21},{5,20},{6,23},{7,22},{8,25},{9,... | collective-permute-start | bytes 786440 | tf_op jit(solution)/shard_map/ppermute | solution.py:81
  30.4 13.0 %collective-permute-start.12 = (bf16[128,1024]{1,0:T(8,128)(2,1)S(1)}, bf16[128,1024]{1,0:T(8,128)(2,1)S(1)}, u32[]{:S(2)}, u32[]{:S(2)}) collective-permute-start(bf16[128,1024]{1,0:T(8,128)(2,1)S(1)} %get-tuple-element.58.refs_4_), channel_id=1, source_target_pairs={{0,1},{1,0},{2,3},{3,2},{4,5},{5,4},{6,7},{7,6},{8,9},{9,8},{10,11... | collective-permute-start | bytes 786440 | tf_op jit(solution)/shard_map/ppermute | solution.py:81
  31.6 11.9 %collective-permute-start.9 = (bf16[128,1024]{1,0:T(8,128)(2,1)S(1)}, bf16[128,1024]{1,0:T(8,128)(2,1)S(1)}, u32[]{:S(2)}, u32[]{:S(2)}) collective-permute-start(bf16[128,1024]{1,0:T(8,128)(2,1)S(1)} %get-tuple-element.58.refs_4_), channel_id=1, source_target_pairs={{0,16},{1,17},{2,18},{3,19},{4,20},{5,21},{6,22},{7,23},{8,24},{9,... | collective-permute-start | bytes 786440 | tf_op jit(solution)/shard_map/ppermute | solution.py:81
  44.3 13.8 %collective-permute-start.22 = (bf16[1,256,1024]{2,1,0:T(8,128)(2,1)S(1)}, bf16[1,256,1024]{2,1,0:T(8,128)(2,1)S(1)}, u32[]{:S(2)}, u32[]{:S(2)}) collective-permute-start(bf16[1,256,1024]{2,1,0:T(8,128)(2,1)S(1)} %get-tuple-element.102.refs_5_), channel_id=1, source_target_pairs={{0,1},{1,0},{2,3},{3,2},{4,5},{5,4},{6,7},{7,6},{8,9},{9,8},{10,11... | collective-permute-start | bytes 1572872 | tf_op jit(solution)/shard_map/ppermute | solution.py:81
  45.8 13.6 %collective-permute-start.8 = (bf16[256,1024]{1,0:T(8,128)(2,1)S(1)}, bf16[256,1024]{1,0:T(8,128)(2,1)S(1)}, u32[]{:S(2)}, u32[]{:S(2)}) collective-permute-start(bf16[256,1024]{1,0:T(8,128)(2,1)S(1)} %copy-done.62), channel_id=1, source_target_pairs={{0,2},{1,3},{2,0},{3,1},{4,6},{5,7},{6,4},{7,5},{8,10},{9,11},{10,... | collective-permute-start | bytes 1572872 | tf_op jit(solution)/shard_map/ppermute | solution.py:81
  47.4 13.3 %collective-permute-start.21 = (bf16[1,256,1024]{2,1,0:T(8,128)(2,1)S(1)}, bf16[1,256,1024]{2,1,0:T(8,128)(2,1)S(1)}, u32[]{:S(2)}, u32[]{:S(2)}) collective-permute-start(bf16[1,256,1024]{2,1,0:T(8,128)(2,1)S(1)} %get-tuple-element.103.refs_4_), channel_id=1, source_target_pairs={{0,16},{1,17},{2,18},{3,19},{4,20},{5,21},{6,22},{7,23},{8,24},{9,... | collective-permute-start | bytes 1572872 | tf_op jit(solution)/shard_map/ppermute | solution.py:81
  59.3 23.9 %collective-permute-start.24 = (bf16[2,256,1024]{2,1,0:T(8,128)(2,1)S(1)}, bf16[2,256,1024]{2,1,0:T(8,128)(2,1)S(1)}, u32[]{:S(2)}, u32[]{:S(2)}) collective-permute-start(bf16[2,256,1024]{2,1,0:T(8,128)(2,1)S(1)} %pad_maximum_fusion.3), channel_id=1, source_target_pairs={{0,16},{1,17},{2,18},{3,19},{4,20},{5,21},{6,22},{7,23},{8,24},{9,... | collective-permute-start | bytes 3145736 | tf_op jit(solution)/shard_map/ppermute | solution.py:81
  60.8 23.7 %collective-permute-start.23 = (bf16[2,256,1024]{2,1,0:T(8,128)(2,1)S(1)}, bf16[2,256,1024]{2,1,0:T(8,128)(2,1)S(1)}, u32[]{:S(2)}, u32[]{:S(2)}) collective-permute-start(bf16[2,256,1024]{2,1,0:T(8,128)(2,1)S(1)} %pad_maximum_fusion.2), channel_id=1, source_target_pairs={{0,1},{1,0},{2,3},{3,2},{4,5},{5,4},{6,7},{7,6},{8,9},{9,8},{10,11... | collective-permute-start | bytes 3145736 | tf_op jit(solution)/shard_map/ppermute | solution.py:81
  64.3 15.5 %collective-permute-start.17 = (bf16[128,1024]{1,0:T(8,128)(2,1)}, bf16[128,1024]{1,0:T(8,128)(2,1)S(1)}, u32[]{:S(2)}, u32[]{:S(2)}) collective-permute-start(bf16[128,1024]{1,0:T(8,128)(2,1)} %get-tuple-element.100), channel_id=1, source_target_pairs={{0,4},{1,5},{2,6},{3,7},{4,0},{5,1},{6,2},{7,3},{8,12},{9,13},{10,... | collective-permute-start | bytes 786440 | tf_op jit(solution)/shard_map/ppermute | solution.py:81
  70.0 18.6 %collective-permute-start.16 = (bf16[256,1024]{1,0:T(8,128)(2,1)}, bf16[256,1024]{1,0:T(8,128)(2,1)S(1)}, u32[]{:S(2)}, u32[]{:S(2)}) collective-permute-start(bf16[256,1024]{1,0:T(8,128)(2,1)} %get-tuple-element.60), channel_id=1, source_target_pairs={{0,2},{1,3},{2,0},{3,1},{4,6},{5,7},{6,4},{7,5},{8,10},{9,11},{10,... | collective-permute-start | bytes 1572872 | tf_op jit(solution)/shard_map/ppermute | solution.py:81
  71.6 17.2 %collective-permute-start.26 = (bf16[1,256,1024]{2,1,0:T(8,128)(2,1)S(1)}, bf16[1,256,1024]{2,1,0:T(8,128)(2,1)S(1)}, u32[]{:S(2)}, u32[]{:S(2)}) collective-permute-start(bf16[1,256,1024]{2,1,0:T(8,128)(2,1)S(1)} %get-tuple-element.102.refs_5_), channel_id=1, source_target_pairs={{0,8},{1,9},{2,10},{3,11},{4,12},{5,13},{6,14},{7,15},{8,0},{9,1},... | collective-permute-start | bytes 1572872 | tf_op jit(solution)/shard_map/ppermute | solution.py:81
  83.3 21.9 %collective-permute-start.30 = (bf16[2,256,1024]{2,1,0:T(8,128)(2,1)S(1)}, bf16[2,256,1024]{2,1,0:T(8,128)(2,1)S(1)}, u32[]{:S(2)}, u32[]{:S(2)}) collective-permute-start(bf16[2,256,1024]{2,1,0:T(8,128)(2,1)S(1)} %collective-permute-done.24.refs_9_), channel_id=1, source_target_pairs={{0,8},{1,9},{2,10},{3,11},{4,12},{5,13},{6,14},{7,15},{8,0},{9,1},... | collective-permute-start | bytes 3145736 | tf_op jit(solution)/shard_map/ppermute | solution.py:81
  84.4 20.7 %collective-permute-start.29 = (bf16[2,256,1024]{2,1,0:T(8,128)(2,1)S(1)}, bf16[2,256,1024]{2,1,0:T(8,128)(2,1)S(1)}, u32[]{:S(2)}, u32[]{:S(2)}) collective-permute-start(bf16[2,256,1024]{2,1,0:T(8,128)(2,1)S(1)} %collective-permute-done.23.refs_8_), channel_id=1, source_target_pairs={{0,8},{1,9},{2,10},{3,11},{4,12},{5,13},{6,14},{7,15},{8,0},{9,1},... | collective-permute-start | bytes 3145736 | tf_op jit(solution)/shard_map/ppermute | solution.py:81
  88.6 16.5 %collective-permute-start.28 = (bf16[1,256,1024]{2,1,0:T(8,128)(2,1)S(1)}, bf16[1,256,1024]{2,1,0:T(8,128)(2,1)S(1)}, u32[]{:S(2)}, u32[]{:S(2)}) collective-permute-start(bf16[1,256,1024]{2,1,0:T(8,128)(2,1)S(1)} %collective-permute-done.22.refs_7_), channel_id=1, source_target_pairs={{0,8},{1,9},{2,10},{3,11},{4,12},{5,13},{6,14},{7,15},{8,0},{9,1},... | collective-permute-start | bytes 1572872 | tf_op jit(solution)/shard_map/ppermute | solution.py:81
  88.8 16.4 %collective-permute-start.27 = (bf16[1,256,1024]{2,1,0:T(8,128)(2,1)S(1)}, bf16[1,256,1024]{2,1,0:T(8,128)(2,1)S(1)}, u32[]{:S(2)}, u32[]{:S(2)}) collective-permute-start(bf16[1,256,1024]{2,1,0:T(8,128)(2,1)S(1)} %collective-permute-done.21.refs_6_), channel_id=1, source_target_pairs={{0,8},{1,9},{2,10},{3,11},{4,12},{5,13},{6,14},{7,15},{8,0},{9,1},... | collective-permute-start | bytes 1572872 | tf_op jit(solution)/shard_map/ppermute | solution.py:81
  90.3 14.8 %collective-permute-start.18 = (bf16[128,1024]{1,0:T(8,128)(2,1)S(1)}, bf16[128,1024]{1,0:T(8,128)(2,1)S(1)}, u32[]{:S(2)}, u32[]{:S(2)}) collective-permute-start(bf16[128,1024]{1,0:T(8,128)(2,1)S(1)} %get-tuple-element.61), channel_id=1, source_target_pairs={{0,4},{1,5},{2,6},{3,7},{4,0},{5,1},{6,2},{7,3},{8,12},{9,13},{10,... | collective-permute-start | bytes 786440 | tf_op jit(solution)/shard_map/ppermute | solution.py:81
  117.2 14.2 %collective-permute-start.31 = (bf16[128,1024]{1,0:T(8,128)(2,1)}, bf16[128,1024]{1,0:T(8,128)(2,1)S(1)}, u32[]{:S(2)}, u32[]{:S(2)}) collective-permute-start(bf16[128,1024]{1,0:T(8,128)(2,1)} %get-tuple-element.68.refs_2_), channel_id=1, source_target_pairs={{0,4},{1,5},{2,6},{3,7},{4,0},{5,1},{6,2},{7,3},{8,12},{9,13},{10,... | collective-permute-start | bytes 786440 | tf_op jit(solution)/shard_map/ppermute | solution.py:81
  118.2 13.1 %collective-permute-start.38 = (bf16[2,2,128,256]{3,2,0,1:T(8,128)(2,1)S(1)}, bf16[2,2,128,256]{3,2,0,1:T(8,128)(2,1)S(1)}, u32[]{:S(2)}, u32[]{:S(2)}) collective-permute-start(bf16[2,2,128,256]{3,2,0,1:T(8,128)(2,1)S(1)} %copy.17), channel_id=1, source_target_pairs={{0,8},{1,9},{2,10},{3,11},{4,12},{5,13},{6,14},{7,15},{8,0},{9,1},... | collective-permute-start | bytes 786440 | tf_op jit(solution)/shard_map/ppermute | solution.py:81
  118.3 14.7 %collective-permute-start.32 = (bf16[1,128,1024]{2,1,0:T(8,128)(2,1)}, bf16[1,128,1024]{2,1,0:T(8,128)(2,1)S(1)}, u32[]{:S(2)}, u32[]{:S(2)}) collective-permute-start(bf16[1,128,1024]{2,1,0:T(8,128)(2,1)} %get-tuple-element.84.refs_0_), channel_id=1, source_target_pairs={{0,16},{1,17},{2,18},{3,19},{4,20},{5,21},{6,22},{7,23},{8,24},{9,... | collective-permute-start | bytes 786440 | tf_op jit(solution)/shard_map/ppermute | solution.py:81
  120.8 12.2 %collective-permute-start.33 = (bf16[1,128,1024]{2,1,0:T(8,128)(2,1)}, bf16[1,128,1024]{2,1,0:T(8,128)(2,1)S(1)}, u32[]{:S(2)}, u32[]{:S(2)}) collective-permute-start(bf16[1,128,1024]{2,1,0:T(8,128)(2,1)} %get-tuple-element.70.refs_1_), channel_id=1, source_target_pairs={{0,1},{1,0},{2,3},{3,2},{4,5},{5,4},{6,7},{7,6},{8,9},{9,8},{10,11... | collective-permute-start | bytes 786440 | tf_op jit(solution)/shard_map/ppermute | solution.py:81
  131.3 13.6 %collective-permute-start.35 = (bf16[128,1024]{1,0:T(8,128)(2,1)}, bf16[128,1024]{1,0:T(8,128)(2,1)S(1)}, u32[]{:S(2)}, u32[]{:S(2)}) collective-permute-start(bf16[128,1024]{1,0:T(8,128)(2,1)} %get-tuple-element.73.refs_2_), channel_id=1, source_target_pairs={{0,4},{1,5},{2,6},{3,7},{4,0},{5,1},{6,2},{7,3},{8,12},{9,13},{10,... | collective-permute-start | bytes 786440 | tf_op jit(solution)/shard_map/ppermute | solution.py:81
  131.4 9.3 %collective-permute-start.39 = (bf16[2,2,128,256]{3,2,0,1:T(8,128)(2,1)S(1)}, bf16[2,2,128,256]{3,2,0,1:T(8,128)(2,1)S(1)}, u32[]{:S(2)}, u32[]{:S(2)}) collective-permute-start(bf16[2,2,128,256]{3,2,0,1:T(8,128)(2,1)S(1)} %get-tuple-element.109), channel_id=1, source_target_pairs={{0,16},{1,17},{2,18},{3,19},{4,20},{5,21},{6,22},{7,23},{8,24},{9,... | collective-permute-start | bytes 786440 | tf_op jit(solution)/shard_map/ppermute | solution.py:81
  133.2 19.8 %collective-permute-start.34 = (bf16[256,1024]{1,0:T(8,128)(2,1)S(1)}, bf16[256,1024]{1,0:T(8,128)(2,1)S(1)}, u32[]{:S(2)}, u32[]{:S(2)}) collective-permute-start(bf16[256,1024]{1,0:T(8,128)(2,1)S(1)} %pad_maximum_fusion.6), channel_id=1, source_target_pairs={{0,2},{1,3},{2,0},{3,1},{4,6},{5,7},{6,4},{7,5},{8,10},{9,11},{10,... | collective-permute-start | bytes 1572872 | tf_op jit(solution)/shard_map/ppermute | solution.py:81
  135.9 17.1 %collective-permute-start.37 = (bf16[2,128,1024]{2,1,0:T(8,128)(2,1)S(1)}, bf16[2,128,1024]{2,1,0:T(8,128)(2,1)S(1)}, u32[]{:S(2)}, u32[]{:S(2)}) collective-permute-start(bf16[2,128,1024]{2,1,0:T(8,128)(2,1)S(1)} %pad_maximum_fusion.8), channel_id=1, source_target_pairs={{0,16},{1,17},{2,18},{3,19},{4,20},{5,21},{6,22},{7,23},{8,24},{9,... | collective-permute-start | bytes 1572872 | tf_op jit(solution)/shard_map/ppermute | solution.py:81
  136.6 16.4 %collective-permute-start.36 = (bf16[2,128,1024]{2,1,0:T(8,128)(2,1)S(1)}, bf16[2,128,1024]{2,1,0:T(8,128)(2,1)S(1)}, u32[]{:S(2)}, u32[]{:S(2)}) collective-permute-start(bf16[2,128,1024]{2,1,0:T(8,128)(2,1)S(1)} %pad_maximum_fusion.7), channel_id=1, source_target_pairs={{0,1},{1,0},{2,3},{3,2},{4,5},{5,4},{6,7},{7,6},{8,9},{9,8},{10,11... | collective-permute-start | bytes 1572872 | tf_op jit(solution)/shard_map/ppermute | solution.py:81
  140.7 14.5 %collective-permute-start.40 = (bf16[2,2,128,256]{3,2,1,0:T(8,128)(2,1)S(1)}, bf16[2,2,128,256]{3,2,1,0:T(8,128)(2,1)S(1)}, u32[]{:S(2)}, u32[]{:S(2)}) collective-permute-start(bf16[2,2,128,256]{3,2,1,0:T(8,128)(2,1)S(1)} %pad_maximum_fusion.10), channel_id=1, source_target_pairs={{0,1},{1,0},{2,3},{3,2},{4,5},{5,4},{6,7},{7,6},{8,9},{9,8},{10,11... | collective-permute-start | bytes 786440 | tf_op jit(solution)/shard_map/ppermute | solution.py:81
  159.1 8.9 %collective-permute-start.51 = (bf16[2,128,1024]{2,1,0:T(8,128)(2,1)S(1)}, bf16[2,128,1024]{2,1,0:T(8,128)(2,1)S(1)}, u32[]{:S(2)}, u32[]{:S(2)}) collective-permute-start(bf16[2,128,1024]{2,1,0:T(8,128)(2,1)S(1)} %collective-permute-done.37.refs_5_), channel_id=1, source_target_pairs={{0,8},{1,9},{2,10},{3,11},{4,12},{5,13},{6,14},{7,15},{8,0},{9,1},... | collective-permute-start | bytes 1572872 | tf_op jit(solution)/shard_map/ppermute | solution.py:81
  159.7 8.4 %collective-permute-start.50 = (bf16[2,128,1024]{2,1,0:T(8,128)(2,1)S(1)}, bf16[2,128,1024]{2,1,0:T(8,128)(2,1)S(1)}, u32[]{:S(2)}, u32[]{:S(2)}) collective-permute-start(bf16[2,128,1024]{2,1,0:T(8,128)(2,1)S(1)} %collective-permute-done.36.refs_4_), channel_id=1, source_target_pairs={{0,8},{1,9},{2,10},{3,11},{4,12},{5,13},{6,14},{7,15},{8,0},{9,1},... | collective-permute-start | bytes 1572872 | tf_op jit(solution)/shard_map/ppermute | solution.py:81
  161.2 14.2 %collective-permute-start.45 = (bf16[256,1024]{1,0:T(8,128)(2,1)S(1)}, bf16[256,1024]{1,0:T(8,128)(2,1)S(1)}, u32[]{:S(2)}, u32[]{:S(2)}) collective-permute-start(bf16[256,1024]{1,0:T(8,128)(2,1)S(1)} %pad_maximum_fusion.9), channel_id=1, source_target_pairs={{0,2},{1,3},{2,0},{3,1},{4,6},{5,7},{6,4},{7,5},{8,10},{9,11},{10,... | collective-permute-start | bytes 1572872 | tf_op jit(solution)/shard_map/ppermute | solution.py:81
  161.6 6.4 %collective-permute-start.49 = (bf16[1,128,1024]{2,1,0:T(8,128)(2,1)S(1)}, bf16[1,128,1024]{2,1,0:T(8,128)(2,1)S(1)}, u32[]{:S(2)}, u32[]{:S(2)}) collective-permute-start(bf16[1,128,1024]{2,1,0:T(8,128)(2,1)S(1)} %collective-permute-done.33.refs_3_), channel_id=1, source_target_pairs={{0,8},{1,9},{2,10},{3,11},{4,12},{5,13},{6,14},{7,15},{8,0},{9,1},... | collective-permute-start | bytes 786440 | tf_op jit(solution)/shard_map/ppermute | solution.py:81
  179.4 15.2 %collective-permute-start.56 = (bf16[128,2176]{1,0:T(8,128)(2,1)S(1)}, bf16[128,2176]{1,0:T(8,128)(2,1)S(1)}, u32[]{:S(2)}, u32[]{:S(2)}) collective-permute-start(bf16[128,2176]{1,0:T(8,128)(2,1)S(1)} %copy-done.61), channel_id=1, source_target_pairs={{0,2},{1,3},{2,0},{3,1},{4,6},{5,7},{6,4},{7,5},{8,10},{9,11},{10,... | collective-permute-start | bytes 1671176 | tf_op jit(solution)/shard_map/ppermute | solution.py:81
  179.8 9.1 %collective-permute-start.42 = (bf16[128,1024]{1,0:T(8,128)(2,1)S(1)}, bf16[128,1024]{1,0:T(8,128)(2,1)S(1)}, u32[]{:S(2)}, u32[]{:S(2)}) collective-permute-start(bf16[128,1024]{1,0:T(8,128)(2,1)S(1)} %copy-done.65), channel_id=1, source_target_pairs={{0,16},{1,17},{2,18},{3,19},{4,20},{5,21},{6,22},{7,23},{8,24},{9,... | collective-permute-start | bytes 786440 | tf_op jit(solution)/shard_map/ppermute | solution.py:81
  180.8 13.8 %collective-permute-start.43 = (bf16[128,1024]{1,0:T(8,128)(2,1)S(1)}, bf16[128,1024]{1,0:T(8,128)(2,1)S(1)}, u32[]{:S(2)}, u32[]{:S(2)}) collective-permute-start(bf16[128,1024]{1,0:T(8,128)(2,1)S(1)} %copy-done.64), channel_id=1, source_target_pairs={{0,1},{1,0},{2,3},{3,2},{4,5},{5,4},{6,7},{7,6},{8,9},{9,8},{10,11... | collective-permute-start | bytes 786440 | tf_op jit(solution)/shard_map/ppermute | solution.py:81
  181.9 12.7 %collective-permute-start.44 = (bf16[128,1024]{1,0:T(8,128)(2,1)S(1)}, bf16[128,1024]{1,0:T(8,128)(2,1)S(1)}, u32[]{:S(2)}, u32[]{:S(2)}) collective-permute-start(bf16[128,1024]{1,0:T(8,128)(2,1)S(1)} %copy-done.63), channel_id=1, source_target_pairs={{0,17},{1,16},{2,19},{3,18},{4,21},{5,20},{6,23},{7,22},{8,25},{9,... | collective-permute-start | bytes 786440 | tf_op jit(solution)/shard_map/ppermute | solution.py:81
  197.9 19.7 %collective-permute-start.57 = (bf16[64,2176]{1,0:T(8,128)(2,1)}, bf16[64,2176]{1,0:T(8,128)(2,1)S(1)}, u32[]{:S(2)}, u32[]{:S(2)}) collective-permute-start(bf16[64,2176]{1,0:T(8,128)(2,1)} %get-tuple-element.95), channel_id=1, source_target_pairs={{0,4},{1,5},{2,6},{3,7},{4,0},{5,1},{6,2},{7,3},{8,12},{9,13},{10,... | collective-permute-start | bytes 835592 | tf_op jit(solution)/shard_map/ppermute | solution.py:81
  199.8 9.2 %collective-permute-start.53 = (bf16[128,1024]{1,0:T(8,128)(2,1)S(1)}, bf16[128,1024]{1,0:T(8,128)(2,1)S(1)}, u32[]{:S(2)}, u32[]{:S(2)}) collective-permute-start(bf16[128,1024]{1,0:T(8,128)(2,1)S(1)} %copy-done.68), channel_id=1, source_target_pairs={{0,16},{1,17},{2,18},{3,19},{4,20},{5,21},{6,22},{7,23},{8,24},{9,... | collective-permute-start | bytes 786440 | tf_op jit(solution)/shard_map/ppermute | solution.py:81
  200.8 12.5 %collective-permute-start.54 = (bf16[128,1024]{1,0:T(8,128)(2,1)S(1)}, bf16[128,1024]{1,0:T(8,128)(2,1)S(1)}, u32[]{:S(2)}, u32[]{:S(2)}) collective-permute-start(bf16[128,1024]{1,0:T(8,128)(2,1)S(1)} %copy-done.67), channel_id=1, source_target_pairs={{0,1},{1,0},{2,3},{3,2},{4,5},{5,4},{6,7},{7,6},{8,9},{9,8},{10,11... | collective-permute-start | bytes 786440 | tf_op jit(solution)/shard_map/ppermute | solution.py:81
  201.9 11.4 %collective-permute-start.55 = (bf16[128,1024]{1,0:T(8,128)(2,1)S(1)}, bf16[128,1024]{1,0:T(8,128)(2,1)S(1)}, u32[]{:S(2)}, u32[]{:S(2)}) collective-permute-start(bf16[128,1024]{1,0:T(8,128)(2,1)S(1)} %copy-done.66), channel_id=1, source_target_pairs={{0,17},{1,16},{2,19},{3,18},{4,21},{5,20},{6,23},{7,22},{8,25},{9,... | collective-permute-start | bytes 786440 | tf_op jit(solution)/shard_map/ppermute | solution.py:81
  (79 other events, 693.5 us)

commit v3 on v2

v3 whole, which is shorter than its diff:
```python
import functools
import math

import jax
import jax.numpy as jnp
from jax import lax
from jax.experimental import pallas as pl
from jax.experimental.pallas import tpu as pltpu
from jax.sharding import PartitionSpec as P

boost = 2.0
AXES = ("row", "col")
CORES = 2
LINE = 4
ORDER = (0, 2, 1, 3)
CUTS = (0, 9, 16)
CHUNKS = len(CUTS) - 1
LOW = jnp.bfloat16
F32 = jnp.float32


def dot(left, right, dims):
    return lax.dot_general(left, right, ((dims[0], dims[1]), ((), ())), preferred_element_type=F32)


def after(value, *others):
    return lax.optimization_barrier((value, *others))[0]


def one_of(value, index, axis):
    return lax.dynamic_index_in_dim(value, index, axis, keepdims=False)


def lookup(table, index):
    found = 0
    for k, entry in enumerate(table):
        found = found + entry * (index == k).astype(jnp.int32)
    return found


def call(kernel, outs, scratch, *operands, numbers=0, outside=0, alone=False):
    whole = pl.BlockSpec(memory_space=pltpu.VMEM)
    specs = [pl.BlockSpec(memory_space=pltpu.SMEM)] * numbers + [pl.BlockSpec(memory_space=pltpu.HBM)] * outside
    specs += [whole] * (len(operands) - len(specs))
    arrays = [v for v in [*operands[numbers:], *outs, *scratch] if hasattr(v.dtype, "itemsize")]
    need = sum(math.prod(v.shape) * v.dtype.itemsize for v in arrays)
    need = 60 * 2**20 if alone else min(need + 6 * 2**20, 60 * 2**20)
    return pl.pallas_call(
        kernel,
        out_shape=outs,
        in_specs=specs,
        out_specs=[whole] * len(outs),
        scratch_shapes=scratch,
        compiler_params=pltpu.CompilerParams(vmem_limit_bytes=need),
        cost_estimate=pl.CostEstimate(flops=1, bytes_accessed=1, transcendentals=0),
    )(*operands)


def like(*shape, kind=LOW):
    return jax.ShapeDtypeStruct(shape, kind)


def bounds(width):
    return [(low * width // CUTS[-1], high * width // CUTS[-1]) for low, high in zip(CUTS, CUTS[1:])]


def join_kernel(pieces, *refs):
    out, row = refs[-1], 0
    for k, start, rows in pieces:
        out[row : row + rows, :] = refs[k][start : start + rows, :]
        row += rows


def join(*pieces):
    pieces = [piece if isinstance(piece, tuple) else (piece, 0, piece.shape[0]) for piece in pieces]
    arrays = list({id(piece[0]): piece[0] for piece in pieces}.values())
    order = {id(array): k for k, array in enumerate(arrays)}
    rows = sum(piece[2] for piece in pieces)
    places = [(order[id(array)], start, count) for array, start, count in pieces]
    return call(functools.partial(join_kernel, places), [like(rows, arrays[0].shape[1])], [], *arrays)[0]


def bounds(width):
    return [(low * width // CUTS[-1], high * width // CUTS[-1]) for low, high in zip(CUTS, CUTS[1:])]


def like(*shape, kind=LOW):
    return jax.ShapeDtypeStruct(shape, kind)


class Place:
    def __init__(self):
        self.rows = lax.axis_size("row")
        self.cols = lax.axis_size("col")
        self.xs = self.rows // CORES
        self.bs = self.cols // LINE
        self.row = lax.axis_index("row")
        self.col = lax.axis_index("col")
        self.x = self.row // CORES
        self.core = self.row % CORES
        self.a = self.col // self.bs
        self.b = self.col % self.bs
        self.chips = [(dx, db) for db in range(self.bs) for dx in range(self.xs)]
        self.numbers = jnp.stack([self.a, self.b, self.x, self.core]).astype(jnp.int32)

    def index(self, x, core, a, b):
        return ((x % self.xs) * CORES + core % CORES) * self.cols + (a % LINE) * self.bs + b % self.bs

    def send(self, value, dx=0, dcore=0, db=0, flip=0):
        pairs = [
            (self.index(x, core, a, b), self.index(x + dx, core + dcore, a ^ flip, b + db))
            for x in range(self.xs)
            for core in range(CORES)
            for a in range(LINE)
            for b in range(self.bs)
        ]
        return lax.ppermute(value, AXES, pairs)


def put_blocks(xs, bs, place, weights, part, mask, db, outs):
    a, b, x, core = (place[i] for i in range(4))
    size = weights.shape[1]
    rows = xs * CORES
    eye = (
        lax.broadcasted_iota(jnp.int32, (size, size), 0) == lax.broadcasted_iota(jnp.int32, (size, size), 1)
    ).astype(F32)
    tile = lax.rem(b + db, bs)
    for k, flip in enumerate(ORDER):
        line = (a ^ flip) * bs + b
        row_block = (x * CORES + core) * (LINE * bs) + line
        diagonal = eye * (boost * weights[pl.ds(line, 1), :])
        values = part(k)
        for dcore in range(CORES):
            for dx in range(xs):
                block = lax.rem(x + dx, xs) * CORES + lax.rem(core + dcore, CORES)
                node_block = a * (bs * rows) + tile * rows + block
                total = diagonal * (row_block == node_block).astype(F32)
                for slot in range(values.shape[1] // size):
                    total = total + values[:, slot * size : (slot + 1) * size] * mask(k, slot, block)
                outs[dcore][k * size : (k + 1) * size, dx * size : (dx + 1) * size] = total.astype(LOW)


def own_blocks_kernel(xs, bs, slots, place, *refs):
    held, outs, scratch, sems = refs[:4], refs[4:-5], refs[-5:-1], refs[-1]
    copies = [pltpu.make_async_copy(held[i], scratch[i], sems.at[i]) for i in range(4)]
    for copy in copies:
        copy.start()
    for copy in copies:
        copy.wait()
    cols, counts, block_vals, weights = scratch
    a, b = place[0], place[1]
    size = weights.shape[1]

    def line(k, dest):
        return (a ^ ORDER[k]) * bs + dest

    def rows(k, dest):
        return block_vals[pl.ds(pl.multiple_of(line(k, dest) * size, size), size), :]

    def column(k, slot, dest):
        at = line(k, dest)
        return jnp.where(slot < counts[0, at], cols[slot, at], -1)

    for db in range(1, bs):
        out = outs[CORES + db - 1]
        dest = lax.rem(b - db + bs, bs)
        for k in range(LINE):
            out[k * size : (k + 1) * size, :] = rows(k, dest)
        at_row = lax.broadcasted_iota(jnp.int32, (16, slots * size), 0)
        head = jnp.zeros((16, slots * size), jnp.int32)
        for k in range(LINE):
            for slot in range(slots):
                head = jnp.where(at_row == k * slots + slot, column(k, slot, dest), head)
        out[LINE * size :, :] = head.astype(F32).astype(LOW)
    put_blocks(
        xs,
        bs,
        place,
        weights,
        lambda k: rows(k, b).astype(F32),
        lambda k, slot, block: (column(k, slot, b) == block).astype(F32),
        0,
        outs[:CORES],
    )


def sent_blocks_kernel(xs, bs, slots, db, place, got, weights, *outs):
    size = weights.shape[1]
    head = got[LINE * size :, :].astype(F32)

    def mask(k, slot, block):
        at = k * slots + slot
        return (head[at : at + 1, :size] == block.astype(F32)).astype(F32)

    put_blocks(
        xs, bs, place, weights, lambda k: got[k * size : (k + 1) * size, :].astype(F32), mask, db, outs
    )


def operator(at, block_vals, block_cols, block_counts, self_weight, size):
    slots = block_cols.shape[0]
    weights = self_weight.reshape(-1, size)
    dense = like(LINE * size, at.xs * size)
    own, other, *sent = call(
        functools.partial(own_blocks_kernel, at.xs, at.bs, slots),
        [dense] * CORES + [like(LINE * size + 16, slots * size)] * (at.bs - 1),
        [
            pltpu.SMEM(block_cols.shape, jnp.int32),
            pltpu.SMEM(block_counts.shape, jnp.int32),
            pltpu.VMEM(block_vals.shape, block_vals.dtype),
            pltpu.VMEM(weights.shape, weights.dtype),
            pltpu.SemaphoreType.DMA((4,)),
        ],
        at.numbers,
        block_cols,
        block_counts,
        block_vals,
        weights,
        numbers=1,
        outside=4,
        alone=True,
    )
    result = [[own, other]]
    arrived = [at.send(value, db=-db) for db, value in enumerate(sent, 1)]
    for db, got in enumerate(arrived, 1):
        kernel = functools.partial(sent_blocks_kernel, at.xs, at.bs, slots, db)
        result.append(call(kernel, [dense] * CORES, [], at.numbers, got, weights, numbers=1))
    return result, sent


def sums_kernel(n_ops, pieces, *refs):
    ops, arrays, (*outs, left, right) = refs[:n_ops], refs[n_ops:-6], refs[-6:]
    size, wide = outs[0].shape[0], ops[0].shape[1]
    for i, op in enumerate(ops):
        left[:, i * wide : (i + 1) * wide] = op[...]
    for i, (k, row) in enumerate(pieces):
        right[i * size : (i + 1) * size, :] = arrays[k][row : row + size, :]
    step = right.shape[1] // 4
    for k in range(4):
        columns = slice(k * step, (k + 1) * step)
        part = dot(left[...], right[:, columns], ((1,), (0,)))
        for i, out in enumerate(outs):
            out[:, columns] = part[i * size : (i + 1) * size].astype(out.dtype)


def sums(at, ops, own, across):
    size, width = own[0, 0].shape
    arrays = [*own.values(), *across]
    pieces = []
    for db in range(at.bs):
        pieces += [(db * at.xs + dx, 0) for dx in range(at.xs)]
        pieces += [(len(own) + 1, (db * at.xs + dx - 1) * size) if db or dx else (len(own), 0) for dx in range(at.xs)]
    rows, depth = LINE * size, len(pieces) * size
    return call(
        functools.partial(sums_kernel, CORES * at.bs, pieces),
        [like(size, width, kind=F32)] * 2 + [like(size, width)] * 2,
        [pltpu.VMEM((rows, depth), LOW), pltpu.VMEM((depth, width), LOW)],
        *[op for pair in ops for op in pair],
        *arrays,
    )


def back_kernel(n_ops, *refs):
    ops, lines, rest = refs[:n_ops], refs[n_ops : n_ops + 3], refs[n_ops + 3 :]
    right = jnp.concatenate([line[...] for line in lines], 0)
    parts = [dot(op[...], right, ((0,), (0,))) for op in ops]
    if len(rest) == 1:
        rows = parts[0].shape[0]
        for i, part in enumerate(parts):
            rest[0][i * rows : (i + 1) * rows, :] = part.astype(LOW)
        return
    got, outs = rest[0], rest[1:]
    size = outs[0].shape[0]
    per = parts[0].shape[0] // size
    for i, out in enumerate(outs):
        k = i % per * size
        total = parts[i // per][k : k + size] + got[i * size : (i + 1) * size, :].astype(F32)
        out[...] = total.astype(out.dtype)


def add_up_kernel(n_keeps, *refs):
    *parts, out = refs
    per = len(parts) // n_keeps
    for k, (start, end) in enumerate(bounds(out.shape[1])):
        total = parts[k * per][...]
        for part in parts[k * per + 1 : (k + 1) * per]:
            total = total + part[...].astype(F32)
        out[:, start:end] = total


def along_x(at, value):
    return [value] + [at.send(value, dx=-dx) for dx in range(1, at.xs)]


def along_b(at, value):
    return [value] + [at.send(value, db=-db) for db in range(1, at.bs)]


def gathered_halves(at, halves, gate):
    rows = halves[0].shape[0]
    left, right = along_x(at, halves[0]), along_b(at, halves[1])
    steps = [left[1:] + right[1:]]
    arrays, held = [join(after(left[0], gate), *left[1:]), join(after(right[0], gate), *right[1:])], {}
    for dx in range(at.xs):
        held[dx, 0, 0] = (0, dx * rows)
    for db in range(at.bs):
        held[0, db, 1] = (1, db * rows)
    left, right = arrays
    for db in range(1, at.bs):
        arrays.append(at.send(left, db=-db))
        for dx in range(at.xs):
            held[dx, db, 0] = (len(arrays) - 1, dx * rows)
    for dx in range(1, at.xs):
        arrays.append(at.send(right, dx=-dx))
        for db in range(at.bs):
            held[dx, db, 1] = (len(arrays) - 1, db * rows)
    return arrays, held, steps + [arrays[2:]]


def both_cores(at, arrays, held, gates):
    count = len(arrays)
    across = [at.send(after(value, *gate), dcore=1) for value, gate in zip(arrays, gates)]
    places = {(0, *place): at for place, at in held.items()}
    places.update({(1, *place): (k + count, i) for place, (k, i) in held.items()})
    return arrays + across, places


def line_kernel(place, weight, far, near, last, left, right):
    count, half = weight.shape[0], left.shape[1]
    for flip, source in zip(ORDER, (weight, far, near, last)):
        rows = pl.ds(pl.multiple_of((place[0] ^ flip) * count, count), count)
        left[rows, :] = source[:, :half]
        right[rows, :] = source[:, half:]


def line_weight(at, weight):
    count, width = weight.shape
    far = at.send(weight, flip=2)
    near = at.send(after(weight, far), flip=1)
    last = at.send(far, flip=1)
    halves = [like(LINE * count, width // 2)] * 2
    return call(line_kernel, halves, [], at.numbers, weight, far, near, last, numbers=1)


def dense_kernel(held, xs, bs, lanes, n_held, place, *refs):
    (bias_in, grad_in), arrays, refs = refs[:2], refs[2 : 2 + n_held], refs[2 + n_held :]
    total, near, far, act_ref, left_ref, right_ref, rows_ref = refs[:7]
    messages, refs = refs[7 : 6 + xs], refs[6 + xs :]
    backs, refs = refs[:CHUNKS], refs[CHUNKS:]
    agg_ref, turned, acc, back, blocks, bias, out_grad, sems = refs
    b, x, core = place[1], place[2], place[3]
    width = bias.shape[1]
    half = width // 2
    group = bs * lanes
    places = [(dcore, dx, db) for dcore in range(CORES) for db in range(bs) for dx in range(xs)]
    number = {(at, h): n for n, (at, h) in enumerate((at, h) for at in places for h in range(2))}

    copies = [pltpu.make_async_copy(bias_in, bias, sems.at[0])]
    for (at, h), n in number.items():
        k, row = held[*at, h]
        block = blocks.at[pl.ds(n * lanes, lanes), :]
        copies.append(pltpu.make_async_copy(arrays[k].at[pl.ds(row, lanes), :], block, sems.at[n + 1]))
    copies.append(pltpu.make_async_copy(grad_in, out_grad, sems.at[len(number) + 1]))
    for copy in copies:
        copy.start()

    def weight(at, h):
        n = number[at, h]
        return blocks[n * lanes : (n + 1) * lanes, :]

    agg_ref[...] = (total[...] + near[...].astype(F32) + far[...].astype(F32)).astype(LOW)
    count = lanes // LINE
    at_in = lax.broadcasted_iota(jnp.int32, (group, group), 0)
    at_out = lax.broadcasted_iota(jnp.int32, (group, group), 1)
    db, inner = at_out // lanes, at_out % lanes
    source = (inner // count) * (bs * count) + lax.rem(b + db, bs) * count + inner % count
    turn = (at_in == source).astype(F32).astype(LOW)
    for r in range(width // group):
        at_r = slice(r * group, (r + 1) * group)
        turned[:, at_r] = dot(agg_ref[:, at_r], turn, ((1,), (0,))).astype(LOW)

    def columns(dcore, dx, db):
        row = lax.rem(x + dx, xs) * CORES + lax.rem(core + dcore, CORES)
        return pl.ds(pl.multiple_of(row * group + db * lanes, lanes), lanes)

    copies[0].wait()
    acc[...] = jnp.broadcast_to(bias[...], acc.shape)
    for at in places:
        left = turned[:, columns(*at)]
        for h in range(2):
            copies[1 + number[at, h]].wait()
            acc[:, h * half : (h + 1) * half] += dot(left, weight(at, h), ((1,), (0,)))
    copies[-1].wait()
    for dx, out in enumerate([rows_ref, *messages]):
        start = half if dx else 0
        for db in range(bs):
            for dcore in range(CORES):
                out[:, start : start + lanes] = turned[:, columns(dcore, dx, db)]
                start += lanes
    pre = acc[...]
    phi = 0.5 * (1.0 + lax.erf(pre * (0.5**0.5)))
    act_ref[...] = (pre * phi).astype(LOW)
    slope = phi + pre * (jnp.exp(-0.5 * pre * pre) * 0.3989422804014327)
    pre_low = (out_grad[...].astype(F32) * slope).astype(LOW)
    for out in (left_ref, *messages):
        out[:, :half] = pre_low[:, :half]
    right_ref[...] = pre_low[:, half:]
    for at in places:
        total = 0.0
        for h, ref in enumerate((left_ref, right_ref)):
            total = total + dot(ref[...], weight(at, h), ((1,), (1,)))
        back[:, columns(*at)] = total.astype(LOW)
    for r in range(width // group):
        part = dot(back[:, r * group : (r + 1) * group], turn, ((1,), (1,))).astype(LOW)
        for k, (start, end) in enumerate(bounds(width)):
            left, right = max(start, r * group), min(end, (r + 1) * group)
            if left < right:
                backs[k][:, left - start : right - start] = part[:, left - r * group : right - r * group]


def pick_kernel(db, *refs):
    left, rows, messages, out = refs[0], refs[1], refs[2:-1], refs[-1]
    size, half = left.shape
    wide = out.shape[1] - half
    out[:size, :half] = left[...]
    out[:size, half:] = rows[:, db * wide : (db + 1) * wide]
    for i, message in enumerate(messages, 1):
        at = slice(i * size, (i + 1) * size)
        out[at, :half] = message[:, :half]
        out[at, half:] = message[:, half + db * wide : half + (db + 1) * wide]


def spread(at, lanes, left, right, rows, messages, gate):
    size, half = left.shape
    arrived = [at.send(message, dx=dx) for dx, message in enumerate(messages, 1)]
    rights = [right] + [at.send(right, db=db) for db in range(1, at.bs)]
    steps = [arrived + rights[1:]]

    def pick(db):
        outs = [like(at.xs * size, half + CORES * lanes)]
        return call(functools.partial(pick_kernel, db), outs, [], after(left, gate), rows, *arrived)[0]

    held = {}

    def keep(k, place, row):
        held[place] = (k, row)

    arrays = [pick(0), join(after(right, gate), *rights[1:])]
    for dx in range(at.xs):
        keep(0, (-dx % at.xs, 0, 0), dx * size)
    for db in range(at.bs):
        keep(1, (0, -db % at.bs, 1), db * size)
    for db in range(1, at.bs):
        arrays.append(at.send(pick(db), db=db))
        for dx in range(at.xs):
            keep(len(arrays) - 1, (-dx % at.xs, -db % at.bs, 0), dx * size)
    for dx in range(1, at.xs):
        arrays.append(at.send(arrays[1], dx=dx))
        for db in range(at.bs):
            keep(len(arrays) - 1, (-dx % at.xs, -db % at.bs, 1), db * size)
    return arrays, held, steps + [arrays[2:]]


def grad_kernel(held, xs, bs, lanes, dcore, n_arrays, place, *refs):
    arrays, (*outs, left, right, product, sums_ref) = refs[:n_arrays], refs[n_arrays:]
    a, b, x, core = (place[i] for i in range(4))
    size, width = left.shape[0] // (xs * bs), right.shape[1]
    half, count, group = width // 2, lanes // LINE, bs * lanes
    for n, (dx, db) in enumerate((dx, db) for db in range(bs) for dx in range(xs)):
        rows = slice(n * size, (n + 1) * size)
        k, row = held[dx, db, 0]
        right[rows, :half] = arrays[k][row : row + size, :half]
        start = half + dcore * lanes
        left[rows, :] = arrays[k][row : row + size, start : start + lanes]
        k, row = held[dx, db, 1]
        right[rows, half:] = arrays[k][row : row + size, :]
    product[:, :width] = dot(left[...], right[...], ((0,), (0,)))
    total = jnp.sum(right[...].astype(F32), 0, keepdims=True)
    sums_ref[...] = jnp.broadcast_to(total, sums_ref.shape)
    row = x * CORES + lax.rem(core + dcore, CORES)
    own = sums_ref[0:1, pl.ds(pl.multiple_of(row * group, group), group)]
    at_row = lax.broadcasted_iota(jnp.int32, (lanes, group), 0)
    at_lane = lax.broadcasted_iota(jnp.int32, (lanes, group), 1)
    source = (at_row // count) * (bs * count) + b * count + at_row % count
    column = jnp.sum(jnp.where(at_lane == source, own, 0.0), 1, keepdims=True)
    product[:, width:] = jnp.broadcast_to(column, (lanes, 128))
    if dcore:
        [out] = outs
        out[:, :width] = product[:, :width].astype(LOW)
        out[:, width:] = two_parts(product[:, width:])
        return
    got, outs = outs[0], outs[1:]
    for out, flip in zip(outs, ORDER):
        rows = pl.ds(pl.multiple_of((a ^ flip) * count, count), count)
        tail = got[rows, width:].astype(F32)
        tail = product[rows, width:] + (tail[:, 0:1] + tail[:, 1:2])
        out[:, :width] = (product[rows, :width] + got[rows, :width].astype(F32)).astype(out.dtype)
        out[:, width : width + 128] = two_parts(tail) if out.dtype == LOW else tail


def two_parts(value):
    high = value.astype(LOW)
    rest = (value - high.astype(F32)).astype(LOW)
    lane = lax.broadcasted_iota(jnp.int32, value.shape, 1)
    return jnp.where(lane == 0, high.astype(F32), jnp.where(lane == 1, rest.astype(F32), 0.0)).astype(LOW)


def fold_kernel(kept, got, far):
    width = got.shape[1] - 128
    tail = got[:, width:].astype(F32)
    far[:, :width] = (kept[:, :width] + got[:, :width].astype(F32)).astype(LOW)
    far[:, width : width + 128] = two_parts(kept[:, width : width + 128] + (tail[:, 0:1] + tail[:, 1:2]))


def last_fold_kernel(kept, *refs):
    *arrived, weight_out, bias_out = refs
    width = weight_out.shape[1]
    total, tail = kept[:, :width], kept[:, width : width + 128]
    for got in arrived:
        total = total + got[:, :width].astype(F32)
        rest = got[:, width : width + 128].astype(F32)
        tail = tail + (rest[:, 0:1] + rest[:, 1:2])
    weight_out[...] = total
    bias_out[...] = tail


def far_kernel(kept, got, far):
    far[...] = (kept[...] + got[...].astype(F32)).astype(LOW)


def shards(node_feats, block_vals, block_cols, block_counts, self_weight, weight, bias, out_grad):
    at = Place()
    size, width = node_feats.shape
    own_rows = weight.shape[0]
    lanes = LINE * own_rows
    aligned = lanes % 128 == 0
    halves = line_weight(at, weight) if aligned else []
    ops, gate = operator(at, block_vals, block_cols, block_counts, self_weight, size)
    node_feats = after(node_feats, *gate)
    own = {(dx, db): at.send(node_feats, dx=-dx, db=-db) if dx or db else node_feats for dx, db in at.chips}
    first, *chips = at.chips
    across = [at.send(own[first], dcore=1), at.send(join(after(own[chips[0]], *ops[-1], *halves), *[own[chip] for chip in chips[1:]]), dcore=1)]
    total, kept, to_near, to_last = sums(at, ops, own, across)
    got = at.send(to_last, flip=1)
    near = at.send(to_near, flip=1)
    [far] = call(far_kernel, [like(size, width)], [], kept, got)
    far = at.send(far, flip=2)

    if not aligned:
        return plain_rest(at, ops, total + near.astype(F32) + far.astype(F32), weight, bias, out_grad)
    halves = [after(half, *own.values(), *ops[-1]) for half in halves]
    arrays, held, steps = gathered_halves(at, halves, to_last)
    early = len(arrays) - len(steps[1])
    arrays, held = both_cores(at, arrays, held, [[]] * early + [[near, far]] * len(steps[1]))
    widths = [end - start for start, end in bounds(width)]
    n_blocks = len(held)
    activations, left, right, rows, *rest = call(
        functools.partial(dense_kernel, held, at.xs, at.bs, lanes, len(arrays)),
        [like(size, width)]
        + [like(size, width // 2)] * 2
        + [like(size, at.bs * CORES * lanes)]
        + [like(size, width // 2 + at.bs * CORES * lanes)] * (at.xs - 1)
        + [like(size, wide) for wide in widths],
        [pltpu.VMEM((size, width), kind) for kind in (LOW, LOW, F32, LOW)]
        + [
            pltpu.VMEM((n_blocks * lanes, width // 2), LOW),
            pltpu.VMEM((1, width), F32),
            pltpu.VMEM((size, width), LOW),
            pltpu.SemaphoreType.DMA((n_blocks + 2,)),
        ],
        at.numbers,
        bias[None, :],
        out_grad,
        *arrays,
        total,
        near,
        far,
        numbers=1,
        outside=2 + len(arrays),
    )
    messages, backs = rest[: at.xs - 1], rest[at.xs - 1 :]

    fars = [at.send(backs[0], flip=2)]
    arrays, held, steps = spread(at, lanes, left, right, rows, messages, fars[0])
    nears = [at.send(join(backs[0], fars[0]), flip=1)]
    for k in range(1, CHUNKS):
        fars.append(at.send(after(backs[k], *fars, *steps[0]), flip=2))
        nears.append(at.send(join(backs[k], fars[k]), flip=1))
    feat, parts = feat_sums(at, ops, backs[0], fars[0], after(nears[0], *fars, *steps[1]))
    gates = feat[1:]
    wide, long = width + 128, width + 256
    scratch = [
        pltpu.VMEM((size * len(at.chips), lanes), LOW),
        pltpu.VMEM((size * len(at.chips), width), LOW),
        pltpu.VMEM((lanes, wide), F32),
        pltpu.VMEM((8, width), F32),
    ]
    kernel = functools.partial(grad_kernel, held, at.xs, at.bs, lanes)
    [across] = call(
        functools.partial(kernel, 1, len(arrays)), [like(lanes, wide)], scratch, at.numbers, *arrays, numbers=1
    )
    got = at.send(across, dcore=1)
    outs = [like(own_rows, wide, kind=F32)] * 2 + [like(own_rows, long), like(own_rows, wide)]
    total, kept, to_near, to_last = call(
        functools.partial(kernel, 0, len(arrays)), outs, scratch, at.numbers, *arrays, got, numbers=1
    )
    got = at.send(to_last, flip=1)
    [sent] = call(fold_kernel, [like(own_rows, long)], [], kept, got)
    for k in range(1, CHUNKS):
        more, parts = feat_sums(at, ops, backs[k], fars[k], after(nears[k], sent, *parts, *gates))
        feat = feat + more
    near = at.send(to_near, flip=1)
    far = at.send(sent, flip=2)
    [feat_grad] = call(functools.partial(add_up_kernel, CHUNKS), [like(size, width, kind=F32)], [], *feat)
    outs = [like(own_rows, width, kind=F32), like(own_rows, 128, kind=F32)]
    weight_grad, bias_grad = call(last_fold_kernel, outs, [], after(total, feat_grad), near, far)
    return activations, feat_grad, weight_grad, bias_grad[:, 0]


def feat_sums(at, ops, *lines):
    size, chunk = lines[0].shape
    rows = len(at.chips) * size
    kernel = functools.partial(back_kernel, len(ops))
    [across] = call(kernel, [like(rows, chunk)], [], *[pair[1] for pair in ops], *lines)
    got = at.send(across, dcore=1)
    outs = [like(size, chunk, kind=F32)] + [like(size, chunk)] * (len(at.chips) - 1)
    parts = call(kernel, outs, [], *[pair[0] for pair in ops], *lines, got)
    sent = [at.send(part, dx=dx, db=db) for part, (dx, db) in zip(parts[1:], at.chips[1:])]
    return [parts[0]] + sent, parts


def plain_rest(at, ops, agg, weight, bias, out_grad):
    size, width = out_grad.shape
    own_rows = weight.shape[0]
    lanes = LINE * own_rows
    agg = agg.astype(LOW)
    whole_weight = lax.all_gather(weight, AXES, axis=0, tiled=True)
    pre = dot(agg, whole_weight, ((1,), (0,))) + bias[None, :]
    phi = 0.5 * (1.0 + lax.erf(pre * (0.5**0.5)))
    activations = (pre * phi).astype(LOW)
    slope = phi + pre * (jnp.exp(-0.5 * pre * pre) * 0.3989422804014327)
    pre_low = (out_grad.astype(F32) * slope).astype(LOW)
    feat = []
    for start, end in bounds(width):
        back = dot(pre_low, whole_weight[start:end], ((1,), (1,))).astype(LOW)
        far = at.send(back, flip=2)
        feat = feat + feat_sums(at, ops, back, far, at.send(join(back, far), flip=1))[0]
    [feat_grad] = call(functools.partial(add_up_kernel, CHUNKS), [like(size, width, kind=F32)], [], *feat)

    groups = agg.reshape(size, at.rows, LINE, at.bs, own_rows)
    groups = jnp.concatenate([lax.dynamic_slice_in_dim(groups, at.a ^ flip, 1, 2) for flip in ORDER], 2)
    messages = []
    for dx, db in at.chips:
        dest_x = (at.x + dx) % at.xs
        wide = one_of(groups, (at.b + db) % at.bs, 3)
        picked = [
            one_of(wide, dest_x * CORES + (at.core + dcore) % CORES, 1).reshape(size, lanes) for dcore in range(CORES)
        ]
        message = jnp.concatenate([pre_low] + picked, 1)
        messages.append(at.send(message, dx=dx, db=db) if dx or db else message)
    own = jnp.concatenate(messages)
    other = at.send(own, dcore=1)
    weight_part = dot(own[:, width : width + lanes], own[:, :width], ((0,), (0,)))
    weight_part = weight_part + dot(other[:, width + lanes :], other[:, :width], ((0,), (0,)))
    bias_part = jnp.sum(own[:, :width].astype(F32), 0) + jnp.sum(other[:, :width].astype(F32), 0)
    bias_part = one_of(one_of(bias_part.reshape(at.rows, LINE, at.bs, own_rows), at.row, 0), at.b, 1)
    bias_part = jnp.concatenate([one_of(bias_part, at.a ^ flip, 0) for flip in ORDER])
    near = at.send(weight_part[2 * own_rows :].astype(LOW), flip=1).astype(F32)
    kept = weight_part[: 2 * own_rows] + near
    far = at.send(kept[own_rows:].astype(LOW), flip=2).astype(F32)
    near_bias = at.send(bias_part[2 * own_rows :], flip=1)
    kept_bias = bias_part[: 2 * own_rows] + near_bias
    bias_grad = kept_bias[:own_rows] + at.send(kept_bias[own_rows:], flip=2)
    return activations, feat_grad, kept[:own_rows] + far, bias_grad


def solution(mesh):
    placed = (
        P(("col", "row"), None),
        P("row", "col"),
        P("col", "row"),
        P("col", "row"),
        P("row"),
        P(("row", "col"), None),
        P(),
        P(("row", "col"), None),
    )
    return jax.shard_map(
        shards,
        mesh=mesh,
        in_specs=placed,
        out_specs=(
            P(("row", "col"), None),
            P(("col", "row"), None),
            P(("row", "col"), None),
            P(("row", "col")),
        ),
        check_vma=False,
    )
```

time: 222 us -> 176 us (0.79)
  Pallas kernels: 47.4 us -> 24.3 us
  local copies, waits for them, and re-layouts: 17.4 us -> 4.41 us
  starting transfers between devices: 46.2 us -> 40.3 us
  other arithmetic: 3.5 us -> 0.65 us
    pallas_call x13 -> x23, Pallas kernels: 47.4 us -> 24.3 us  [call(): pl.pallas_call(kernel, out_shape=outs, in_specs=specs, out_specs=[whole]...]
    unnamed x138 -> x20, local copies, waits for them, and re-layouts: 11 us -> 3.79 us
    ppermute x58 -> x40, starting transfers between devices: 46.2 us -> 40.3 us  [send(): return lax.ppermute(value, AXES, pairs)]
    ppermute x58 -> x40, waiting for transfers between devices: 106 us -> 105 us  [send(): return lax.ppermute(value, AXES, pairs)]
  transfers between devices with their start and end apart: 58 -> 40, of which waited for: 27 -> 18; matrix products, arithmetic and copies ran while one was open for 4% -> 0% of each run, Pallas kernels for 12% -> 6%
where the time goes in v3:
time: 176 us
  waiting for transfers between devices  105 us (60%)
  starting transfers between devices  40.3 us (23%)
  Pallas kernels  24.3 us (14%)
  local copies, waits for them, and re-layouts  4.41 us (3%)
    ppermute x40, waiting for transfers between devices, send(): return lax.ppermute(value, AXES, pairs)  105 us
    ppermute x40, starting transfers between devices, send(): return lax.ppermute(value, AXES, pairs)  40.3 us
    pallas_call x23, Pallas kernels, call(): pl.pallas_call(kernel, out_shape=outs, in_specs=specs, out_specs=[whole]...  24.3 us
    unnamed x20, local copies, waits for them, and re-layouts  3.79 us
  transfers between devices with their start and end apart: 40, of which 18 were waited for; matrix products, arithmetic and copies ran while one was open for 0% of the time, Pallas kernels for 6%

profile of v3, /device:TPU:0, one launch (start us, length us, event | category | flops | bytes accessed | tf_op | source)
XLA Modules:
  0.0 176.0 jit_solution(7837957633667358228)
XLA Ops:
  1.3 2.8 %shard_map.112 = (bf16[512,256]{1,0:T(8,128)(2,1)}, bf16[512,256]{1,0:T(8,128)(2,1)}, bf16[528,256]{1,0:T(8,128)(2,1)}) custom-call(s32[4]{0:T(128)} %pad_add_fusion.place, s32[2,8]{1,0:T(2,128)} %refs_0_.1, s32[1,8]{1,0:T(1,128)} %refs_1_.2, bf16[1024,256]{1,0:T(8,128)(2,1)} %refs_2_.1, f32[8,128]{1,0:T(8,128)} %bitcast.6), custom_call_target="tpu_custom_call" | custom-call | flops 1 | bytes 1 | tf_op jit(solution)/shard_map/pallas_call | solution.py:48
  4.1 3.0 %collective-permute-start.6 = (bf16[528,256]{1,0:T(8,128)(2,1)}, bf16[528,256]{1,0:T(8,128)(2,1)S(1)}, u32[]{:S(2)}, u32[]{:S(2)}) collective-permute-start(bf16[528,256]{1,0:T(8,128)(2,1)} %get-tuple-element.53), channel_id=1, source_target_pairs={{0,1},{1,0},{2,3},{3,2},{4,5},{5,4},{6,7},{7,6},{8,9},{9,8},{10,11... | collective-permute-start | bytes 811016 | tf_op jit(solution)/shard_map/ppermute | solution.py:117
  7.2 2.6 %collective-permute-start = (bf16[64,2048]{1,0:T(8,128)(2,1)}, bf16[64,2048]{1,0:T(8,128)(2,1)S(1)}, u32[]{:S(2)}, u32[]{:S(2)}) collective-permute-start(bf16[64,2048]{1,0:T(8,128)(2,1)} %weight.1), channel_id=1, source_target_pairs={{0,4},{1,5},{2,6},{3,7},{4,0},{5,1},{6,2},{7,3},{8,12},{9,13},{10,... | collective-permute-start | bytes 786440 | tf_op jit(solution)/shard_map/ppermute | solution.py:117
  9.8 1.5 collective-permute-start.3
  11.7 1.5 collective-permute-start.4
  13.2 8.4 %collective-permute-done.far = bf16[64,2048]{1,0:T(8,128)(2,1)S(1)} collective-permute-done((bf16[64,2048]{1,0:T(8,128)(2,1)}, bf16[64,2048]{1,0:T(8,128)(2,1)S(1)}, u32[]{:S(2)}, u32[]{:S(2)}) %collective-permute-start) | collective-permute-done | bytes 262176 | tf_op jit(solution)/shard_map/ppermute | solution.py:117
  22.4 1.2 collective-permute-start.2
  25.8 5.3 %collective-permute-done.1.near = bf16[64,2048]{1,0:T(8,128)(2,1)S(1)} collective-permute-done((bf16[64,2048]{1,0:T(8,128)(2,1)}, bf16[64,2048]{1,0:T(8,128)(2,1)S(1)}, u32[]{:S(2)}, u32[]{:S(2)}) %collective-permute-start.1) | collective-permute-done | bytes 262176 | tf_op jit(solution)/shard_map/ppermute | solution.py:117
  31.1 3.6 %collective-permute-done.2.last = bf16[64,2048]{1,0:T(8,128)(2,1)S(1)} collective-permute-done((bf16[64,2048]{1,0:T(8,128)(2,1)S(1)}, bf16[64,2048]{1,0:T(8,128)(2,1)S(1)}, u32[]{:S(2)}, u32[]{:S(2)}) %collective-permute-start.2) | collective-permute-done | bytes 262176 | tf_op jit(solution)/shard_map/ppermute | solution.py:117
  34.8 0.9 copy-done.4
  37.2 0.8 copy-done.2
  38.0 1.5 collective-permute-start.9
  40.2 1.1 collective-permute-done.7.refs_8_
  41.4 2.4 %shard_map.115 = (f32[128,2048]{1,0:T(8,128)S(1)}, f32[128,2048]{1,0:T(8,128)S(1)}, bf16[128,2048]{1,0:T(8,128)(2,1)S(1)}, bf16[128,2048]{1,0:T(8,128)(2,1)S(1)}) custom-call(bf16[512,256]{1,0:T(8,128)(2,1)S(1)} %copy-done, bf16[512,256]{1,0:T(8,128)(2,1)S(1)} %copy-done.1, bf16[512,256]{1,0:T(8,128)(2,1)S(1)} %get-tuple-element.55.refs_2_.refs_1_, ...), custom_call_target="tpu_custom_call" | custom-call | flops 1 | bytes 1 | tf_op jit(solution)/shard_map/pallas_call | solution.py:48
  43.8 1.8 %collective-permute-start.16 = (bf16[128,2048]{1,0:T(8,128)(2,1)S(1)}, bf16[128,2048]{1,0:T(8,128)(2,1)S(1)}, u32[]{:S(2)}, u32[]{:S(2)}) collective-permute-start(bf16[128,2048]{1,0:T(8,128)(2,1)S(1)} %get-tuple-element.62), channel_id=1, source_target_pairs={{0,2},{1,3},{2,0},{3,1},{4,6},{5,7},{6,4},{7,5},{8,10},{9,11},{10,... | collective-permute-start | bytes 1572872 | tf_op jit(solution)/shard_map/ppermute | solution.py:117
  45.6 6.8 %collective-permute-done.9.refs_1_ = bf16[256,1024]{1,0:T(8,128)(2,1)S(1)} collective-permute-done((bf16[256,1024]{1,0:T(8,128)(2,1)S(1)}, bf16[256,1024]{1,0:T(8,128)(2,1)S(1)}, u32[]{:S(2)}, u32[]{:S(2)}) %collective-permute-start.9) | collective-permute-done | bytes 524320 | tf_op jit(solution)/shard_map/ppermute | solution.py:117
  53.7 1.0 collective-permute-start.12
  54.7 1.7 collective-permute-start.15
  56.4 2.2 %collective-permute-done.16.got = bf16[128,2048]{1,0:T(8,128)(2,1)S(1)} collective-permute-done((bf16[128,2048]{1,0:T(8,128)(2,1)S(1)}, bf16[128,2048]{1,0:T(8,128)(2,1)S(1)}, u32[]{:S(2)}, u32[]{:S(2)}) %collective-permute-start.16) | collective-permute-done | bytes 524320 | tf_op jit(solution)/shard_map/ppermute | solution.py:117
  58.7 3.3 %collective-permute-start.17 = (bf16[128,2048]{1,0:T(8,128)(2,1)S(1)}, bf16[128,2048]{1,0:T(8,128)(2,1)S(1)}, u32[]{:S(2)}, u32[]{:S(2)}) collective-permute-start(bf16[128,2048]{1,0:T(8,128)(2,1)S(1)} %shard_map.118), channel_id=1, source_target_pairs={{0,4},{1,5},{2,6},{3,7},{4,0},{5,1},{6,2},{7,3},{8,12},{9,13},{10,... | collective-permute-start | bytes 1572872 | tf_op jit(solution)/shard_map/ppermute | solution.py:117
  62.0 17.4 %collective-permute-done.15.refs_11_ = bf16[128,2048]{1,0:T(8,128)(2,1)S(1)} collective-permute-done((bf16[128,2048]{1,0:T(8,128)(2,1)S(1)}, bf16[128,2048]{1,0:T(8,128)(2,1)S(1)}, u32[]{:S(2)}, u32[]{:S(2)}) %collective-permute-start.15) | collective-permute-done | bytes 524320 | tf_op jit(solution)/shard_map/ppermute | solution.py:117
  79.4 4.5 %collective-permute-done.17.refs_12_ = bf16[128,2048]{1,0:T(8,128)(2,1)S(1)} collective-permute-done((bf16[128,2048]{1,0:T(8,128)(2,1)S(1)}, bf16[128,2048]{1,0:T(8,128)(2,1)S(1)}, u32[]{:S(2)}, u32[]{:S(2)}) %collective-permute-start.17) | collective-permute-done | bytes 524320 | tf_op jit(solution)/shard_map/ppermute | solution.py:117
  84.4 2.1 %collective-permute-done.18.refs_8_ = bf16[512,1024]{1,0:T(8,128)(2,1)S(1)} collective-permute-done((bf16[512,1024]{1,0:T(8,128)(2,1)S(1)}, bf16[512,1024]{1,0:T(8,128)(2,1)S(1)}, u32[]{:S(2)}, u32[]{:S(2)}) %collective-permute-start.18) | collective-permute-done | bytes 1048608 | tf_op jit(solution)/shard_map/ppermute | solution.py:117
  86.6 1.5 collective-permute-done.19.refs_9_
  88.1 8.6 %shard_map.119 = (bf16[128,2048]{1,0:T(8,128)(2,1)}, bf16[128,1024]{1,0:T(8,128)(2,1)S(1)}, bf16[128,1024]{1,0:T(8,128)(2,1)S(1)}, bf16[128,1024]{1,0:T(8,128)(2...) custom-call(s32[4]{0:T(128)S(1)} %copy-done.7, ...), custom_call_target="tpu_custom_call" | custom-call | flops 1 | bytes 1 | tf_op jit(solution)/shard_map/pallas_call | solution.py:48
  96.7 1.6 collective-permute-start.22
  98.7 15.5 %collective-permute-done.20.refs_1_.refs_3_ = bf16[128,1152]{1,0:T(8,128)(2,1)S(1)} collective-permute-done((bf16[128,1152]{1,0:T(8,128)(2,1)S(1)}, bf16[128,1152]{1,0:T(8,128)(2,1)S(1)}, u32[]{:S(2)}, u32[]{:S(2)}) %collective-permute-start.20) | collective-permute-done | bytes 294944 | tf_op jit(solution)/shard_map/ppermute | solution.py:117
  115.6 1.8 %collective-permute-start.24 = (bf16[128,896]{1,0:T(8,128)(2,1)S(1)}, bf16[128,896]{1,0:T(8,128)(2,1)S(1)}, u32[]{:S(2)}, u32[]{:S(2)}) collective-permute-start(bf16[128,896]{1,0:T(8,128)(2,1)S(1)} %get-tuple-element.76.refs_0_.refs_2_), channel_id=1, source_target_pairs={{0,4},{1,5},{2,6},{3,7},{4,0},{5,1},{6,2},{7,3},{8,12},{9,13},{10,... | collective-permute-start | bytes 688136 | tf_op jit(solution)/shard_map/ppermute | solution.py:117
  117.4 14.2 %collective-permute-done.24.refs_1_.refs_3_ = bf16[128,896]{1,0:T(8,128)(2,1)S(1)} collective-permute-done((bf16[128,896]{1,0:T(8,128)(2,1)S(1)}, bf16[128,896]{1,0:T(8,128)(2,1)S(1)}, u32[]{:S(2)}, u32[]{:S(2)}) %collective-permute-start.24) | collective-permute-done | bytes 229408 | tf_op jit(solution)/shard_map/ppermute | solution.py:117
  131.6 2.2 %collective-permute-done.21.refs_4_ = bf16[256,1152]{1,0:T(8,128)(2,1)S(1)} collective-permute-done((bf16[256,1152]{1,0:T(8,128)(2,1)S(1)}, bf16[256,1152]{1,0:T(8,128)(2,1)S(1)}, u32[]{:S(2)}, u32[]{:S(2)}) %collective-permute-start.21) | collective-permute-done | bytes 589856 | tf_op jit(solution)/shard_map/ppermute | solution.py:117
  133.7 0.9 shard_map.123
  134.8 1.3 shard_map.127
  136.7 1.1 collective-permute-start.31
  137.8 0.9 shard_map.124
  139.3 1.5 collective-permute-start.29
  140.9 1.4 collective-permute-start.30
  142.3 1.7 shard_map.128
  144.0 1.0 collective-permute-start.33
  145.0 10.1 %collective-permute-done.33.got = bf16[64,2176]{1,0:T(8,128)(2,1)S(1)} collective-permute-done((bf16[64,2176]{1,0:T(8,128)(2,1)S(1)}, bf16[64,2176]{1,0:T(8,128)(2,1)S(1)}, u32[]{:S(2)}, u32[]{:S(2)}) %collective-permute-start.33) | collective-permute-done | bytes 278560 | tf_op jit(solution)/shard_map/ppermute | solution.py:117
  156.2 1.1 collective-permute-start.38
  157.3 1.7 collective-permute-start.39
  160.4 1.5 collective-permute-start.36
  162.0 1.4 collective-permute-start.37
  163.4 5.0 %collective-permute-done.35.refs_5_ = bf16[128,896]{1,0:T(8,128)(2,1)S(1)} collective-permute-done((bf16[128,896]{1,0:T(8,128)(2,1)S(1)}, bf16[128,896]{1,0:T(8,128)(2,1)S(1)}, u32[]{:S(2)}, u32[]{:S(2)}) %collective-permute-start.35) | collective-permute-done | bytes 229408 | tf_op jit(solution)/shard_map/ppermute | solution.py:117
  168.4 3.2 %collective-permute-done.36.refs_6_ = bf16[128,896]{1,0:T(8,128)(2,1)S(1)} collective-permute-done((bf16[128,896]{1,0:T(8,128)(2,1)S(1)}, bf16[128,896]{1,0:T(8,128)(2,1)S(1)}, u32[]{:S(2)}, u32[]{:S(2)}) %collective-permute-start.36) | collective-permute-done | bytes 229408 | tf_op jit(solution)/shard_map/ppermute | solution.py:117
  171.6 1.6 collective-permute-done.37.refs_7_
  173.2 1.2 shard_map.132
  174.4 1.0 shard_map.133
  (77 shorter events, 14.4 us)
Async XLA Ops:
  4.1 18.3 %collective-permute-start.6 = (bf16[528,256]{1,0:T(8,128)(2,1)}, bf16[528,256]{1,0:T(8,128)(2,1)S(1)}, u32[]{:S(2)}, u32[]{:S(2)}) collective-permute-start(bf16[528,256]{1,0:T(8,128)(2,1)} %get-tuple-element.53), channel_id=1, source_target_pairs={{0,1},{1,0},{2,3},{3,2},{4,5},{5,4},{6,7},{7,6},{8,9},{9,8},{10,11... | collective-permute-start | bytes 811016 | tf_op jit(solution)/shard_map/ppermute | solution.py:117
  7.2 14.5 %collective-permute-start = (bf16[64,2048]{1,0:T(8,128)(2,1)}, bf16[64,2048]{1,0:T(8,128)(2,1)S(1)}, u32[]{:S(2)}, u32[]{:S(2)}) collective-permute-start(bf16[64,2048]{1,0:T(8,128)(2,1)} %weight.1), channel_id=1, source_target_pairs={{0,4},{1,5},{2,6},{3,7},{4,0},{5,1},{6,2},{7,3},{8,12},{9,13},{10,... | collective-permute-start | bytes 786440 | tf_op jit(solution)/shard_map/ppermute | solution.py:117
  9.8 27.2 %collective-permute-start.3 = (bf16[128,2048]{1,0:T(8,128)(2,1)}, bf16[128,2048]{1,0:T(8,128)(2,1)S(1)}, u32[]{:S(2)}, u32[]{:S(2)}) collective-permute-start(bf16[128,2048]{1,0:T(8,128)(2,1)} %refs_4_), channel_id=1, source_target_pairs={{0,16},{1,17},{2,18},{3,19},{4,20},{5,21},{6,22},{7,23},{8,24},{9,... | collective-permute-start | bytes 1572872 | tf_op jit(solution)/shard_map/ppermute | solution.py:117
  11.2 25.8 %collective-permute-start.5 = (bf16[128,2048]{1,0:T(8,128)(2,1)}, bf16[128,2048]{1,0:T(8,128)(2,1)S(1)}, u32[]{:S(2)}, u32[]{:S(2)}) collective-permute-start(bf16[128,2048]{1,0:T(8,128)(2,1)} %refs_4_), channel_id=1, source_target_pairs={{0,17},{1,16},{2,19},{3,18},{4,21},{5,20},{6,23},{7,22},{8,25},{9,... | collective-permute-start | bytes 1572872 | tf_op jit(solution)/shard_map/ppermute | solution.py:117
  11.7 25.3 %collective-permute-start.4 = (bf16[128,2048]{1,0:T(8,128)(2,1)}, bf16[128,2048]{1,0:T(8,128)(2,1)S(1)}, u32[]{:S(2)}, u32[]{:S(2)}) collective-permute-start(bf16[128,2048]{1,0:T(8,128)(2,1)} %refs_4_), channel_id=1, source_target_pairs={{0,1},{1,0},{2,3},{3,2},{4,5},{5,4},{6,7},{7,6},{8,9},{9,8},{10,11... | collective-permute-start | bytes 1572872 | tf_op jit(solution)/shard_map/ppermute | solution.py:117
  21.7 9.5 %collective-permute-start.1 = (bf16[64,2048]{1,0:T(8,128)(2,1)}, bf16[64,2048]{1,0:T(8,128)(2,1)S(1)}, u32[]{:S(2)}, u32[]{:S(2)}) collective-permute-start(bf16[64,2048]{1,0:T(8,128)(2,1)} %weight.1), channel_id=1, source_target_pairs={{0,2},{1,3},{2,0},{3,1},{4,6},{5,7},{6,4},{7,5},{8,10},{9,11},{10,... | collective-permute-start | bytes 786440 | tf_op jit(solution)/shard_map/ppermute | solution.py:117
  22.4 12.3 %collective-permute-start.2 = (bf16[64,2048]{1,0:T(8,128)(2,1)S(1)}, bf16[64,2048]{1,0:T(8,128)(2,1)S(1)}, u32[]{:S(2)}, u32[]{:S(2)}) collective-permute-start(bf16[64,2048]{1,0:T(8,128)(2,1)S(1)} %collective-permute-done.far), channel_id=1, source_target_pairs={{0,2},{1,3},{2,0},{3,1},{4,6},{5,7},{6,4},{7,5},{8,10},{9,11},{10,... | collective-permute-start | bytes 786440 | tf_op jit(solution)/shard_map/ppermute | solution.py:117
  24.4 0.7 copy-start.8
  34.8 1.0 copy-start.4
  37.0 1.0 copy-start.2
  37.0 4.4 %copy-start = (bf16[512,256]{1,0:T(8,128)(2,1)S(1)}, bf16[512,256]{1,0:T(8,128)(2,1)}, u32[]{:S(2)}) copy-start(bf16[512,256]{1,0:T(8,128)(2,1)} %get-tuple-element.58.refs_0_) | copy-start | bytes 786436
  37.0 4.4 %copy-start.1 = (bf16[512,256]{1,0:T(8,128)(2,1)S(1)}, bf16[512,256]{1,0:T(8,128)(2,1)}, u32[]{:S(2)}) copy-start(bf16[512,256]{1,0:T(8,128)(2,1)} %get-tuple-element.59.refs_1_.refs_0_) | copy-start | bytes 786436
  37.2 4.2 %collective-permute-start.8 = (bf16[384,2048]{1,0:T(8,128)(2,1)S(1)}, bf16[384,2048]{1,0:T(8,128)(2,1)S(1)}, u32[]{:S(2)}, u32[]{:S(2)}) collective-permute-start(bf16[384,2048]{1,0:T(8,128)(2,1)S(1)} %shard_map.114), channel_id=1, source_target_pairs={{0,8},{1,9},{2,10},{3,11},{4,12},{5,13},{6,14},{7,15},{8,0},{9,1},... | collective-permute-start | bytes 4718600 | tf_op jit(solution)/shard_map/ppermute | solution.py:117
  38.0 3.3 %collective-permute-start.7 = (bf16[128,2048]{1,0:T(8,128)(2,1)S(1)}, bf16[128,2048]{1,0:T(8,128)(2,1)S(1)}, u32[]{:S(2)}, u32[]{:S(2)}) collective-permute-start(bf16[128,2048]{1,0:T(8,128)(2,1)S(1)} %copy-done.2), channel_id=1, source_target_pairs={{0,8},{1,9},{2,10},{3,11},{4,12},{5,13},{6,14},{7,15},{8,0},{9,1},... | collective-permute-start | bytes 1572872 | tf_op jit(solution)/shard_map/ppermute | solution.py:117
  38.0 14.3 %collective-permute-start.9 = (bf16[256,1024]{1,0:T(8,128)(2,1)S(1)}, bf16[256,1024]{1,0:T(8,128)(2,1)S(1)}, u32[]{:S(2)}, u32[]{:S(2)}) collective-permute-start(bf16[256,1024]{1,0:T(8,128)(2,1)S(1)} %get-tuple-element.63.refs_0_), channel_id=1, source_target_pairs={{0,16},{1,17},{2,18},{3,19},{4,20},{5,21},{6,22},{7,23},{8,24},{9,... | collective-permute-start | bytes 1572872 | tf_op jit(solution)/shard_map/ppermute | solution.py:117
  39.5 14.1 %collective-permute-start.10 = (bf16[256,1024]{1,0:T(8,128)(2,1)S(1)}, bf16[256,1024]{1,0:T(8,128)(2,1)S(1)}, u32[]{:S(2)}, u32[]{:S(2)}) collective-permute-start(bf16[256,1024]{1,0:T(8,128)(2,1)S(1)} %get-tuple-element.65.refs_0_), channel_id=1, source_target_pairs={{0,1},{1,0},{2,3},{3,2},{4,5},{5,4},{6,7},{7,6},{8,9},{9,8},{10,11... | collective-permute-start | bytes 1572872 | tf_op jit(solution)/shard_map/ppermute | solution.py:117
  43.8 14.8 %collective-permute-start.16 = (bf16[128,2048]{1,0:T(8,128)(2,1)S(1)}, bf16[128,2048]{1,0:T(8,128)(2,1)S(1)}, u32[]{:S(2)}, u32[]{:S(2)}) collective-permute-start(bf16[128,2048]{1,0:T(8,128)(2,1)S(1)} %get-tuple-element.62), channel_id=1, source_target_pairs={{0,2},{1,3},{2,0},{3,1},{4,6},{5,7},{6,4},{7,5},{8,10},{9,11},{10,... | collective-permute-start | bytes 1572872 | tf_op jit(solution)/shard_map/ppermute | solution.py:117
  52.5 27.0 %collective-permute-start.11 = (bf16[512,1024]{1,0:T(8,128)(2,1)S(1)}, bf16[512,1024]{1,0:T(8,128)(2,1)S(1)}, u32[]{:S(2)}, u32[]{:S(2)}) collective-permute-start(bf16[512,1024]{1,0:T(8,128)(2,1)S(1)} %shard_map.116.refs_2_), channel_id=1, source_target_pairs={{0,1},{1,0},{2,3},{3,2},{4,5},{5,4},{6,7},{7,6},{8,9},{9,8},{10,11... | collective-permute-start | bytes 3145736 | tf_op jit(solution)/shard_map/ppermute | solution.py:117
  53.7 34.4 %copy-start.3 = (bf16[128,2048]{1,0:T(8,128)(2,1)S(1)}, bf16[128,2048]{1,0:T(8,128)(2,1)}, u32[]{:S(2)}) copy-start(bf16[128,2048]{1,0:T(8,128)(2,1)} %refs_1_.3) | copy-start | bytes 1572868
  53.7 34.4 %copy-start.7 = (s32[4]{0:T(128)S(1)}, s32[4]{0:T(128)}, u32[]{:S(2)}) copy-start(s32[4]{0:T(128)} %pad_add_fusion.place) | copy-start | bytes 52
  53.7 34.4 %copy-start.9 = (f32[2048]{0:T(1024)S(1)}, f32[2048]{0:T(1024)}, u32[]{:S(2)}) copy-start(f32[2048]{0:T(1024)} %param.14) | copy-start | bytes 24580
  53.7 30.2 %collective-permute-start.12 = (bf16[512,1024]{1,0:T(8,128)(2,1)S(1)}, bf16[512,1024]{1,0:T(8,128)(2,1)S(1)}, u32[]{:S(2)}, u32[]{:S(2)}) collective-permute-start(bf16[512,1024]{1,0:T(8,128)(2,1)S(1)} %shard_map.117.refs_3_), channel_id=1, source_target_pairs={{0,16},{1,17},{2,18},{3,19},{4,20},{5,21},{6,22},{7,23},{8,24},{9,... | collective-permute-start | bytes 3145736 | tf_op jit(solution)/shard_map/ppermute | solution.py:117
  54.7 24.7 %collective-permute-start.15 = (bf16[128,2048]{1,0:T(8,128)(2,1)S(1)}, bf16[128,2048]{1,0:T(8,128)(2,1)S(1)}, u32[]{:S(2)}, u32[]{:S(2)}) collective-permute-start(bf16[128,2048]{1,0:T(8,128)(2,1)S(1)} %get-tuple-element.66), channel_id=1, source_target_pairs={{0,2},{1,3},{2,0},{3,1},{4,6},{5,7},{6,4},{7,5},{8,10},{9,11},{10,... | collective-permute-start | bytes 1572872 | tf_op jit(solution)/shard_map/ppermute | solution.py:117
  58.7 25.2 %collective-permute-start.17 = (bf16[128,2048]{1,0:T(8,128)(2,1)S(1)}, bf16[128,2048]{1,0:T(8,128)(2,1)S(1)}, u32[]{:S(2)}, u32[]{:S(2)}) collective-permute-start(bf16[128,2048]{1,0:T(8,128)(2,1)S(1)} %shard_map.118), channel_id=1, source_target_pairs={{0,4},{1,5},{2,6},{3,7},{4,0},{5,1},{6,2},{7,3},{8,12},{9,13},{10,... | collective-permute-start | bytes 1572872 | tf_op jit(solution)/shard_map/ppermute | solution.py:117
  62.0 22.4 %collective-permute-start.13 = (bf16[512,1024]{1,0:T(8,128)(2,1)S(1)}, bf16[512,1024]{1,0:T(8,128)(2,1)S(1)}, u32[]{:S(2)}, u32[]{:S(2)}) collective-permute-start(bf16[512,1024]{1,0:T(8,128)(2,1)S(1)} %shard_map.116.refs_2_), channel_id=1, source_target_pairs={{0,8},{1,9},{2,10},{3,11},{4,12},{5,13},{6,14},{7,15},{8,0},{9,1},... | collective-permute-start | bytes 3145736 | tf_op jit(solution)/shard_map/ppermute | solution.py:117
  79.4 5.0 %collective-permute-start.14 = (bf16[512,1024]{1,0:T(8,128)(2,1)S(1)}, bf16[512,1024]{1,0:T(8,128)(2,1)S(1)}, u32[]{:S(2)}, u32[]{:S(2)}) collective-permute-start(bf16[512,1024]{1,0:T(8,128)(2,1)S(1)} %shard_map.117.refs_3_), channel_id=1, source_target_pairs={{0,8},{1,9},{2,10},{3,11},{4,12},{5,13},{6,14},{7,15},{8,0},{9,1},... | collective-permute-start | bytes 3145736 | tf_op jit(solution)/shard_map/ppermute | solution.py:117
  83.9 2.7 %collective-permute-start.18 = (bf16[512,1024]{1,0:T(8,128)(2,1)S(1)}, bf16[512,1024]{1,0:T(8,128)(2,1)S(1)}, u32[]{:S(2)}, u32[]{:S(2)}) collective-permute-start(bf16[512,1024]{1,0:T(8,128)(2,1)S(1)} %collective-permute-done.11.refs_4_), channel_id=1, source_target_pairs={{0,8},{1,9},{2,10},{3,11},{4,12},{5,13},{6,14},{7,15},{8,0},{9,1},... | collective-permute-start | bytes 3145736 | tf_op jit(solution)/shard_map/ppermute | solution.py:117
  83.9 4.2 %collective-permute-start.19 = (bf16[512,1024]{1,0:T(8,128)(2,1)S(1)}, bf16[512,1024]{1,0:T(8,128)(2,1)S(1)}, u32[]{:S(2)}, u32[]{:S(2)}) collective-permute-start(bf16[512,1024]{1,0:T(8,128)(2,1)S(1)} %collective-permute-done.12.refs_5_), channel_id=1, source_target_pairs={{0,8},{1,9},{2,10},{3,11},{4,12},{5,13},{6,14},{7,15},{8,0},{9,1},... | collective-permute-start | bytes 3145736 | tf_op jit(solution)/shard_map/ppermute | solution.py:117
  96.7 17.5 %collective-permute-start.22 = (bf16[128,2048]{1,0:T(8,128)(2,1)S(1)}, bf16[128,2048]{1,0:T(8,128)(2,1)S(1)}, u32[]{:S(2)}, u32[]{:S(2)}) collective-permute-start(bf16[128,2048]{1,0:T(8,128)(2,1)S(1)} %get-tuple-element.74), channel_id=1, source_target_pairs={{0,16},{1,17},{2,18},{3,19},{4,20},{5,21},{6,22},{7,23},{8,24},{9,... | collective-permute-start | bytes 1572872 | tf_op jit(solution)/shard_map/ppermute | solution.py:117
  98.2 16.0 %collective-permute-start.20 = (bf16[128,1152]{1,0:T(8,128)(2,1)S(1)}, bf16[128,1152]{1,0:T(8,128)(2,1)S(1)}, u32[]{:S(2)}, u32[]{:S(2)}) collective-permute-start(bf16[128,1152]{1,0:T(8,128)(2,1)S(1)} %get-tuple-element.72.refs_0_.refs_2_), channel_id=1, source_target_pairs={{0,4},{1,5},{2,6},{3,7},{4,0},{5,1},{6,2},{7,3},{8,12},{9,13},{10,... | collective-permute-start | bytes 884744 | tf_op jit(solution)/shard_map/ppermute | solution.py:117
  98.2 16.7 %collective-permute-start.23 = (bf16[128,1024]{1,0:T(8,128)(2,1)S(1)}, bf16[128,1024]{1,0:T(8,128)(2,1)S(1)}, u32[]{:S(2)}, u32[]{:S(2)}) collective-permute-start(bf16[128,1024]{1,0:T(8,128)(2,1)S(1)} %get-tuple-element.80.refs_0_), channel_id=1, source_target_pairs={{0,1},{1,0},{2,3},{3,2},{4,5},{5,4},{6,7},{7,6},{8,9},{9,8},{10,11... | collective-permute-start | bytes 786440 | tf_op jit(solution)/shard_map/ppermute | solution.py:117
  114.2 19.5 %collective-permute-start.25 = (bf16[256,1536]{1,0:T(8,128)(2,1)S(1)}, bf16[256,1536]{1,0:T(8,128)(2,1)S(1)}, u32[]{:S(2)}, u32[]{:S(2)}) collective-permute-start(bf16[256,1536]{1,0:T(8,128)(2,1)S(1)} %shard_map.121), channel_id=1, source_target_pairs={{0,1},{1,0},{2,3},{3,2},{4,5},{5,4},{6,7},{7,6},{8,9},{9,8},{10,11... | collective-permute-start | bytes 2359304 | tf_op jit(solution)/shard_map/ppermute | solution.py:117
  114.8 18.9 %collective-permute-start.21 = (bf16[256,1152]{1,0:T(8,128)(2,1)S(1)}, bf16[256,1152]{1,0:T(8,128)(2,1)S(1)}, u32[]{:S(2)}, u32[]{:S(2)}) collective-permute-start(bf16[256,1152]{1,0:T(8,128)(2,1)S(1)} %shard_map.120), channel_id=1, source_target_pairs={{0,2},{1,3},{2,0},{3,1},{4,6},{5,7},{6,4},{7,5},{8,10},{9,11},{10,... | collective-permute-start | bytes 1769480 | tf_op jit(solution)/shard_map/ppermute | solution.py:117
  115.0 16.6 %collective-permute-start.26 = (bf16[256,1024]{1,0:T(8,128)(2,1)S(1)}, bf16[256,1024]{1,0:T(8,128)(2,1)S(1)}, u32[]{:S(2)}, u32[]{:S(2)}) collective-permute-start(bf16[256,1024]{1,0:T(8,128)(2,1)S(1)} %shard_map.122.refs_1_), channel_id=1, source_target_pairs={{0,16},{1,17},{2,18},{3,19},{4,20},{5,21},{6,22},{7,23},{8,24},{9,... | collective-permute-start | bytes 1572872 | tf_op jit(solution)/shard_map/ppermute | solution.py:117
  115.6 15.9 %collective-permute-start.24 = (bf16[128,896]{1,0:T(8,128)(2,1)S(1)}, bf16[128,896]{1,0:T(8,128)(2,1)S(1)}, u32[]{:S(2)}, u32[]{:S(2)}) collective-permute-start(bf16[128,896]{1,0:T(8,128)(2,1)S(1)} %get-tuple-element.76.refs_0_.refs_2_), channel_id=1, source_target_pairs={{0,4},{1,5},{2,6},{3,7},{4,0},{5,1},{6,2},{7,3},{8,12},{9,13},{10,... | collective-permute-start | bytes 688136 | tf_op jit(solution)/shard_map/ppermute | solution.py:117
  134.6 3.2 %collective-permute-start.27 = (bf16[512,1152]{1,0:T(8,128)(2,1)S(1)}, bf16[512,1152]{1,0:T(8,128)(2,1)S(1)}, u32[]{:S(2)}, u32[]{:S(2)}) collective-permute-start(bf16[512,1152]{1,0:T(8,128)(2,1)S(1)} %shard_map.123), channel_id=1, source_target_pairs={{0,8},{1,9},{2,10},{3,11},{4,12},{5,13},{6,14},{7,15},{8,0},{9,1},... | collective-permute-start | bytes 3538952 | tf_op jit(solution)/shard_map/ppermute | solution.py:117
  136.1 6.2 %collective-permute-start.32 = (bf16[256,2176]{1,0:T(8,128)(2,1)S(1)}, bf16[256,2176]{1,0:T(8,128)(2,1)S(1)}, u32[]{:S(2)}, u32[]{:S(2)}) collective-permute-start(bf16[256,2176]{1,0:T(8,128)(2,1)S(1)} %shard_map.127), channel_id=1, source_target_pairs={{0,8},{1,9},{2,10},{3,11},{4,12},{5,13},{6,14},{7,15},{8,0},{9,1},... | collective-permute-start | bytes 3342344 | tf_op jit(solution)/shard_map/ppermute | solution.py:117
  136.7 18.7 %collective-permute-start.31 = (bf16[256,896]{1,0:T(8,128)(2,1)S(1)}, bf16[256,896]{1,0:T(8,128)(2,1)S(1)}, u32[]{:S(2)}, u32[]{:S(2)}) collective-permute-start(bf16[256,896]{1,0:T(8,128)(2,1)S(1)} %shard_map.125), channel_id=1, source_target_pairs={{0,2},{1,3},{2,0},{3,1},{4,6},{5,7},{6,4},{7,5},{8,10},{9,11},{10,... | collective-permute-start | bytes 1376264 | tf_op jit(solution)/shard_map/ppermute | solution.py:117
  138.7 16.6 %collective-permute-start.28 = (bf16[128,1152]{1,0:T(8,128)(2,1)S(1)}, bf16[128,1152]{1,0:T(8,128)(2,1)S(1)}, u32[]{:S(2)}, u32[]{:S(2)}) collective-permute-start(bf16[128,1152]{1,0:T(8,128)(2,1)S(1)} %get-tuple-element.83), channel_id=1, source_target_pairs={{0,16},{1,17},{2,18},{3,19},{4,20},{5,21},{6,22},{7,23},{8,24},{9,... | collective-permute-start | bytes 884744 | tf_op jit(solution)/shard_map/ppermute | solution.py:117
  139.3 16.0 %collective-permute-start.29 = (bf16[128,1152]{1,0:T(8,128)(2,1)S(1)}, bf16[128,1152]{1,0:T(8,128)(2,1)S(1)}, u32[]{:S(2)}, u32[]{:S(2)}) collective-permute-start(bf16[128,1152]{1,0:T(8,128)(2,1)S(1)} %get-tuple-element.84), channel_id=1, source_target_pairs={{0,1},{1,0},{2,3},{3,2},{4,5},{5,4},{6,7},{7,6},{8,9},{9,8},{10,11... | collective-permute-start | bytes 884744 | tf_op jit(solution)/shard_map/ppermute | solution.py:117
  140.9 14.5 %collective-permute-start.30 = (bf16[128,1152]{1,0:T(8,128)(2,1)S(1)}, bf16[128,1152]{1,0:T(8,128)(2,1)S(1)}, u32[]{:S(2)}, u32[]{:S(2)}) collective-permute-start(bf16[128,1152]{1,0:T(8,128)(2,1)S(1)} %get-tuple-element.85), channel_id=1, source_target_pairs={{0,17},{1,16},{2,19},{3,18},{4,21},{5,20},{6,23},{7,22},{8,25},{9,... | collective-permute-start | bytes 884744 | tf_op jit(solution)/shard_map/ppermute | solution.py:117
  144.0 11.1 %collective-permute-start.33 = (bf16[64,2176]{1,0:T(8,128)(2,1)S(1)}, bf16[64,2176]{1,0:T(8,128)(2,1)S(1)}, u32[]{:S(2)}, u32[]{:S(2)}) collective-permute-start(bf16[64,2176]{1,0:T(8,128)(2,1)S(1)} %get-tuple-element.87), channel_id=1, source_target_pairs={{0,2},{1,3},{2,0},{3,1},{4,6},{5,7},{6,4},{7,5},{8,10},{9,11},{10,... | collective-permute-start | bytes 835592 | tf_op jit(solution)/shard_map/ppermute | solution.py:117
  156.1 3.0 %collective-permute-start.34 = (bf16[512,896]{1,0:T(8,128)(2,1)S(1)}, bf16[512,896]{1,0:T(8,128)(2,1)S(1)}, u32[]{:S(2)}, u32[]{:S(2)}) collective-permute-start(bf16[512,896]{1,0:T(8,128)(2,1)S(1)} %shard_map.130), channel_id=1, source_target_pairs={{0,8},{1,9},{2,10},{3,11},{4,12},{5,13},{6,14},{7,15},{8,0},{9,1},... | collective-permute-start | bytes 2752520 | tf_op jit(solution)/shard_map/ppermute | solution.py:117
  156.2 18.2 %collective-permute-start.38 = (bf16[64,2304]{1,0:T(8,128)(2,1)S(1)}, bf16[64,2304]{1,0:T(8,128)(2,1)S(1)}, u32[]{:S(2)}, u32[]{:S(2)}) collective-permute-start(bf16[64,2304]{1,0:T(8,128)(2,1)S(1)} %get-tuple-element.95), channel_id=1, source_target_pairs={{0,2},{1,3},{2,0},{3,1},{4,6},{5,7},{6,4},{7,5},{8,10},{9,11},{10,... | collective-permute-start | bytes 884744 | tf_op jit(solution)/shard_map/ppermute | solution.py:117
  157.3 17.0 %collective-permute-start.39 = (bf16[64,2304]{1,0:T(8,128)(2,1)S(1)}, bf16[64,2304]{1,0:T(8,128)(2,1)S(1)}, u32[]{:S(2)}, u32[]{:S(2)}) collective-permute-start(bf16[64,2304]{1,0:T(8,128)(2,1)S(1)} %shard_map.129), channel_id=1, source_target_pairs={{0,4},{1,5},{2,6},{3,7},{4,0},{5,1},{6,2},{7,3},{8,12},{9,13},{10,... | collective-permute-start | bytes 884744 | tf_op jit(solution)/shard_map/ppermute | solution.py:117
  159.8 8.6 %collective-permute-start.35 = (bf16[128,896]{1,0:T(8,128)(2,1)S(1)}, bf16[128,896]{1,0:T(8,128)(2,1)S(1)}, u32[]{:S(2)}, u32[]{:S(2)}) collective-permute-start(bf16[128,896]{1,0:T(8,128)(2,1)S(1)} %get-tuple-element.90), channel_id=1, source_target_pairs={{0,16},{1,17},{2,18},{3,19},{4,20},{5,21},{6,22},{7,23},{8,24},{9,... | collective-permute-start | bytes 688136 | tf_op jit(solution)/shard_map/ppermute | solution.py:117
  160.4 11.1 %collective-permute-start.36 = (bf16[128,896]{1,0:T(8,128)(2,1)S(1)}, bf16[128,896]{1,0:T(8,128)(2,1)S(1)}, u32[]{:S(2)}, u32[]{:S(2)}) collective-permute-start(bf16[128,896]{1,0:T(8,128)(2,1)S(1)} %get-tuple-element.91), channel_id=1, source_target_pairs={{0,1},{1,0},{2,3},{3,2},{4,5},{5,4},{6,7},{7,6},{8,9},{9,8},{10,11... | collective-permute-start | bytes 688136 | tf_op jit(solution)/shard_map/ppermute | solution.py:117
  162.0 11.2 %collective-permute-start.37 = (bf16[128,896]{1,0:T(8,128)(2,1)S(1)}, bf16[128,896]{1,0:T(8,128)(2,1)S(1)}, u32[]{:S(2)}, u32[]{:S(2)}) collective-permute-start(bf16[128,896]{1,0:T(8,128)(2,1)S(1)} %get-tuple-element.92), channel_id=1, source_target_pairs={{0,17},{1,16},{2,19},{3,18},{4,21},{5,20},{6,23},{7,22},{8,25},{9,... | collective-permute-start | bytes 688136 | tf_op jit(solution)/shard_map/ppermute | solution.py:117
  (2 other events, 1.3 us)

commit v4 on v3

--- a/solution.py
+++ b/solution.py
@@ -225,7 +225,7 @@
     for db, got in enumerate(arrived, 1):
         kernel = functools.partial(sent_blocks_kernel, at.xs, at.bs, slots, db)
         result.append(call(kernel, [dense] * CORES, [], at.numbers, got, weights, numbers=1))
-    return result, sent
+    return result, sent, arrived
 
 
 def sums_kernel(n_ops, pieces, *refs):
@@ -333,112 +333,133 @@
         right[rows, :] = source[:, half:]
 
 
-def line_weight(at, weight):
+def line_weight(at, weight, *gates):
     count, width = weight.shape
     far = at.send(weight, flip=2)
-    near = at.send(after(weight, far), flip=1)
+    near = at.send(weight, flip=1)
     last = at.send(far, flip=1)
     halves = [like(LINE * count, width // 2)] * 2
-    return call(line_kernel, halves, [], at.numbers, weight, far, near, last, numbers=1)
+    return call(line_kernel, halves, [], at.numbers, weight, far, near, after(last, *gates), numbers=1)
+
+
+def turned_halves(value, swap):
+    parts = [value[:, i : i + 128] for i in range(0, value.shape[1], 128)]
+    return [jnp.where(swap, pltpu.roll(part, 64, 1), part) for part in parts]
+
+
+def apart(value, b):
+    parts = turned_halves(value, b == 1)
+    left = lax.broadcasted_iota(jnp.int32, parts[0].shape, 1) < 64
+    own, other = [], []
+    for one, two in zip(parts[::2], parts[1::2]):
+        own.append(jnp.where(left, one, pltpu.roll(two, 64, 1)))
+        other.append(jnp.where(left, pltpu.roll(one, 64, 1), two))
+    return jnp.concatenate(own, 1), jnp.concatenate(other, 1)
+
+
+def together(own, other, b):
+    parts = []
+    left = lax.broadcasted_iota(jnp.int32, (own.shape[0], 128), 1) < 64
+    for i in range(0, own.shape[1], 128):
+        one, two = own[:, i : i + 128], other[:, i : i + 128]
+        parts.append(jnp.where(left, one, pltpu.roll(two, 64, 1)))
+        parts.append(jnp.where(left, pltpu.roll(one, 64, 1), two))
+    return jnp.concatenate(turned_halves(jnp.concatenate(parts, 1), b == 1), 1)
+
+
+def pieces_of(held):
+    pieces = {}
+    for (*at, h), (k, row) in sorted(held.items(), key=lambda item: item[1]):
+        pieces.setdefault((h, k), []).append(tuple(at))
+    return pieces
+
+
+def first_dense_kernel(held, xs, bs, lanes, n_held, place, *refs):
+    arrays, (total, near, far, bias, turned, pre, agg) = refs[:n_held], refs[n_held:]
+    b, x, core = place[1], place[2], place[3]
+    half, group = bias.shape[1] // 2, bs * lanes
+    agg[...] = total[...] + near[...].astype(F32) + far[...].astype(F32)
+    n = 0
+    for dcore in range(CORES):
+        for dx in range(xs):
+            row = lax.rem(x + dx, xs) * CORES + lax.rem(core + dcore, CORES)
+            for part in apart(agg[:, pl.ds(pl.multiple_of(row * group, group), group)], b):
+                turned[:, n * lanes : (n + 1) * lanes] = part.astype(LOW)
+                n += 1
+    for h in range(2):
+        part = slice(h * half, (h + 1) * half)
+        pre[:, part] = products(held, arrays, turned, h, xs, bs, lanes) + bias[:, part]
+
+
+def products(held, arrays, turned, h, xs, bs, lanes):
+    total = 0.0
+    for (side, k), ats in pieces_of(held).items():
+        if side == h and k < len(arrays):
+            rows = [((dcore * xs + dx) * bs + db) * lanes for dcore, dx, db in ats]
+            left = jnp.concatenate([turned[:, row : row + lanes] for row in rows], 1)
+            total = total + dot(left, arrays[k][...], ((1,), (0,)))
+    return total
 
 
 def dense_kernel(held, xs, bs, lanes, n_held, place, *refs):
-    (bias_in, grad_in), arrays, refs = refs[:2], refs[2 : 2 + n_held], refs[2 + n_held :]
-    total, near, far, act_ref, left_ref, right_ref, rows_ref = refs[:7]
-    messages, refs = refs[7 : 6 + xs], refs[6 + xs :]
-    backs, refs = refs[:CHUNKS], refs[CHUNKS:]
-    agg_ref, turned, acc, back, blocks, bias, out_grad, sems = refs
+    arrays, refs = refs[:n_held], refs[n_held:]
+    turned, first, out_grad, act, left_ref, right_ref = refs[:6]
+    backs, [back] = refs[6 : 6 + CHUNKS], refs[6 + CHUNKS :]
     b, x, core = place[1], place[2], place[3]
-    width = bias.shape[1]
-    half = width // 2
-    group = bs * lanes
-    places = [(dcore, dx, db) for dcore in range(CORES) for db in range(bs) for dx in range(xs)]
-    number = {(at, h): n for n, (at, h) in enumerate((at, h) for at in places for h in range(2))}
-
-    copies = [pltpu.make_async_copy(bias_in, bias, sems.at[0])]
-    for (at, h), n in number.items():
-        k, row = held[*at, h]
-        block = blocks.at[pl.ds(n * lanes, lanes), :]
-        copies.append(pltpu.make_async_copy(arrays[k].at[pl.ds(row, lanes), :], block, sems.at[n + 1]))
-    copies.append(pltpu.make_async_copy(grad_in, out_grad, sems.at[len(number) + 1]))
-    for copy in copies:
-        copy.start()
-
-    def weight(at, h):
-        n = number[at, h]
-        return blocks[n * lanes : (n + 1) * lanes, :]
-
-    agg_ref[...] = (total[...] + near[...].astype(F32) + far[...].astype(F32)).astype(LOW)
-    count = lanes // LINE
-    at_in = lax.broadcasted_iota(jnp.int32, (group, group), 0)
-    at_out = lax.broadcasted_iota(jnp.int32, (group, group), 1)
-    db, inner = at_out // lanes, at_out % lanes
-    source = (inner // count) * (bs * count) + lax.rem(b + db, bs) * count + inner % count
-    turn = (at_in == source).astype(F32).astype(LOW)
-    for r in range(width // group):
-        at_r = slice(r * group, (r + 1) * group)
-        turned[:, at_r] = dot(agg_ref[:, at_r], turn, ((1,), (0,))).astype(LOW)
-
-    def columns(dcore, dx, db):
-        row = lax.rem(x + dx, xs) * CORES + lax.rem(core + dcore, CORES)
-        return pl.ds(pl.multiple_of(row * group + db * lanes, lanes), lanes)
-
-    copies[0].wait()
-    acc[...] = jnp.broadcast_to(bias[...], acc.shape)
-    for at in places:
-        left = turned[:, columns(*at)]
-        for h in range(2):
-            copies[1 + number[at, h]].wait()
-            acc[:, h * half : (h + 1) * half] += dot(left, weight(at, h), ((1,), (0,)))
-    copies[-1].wait()
-    for dx, out in enumerate([rows_ref, *messages]):
-        start = half if dx else 0
-        for db in range(bs):
-            for dcore in range(CORES):
-                out[:, start : start + lanes] = turned[:, columns(dcore, dx, db)]
-                start += lanes
-    pre = acc[...]
-    phi = 0.5 * (1.0 + lax.erf(pre * (0.5**0.5)))
-    act_ref[...] = (pre * phi).astype(LOW)
-    slope = phi + pre * (jnp.exp(-0.5 * pre * pre) * 0.3989422804014327)
-    pre_low = (out_grad[...].astype(F32) * slope).astype(LOW)
-    for out in (left_ref, *messages):
-        out[:, :half] = pre_low[:, :half]
-    right_ref[...] = pre_low[:, half:]
-    for at in places:
-        total = 0.0
-        for h, ref in enumerate((left_ref, right_ref)):
-            total = total + dot(ref[...], weight(at, h), ((1,), (1,)))
-        back[:, columns(*at)] = total.astype(LOW)
-    for r in range(width // group):
-        part = dot(back[:, r * group : (r + 1) * group], turn, ((1,), (1,))).astype(LOW)
-        for k, (start, end) in enumerate(bounds(width)):
-            left, right = max(start, r * group), min(end, (r + 1) * group)
-            if left < right:
-                backs[k][:, left - start : right - start] = part[:, left - r * group : right - r * group]
+    half, group = out_grad.shape[1] // 2, bs * lanes
+    others = {at: (k - n_held // 2, row) for at, (k, row) in held.items() if at[0]}
+    for h, out in enumerate((left_ref, right_ref)):
+        part = slice(h * half, (h + 1) * half)
+        pre = first[:, part] + products(others, arrays[n_held // 2 :], turned, h, xs, bs, lanes)
+        phi = 0.5 * (1.0 + lax.erf(pre * (0.5**0.5)))
+        act[:, part] = (pre * phi).astype(LOW)
+        slope = phi + pre * (jnp.exp(-0.5 * pre * pre) * 0.3989422804014327)
+        out[...] = (out_grad[:, part].astype(F32) * slope).astype(LOW)
+    found = {}
+    for (h, k), ats in pieces_of(held).items():
+        more = dot((left_ref, right_ref)[h][...], arrays[k][...], ((1,), (1,)))
+        for i, at in enumerate(ats):
+            part = more[:, i * lanes : (i + 1) * lanes]
+            found[at] = found[at] + part if at in found else part
+    for dcore in range(CORES):
+        for dx in range(xs):
+            row = lax.rem(x + dx, xs) * CORES + lax.rem(core + dcore, CORES)
+            part = together(found[dcore, dx, 0], found[dcore, dx, 1], b)
+            back[:, pl.ds(pl.multiple_of(row * group, group), group)] = part.astype(LOW)
+    for k, (start, end) in enumerate(bounds(out_grad.shape[1])):
+        backs[k][...] = back[:, start:end]
+
+
+def rows_kernel(xs, bs, lanes, turned, *outs):
+    for dx, out in enumerate(outs):
+        for dcore in range(CORES):
+            for db in range(bs):
+                row = ((dcore * xs + dx) * bs + db) * lanes
+                to = (db * CORES + dcore) * lanes
+                out[:, to : to + lanes] = turned[:, row : row + lanes]
 
 
 def pick_kernel(db, *refs):
-    left, rows, messages, out = refs[0], refs[1], refs[2:-1], refs[-1]
+    *refs, out = refs
+    lefts, rows = refs[: len(refs) // 2], refs[len(refs) // 2 :]
+    size, half = lefts[0].shape
+    wide = out.shape[1] - half
+    for i, (left, row) in enumerate(zip(lefts, rows)):
+        at = slice(i * size, (i + 1) * size)
+        out[at, :half] = left[...]
+        out[at, half:] = row[:, db * wide : (db + 1) * wide]
+
+
+def spread(at, lanes, left, right, rows, gate):
     size, half = left.shape
-    wide = out.shape[1] - half
-    out[:size, :half] = left[...]
-    out[:size, half:] = rows[:, db * wide : (db + 1) * wide]
-    for i, message in enumerate(messages, 1):
-        at = slice(i * size, (i + 1) * size)
-        out[at, :half] = message[:, :half]
-        out[at, half:] = message[:, half + db * wide : half + (db + 1) * wide]
-
-
-def spread(at, lanes, left, right, rows, messages, gate):
-    size, half = left.shape
-    arrived = [at.send(message, dx=dx) for dx, message in enumerate(messages, 1)]
+    lefts = [left] + [at.send(left, dx=dx) for dx in range(1, at.xs)]
+    rows = rows[:1] + [at.send(row, dx=dx) for dx, row in enumerate(rows[1:], 1)]
     rights = [right] + [at.send(right, db=db) for db in range(1, at.bs)]
-    steps = [arrived + rights[1:]]
+    steps = [lefts[1:] + rights[1:] + rows[1:]]
 
     def pick(db):
         outs = [like(at.xs * size, half + CORES * lanes)]
-        return call(functools.partial(pick_kernel, db), outs, [], after(left, gate), rows, *arrived)[0]
+        return call(functools.partial(pick_kernel, db), outs, [], after(left, gate), *lefts[1:], *rows)[0]
 
     held = {}
 
@@ -521,7 +542,7 @@
         rest = got[:, width : width + 128].astype(F32)
         tail = tail + (rest[:, 0:1] + rest[:, 1:2])
     weight_out[...] = total
-    bias_out[...] = tail
+    bias_out[...] = jnp.transpose(tail)[0:1, :]
 
 
 def far_kernel(kept, got, far):
@@ -533,13 +554,12 @@
     size, width = node_feats.shape
     own_rows = weight.shape[0]
     lanes = LINE * own_rows
-    aligned = lanes % 128 == 0
-    halves = line_weight(at, weight) if aligned else []
-    ops, gate = operator(at, block_vals, block_cols, block_counts, self_weight, size)
-    node_feats = after(node_feats, *gate)
+    aligned = own_rows * at.bs == 128
+    ops, gate, arrived = operator(at, block_vals, block_cols, block_counts, self_weight, size)
     own = {(dx, db): at.send(node_feats, dx=-dx, db=-db) if dx or db else node_feats for dx, db in at.chips}
+    halves = line_weight(at, weight, *arrived) if aligned else []
     first, *chips = at.chips
-    across = [at.send(own[first], dcore=1), at.send(join(after(own[chips[0]], *ops[-1], *halves), *[own[chip] for chip in chips[1:]]), dcore=1)]
+    across = [at.send(own[first], dcore=1), at.send(join(after(own[chips[0]], *halves), *[own[chip] for chip in chips[1:]]), dcore=1)]
     total, kept, to_near, to_last = sums(at, ops, own, across)
     got = at.send(to_last, flip=1)
     near = at.send(to_near, flip=1)
@@ -553,35 +573,36 @@
     early = len(arrays) - len(steps[1])
     arrays, held = both_cores(at, arrays, held, [[]] * early + [[near, far]] * len(steps[1]))
     widths = [end - start for start, end in bounds(width)]
-    n_blocks = len(held)
-    activations, left, right, rows, *rest = call(
-        functools.partial(dense_kernel, held, at.xs, at.bs, lanes, len(arrays)),
-        [like(size, width)]
-        + [like(size, width // 2)] * 2
-        + [like(size, at.bs * CORES * lanes)]
-        + [like(size, width // 2 + at.bs * CORES * lanes)] * (at.xs - 1)
-        + [like(size, wide) for wide in widths],
-        [pltpu.VMEM((size, width), kind) for kind in (LOW, LOW, F32, LOW)]
-        + [
-            pltpu.VMEM((n_blocks * lanes, width // 2), LOW),
-            pltpu.VMEM((1, width), F32),
-            pltpu.VMEM((size, width), LOW),
-            pltpu.SemaphoreType.DMA((n_blocks + 2,)),
-        ],
+    own_held = {at: where for at, where in held.items() if not at[0]}
+    count = len(arrays) // 2
+    turned, pre = call(
+        functools.partial(first_dense_kernel, own_held, at.xs, at.bs, lanes, count),
+        [like(size, width), like(size, width, kind=F32)],
+        [pltpu.VMEM((size, width), F32)],
         at.numbers,
-        bias[None, :],
-        out_grad,
-        *arrays,
+        *arrays[:count],
         total,
         near,
         far,
+        bias[None, :],
         numbers=1,
-        outside=2 + len(arrays),
-    )
-    messages, backs = rest[: at.xs - 1], rest[at.xs - 1 :]
+    )
+    activations, left, right, *backs = call(
+        functools.partial(dense_kernel, held, at.xs, at.bs, lanes, len(arrays)),
+        [like(size, width)] + [like(size, width // 2)] * 2 + [like(size, wide) for wide in widths],
+        [pltpu.VMEM((size, width), LOW)],
+        at.numbers,
+        *arrays,
+        turned,
+        pre,
+        out_grad,
+        numbers=1,
+    )
+    kernel = functools.partial(rows_kernel, at.xs, at.bs, lanes)
+    rows = list(call(kernel, [like(size, at.bs * CORES * lanes)] * at.xs, [], turned))
 
     fars = [at.send(backs[0], flip=2)]
-    arrays, held, steps = spread(at, lanes, left, right, rows, messages, fars[0])
+    arrays, held, steps = spread(at, lanes, left, right, rows, fars[0])
     nears = [at.send(join(backs[0], fars[0]), flip=1)]
     for k in range(1, CHUNKS):
         fars.append(at.send(after(backs[k], *fars, *steps[0]), flip=2))
@@ -612,9 +633,9 @@
     near = at.send(to_near, flip=1)
     far = at.send(sent, flip=2)
     [feat_grad] = call(functools.partial(add_up_kernel, CHUNKS), [like(size, width, kind=F32)], [], *feat)
-    outs = [like(own_rows, width, kind=F32), like(own_rows, 128, kind=F32)]
+    outs = [like(own_rows, width, kind=F32), like(1, own_rows, kind=F32)]
     weight_grad, bias_grad = call(last_fold_kernel, outs, [], after(total, feat_grad), near, far)
-    return activations, feat_grad, weight_grad, bias_grad[:, 0]
+    return activations, feat_grad, weight_grad, bias_grad[0]
 
 
 def feat_sums(at, ops, *lines):

time: 176 us -> 171 us (0.972)
  waiting for transfers between devices: 105 us -> 101 us
  starting transfers between devices: 40.3 us -> 43.1 us
  local copies, waits for them, and re-layouts: 4.41 us -> 2.34 us
    ppermute x40 -> x41, waiting for transfers between devices: 105 us -> 101 us  [send(): return lax.ppermute(value, AXES, pairs)]
    ppermute x40 -> x41, starting transfers between devices: 40.3 us -> 43.1 us  [send(): return lax.ppermute(value, AXES, pairs)]
    pallas_call x23 -> x25, Pallas kernels: 24.3 us -> 22.8 us  [call(): pl.pallas_call(kernel, out_shape=outs, in_specs=specs, out_specs=[whole]...]
    unnamed x20 -> x18, local copies, waits for them, and re-layouts: 3.79 us -> 2.34 us
  transfers between devices with their start and end apart: 40 -> 41, of which waited for: 18 -> 16; matrix products, arithmetic and copies ran while one was open for 0% -> 0% of each run, Pallas kernels for 6% -> 7%
where the time goes in v4:
time: 171 us
  waiting for transfers between devices  101 us (59%)
  starting transfers between devices  43.1 us (25%)
  Pallas kernels  22.8 us (13%)
  local copies, waits for them, and re-layouts  2.34 us (1%)
    ppermute x41, waiting for transfers between devices, send(): return lax.ppermute(value, AXES, pairs)  101 us
    ppermute x41, starting transfers between devices, send(): return lax.ppermute(value, AXES, pairs)  43.1 us
    pallas_call x25, Pallas kernels, call(): pl.pallas_call(kernel, out_shape=outs, in_specs=specs, out_specs=[whole]...  22.8 us
  transfers between devices with their start and end apart: 41, of which 16 were waited for; matrix products, arithmetic and copies ran while one was open for 0% of the time, Pallas kernels for 7%

profile of v4, /device:TPU:0, one launch (start us, length us, event | category | flops | bytes accessed | tf_op | source)
XLA Modules:
  0.0 170.9 jit_solution(5749552824561678005)
XLA Ops:
  1.2 2.8 %shard_map.111 = (bf16[512,256]{1,0:T(8,128)(2,1)}, bf16[512,256]{1,0:T(8,128)(2,1)}, bf16[528,256]{1,0:T(8,128)(2,1)}) custom-call(s32[4]{0:T(128)} %pad_add_fusion.place, s32[2,8]{1,0:T(2,128)} %refs_0_.1, s32[1,8]{1,0:T(1,128)} %refs_1_.1, bf16[1024,256]{1,0:T(8,128)(2,1)} %refs_2_.1, f32[8,128]{1,0:T(8,128)} %bitcast.7), custom_call_target="tpu_custom_call" | custom-call | flops 1 | bytes 1 | tf_op jit(solution)/shard_map/pallas_call | solution.py:48
  4.0 3.0 %collective-permute-start.3 = (bf16[528,256]{1,0:T(8,128)(2,1)}, bf16[528,256]{1,0:T(8,128)(2,1)S(1)}, u32[]{:S(2)}, u32[]{:S(2)}) collective-permute-start(bf16[528,256]{1,0:T(8,128)(2,1)} %get-tuple-element.52), channel_id=1, source_target_pairs={{0,1},{1,0},{2,3},{3,2},{4,5},{5,4},{6,7},{7,6},{8,9},{9,8},{10,11... | collective-permute-start | bytes 811016 | tf_op jit(solution)/shard_map/ppermute | solution.py:117
  7.1 2.6 %collective-permute-start = (bf16[64,2048]{1,0:T(8,128)(2,1)}, bf16[64,2048]{1,0:T(8,128)(2,1)S(1)}, u32[]{:S(2)}, u32[]{:S(2)}) collective-permute-start(bf16[64,2048]{1,0:T(8,128)(2,1)} %weight.1), channel_id=1, source_target_pairs={{0,4},{1,5},{2,6},{3,7},{4,0},{5,1},{6,2},{7,3},{8,12},{9,13},{10,... | collective-permute-start | bytes 786440 | tf_op jit(solution)/shard_map/ppermute | solution.py:117
  9.7 1.5 collective-permute-start.4
  11.7 1.5 collective-permute-start.6
  13.2 8.4 %collective-permute-done.far = bf16[64,2048]{1,0:T(8,128)(2,1)S(1)} collective-permute-done((bf16[64,2048]{1,0:T(8,128)(2,1)}, bf16[64,2048]{1,0:T(8,128)(2,1)S(1)}, u32[]{:S(2)}, u32[]{:S(2)}) %collective-permute-start) | collective-permute-done | bytes 262176 | tf_op jit(solution)/shard_map/ppermute | solution.py:117
  22.4 1.2 collective-permute-start.1
  23.6 7.2 %collective-permute-done.2.last = bf16[64,2048]{1,0:T(8,128)(2,1)S(1)} collective-permute-done((bf16[64,2048]{1,0:T(8,128)(2,1)S(1)}, bf16[64,2048]{1,0:T(8,128)(2,1)S(1)}, u32[]{:S(2)}, u32[]{:S(2)}) %collective-permute-start.2) | collective-permute-done | bytes 262176 | tf_op jit(solution)/shard_map/ppermute | solution.py:117
  30.8 3.6 %collective-permute-done.1.near = bf16[64,2048]{1,0:T(8,128)(2,1)S(1)} collective-permute-done((bf16[64,2048]{1,0:T(8,128)(2,1)}, bf16[64,2048]{1,0:T(8,128)(2,1)S(1)}, u32[]{:S(2)}, u32[]{:S(2)}) %collective-permute-start.1) | collective-permute-done | bytes 262176 | tf_op jit(solution)/shard_map/ppermute | solution.py:117
  34.5 0.9 copy-done.4
  38.5 1.1 collective-permute-start.10
  39.5 1.5 collective-permute-start.9
  41.1 2.4 %shard_map.115 = (f32[128,2048]{1,0:T(8,128)S(1)}, f32[128,2048]{1,0:T(8,128)S(1)}, bf16[128,2048]{1,0:T(8,128)(2,1)S(1)}, bf16[128,2048]{1,0:T(8,128)(2,1)S(1)}) custom-call(bf16[512,256]{1,0:T(8,128)(2,1)S(1)} %copy-done, bf16[512,256]{1,0:T(8,128)(2,1)S(1)} %copy-done.1, bf16[512,256]{1,0:T(8,128)(2,1)S(1)} %get-tuple-element.55.refs_2_.refs_1_, ...), custom_call_target="tpu_custom_call" | custom-call | flops 1 | bytes 1 | tf_op jit(solution)/shard_map/pallas_call | solution.py:48
  43.4 1.8 %collective-permute-start.16 = (bf16[128,2048]{1,0:T(8,128)(2,1)S(1)}, bf16[128,2048]{1,0:T(8,128)(2,1)S(1)}, u32[]{:S(2)}, u32[]{:S(2)}) collective-permute-start(bf16[128,2048]{1,0:T(8,128)(2,1)S(1)} %get-tuple-element.62), channel_id=1, source_target_pairs={{0,2},{1,3},{2,0},{3,1},{4,6},{5,7},{6,4},{7,5},{8,10},{9,11},{10,... | collective-permute-start | bytes 1572872 | tf_op jit(solution)/shard_map/ppermute | solution.py:117
  45.2 7.7 %collective-permute-done.10.refs_1_ = bf16[256,1024]{1,0:T(8,128)(2,1)S(1)} collective-permute-done((bf16[256,1024]{1,0:T(8,128)(2,1)S(1)}, bf16[256,1024]{1,0:T(8,128)(2,1)S(1)}, u32[]{:S(2)}, u32[]{:S(2)}) %collective-permute-start.10) | collective-permute-done | bytes 524320 | tf_op jit(solution)/shard_map/ppermute | solution.py:117
  52.9 1.6 collective-permute-start.12
  55.2 1.7 collective-permute-start.15
  56.9 1.1 collective-permute-done.16.got
  58.1 3.2 %collective-permute-start.17 = (bf16[128,2048]{1,0:T(8,128)(2,1)S(1)}, bf16[128,2048]{1,0:T(8,128)(2,1)S(1)}, u32[]{:S(2)}, u32[]{:S(2)}) collective-permute-start(bf16[128,2048]{1,0:T(8,128)(2,1)S(1)} %shard_map.118), channel_id=1, source_target_pairs={{0,4},{1,5},{2,6},{3,7},{4,0},{5,1},{6,2},{7,3},{8,12},{9,13},{10,... | collective-permute-start | bytes 1572872 | tf_op jit(solution)/shard_map/ppermute | solution.py:117
  61.3 17.8 %collective-permute-done.15.refs_5_ = bf16[128,2048]{1,0:T(8,128)(2,1)S(1)} collective-permute-done((bf16[128,2048]{1,0:T(8,128)(2,1)S(1)}, bf16[128,2048]{1,0:T(8,128)(2,1)S(1)}, u32[]{:S(2)}, u32[]{:S(2)}) %collective-permute-start.15) | collective-permute-done | bytes 524320 | tf_op jit(solution)/shard_map/ppermute | solution.py:117
  79.1 4.4 %collective-permute-done.17.refs_6_ = bf16[128,2048]{1,0:T(8,128)(2,1)S(1)} collective-permute-done((bf16[128,2048]{1,0:T(8,128)(2,1)S(1)}, bf16[128,2048]{1,0:T(8,128)(2,1)S(1)}, u32[]{:S(2)}, u32[]{:S(2)}) %collective-permute-start.17) | collective-permute-done | bytes 524320 | tf_op jit(solution)/shard_map/ppermute | solution.py:117
  84.0 1.7 shard_map.119
  86.2 1.5 collective-permute-done.18.refs_6_
  87.7 5.1 %shard_map.120 = (bf16[128,2048]{1,0:T(8,128)(2,1)}, bf16[128,1024]{1,0:T(8,128)(2,1)S(1)}, bf16[128,1024]{1,0:T(8,128)(2,1)S(1)}, bf16[128,1152]{1,0:T(8,128)(2,1)S(1)}, bf16[128,896]{1,0:T(8,128)(2,1)S(1)}) custom-call(s32[4]{0:T(128)S(1)} %copy-done.6, bf16[512,1024]{1,0:T(8,128)(2,1)S(1)} %shard_map.116.refs_0_, ...), custom_call_target="tpu_custom_call" | custom-call | flops 1 | bytes 1 | tf_op jit(solution)/shard_map/pallas_call | solution.py:48
  92.8 1.6 collective-permute-start.24
  95.6 13.5 %collective-permute-done.20.refs_1_.refs_3_ = bf16[128,1152]{1,0:T(8,128)(2,1)S(1)} collective-permute-done((bf16[128,1152]{1,0:T(8,128)(2,1)S(1)}, bf16[128,1152]{1,0:T(8,128)(2,1)S(1)}, u32[]{:S(2)}, u32[]{:S(2)}) %collective-permute-start.20) | collective-permute-done | bytes 294944 | tf_op jit(solution)/shard_map/ppermute | solution.py:117
  109.9 1.9 %collective-permute-start.21 = (bf16[256,1152]{1,0:T(8,128)(2,1)S(1)}, bf16[256,1152]{1,0:T(8,128)(2,1)S(1)}, u32[]{:S(2)}, u32[]{:S(2)}) collective-permute-start(bf16[256,1152]{1,0:T(8,128)(2,1)S(1)} %shard_map.121), channel_id=1, source_target_pairs={{0,2},{1,3},{2,0},{3,1},{4,6},{5,7},{6,4},{7,5},{8,10},{9,11},{10,... | collective-permute-start | bytes 1769480 | tf_op jit(solution)/shard_map/ppermute | solution.py:117
  111.9 1.4 collective-permute-start.27
  113.6 14.6 %collective-permute-done.25.refs_1_.refs_3_ = bf16[128,896]{1,0:T(8,128)(2,1)S(1)} collective-permute-done((bf16[128,896]{1,0:T(8,128)(2,1)S(1)}, bf16[128,896]{1,0:T(8,128)(2,1)S(1)}, u32[]{:S(2)}, u32[]{:S(2)}) %collective-permute-start.25) | collective-permute-done | bytes 229408 | tf_op jit(solution)/shard_map/ppermute | solution.py:117
  128.2 0.9 collective-permute-done.21.refs_4_
  129.1 0.9 shard_map.125
  130.2 1.3 shard_map.129
  132.1 0.8 collective-permute-start.32
  132.9 0.9 shard_map.126
  133.8 1.6 collective-permute-start.29
  135.4 1.4 collective-permute-start.30
  137.4 1.9 %shard_map.130 = (f32[64,2176]{1,0:T(8,128)S(1)}, f32[64,2176]{1,0:T(8,128)S(1)}, bf16[64,2304]{1,0:T(8,128)(2,1)S(1)}, bf16[64,2176]{1,0:T(8,128)(2,1)S(1)}) custom-call(s32[4]{0:T(128)S(1)} %copy-done.6, bf16[256,1536]{1,0:T(8,128)(2,1)S(1)} %shard_map.128.refs_0_, bf16[256,1024]{1,0:T(8,128)(2,1)S(1)} %shard_map.124.refs_1_, ...), custom_call_target="tpu_custom_call" | custom-call | flops 1 | bytes 1 | tf_op jit(solution)/shard_map/pallas_call | solution.py:48
  139.3 1.3 collective-permute-start.34
  140.6 9.9 %collective-permute-done.34.got = bf16[64,2176]{1,0:T(8,128)(2,1)S(1)} collective-permute-done((bf16[64,2176]{1,0:T(8,128)(2,1)S(1)}, bf16[64,2176]{1,0:T(8,128)(2,1)S(1)}, u32[]{:S(2)}, u32[]{:S(2)}) %collective-permute-start.34) | collective-permute-done | bytes 278560 | tf_op jit(solution)/shard_map/ppermute | solution.py:117
  151.6 0.8 collective-permute-start.39
  152.4 2.1 %collective-permute-start.40 = (bf16[64,2304]{1,0:T(8,128)(2,1)S(1)}, bf16[64,2304]{1,0:T(8,128)(2,1)S(1)}, u32[]{:S(2)}, u32[]{:S(2)}) collective-permute-start(bf16[64,2304]{1,0:T(8,128)(2,1)S(1)} %shard_map.131), channel_id=1, source_target_pairs={{0,4},{1,5},{2,6},{3,7},{4,0},{5,1},{6,2},{7,3},{8,12},{9,13},{10,... | collective-permute-start | bytes 884744 | tf_op jit(solution)/shard_map/ppermute | solution.py:117
  155.3 1.3 collective-permute-start.36
  156.6 1.5 collective-permute-start.37
  158.8 5.0 %collective-permute-done.36.refs_5_ = bf16[128,896]{1,0:T(8,128)(2,1)S(1)} collective-permute-done((bf16[128,896]{1,0:T(8,128)(2,1)S(1)}, bf16[128,896]{1,0:T(8,128)(2,1)S(1)}, u32[]{:S(2)}, u32[]{:S(2)}) %collective-permute-start.36) | collective-permute-done | bytes 229408 | tf_op jit(solution)/shard_map/ppermute | solution.py:117
  163.8 3.8 %collective-permute-done.37.refs_6_ = bf16[128,896]{1,0:T(8,128)(2,1)S(1)} collective-permute-done((bf16[128,896]{1,0:T(8,128)(2,1)S(1)}, bf16[128,896]{1,0:T(8,128)(2,1)S(1)}, u32[]{:S(2)}, u32[]{:S(2)}) %collective-permute-start.37) | collective-permute-done | bytes 229408 | tf_op jit(solution)/shard_map/ppermute | solution.py:117
  167.7 1.0 collective-permute-done.38.refs_7_
  168.6 1.2 shard_map.134
  169.8 1.1 shard_map.135
  (78 shorter events, 12.9 us)
Async XLA Ops:
  4.0 18.3 %collective-permute-start.3 = (bf16[528,256]{1,0:T(8,128)(2,1)}, bf16[528,256]{1,0:T(8,128)(2,1)S(1)}, u32[]{:S(2)}, u32[]{:S(2)}) collective-permute-start(bf16[528,256]{1,0:T(8,128)(2,1)} %get-tuple-element.52), channel_id=1, source_target_pairs={{0,1},{1,0},{2,3},{3,2},{4,5},{5,4},{6,7},{7,6},{8,9},{9,8},{10,11... | collective-permute-start | bytes 811016 | tf_op jit(solution)/shard_map/ppermute | solution.py:117
  7.1 14.5 %collective-permute-start = (bf16[64,2048]{1,0:T(8,128)(2,1)}, bf16[64,2048]{1,0:T(8,128)(2,1)S(1)}, u32[]{:S(2)}, u32[]{:S(2)}) collective-permute-start(bf16[64,2048]{1,0:T(8,128)(2,1)} %weight.1), channel_id=1, source_target_pairs={{0,4},{1,5},{2,6},{3,7},{4,0},{5,1},{6,2},{7,3},{8,12},{9,13},{10,... | collective-permute-start | bytes 786440 | tf_op jit(solution)/shard_map/ppermute | solution.py:117
  9.7 26.9 %collective-permute-start.4 = (bf16[128,2048]{1,0:T(8,128)(2,1)}, bf16[128,2048]{1,0:T(8,128)(2,1)S(1)}, u32[]{:S(2)}, u32[]{:S(2)}) collective-permute-start(bf16[128,2048]{1,0:T(8,128)(2,1)} %refs_4_.1), channel_id=1, source_target_pairs={{0,16},{1,17},{2,18},{3,19},{4,20},{5,21},{6,22},{7,23},{8,24},{9,... | collective-permute-start | bytes 1572872 | tf_op jit(solution)/shard_map/ppermute | solution.py:117
  11.2 25.5 %collective-permute-start.5 = (bf16[128,2048]{1,0:T(8,128)(2,1)}, bf16[128,2048]{1,0:T(8,128)(2,1)S(1)}, u32[]{:S(2)}, u32[]{:S(2)}) collective-permute-start(bf16[128,2048]{1,0:T(8,128)(2,1)} %refs_4_.1), channel_id=1, source_target_pairs={{0,1},{1,0},{2,3},{3,2},{4,5},{5,4},{6,7},{7,6},{8,9},{9,8},{10,11... | collective-permute-start | bytes 1572872 | tf_op jit(solution)/shard_map/ppermute | solution.py:117
  11.7 25.0 %collective-permute-start.6 = (bf16[128,2048]{1,0:T(8,128)(2,1)}, bf16[128,2048]{1,0:T(8,128)(2,1)S(1)}, u32[]{:S(2)}, u32[]{:S(2)}) collective-permute-start(bf16[128,2048]{1,0:T(8,128)(2,1)} %refs_4_.1), channel_id=1, source_target_pairs={{0,17},{1,16},{2,19},{3,18},{4,21},{5,20},{6,23},{7,22},{8,25},{9,... | collective-permute-start | bytes 1572872 | tf_op jit(solution)/shard_map/ppermute | solution.py:117
  21.6 9.2 %collective-permute-start.2 = (bf16[64,2048]{1,0:T(8,128)(2,1)S(1)}, bf16[64,2048]{1,0:T(8,128)(2,1)S(1)}, u32[]{:S(2)}, u32[]{:S(2)}) collective-permute-start(bf16[64,2048]{1,0:T(8,128)(2,1)S(1)} %collective-permute-done.far), channel_id=1, source_target_pairs={{0,2},{1,3},{2,0},{3,1},{4,6},{5,7},{6,4},{7,5},{8,10},{9,11},{10,... | collective-permute-start | bytes 786440 | tf_op jit(solution)/shard_map/ppermute | solution.py:117
  22.4 12.1 %collective-permute-start.1 = (bf16[64,2048]{1,0:T(8,128)(2,1)}, bf16[64,2048]{1,0:T(8,128)(2,1)S(1)}, u32[]{:S(2)}, u32[]{:S(2)}) collective-permute-start(bf16[64,2048]{1,0:T(8,128)(2,1)} %weight.1), channel_id=1, source_target_pairs={{0,2},{1,3},{2,0},{3,1},{4,6},{5,7},{6,4},{7,5},{8,10},{9,11},{10,... | collective-permute-start | bytes 786440 | tf_op jit(solution)/shard_map/ppermute | solution.py:117
  36.6 1.0 copy-start.2
  36.6 1.0 copy-start.6
  36.6 1.0 copy-start.7
  36.6 4.4 %copy-start = (bf16[512,256]{1,0:T(8,128)(2,1)S(1)}, bf16[512,256]{1,0:T(8,128)(2,1)}, u32[]{:S(2)}) copy-start(bf16[512,256]{1,0:T(8,128)(2,1)} %get-tuple-element.58.refs_0_) | copy-start | bytes 786436
  36.7 4.4 %copy-start.1 = (bf16[512,256]{1,0:T(8,128)(2,1)S(1)}, bf16[512,256]{1,0:T(8,128)(2,1)}, u32[]{:S(2)}) copy-start(bf16[512,256]{1,0:T(8,128)(2,1)} %get-tuple-element.59.refs_1_.refs_0_) | copy-start | bytes 786436
  36.8 4.2 %collective-permute-start.8 = (bf16[384,2048]{1,0:T(8,128)(2,1)S(1)}, bf16[384,2048]{1,0:T(8,128)(2,1)S(1)}, u32[]{:S(2)}, u32[]{:S(2)}) collective-permute-start(bf16[384,2048]{1,0:T(8,128)(2,1)S(1)} %shard_map.114), channel_id=1, source_target_pairs={{0,8},{1,9},{2,10},{3,11},{4,12},{5,13},{6,14},{7,15},{8,0},{9,1},... | collective-permute-start | bytes 4718600 | tf_op jit(solution)/shard_map/ppermute | solution.py:117
  37.7 3.4 %collective-permute-start.7 = (bf16[128,2048]{1,0:T(8,128)(2,1)S(1)}, bf16[128,2048]{1,0:T(8,128)(2,1)S(1)}, u32[]{:S(2)}, u32[]{:S(2)}) collective-permute-start(bf16[128,2048]{1,0:T(8,128)(2,1)S(1)} %copy-done.2), channel_id=1, source_target_pairs={{0,8},{1,9},{2,10},{3,11},{4,12},{5,13},{6,14},{7,15},{8,0},{9,1},... | collective-permute-start | bytes 1572872 | tf_op jit(solution)/shard_map/ppermute | solution.py:117
  38.5 14.4 %collective-permute-start.10 = (bf16[256,1024]{1,0:T(8,128)(2,1)S(1)}, bf16[256,1024]{1,0:T(8,128)(2,1)S(1)}, u32[]{:S(2)}, u32[]{:S(2)}) collective-permute-start(bf16[256,1024]{1,0:T(8,128)(2,1)S(1)} %get-tuple-element.65.refs_0_), channel_id=1, source_target_pairs={{0,1},{1,0},{2,3},{3,2},{4,5},{5,4},{6,7},{7,6},{8,9},{9,8},{10,11... | collective-permute-start | bytes 1572872 | tf_op jit(solution)/shard_map/ppermute | solution.py:117
  39.5 15.0 %collective-permute-start.9 = (bf16[256,1024]{1,0:T(8,128)(2,1)S(1)}, bf16[256,1024]{1,0:T(8,128)(2,1)S(1)}, u32[]{:S(2)}, u32[]{:S(2)}) collective-permute-start(bf16[256,1024]{1,0:T(8,128)(2,1)S(1)} %get-tuple-element.63.refs_0_), channel_id=1, source_target_pairs={{0,16},{1,17},{2,18},{3,19},{4,20},{5,21},{6,22},{7,23},{8,24},{9,... | collective-permute-start | bytes 1572872 | tf_op jit(solution)/shard_map/ppermute | solution.py:117
  43.4 14.6 %collective-permute-start.16 = (bf16[128,2048]{1,0:T(8,128)(2,1)S(1)}, bf16[128,2048]{1,0:T(8,128)(2,1)S(1)}, u32[]{:S(2)}, u32[]{:S(2)}) collective-permute-start(bf16[128,2048]{1,0:T(8,128)(2,1)S(1)} %get-tuple-element.62), channel_id=1, source_target_pairs={{0,2},{1,3},{2,0},{3,1},{4,6},{5,7},{6,4},{7,5},{8,10},{9,11},{10,... | collective-permute-start | bytes 1572872 | tf_op jit(solution)/shard_map/ppermute | solution.py:117
  52.9 26.2 %collective-permute-start.12 = (bf16[512,1024]{1,0:T(8,128)(2,1)S(1)}, bf16[512,1024]{1,0:T(8,128)(2,1)S(1)}, u32[]{:S(2)}, u32[]{:S(2)}) collective-permute-start(bf16[512,1024]{1,0:T(8,128)(2,1)S(1)} %shard_map.117.refs_1_), channel_id=1, source_target_pairs={{0,16},{1,17},{2,18},{3,19},{4,20},{5,21},{6,22},{7,23},{8,24},{9,... | collective-permute-start | bytes 3145736 | tf_op jit(solution)/shard_map/ppermute | solution.py:117
  54.6 29.5 %copy-start.8 = (f32[2048]{0:T(1024)S(1)}, f32[2048]{0:T(1024)}, u32[]{:S(2)}) copy-start(f32[2048]{0:T(1024)} %param.14) | copy-start | bytes 24580
  54.6 29.0 %collective-permute-start.11 = (bf16[512,1024]{1,0:T(8,128)(2,1)S(1)}, bf16[512,1024]{1,0:T(8,128)(2,1)S(1)}, u32[]{:S(2)}, u32[]{:S(2)}) collective-permute-start(bf16[512,1024]{1,0:T(8,128)(2,1)S(1)} %shard_map.116.refs_0_), channel_id=1, source_target_pairs={{0,1},{1,0},{2,3},{3,2},{4,5},{5,4},{6,7},{7,6},{8,9},{9,8},{10,11... | collective-permute-start | bytes 3145736 | tf_op jit(solution)/shard_map/ppermute | solution.py:117
  55.2 23.8 %collective-permute-start.15 = (bf16[128,2048]{1,0:T(8,128)(2,1)S(1)}, bf16[128,2048]{1,0:T(8,128)(2,1)S(1)}, u32[]{:S(2)}, u32[]{:S(2)}) collective-permute-start(bf16[128,2048]{1,0:T(8,128)(2,1)S(1)} %get-tuple-element.66), channel_id=1, source_target_pairs={{0,2},{1,3},{2,0},{3,1},{4,6},{5,7},{6,4},{7,5},{8,10},{9,11},{10,... | collective-permute-start | bytes 1572872 | tf_op jit(solution)/shard_map/ppermute | solution.py:117
  58.1 25.4 %collective-permute-start.17 = (bf16[128,2048]{1,0:T(8,128)(2,1)S(1)}, bf16[128,2048]{1,0:T(8,128)(2,1)S(1)}, u32[]{:S(2)}, u32[]{:S(2)}) collective-permute-start(bf16[128,2048]{1,0:T(8,128)(2,1)S(1)} %shard_map.118), channel_id=1, source_target_pairs={{0,4},{1,5},{2,6},{3,7},{4,0},{5,1},{6,2},{7,3},{8,12},{9,13},{10,... | collective-permute-start | bytes 1572872 | tf_op jit(solution)/shard_map/ppermute | solution.py:117
  61.3 24.4 %collective-permute-start.14 = (bf16[512,1024]{1,0:T(8,128)(2,1)S(1)}, bf16[512,1024]{1,0:T(8,128)(2,1)S(1)}, u32[]{:S(2)}, u32[]{:S(2)}) collective-permute-start(bf16[512,1024]{1,0:T(8,128)(2,1)S(1)} %shard_map.117.refs_1_), channel_id=1, source_target_pairs={{0,8},{1,9},{2,10},{3,11},{4,12},{5,13},{6,14},{7,15},{8,0},{9,1},... | collective-permute-start | bytes 3145736 | tf_op jit(solution)/shard_map/ppermute | solution.py:117
  79.1 6.7 %collective-permute-start.13 = (bf16[512,1024]{1,0:T(8,128)(2,1)S(1)}, bf16[512,1024]{1,0:T(8,128)(2,1)S(1)}, u32[]{:S(2)}, u32[]{:S(2)}) collective-permute-start(bf16[512,1024]{1,0:T(8,128)(2,1)S(1)} %shard_map.116.refs_0_), channel_id=1, source_target_pairs={{0,8},{1,9},{2,10},{3,11},{4,12},{5,13},{6,14},{7,15},{8,0},{9,1},... | collective-permute-start | bytes 3145736 | tf_op jit(solution)/shard_map/ppermute | solution.py:117
  83.5 2.7 %collective-permute-start.19 = (bf16[512,1024]{1,0:T(8,128)(2,1)S(1)}, bf16[512,1024]{1,0:T(8,128)(2,1)S(1)}, u32[]{:S(2)}, u32[]{:S(2)}) collective-permute-start(bf16[512,1024]{1,0:T(8,128)(2,1)S(1)} %collective-permute-done.12.refs_3_), channel_id=1, source_target_pairs={{0,8},{1,9},{2,10},{3,11},{4,12},{5,13},{6,14},{7,15},{8,0},{9,1},... | collective-permute-start | bytes 3145736 | tf_op jit(solution)/shard_map/ppermute | solution.py:117
  83.5 4.2 %collective-permute-start.18 = (bf16[512,1024]{1,0:T(8,128)(2,1)S(1)}, bf16[512,1024]{1,0:T(8,128)(2,1)S(1)}, u32[]{:S(2)}, u32[]{:S(2)}) collective-permute-start(bf16[512,1024]{1,0:T(8,128)(2,1)S(1)} %collective-permute-done.11.refs_2_), channel_id=1, source_target_pairs={{0,8},{1,9},{2,10},{3,11},{4,12},{5,13},{6,14},{7,15},{8,0},{9,1},... | collective-permute-start | bytes 3145736 | tf_op jit(solution)/shard_map/ppermute | solution.py:117
  84.0 3.6 %copy-start.3 = (bf16[128,2048]{1,0:T(8,128)(2,1)S(1)}, bf16[128,2048]{1,0:T(8,128)(2,1)}, u32[]{:S(2)}) copy-start(bf16[128,2048]{1,0:T(8,128)(2,1)} %refs_10_.1) | copy-start | bytes 1572868
  92.8 16.3 %collective-permute-start.20 = (bf16[128,1152]{1,0:T(8,128)(2,1)S(1)}, bf16[128,1152]{1,0:T(8,128)(2,1)S(1)}, u32[]{:S(2)}, u32[]{:S(2)}) collective-permute-start(bf16[128,1152]{1,0:T(8,128)(2,1)S(1)} %get-tuple-element.74.refs_0_.refs_2_), channel_id=1, source_target_pairs={{0,4},{1,5},{2,6},{3,7},{4,0},{5,1},{6,2},{7,3},{8,12},{9,13},{10,... | collective-permute-start | bytes 884744 | tf_op jit(solution)/shard_map/ppermute | solution.py:117
  92.8 16.2 %collective-permute-start.24 = (bf16[128,1024]{1,0:T(8,128)(2,1)S(1)}, bf16[128,1024]{1,0:T(8,128)(2,1)S(1)}, u32[]{:S(2)}, u32[]{:S(2)}) collective-permute-start(bf16[128,1024]{1,0:T(8,128)(2,1)S(1)} %get-tuple-element.78), channel_id=1, source_target_pairs={{0,16},{1,17},{2,18},{3,19},{4,20},{5,21},{6,22},{7,23},{8,24},{9,... | collective-permute-start | bytes 786440 | tf_op jit(solution)/shard_map/ppermute | solution.py:117
  94.4 14.7 %collective-permute-start.22 = (bf16[128,1024]{1,0:T(8,128)(2,1)S(1)}, bf16[128,1024]{1,0:T(8,128)(2,1)S(1)}, u32[]{:S(2)}, u32[]{:S(2)}) collective-permute-start(bf16[128,1024]{1,0:T(8,128)(2,1)S(1)} %get-tuple-element.80.refs_0_), channel_id=1, source_target_pairs={{0,16},{1,17},{2,18},{3,19},{4,20},{5,21},{6,22},{7,23},{8,24},{9,... | collective-permute-start | bytes 786440 | tf_op jit(solution)/shard_map/ppermute | solution.py:117
  94.9 16.9 %collective-permute-start.23 = (bf16[128,1024]{1,0:T(8,128)(2,1)S(1)}, bf16[128,1024]{1,0:T(8,128)(2,1)S(1)}, u32[]{:S(2)}, u32[]{:S(2)}) collective-permute-start(bf16[128,1024]{1,0:T(8,128)(2,1)S(1)} %get-tuple-element.82.refs_0_), channel_id=1, source_target_pairs={{0,1},{1,0},{2,3},{3,2},{4,5},{5,4},{6,7},{7,6},{8,9},{9,8},{10,11... | collective-permute-start | bytes 786440 | tf_op jit(solution)/shard_map/ppermute | solution.py:117
  109.1 20.0 %collective-permute-start.26 = (bf16[256,1536]{1,0:T(8,128)(2,1)S(1)}, bf16[256,1536]{1,0:T(8,128)(2,1)S(1)}, u32[]{:S(2)}, u32[]{:S(2)}) collective-permute-start(bf16[256,1536]{1,0:T(8,128)(2,1)S(1)} %shard_map.123), channel_id=1, source_target_pairs={{0,1},{1,0},{2,3},{3,2},{4,5},{5,4},{6,7},{7,6},{8,9},{9,8},{10,11... | collective-permute-start | bytes 2359304 | tf_op jit(solution)/shard_map/ppermute | solution.py:117
  109.9 19.2 %collective-permute-start.21 = (bf16[256,1152]{1,0:T(8,128)(2,1)S(1)}, bf16[256,1152]{1,0:T(8,128)(2,1)S(1)}, u32[]{:S(2)}, u32[]{:S(2)}) collective-permute-start(bf16[256,1152]{1,0:T(8,128)(2,1)S(1)} %shard_map.121), channel_id=1, source_target_pairs={{0,2},{1,3},{2,0},{3,1},{4,6},{5,7},{6,4},{7,5},{8,10},{9,11},{10,... | collective-permute-start | bytes 1769480 | tf_op jit(solution)/shard_map/ppermute | solution.py:117
  111.9 16.3 %collective-permute-start.27 = (bf16[256,1024]{1,0:T(8,128)(2,1)S(1)}, bf16[256,1024]{1,0:T(8,128)(2,1)S(1)}, u32[]{:S(2)}, u32[]{:S(2)}) collective-permute-start(bf16[256,1024]{1,0:T(8,128)(2,1)S(1)} %shard_map.124.refs_1_), channel_id=1, source_target_pairs={{0,16},{1,17},{2,18},{3,19},{4,20},{5,21},{6,22},{7,23},{8,24},{9,... | collective-permute-start | bytes 1572872 | tf_op jit(solution)/shard_map/ppermute | solution.py:117
  113.3 14.9 %collective-permute-start.25 = (bf16[128,896]{1,0:T(8,128)(2,1)S(1)}, bf16[128,896]{1,0:T(8,128)(2,1)S(1)}, u32[]{:S(2)}, u32[]{:S(2)}) collective-permute-start(bf16[128,896]{1,0:T(8,128)(2,1)S(1)} %get-tuple-element.79.refs_0_.refs_2_), channel_id=1, source_target_pairs={{0,4},{1,5},{2,6},{3,7},{4,0},{5,1},{6,2},{7,3},{8,12},{9,13},{10,... | collective-permute-start | bytes 688136 | tf_op jit(solution)/shard_map/ppermute | solution.py:117
  130.0 2.9 %collective-permute-start.28 = (bf16[512,1152]{1,0:T(8,128)(2,1)S(1)}, bf16[512,1152]{1,0:T(8,128)(2,1)S(1)}, u32[]{:S(2)}, u32[]{:S(2)}) collective-permute-start(bf16[512,1152]{1,0:T(8,128)(2,1)S(1)} %shard_map.125), channel_id=1, source_target_pairs={{0,8},{1,9},{2,10},{3,11},{4,12},{5,13},{6,14},{7,15},{8,0},{9,1},... | collective-permute-start | bytes 3538952 | tf_op jit(solution)/shard_map/ppermute | solution.py:117
  131.5 5.9 %collective-permute-start.33 = (bf16[256,2176]{1,0:T(8,128)(2,1)S(1)}, bf16[256,2176]{1,0:T(8,128)(2,1)S(1)}, u32[]{:S(2)}, u32[]{:S(2)}) collective-permute-start(bf16[256,2176]{1,0:T(8,128)(2,1)S(1)} %shard_map.129), channel_id=1, source_target_pairs={{0,8},{1,9},{2,10},{3,11},{4,12},{5,13},{6,14},{7,15},{8,0},{9,1},... | collective-permute-start | bytes 3342344 | tf_op jit(solution)/shard_map/ppermute | solution.py:117
  132.1 18.7 %collective-permute-start.32 = (bf16[256,896]{1,0:T(8,128)(2,1)S(1)}, bf16[256,896]{1,0:T(8,128)(2,1)S(1)}, u32[]{:S(2)}, u32[]{:S(2)}) collective-permute-start(bf16[256,896]{1,0:T(8,128)(2,1)S(1)} %shard_map.127), channel_id=1, source_target_pairs={{0,2},{1,3},{2,0},{3,1},{4,6},{5,7},{6,4},{7,5},{8,10},{9,11},{10,... | collective-permute-start | bytes 1376264 | tf_op jit(solution)/shard_map/ppermute | solution.py:117
  133.8 16.9 %collective-permute-start.29 = (bf16[128,1152]{1,0:T(8,128)(2,1)S(1)}, bf16[128,1152]{1,0:T(8,128)(2,1)S(1)}, u32[]{:S(2)}, u32[]{:S(2)}) collective-permute-start(bf16[128,1152]{1,0:T(8,128)(2,1)S(1)} %get-tuple-element.85), channel_id=1, source_target_pairs={{0,16},{1,17},{2,18},{3,19},{4,20},{5,21},{6,22},{7,23},{8,24},{9,... | collective-permute-start | bytes 884744 | tf_op jit(solution)/shard_map/ppermute | solution.py:117
  135.4 15.4 %collective-permute-start.30 = (bf16[128,1152]{1,0:T(8,128)(2,1)S(1)}, bf16[128,1152]{1,0:T(8,128)(2,1)S(1)}, u32[]{:S(2)}, u32[]{:S(2)}) collective-permute-start(bf16[128,1152]{1,0:T(8,128)(2,1)S(1)} %get-tuple-element.86), channel_id=1, source_target_pairs={{0,1},{1,0},{2,3},{3,2},{4,5},{5,4},{6,7},{7,6},{8,9},{9,8},{10,11... | collective-permute-start | bytes 884744 | tf_op jit(solution)/shard_map/ppermute | solution.py:117
  136.8 14.0 %collective-permute-start.31 = (bf16[128,1152]{1,0:T(8,128)(2,1)S(1)}, bf16[128,1152]{1,0:T(8,128)(2,1)S(1)}, u32[]{:S(2)}, u32[]{:S(2)}) collective-permute-start(bf16[128,1152]{1,0:T(8,128)(2,1)S(1)} %get-tuple-element.87), channel_id=1, source_target_pairs={{0,17},{1,16},{2,19},{3,18},{4,21},{5,20},{6,23},{7,22},{8,25},{9,... | collective-permute-start | bytes 884744 | tf_op jit(solution)/shard_map/ppermute | solution.py:117
  139.3 11.2 %collective-permute-start.34 = (bf16[64,2176]{1,0:T(8,128)(2,1)S(1)}, bf16[64,2176]{1,0:T(8,128)(2,1)S(1)}, u32[]{:S(2)}, u32[]{:S(2)}) collective-permute-start(bf16[64,2176]{1,0:T(8,128)(2,1)S(1)} %get-tuple-element.89), channel_id=1, source_target_pairs={{0,2},{1,3},{2,0},{3,1},{4,6},{5,7},{6,4},{7,5},{8,10},{9,11},{10,... | collective-permute-start | bytes 835592 | tf_op jit(solution)/shard_map/ppermute | solution.py:117
  151.5 3.0 %collective-permute-start.35 = (bf16[512,896]{1,0:T(8,128)(2,1)S(1)}, bf16[512,896]{1,0:T(8,128)(2,1)S(1)}, u32[]{:S(2)}, u32[]{:S(2)}) collective-permute-start(bf16[512,896]{1,0:T(8,128)(2,1)S(1)} %shard_map.132), channel_id=1, source_target_pairs={{0,8},{1,9},{2,10},{3,11},{4,12},{5,13},{6,14},{7,15},{8,0},{9,1},... | collective-permute-start | bytes 2752520 | tf_op jit(solution)/shard_map/ppermute | solution.py:117
  151.6 18.3 %collective-permute-start.39 = (bf16[64,2304]{1,0:T(8,128)(2,1)S(1)}, bf16[64,2304]{1,0:T(8,128)(2,1)S(1)}, u32[]{:S(2)}, u32[]{:S(2)}) collective-permute-start(bf16[64,2304]{1,0:T(8,128)(2,1)S(1)} %get-tuple-element.97), channel_id=1, source_target_pairs={{0,2},{1,3},{2,0},{3,1},{4,6},{5,7},{6,4},{7,5},{8,10},{9,11},{10,... | collective-permute-start | bytes 884744 | tf_op jit(solution)/shard_map/ppermute | solution.py:117
  152.4 17.4 %collective-permute-start.40 = (bf16[64,2304]{1,0:T(8,128)(2,1)S(1)}, bf16[64,2304]{1,0:T(8,128)(2,1)S(1)}, u32[]{:S(2)}, u32[]{:S(2)}) collective-permute-start(bf16[64,2304]{1,0:T(8,128)(2,1)S(1)} %shard_map.131), channel_id=1, source_target_pairs={{0,4},{1,5},{2,6},{3,7},{4,0},{5,1},{6,2},{7,3},{8,12},{9,13},{10,... | collective-permute-start | bytes 884744 | tf_op jit(solution)/shard_map/ppermute | solution.py:117
  155.3 8.6 %collective-permute-start.36 = (bf16[128,896]{1,0:T(8,128)(2,1)S(1)}, bf16[128,896]{1,0:T(8,128)(2,1)S(1)}, u32[]{:S(2)}, u32[]{:S(2)}) collective-permute-start(bf16[128,896]{1,0:T(8,128)(2,1)S(1)} %get-tuple-element.92), channel_id=1, source_target_pairs={{0,16},{1,17},{2,18},{3,19},{4,20},{5,21},{6,22},{7,23},{8,24},{9,... | collective-permute-start | bytes 688136 | tf_op jit(solution)/shard_map/ppermute | solution.py:117
  156.6 11.1 %collective-permute-start.37 = (bf16[128,896]{1,0:T(8,128)(2,1)S(1)}, bf16[128,896]{1,0:T(8,128)(2,1)S(1)}, u32[]{:S(2)}, u32[]{:S(2)}) collective-permute-start(bf16[128,896]{1,0:T(8,128)(2,1)S(1)} %get-tuple-element.93), channel_id=1, source_target_pairs={{0,1},{1,0},{2,3},{3,2},{4,5},{5,4},{6,7},{7,6},{8,9},{9,8},{10,11... | collective-permute-start | bytes 688136 | tf_op jit(solution)/shard_map/ppermute | solution.py:117
  158.1 10.5 %collective-permute-start.38 = (bf16[128,896]{1,0:T(8,128)(2,1)S(1)}, bf16[128,896]{1,0:T(8,128)(2,1)S(1)}, u32[]{:S(2)}, u32[]{:S(2)}) collective-permute-start(bf16[128,896]{1,0:T(8,128)(2,1)S(1)} %get-tuple-element.94), channel_id=1, source_target_pairs={{0,17},{1,16},{2,19},{3,18},{4,21},{5,20},{6,23},{7,22},{8,25},{9,... | collective-permute-start | bytes 688136 | tf_op jit(solution)/shard_map/ppermute | solution.py:117
  (2 other events, 1.5 us)

commit v5 on v4

--- a/solution.py
+++ b/solution.py
@@ -15,6 +15,22 @@
 ORDER = (0, 2, 1, 3)
 CUTS = (0, 9, 16)
 CHUNKS = len(CUTS) - 1
+PINS = {
+    "weight_core1": ("operator",),
+    "features_join": ("operator", "weight_near", "weight_last"),
+    "weight_halves": ("features", "operator", "weight_near"),
+    "weight_join1": ("sums",),
+    "weight_join2": ("sums",),
+    "weight_core2": ("sum_near", "sum_far", "sum_last"),
+    "pick": ("far0",),
+    "join_right": ("far0",),
+    "far1": ("far0", "left", "rows", "right"),
+    "across0": ("far1", "left2", "right2"),
+    "grad_far": ("left2",),
+    "across1": ("grad_fold", "feat0"),
+    "add": ("grad",),
+}
+NEAR_PAD, FAR_PAD, LAST_PAD = 256, 256, 128
 LOW = jnp.bfloat16
 F32 = jnp.float32
 
@@ -29,13 +45,6 @@
 
 def one_of(value, index, axis):
     return lax.dynamic_index_in_dim(value, index, axis, keepdims=False)
-
-
-def lookup(table, index):
-    found = 0
-    for k, entry in enumerate(table):
-        found = found + entry * (index == k).astype(jnp.int32)
-    return found
 
 
 def call(kernel, outs, scratch, *operands, numbers=0, outside=0, alone=False):
@@ -102,6 +111,15 @@
         self.b = self.col % self.bs
         self.chips = [(dx, db) for db in range(self.bs) for dx in range(self.xs)]
         self.numbers = jnp.stack([self.a, self.b, self.x, self.core]).astype(jnp.int32)
+        self.tokens = {}
+
+    def token(self, name, value):
+        self.tokens[name] = value if isinstance(value, (list, tuple)) else [value]
+        return value
+
+    def gate(self, name, value):
+        others = [array for step in PINS.get(name, ()) for array in self.tokens.get(step, ())]
+        return after(value, *others) if others else value
 
     def index(self, x, core, a, b):
         return ((x % self.xs) * CORES + core % CORES) * self.cols + (a % LINE) * self.bs + b % self.bs
@@ -214,18 +232,20 @@
         at.numbers,
         block_cols,
         block_counts,
-        block_vals,
+        at.gate("blocks", block_vals),
         weights,
         numbers=1,
         outside=4,
         alone=True,
     )
     result = [[own, other]]
-    arrived = [at.send(value, db=-db) for db, value in enumerate(sent, 1)]
+    arrived = at.token("blocks", [at.send(value, db=-db) for db, value in enumerate(sent, 1)])
     for db, got in enumerate(arrived, 1):
         kernel = functools.partial(sent_blocks_kernel, at.xs, at.bs, slots, db)
+        got = at.gate("operator", got)
         result.append(call(kernel, [dense] * CORES, [], at.numbers, got, weights, numbers=1))
-    return result, sent, arrived
+    at.token("operator", result[-1])
+    return result
 
 
 def sums_kernel(n_ops, pieces, *refs):
@@ -296,11 +316,13 @@
     return [value] + [at.send(value, db=-db) for db in range(1, at.bs)]
 
 
-def gathered_halves(at, halves, gate):
+def gathered_halves(at, halves):
     rows = halves[0].shape[0]
     left, right = along_x(at, halves[0]), along_b(at, halves[1])
-    steps = [left[1:] + right[1:]]
-    arrays, held = [join(after(left[0], gate), *left[1:]), join(after(right[0], gate), *right[1:])], {}
+    at.token("weight_step1", left[1:] + right[1:])
+    lefts = [at.gate("weight_join1", left[0]), *left[1:]]
+    rights = [at.gate("weight_join2", right[0]), *right[1:]]
+    arrays, held = [at.token("weight_join1", join(*lefts)), at.token("weight_join2", join(*rights))], {}
     for dx in range(at.xs):
         held[dx, 0, 0] = (0, dx * rows)
     for db in range(at.bs):
@@ -314,12 +336,15 @@
         arrays.append(at.send(right, dx=-dx))
         for db in range(at.bs):
             held[dx, db, 1] = (len(arrays) - 1, db * rows)
-    return arrays, held, steps + [arrays[2:]]
-
-
-def both_cores(at, arrays, held, gates):
+    at.token("weight_step2", arrays[2:])
+    return arrays, held
+
+
+def both_cores(at, arrays, held):
     count = len(arrays)
-    across = [at.send(after(value, *gate), dcore=1) for value, gate in zip(arrays, gates)]
+    across = [at.send(at.gate("weight_core1", value), dcore=1) for value in arrays[:2]]
+    at.token("weight_core1", across)
+    across += [at.send(at.gate("weight_core2", value), dcore=1) for value in arrays[2:]]
     places = {(0, *place): at for place, at in held.items()}
     places.update({(1, *place): (k + count, i) for place, (k, i) in held.items()})
     return arrays + across, places
@@ -333,13 +358,14 @@
         right[rows, :] = source[:, half:]
 
 
-def line_weight(at, weight, *gates):
+def line_weight(at, weight):
     count, width = weight.shape
-    far = at.send(weight, flip=2)
-    near = at.send(weight, flip=1)
-    last = at.send(far, flip=1)
+    far = at.token("weight_far", at.send(at.gate("weight_far", weight), flip=2))
+    near = at.token("weight_near", at.send(at.gate("weight_near", weight), flip=1))
+    last = at.token("weight_last", at.send(at.gate("weight_last", far), flip=1))
     halves = [like(LINE * count, width // 2)] * 2
-    return call(line_kernel, halves, [], at.numbers, weight, far, near, after(last, *gates), numbers=1)
+    last = at.gate("weight_line", last)
+    return at.token("weight_line", call(line_kernel, halves, [], at.numbers, weight, far, near, last, numbers=1))
 
 
 def turned_halves(value, swap):
@@ -450,23 +476,26 @@
         out[at, half:] = row[:, db * wide : (db + 1) * wide]
 
 
-def spread(at, lanes, left, right, rows, gate):
+def spread(at, lanes, left, right, rows):
     size, half = left.shape
-    lefts = [left] + [at.send(left, dx=dx) for dx in range(1, at.xs)]
-    rows = rows[:1] + [at.send(row, dx=dx) for dx, row in enumerate(rows[1:], 1)]
-    rights = [right] + [at.send(right, db=db) for db in range(1, at.bs)]
-    steps = [lefts[1:] + rights[1:] + rows[1:]]
+    lefts = [left] + [at.send(at.gate("left", left), dx=dx) for dx in range(1, at.xs)]
+    rows = rows[:1] + [at.send(at.gate("rows", row), dx=dx) for dx, row in enumerate(rows[1:], 1)]
+    rights = [right] + [at.send(at.gate("right", right), db=db) for db in range(1, at.bs)]
+    at.token("left", lefts[1:])
+    at.token("rows", rows[1:])
+    at.token("right", rights[1:])
 
     def pick(db):
         outs = [like(at.xs * size, half + CORES * lanes)]
-        return call(functools.partial(pick_kernel, db), outs, [], after(left, gate), *lefts[1:], *rows)[0]
+        refs = [at.gate("pick", left), *lefts[1:], *rows]
+        return call(functools.partial(pick_kernel, db), outs, [], *refs)[0]
 
     held = {}
 
     def keep(k, place, row):
         held[place] = (k, row)
 
-    arrays = [pick(0), join(after(right, gate), *rights[1:])]
+    arrays = [pick(0), join(at.gate("join_right", right), *rights[1:])]
     for dx in range(at.xs):
         keep(0, (-dx % at.xs, 0, 0), dx * size)
     for db in range(at.bs):
@@ -479,7 +508,9 @@
         arrays.append(at.send(arrays[1], dx=dx))
         for db in range(at.bs):
             keep(len(arrays) - 1, (-dx % at.xs, -db % at.bs, 1), db * size)
-    return arrays, held, steps + [arrays[2:]]
+    at.token("left2", arrays[2 : 1 + at.bs])
+    at.token("right2", arrays[1 + at.bs :])
+    return arrays, held
 
 
 def grad_kernel(held, xs, bs, lanes, dcore, n_arrays, place, *refs):
@@ -527,8 +558,8 @@
 
 
 def fold_kernel(kept, got, far):
-    width = got.shape[1] - 128
-    tail = got[:, width:].astype(F32)
+    width = kept.shape[1] - 128
+    tail = got[:, width : width + 128].astype(F32)
     far[:, :width] = (kept[:, :width] + got[:, :width].astype(F32)).astype(LOW)
     far[:, width : width + 128] = two_parts(kept[:, width : width + 128] + (tail[:, 0:1] + tail[:, 1:2]))
 
@@ -555,23 +586,27 @@
     own_rows = weight.shape[0]
     lanes = LINE * own_rows
     aligned = own_rows * at.bs == 128
-    ops, gate, arrived = operator(at, block_vals, block_cols, block_counts, self_weight, size)
-    own = {(dx, db): at.send(node_feats, dx=-dx, db=-db) if dx or db else node_feats for dx, db in at.chips}
-    halves = line_weight(at, weight, *arrived) if aligned else []
+    halves = line_weight(at, weight) if aligned else []
     first, *chips = at.chips
-    across = [at.send(own[first], dcore=1), at.send(join(after(own[chips[0]], *halves), *[own[chip] for chip in chips[1:]]), dcore=1)]
-    total, kept, to_near, to_last = sums(at, ops, own, across)
-    got = at.send(to_last, flip=1)
-    near = at.send(to_near, flip=1)
-    [far] = call(far_kernel, [like(size, width)], [], kept, got)
-    far = at.send(far, flip=2)
+    own = {first: node_feats}
+    for dx, db in chips:
+        own[dx, db] = at.send(at.gate("features", node_feats), dx=-dx, db=-db)
+    at.token("features", [own[chip] for chip in chips])
+    ops = operator(at, block_vals, block_cols, block_counts, self_weight, size)
+    others = at.token("features_join", join(at.gate("features_join", own[chips[0]]), *[own[chip] for chip in chips[1:]]))
+    across = [at.send(node_feats, dcore=1), at.send(others, dcore=1)]
+    across[0] = at.gate("sums", across[0])
+    total, kept, to_near, to_last = at.token("sums", sums(at, ops, own, across))
+    got = at.token("sum_last", at.send(to_last, flip=1))
+    [far] = at.token("sum_fold", call(far_kernel, [like(size, width)], [], kept, at.gate("sum_fold", got)))
+    near = at.token("sum_near", at.send(at.gate("sum_near", to_near), flip=1))
+    far = at.token("sum_far", at.send(far, flip=2))
 
     if not aligned:
         return plain_rest(at, ops, total + near.astype(F32) + far.astype(F32), weight, bias, out_grad)
-    halves = [after(half, *own.values(), *ops[-1]) for half in halves]
-    arrays, held, steps = gathered_halves(at, halves, to_last)
-    early = len(arrays) - len(steps[1])
-    arrays, held = both_cores(at, arrays, held, [[]] * early + [[near, far]] * len(steps[1]))
+    halves = [at.gate("weight_halves", half) for half in halves]
+    arrays, held = gathered_halves(at, halves)
+    arrays, held = both_cores(at, arrays, held)
     widths = [end - start for start, end in bounds(width)]
     own_held = {at: where for at, where in held.items() if not at[0]}
     count = len(arrays) // 2
@@ -598,18 +633,18 @@
         out_grad,
         numbers=1,
     )
+
+    fars = [at.token("far0", at.send(backs[0], flip=2))]
     kernel = functools.partial(rows_kernel, at.xs, at.bs, lanes)
-    rows = list(call(kernel, [like(size, at.bs * CORES * lanes)] * at.xs, [], turned))
-
-    fars = [at.send(backs[0], flip=2)]
-    arrays, held, steps = spread(at, lanes, left, right, rows, fars[0])
-    nears = [at.send(join(backs[0], fars[0]), flip=1)]
+    rows = list(call(kernel, [like(size, at.bs * CORES * lanes)] * at.xs, [], at.gate("rows_kernel", turned)))
+    arrays, held = spread(at, lanes, left, right, rows)
+    nears = [at.token("near0", at.send(join(at.gate("near0", backs[0]), fars[0]), flip=1))]
     for k in range(1, CHUNKS):
-        fars.append(at.send(after(backs[k], *fars, *steps[0]), flip=2))
-        nears.append(at.send(join(backs[k], fars[k]), flip=1))
-    feat, parts = feat_sums(at, ops, backs[0], fars[0], after(nears[0], *fars, *steps[1]))
-    gates = feat[1:]
-    wide, long = width + 128, width + 256
+        fars.append(at.token("far1", at.send(at.gate("far1", backs[k]), flip=2)))
+        nears.append(at.token("near1", at.send(join(at.gate("near1", backs[k]), fars[k]), flip=1)))
+
+    across0 = feat_across(at, ops, "0", backs[0], fars[0], nears[0])
+    wide = width + 128
     scratch = [
         pltpu.VMEM((size * len(at.chips), lanes), LOW),
         pltpu.VMEM((size * len(at.chips), width), LOW),
@@ -617,37 +652,60 @@
         pltpu.VMEM((8, width), F32),
     ]
     kernel = functools.partial(grad_kernel, held, at.xs, at.bs, lanes)
+    first = at.gate("grad_across", arrays[0])
     [across] = call(
-        functools.partial(kernel, 1, len(arrays)), [like(lanes, wide)], scratch, at.numbers, *arrays, numbers=1
-    )
-    got = at.send(across, dcore=1)
-    outs = [like(own_rows, wide, kind=F32)] * 2 + [like(own_rows, long), like(own_rows, wide)]
+        functools.partial(kernel, 1, len(arrays)), [like(lanes, wide)], scratch, at.numbers, first, *arrays[1:], numbers=1
+    )
+    at.token("grad_across", across)
+    got = at.token("grad_core", at.send(across, dcore=1))
+    feat = feat_own(at, ops, "0", across0, backs[0], fars[0], nears[0])
+    outs = [like(own_rows, wide, kind=F32)] * 2 + [like(own_rows, width + NEAR_PAD), like(own_rows, width + LAST_PAD)]
     total, kept, to_near, to_last = call(
-        functools.partial(kernel, 0, len(arrays)), outs, scratch, at.numbers, *arrays, got, numbers=1
-    )
-    got = at.send(to_last, flip=1)
-    [sent] = call(fold_kernel, [like(own_rows, long)], [], kept, got)
+        functools.partial(kernel, 0, len(arrays)),
+        outs,
+        scratch,
+        at.numbers,
+        *arrays,
+        at.gate("grad", got),
+        numbers=1,
+    )
+    at.token("grad", to_last)
+    got = at.token("grad_last", at.send(to_last, flip=1))
+    [sent] = call(fold_kernel, [like(own_rows, width + FAR_PAD)], [], kept, at.gate("grad_fold", got))
+    at.token("grad_fold", sent)
+    far = at.token("grad_far", at.send(at.gate("grad_far", sent), flip=2))
     for k in range(1, CHUNKS):
-        more, parts = feat_sums(at, ops, backs[k], fars[k], after(nears[k], sent, *parts, *gates))
-        feat = feat + more
-    near = at.send(to_near, flip=1)
-    far = at.send(sent, flip=2)
+        across1 = feat_across(at, ops, "1", backs[k], fars[k], nears[k])
+        feat = feat + feat_own(at, ops, "1", across1, backs[k], fars[k], nears[k])
+    near = at.token("grad_near", at.send(at.gate("grad_near", to_near), flip=1))
+    feat[0] = at.gate("add", feat[0])
     [feat_grad] = call(functools.partial(add_up_kernel, CHUNKS), [like(size, width, kind=F32)], [], *feat)
+    at.token("add", feat_grad)
     outs = [like(own_rows, width, kind=F32), like(1, own_rows, kind=F32)]
-    weight_grad, bias_grad = call(last_fold_kernel, outs, [], after(total, feat_grad), near, far)
+    weight_grad, bias_grad = call(last_fold_kernel, outs, [], at.gate("last", total), near, far)
     return activations, feat_grad, weight_grad, bias_grad[0]
 
 
-def feat_sums(at, ops, *lines):
+def feat_across(at, ops, name, *lines):
     size, chunk = lines[0].shape
     rows = len(at.chips) * size
+    *lines, near = lines
+    lines = [*lines, at.gate("across" + name, near)]
     kernel = functools.partial(back_kernel, len(ops))
     [across] = call(kernel, [like(rows, chunk)], [], *[pair[1] for pair in ops], *lines)
-    got = at.send(across, dcore=1)
+    at.token("across" + name, across)
+    return at.token("core" + name, at.send(across, dcore=1))
+
+
+def feat_own(at, ops, name, got, *lines):
+    size, chunk = lines[0].shape
+    kernel = functools.partial(back_kernel, len(ops))
     outs = [like(size, chunk, kind=F32)] + [like(size, chunk)] * (len(at.chips) - 1)
-    parts = call(kernel, outs, [], *[pair[0] for pair in ops], *lines, got)
+    parts = call(kernel, outs, [], *[pair[0] for pair in ops], *lines, at.gate("own" + name, got))
+    at.token("own" + name, parts)
     sent = [at.send(part, dx=dx, db=db) for part, (dx, db) in zip(parts[1:], at.chips[1:])]
-    return [parts[0]] + sent, parts
+    at.token("feat" + name, sent)
+    return [parts[0]] + sent
 
 
 def plain_rest(at, ops, agg, weight, bias, out_grad):
@@ -665,7 +723,8 @@
     for start, end in bounds(width):
         back = dot(pre_low, whole_weight[start:end], ((1,), (1,))).astype(LOW)
         far = at.send(back, flip=2)
-        feat = feat + feat_sums(at, ops, back, far, at.send(join(back, far), flip=1))[0]
+        lines = [back, far, at.send(join(back, far), flip=1)]
+        feat = feat + feat_own(at, ops, "", feat_across(at, ops, "", *lines), *lines)
     [feat_grad] = call(functools.partial(add_up_kernel, CHUNKS), [like(size, width, kind=F32)], [], *feat)
 
     groups = agg.reshape(size, at.rows, LINE, at.bs, own_rows)

time: 171 us -> 170 us (level)
  starting transfers between devices: 43.1 us -> 47 us
  waiting for transfers between devices: 101 us -> 97.2 us
    ppermute x41, starting transfers between devices: 43.1 us -> 47 us  [send(): return lax.ppermute(value, AXES, pairs)]
    ppermute x41, waiting for transfers between devices: 101 us -> 97.2 us  [send(): return lax.ppermute(value, AXES, pairs)]
where the time goes in v5:
time: 170 us
  waiting for transfers between devices  97.2 us (57%)
  starting transfers between devices  47 us (28%)
  Pallas kernels  22.8 us (13%)
    ppermute x41, waiting for transfers between devices, send(): return lax.ppermute(value, AXES, pairs)  97.2 us
    ppermute x41, starting transfers between devices, send(): return lax.ppermute(value, AXES, pairs)  47 us
    pallas_call x25, Pallas kernels, call(): pl.pallas_call(kernel, out_shape=outs, in_specs=specs, out_specs=[whole]...  22.8 us
  transfers between devices with their start and end apart: 41, of which 16 were waited for; matrix products, arithmetic and copies ran while one was open for 0% of the time, Pallas kernels for 7%

profile of v5, /device:TPU:0, one launch (start us, length us, event | category | flops | bytes accessed | tf_op | source)
XLA Modules:
  0.0 169.9 jit_solution(4672775452715136778)
XLA Ops:
  1.2 2.8 %shard_map.112 = (bf16[512,256]{1,0:T(8,128)(2,1)}, bf16[512,256]{1,0:T(8,128)(2,1)}, bf16[528,256]{1,0:T(8,128)(2,1)}) custom-call(s32[4]{0:T(128)} %pad_add_fusion.place, s32[2,8]{1,0:T(2,128)} %refs_0_.1, s32[1,8]{1,0:T(1,128)} %refs_1_.1, bf16[1024,256]{1,0:T(8,128)(2,1)} %refs_2_.1, f32[8,128]{1,0:T(8,128)} %bitcast.7), custom_call_target="tpu_custom_call" | custom-call | flops 1 | bytes 1 | tf_op jit(solution)/shard_map/pallas_call | solution.py:57
  4.0 3.0 %collective-permute-start.6 = (bf16[528,256]{1,0:T(8,128)(2,1)}, bf16[528,256]{1,0:T(8,128)(2,1)S(1)}, u32[]{:S(2)}, u32[]{:S(2)}) collective-permute-start(bf16[528,256]{1,0:T(8,128)(2,1)} %get-tuple-element.55), channel_id=1, source_target_pairs={{0,1},{1,0},{2,3},{3,2},{4,5},{5,4},{6,7},{7,6},{8,9},{9,8},{10,11... | collective-permute-start | bytes 811016 | tf_op jit(solution)/shard_map/ppermute | solution.py:135
  7.1 2.6 %collective-permute-start = (bf16[64,2048]{1,0:T(8,128)(2,1)}, bf16[64,2048]{1,0:T(8,128)(2,1)S(1)}, u32[]{:S(2)}, u32[]{:S(2)}) collective-permute-start(bf16[64,2048]{1,0:T(8,128)(2,1)} %weight.1), channel_id=1, source_target_pairs={{0,4},{1,5},{2,6},{3,7},{4,0},{5,1},{6,2},{7,3},{8,12},{9,13},{10,... | collective-permute-start | bytes 786440 | tf_op jit(solution)/shard_map/ppermute | solution.py:135
  9.7 1.5 collective-permute-start.3
  11.7 1.5 collective-permute-start.5
  13.2 8.4 %collective-permute-done.far = bf16[64,2048]{1,0:T(8,128)(2,1)S(1)} collective-permute-done((bf16[64,2048]{1,0:T(8,128)(2,1)}, bf16[64,2048]{1,0:T(8,128)(2,1)S(1)}, u32[]{:S(2)}, u32[]{:S(2)}) %collective-permute-start) | collective-permute-done | bytes 262176 | tf_op jit(solution)/shard_map/ppermute | solution.py:135
  22.4 1.2 collective-permute-start.2
  25.7 5.4 %collective-permute-done.1.near = bf16[64,2048]{1,0:T(8,128)(2,1)S(1)} collective-permute-done((bf16[64,2048]{1,0:T(8,128)(2,1)}, bf16[64,2048]{1,0:T(8,128)(2,1)S(1)}, u32[]{:S(2)}, u32[]{:S(2)}) %collective-permute-start.1) | collective-permute-done | bytes 262176 | tf_op jit(solution)/shard_map/ppermute | solution.py:135
  31.0 3.6 %collective-permute-done.2.last = bf16[64,2048]{1,0:T(8,128)(2,1)S(1)} collective-permute-done((bf16[64,2048]{1,0:T(8,128)(2,1)S(1)}, bf16[64,2048]{1,0:T(8,128)(2,1)S(1)}, u32[]{:S(2)}, u32[]{:S(2)}) %collective-permute-start.2) | collective-permute-done | bytes 262176 | tf_op jit(solution)/shard_map/ppermute | solution.py:135
  34.7 1.6 collective-permute-done.4.refs_1_.refs_6_
  37.6 1.8 %collective-permute-start.10 = (bf16[256,1024]{1,0:T(8,128)(2,1)S(1)}, bf16[256,1024]{1,0:T(8,128)(2,1)S(1)}, u32[]{:S(2)}, u32[]{:S(2)}) collective-permute-start(bf16[256,1024]{1,0:T(8,128)(2,1)S(1)} %get-tuple-element.69.refs_0_), channel_id=1, source_target_pairs={{0,1},{1,0},{2,3},{3,2},{4,5},{5,4},{6,7},{7,6},{8,9},{9,8},{10,11... | collective-permute-start | bytes 1572872 | tf_op jit(solution)/shard_map/ppermute | solution.py:135
  39.4 1.5 collective-permute-start.9
  40.9 2.4 %shard_map.115 = (f32[128,2048]{1,0:T(8,128)S(1)}, f32[128,2048]{1,0:T(8,128)S(1)}, bf16[128,2048]{1,0:T(8,128)(2,1)S(1)}, bf16[128,2048]{1,0:T(8,128)(2,1)S(1)}) custom-call(bf16[512,256]{1,0:T(8,128)(2,1)S(1)} %copy-done, bf16[512,256]{1,0:T(8,128)(2,1)S(1)} %copy-done.1, bf16[512,256]{1,0:T(8,128)(2,1)S(1)} %get-tuple-element.56.refs_2_.refs_1_, ...), custom_call_target="tpu_custom_call" | custom-call | flops 1 | bytes 1 | tf_op jit(solution)/shard_map/pallas_call | solution.py:57
  43.3 1.6 collective-permute-start.16
  44.9 6.7 %collective-permute-done.10.refs_1_ = bf16[256,1024]{1,0:T(8,128)(2,1)S(1)} collective-permute-done((bf16[256,1024]{1,0:T(8,128)(2,1)S(1)}, bf16[256,1024]{1,0:T(8,128)(2,1)S(1)}, u32[]{:S(2)}, u32[]{:S(2)}) %collective-permute-start.10) | collective-permute-done | bytes 524320 | tf_op jit(solution)/shard_map/ppermute | solution.py:135
  51.6 1.8 %collective-permute-start.12 = (bf16[512,1024]{1,0:T(8,128)(2,1)S(1)}, bf16[512,1024]{1,0:T(8,128)(2,1)S(1)}, u32[]{:S(2)}, u32[]{:S(2)}) collective-permute-start(bf16[512,1024]{1,0:T(8,128)(2,1)S(1)} %shard_map.117.refs_1_), channel_id=1, source_target_pairs={{0,16},{1,17},{2,18},{3,19},{4,20},{5,21},{6,22},{7,23},{8,24},{9,... | collective-permute-start | bytes 3145736 | tf_op jit(solution)/shard_map/ppermute | solution.py:135
  53.5 1.6 collective-permute-start.11
  55.1 1.6 collective-permute-start.15
  56.7 1.0 collective-permute-done.16.got
  57.8 3.0 %collective-permute-start.17 = (bf16[128,2048]{1,0:T(8,128)(2,1)S(1)}, bf16[128,2048]{1,0:T(8,128)(2,1)S(1)}, u32[]{:S(2)}, u32[]{:S(2)}) collective-permute-start(bf16[128,2048]{1,0:T(8,128)(2,1)S(1)} %shard_map.118), channel_id=1, source_target_pairs={{0,4},{1,5},{2,6},{3,7},{4,0},{5,1},{6,2},{7,3},{8,12},{9,13},{10,... | collective-permute-start | bytes 1572872 | tf_op jit(solution)/shard_map/ppermute | solution.py:135
  60.8 18.0 %collective-permute-done.15.refs_5_ = bf16[128,2048]{1,0:T(8,128)(2,1)S(1)} collective-permute-done((bf16[128,2048]{1,0:T(8,128)(2,1)S(1)}, bf16[128,2048]{1,0:T(8,128)(2,1)S(1)}, u32[]{:S(2)}, u32[]{:S(2)}) %collective-permute-start.15) | collective-permute-done | bytes 524320 | tf_op jit(solution)/shard_map/ppermute | solution.py:135
  78.8 3.8 %collective-permute-done.17.refs_6_ = bf16[128,2048]{1,0:T(8,128)(2,1)S(1)} collective-permute-done((bf16[128,2048]{1,0:T(8,128)(2,1)S(1)}, bf16[128,2048]{1,0:T(8,128)(2,1)S(1)}, u32[]{:S(2)}, u32[]{:S(2)}) %collective-permute-start.17) | collective-permute-done | bytes 524320 | tf_op jit(solution)/shard_map/ppermute | solution.py:135
  83.1 1.7 shard_map.119
  85.2 1.5 collective-permute-done.18.refs_6_
  86.7 5.1 %shard_map.120 = (bf16[128,2048]{1,0:T(8,128)(2,1)}, bf16[128,1024]{1,0:T(8,128)(2,1)S(1)}, bf16[128,1024]{1,0:T(8,128)(2,1)S(1)}, bf16[128,1152]{1,0:T(8,128)(2,1)S(1)}, bf16[128,896]{1,0:T(8,128)(2,1)S(1)}) custom-call(s32[4]{0:T(128)S(1)} %copy-done.6, bf16[512,1024]{1,0:T(8,128)(2,1)S(1)} %shard_map.116.refs_0_, ...), custom_call_target="tpu_custom_call" | custom-call | flops 1 | bytes 1 | tf_op jit(solution)/shard_map/pallas_call | solution.py:57
  91.9 1.7 collective-permute-start.23
  94.0 1.6 collective-permute-start.24
  95.6 12.5 %collective-permute-done.20.refs_1_.refs_3_ = bf16[128,1152]{1,0:T(8,128)(2,1)S(1)} collective-permute-done((bf16[128,1152]{1,0:T(8,128)(2,1)S(1)}, bf16[128,1152]{1,0:T(8,128)(2,1)S(1)}, u32[]{:S(2)}, u32[]{:S(2)}) %collective-permute-start.20) | collective-permute-done | bytes 294944 | tf_op jit(solution)/shard_map/ppermute | solution.py:135
  108.2 1.7 %collective-permute-start.26 = (bf16[256,1536]{1,0:T(8,128)(2,1)S(1)}, bf16[256,1536]{1,0:T(8,128)(2,1)S(1)}, u32[]{:S(2)}, u32[]{:S(2)}) collective-permute-start(bf16[256,1536]{1,0:T(8,128)(2,1)S(1)} %shard_map.123), channel_id=1, source_target_pairs={{0,1},{1,0},{2,3},{3,2},{4,5},{5,4},{6,7},{7,6},{8,9},{9,8},{10,11... | collective-permute-start | bytes 2359304 | tf_op jit(solution)/shard_map/ppermute | solution.py:135
  109.9 1.8 %collective-permute-start.21 = (bf16[256,1152]{1,0:T(8,128)(2,1)S(1)}, bf16[256,1152]{1,0:T(8,128)(2,1)S(1)}, u32[]{:S(2)}, u32[]{:S(2)}) collective-permute-start(bf16[256,1152]{1,0:T(8,128)(2,1)S(1)} %shard_map.121), channel_id=1, source_target_pairs={{0,2},{1,3},{2,0},{3,1},{4,6},{5,7},{6,4},{7,5},{8,10},{9,11},{10,... | collective-permute-start | bytes 1769480 | tf_op jit(solution)/shard_map/ppermute | solution.py:135
  111.7 1.6 collective-permute-start.27
  113.6 14.5 %collective-permute-done.25.refs_1_.refs_3_ = bf16[128,896]{1,0:T(8,128)(2,1)S(1)} collective-permute-done((bf16[128,896]{1,0:T(8,128)(2,1)S(1)}, bf16[128,896]{1,0:T(8,128)(2,1)S(1)}, u32[]{:S(2)}, u32[]{:S(2)}) %collective-permute-start.25) | collective-permute-done | bytes 229408 | tf_op jit(solution)/shard_map/ppermute | solution.py:135
  128.1 1.1 collective-permute-done.21.refs_4_
  129.1 0.9 shard_map.125
  130.2 1.3 shard_map.128
  132.9 0.9 shard_map.126
  133.8 1.6 collective-permute-start.30
  135.9 1.5 collective-permute-start.32
  137.4 1.9 %shard_map.129 = (f32[64,2176]{1,0:T(8,128)S(1)}, f32[64,2176]{1,0:T(8,128)S(1)}, bf16[64,2304]{1,0:T(8,128)(2,1)S(1)}, bf16[64,2176]{1,0:T(8,128)(2,1)S(1)}) custom-call(s32[4]{0:T(128)S(1)} %copy-done.6, bf16[256,1536]{1,0:T(8,128)(2,1)S(1)} %shard_map.127.refs_0_, bf16[256,1024]{1,0:T(8,128)(2,1)S(1)} %shard_map.124.refs_1_, ...), custom_call_target="tpu_custom_call" | custom-call | flops 1 | bytes 1 | tf_op jit(solution)/shard_map/pallas_call | solution.py:57
  139.3 1.3 collective-permute-start.34
  140.6 9.9 %collective-permute-done.34.got = bf16[64,2176]{1,0:T(8,128)(2,1)S(1)} collective-permute-done((bf16[64,2176]{1,0:T(8,128)(2,1)S(1)}, bf16[64,2176]{1,0:T(8,128)(2,1)S(1)}, u32[]{:S(2)}, u32[]{:S(2)}) %collective-permute-start.34) | collective-permute-done | bytes 278560 | tf_op jit(solution)/shard_map/ppermute | solution.py:135
  151.6 0.8 collective-permute-start.39
  152.4 2.1 %collective-permute-start.40 = (bf16[64,2304]{1,0:T(8,128)(2,1)S(1)}, bf16[64,2304]{1,0:T(8,128)(2,1)S(1)}, u32[]{:S(2)}, u32[]{:S(2)}) collective-permute-start(bf16[64,2304]{1,0:T(8,128)(2,1)S(1)} %shard_map.131), channel_id=1, source_target_pairs={{0,4},{1,5},{2,6},{3,7},{4,0},{5,1},{6,2},{7,3},{8,12},{9,13},{10,... | collective-permute-start | bytes 884744 | tf_op jit(solution)/shard_map/ppermute | solution.py:135
  155.2 1.3 collective-permute-start.36
  157.1 1.7 %collective-permute-start.38 = (bf16[128,896]{1,0:T(8,128)(2,1)S(1)}, bf16[128,896]{1,0:T(8,128)(2,1)S(1)}, u32[]{:S(2)}, u32[]{:S(2)}) collective-permute-start(bf16[128,896]{1,0:T(8,128)(2,1)S(1)} %get-tuple-element.98), channel_id=1, source_target_pairs={{0,17},{1,16},{2,19},{3,18},{4,21},{5,20},{6,23},{7,22},{8,25},{9,... | collective-permute-start | bytes 688136 | tf_op jit(solution)/shard_map/ppermute | solution.py:135
  158.8 8.5 %collective-permute-done.39.refs_0_ = bf16[64,2304]{1,0:T(8,128)(2,1)S(1)} collective-permute-done((bf16[64,2304]{1,0:T(8,128)(2,1)S(1)}, bf16[64,2304]{1,0:T(8,128)(2,1)S(1)}, u32[]{:S(2)}, u32[]{:S(2)}) %collective-permute-start.39) | collective-permute-done | bytes 294944 | tf_op jit(solution)/shard_map/ppermute | solution.py:135
  167.3 1.1 shard_map.135
  168.7 1.2 shard_map.134
  (78 shorter events, 11.9 us)
Async XLA Ops:
  4.0 18.3 %collective-permute-start.6 = (bf16[528,256]{1,0:T(8,128)(2,1)}, bf16[528,256]{1,0:T(8,128)(2,1)S(1)}, u32[]{:S(2)}, u32[]{:S(2)}) collective-permute-start(bf16[528,256]{1,0:T(8,128)(2,1)} %get-tuple-element.55), channel_id=1, source_target_pairs={{0,1},{1,0},{2,3},{3,2},{4,5},{5,4},{6,7},{7,6},{8,9},{9,8},{10,11... | collective-permute-start | bytes 811016 | tf_op jit(solution)/shard_map/ppermute | solution.py:135
  7.1 14.5 %collective-permute-start = (bf16[64,2048]{1,0:T(8,128)(2,1)}, bf16[64,2048]{1,0:T(8,128)(2,1)S(1)}, u32[]{:S(2)}, u32[]{:S(2)}) collective-permute-start(bf16[64,2048]{1,0:T(8,128)(2,1)} %weight.1), channel_id=1, source_target_pairs={{0,4},{1,5},{2,6},{3,7},{4,0},{5,1},{6,2},{7,3},{8,12},{9,13},{10,... | collective-permute-start | bytes 786440 | tf_op jit(solution)/shard_map/ppermute | solution.py:135
  9.7 21.4 %collective-permute-start.3 = (bf16[128,2048]{1,0:T(8,128)(2,1)}, bf16[128,2048]{1,0:T(8,128)(2,1)S(1)}, u32[]{:S(2)}, u32[]{:S(2)}) collective-permute-start(bf16[128,2048]{1,0:T(8,128)(2,1)} %refs_4_.1), channel_id=1, source_target_pairs={{0,16},{1,17},{2,18},{3,19},{4,20},{5,21},{6,22},{7,23},{8,24},{9,... | collective-permute-start | bytes 1572872 | tf_op jit(solution)/shard_map/ppermute | solution.py:135
  11.2 25.1 %collective-permute-start.4 = (bf16[128,2048]{1,0:T(8,128)(2,1)}, bf16[128,2048]{1,0:T(8,128)(2,1)S(1)}, u32[]{:S(2)}, u32[]{:S(2)}) collective-permute-start(bf16[128,2048]{1,0:T(8,128)(2,1)} %refs_4_.1), channel_id=1, source_target_pairs={{0,1},{1,0},{2,3},{3,2},{4,5},{5,4},{6,7},{7,6},{8,9},{9,8},{10,11... | collective-permute-start | bytes 1572872 | tf_op jit(solution)/shard_map/ppermute | solution.py:135
  11.7 24.6 %collective-permute-start.5 = (bf16[128,2048]{1,0:T(8,128)(2,1)}, bf16[128,2048]{1,0:T(8,128)(2,1)S(1)}, u32[]{:S(2)}, u32[]{:S(2)}) collective-permute-start(bf16[128,2048]{1,0:T(8,128)(2,1)} %refs_4_.1), channel_id=1, source_target_pairs={{0,17},{1,16},{2,19},{3,18},{4,21},{5,20},{6,23},{7,22},{8,25},{9,... | collective-permute-start | bytes 1572872 | tf_op jit(solution)/shard_map/ppermute | solution.py:135
  21.6 9.5 %collective-permute-start.1 = (bf16[64,2048]{1,0:T(8,128)(2,1)}, bf16[64,2048]{1,0:T(8,128)(2,1)S(1)}, u32[]{:S(2)}, u32[]{:S(2)}) collective-permute-start(bf16[64,2048]{1,0:T(8,128)(2,1)} %weight.1), channel_id=1, source_target_pairs={{0,2},{1,3},{2,0},{3,1},{4,6},{5,7},{6,4},{7,5},{8,10},{9,11},{10,... | collective-permute-start | bytes 786440 | tf_op jit(solution)/shard_map/ppermute | solution.py:135
  22.4 12.3 %collective-permute-start.2 = (bf16[64,2048]{1,0:T(8,128)(2,1)S(1)}, bf16[64,2048]{1,0:T(8,128)(2,1)S(1)}, u32[]{:S(2)}, u32[]{:S(2)}) collective-permute-start(bf16[64,2048]{1,0:T(8,128)(2,1)S(1)} %collective-permute-done.far), channel_id=1, source_target_pairs={{0,2},{1,3},{2,0},{3,1},{4,6},{5,7},{6,4},{7,5},{8,10},{9,11},{10,... | collective-permute-start | bytes 786440 | tf_op jit(solution)/shard_map/ppermute | solution.py:135
  34.7 1.8 %copy-start.2 = (bf16[128,2048]{1,0:T(8,128)(2,1)S(1)}, bf16[128,2048]{1,0:T(8,128)(2,1)}, u32[]{:S(2)}) copy-start(bf16[128,2048]{1,0:T(8,128)(2,1)} %refs_4_.1) | copy-start | bytes 1572868
  34.7 2.3 %copy-start.4 = (bf16[64,2048]{1,0:T(8,128)(2,1)S(1)}, bf16[64,2048]{1,0:T(8,128)(2,1)}, u32[]{:S(2)}) copy-start(bf16[64,2048]{1,0:T(8,128)(2,1)} %weight.1) | copy-start | bytes 786436
  34.7 2.3 %copy-start.6 = (s32[4]{0:T(128)S(1)}, s32[4]{0:T(128)}, u32[]{:S(2)}) copy-start(s32[4]{0:T(128)} %pad_add_fusion.place) | copy-start | bytes 52
  36.4 4.5 %copy-start = (bf16[512,256]{1,0:T(8,128)(2,1)S(1)}, bf16[512,256]{1,0:T(8,128)(2,1)}, u32[]{:S(2)}) copy-start(bf16[512,256]{1,0:T(8,128)(2,1)} %get-tuple-element.59.refs_0_) | copy-start | bytes 786436
  36.4 4.5 %copy-start.1 = (bf16[512,256]{1,0:T(8,128)(2,1)S(1)}, bf16[512,256]{1,0:T(8,128)(2,1)}, u32[]{:S(2)}) copy-start(bf16[512,256]{1,0:T(8,128)(2,1)} %get-tuple-element.60.refs_1_.refs_0_) | copy-start | bytes 786436
  36.4 4.5 %collective-permute-start.8 = (bf16[384,2048]{1,0:T(8,128)(2,1)S(1)}, bf16[384,2048]{1,0:T(8,128)(2,1)S(1)}, u32[]{:S(2)}, u32[]{:S(2)}) collective-permute-start(bf16[384,2048]{1,0:T(8,128)(2,1)S(1)} %shard_map.114), channel_id=1, source_target_pairs={{0,8},{1,9},{2,10},{3,11},{4,12},{5,13},{6,14},{7,15},{8,0},{9,1},... | collective-permute-start | bytes 4718600 | tf_op jit(solution)/shard_map/ppermute | solution.py:135
  36.5 4.4 %collective-permute-start.7 = (bf16[128,2048]{1,0:T(8,128)(2,1)S(1)}, bf16[128,2048]{1,0:T(8,128)(2,1)S(1)}, u32[]{:S(2)}, u32[]{:S(2)}) collective-permute-start(bf16[128,2048]{1,0:T(8,128)(2,1)S(1)} %copy-done.2), channel_id=1, source_target_pairs={{0,8},{1,9},{2,10},{3,11},{4,12},{5,13},{6,14},{7,15},{8,0},{9,1},... | collective-permute-start | bytes 1572872 | tf_op jit(solution)/shard_map/ppermute | solution.py:135
  37.6 14.0 %collective-permute-start.10 = (bf16[256,1024]{1,0:T(8,128)(2,1)S(1)}, bf16[256,1024]{1,0:T(8,128)(2,1)S(1)}, u32[]{:S(2)}, u32[]{:S(2)}) collective-permute-start(bf16[256,1024]{1,0:T(8,128)(2,1)S(1)} %get-tuple-element.69.refs_0_), channel_id=1, source_target_pairs={{0,1},{1,0},{2,3},{3,2},{4,5},{5,4},{6,7},{7,6},{8,9},{9,8},{10,11... | collective-permute-start | bytes 1572872 | tf_op jit(solution)/shard_map/ppermute | solution.py:135
  39.4 14.0 %collective-permute-start.9 = (bf16[256,1024]{1,0:T(8,128)(2,1)S(1)}, bf16[256,1024]{1,0:T(8,128)(2,1)S(1)}, u32[]{:S(2)}, u32[]{:S(2)}) collective-permute-start(bf16[256,1024]{1,0:T(8,128)(2,1)S(1)} %get-tuple-element.66.refs_0_), channel_id=1, source_target_pairs={{0,16},{1,17},{2,18},{3,19},{4,20},{5,21},{6,22},{7,23},{8,24},{9,... | collective-permute-start | bytes 1572872 | tf_op jit(solution)/shard_map/ppermute | solution.py:135
  43.3 14.4 %collective-permute-start.16 = (bf16[128,2048]{1,0:T(8,128)(2,1)S(1)}, bf16[128,2048]{1,0:T(8,128)(2,1)S(1)}, u32[]{:S(2)}, u32[]{:S(2)}) collective-permute-start(bf16[128,2048]{1,0:T(8,128)(2,1)S(1)} %get-tuple-element.65), channel_id=1, source_target_pairs={{0,2},{1,3},{2,0},{3,1},{4,6},{5,7},{6,4},{7,5},{8,10},{9,11},{10,... | collective-permute-start | bytes 1572872 | tf_op jit(solution)/shard_map/ppermute | solution.py:135
  51.6 27.2 %collective-permute-start.12 = (bf16[512,1024]{1,0:T(8,128)(2,1)S(1)}, bf16[512,1024]{1,0:T(8,128)(2,1)S(1)}, u32[]{:S(2)}, u32[]{:S(2)}) collective-permute-start(bf16[512,1024]{1,0:T(8,128)(2,1)S(1)} %shard_map.117.refs_1_), channel_id=1, source_target_pairs={{0,16},{1,17},{2,18},{3,19},{4,20},{5,21},{6,22},{7,23},{8,24},{9,... | collective-permute-start | bytes 3145736 | tf_op jit(solution)/shard_map/ppermute | solution.py:135
  53.5 29.6 %copy-start.8 = (f32[2048]{0:T(1024)S(1)}, f32[2048]{0:T(1024)}, u32[]{:S(2)}) copy-start(f32[2048]{0:T(1024)} %param.14) | copy-start | bytes 24580
  53.5 29.1 %collective-permute-start.11 = (bf16[512,1024]{1,0:T(8,128)(2,1)S(1)}, bf16[512,1024]{1,0:T(8,128)(2,1)S(1)}, u32[]{:S(2)}, u32[]{:S(2)}) collective-permute-start(bf16[512,1024]{1,0:T(8,128)(2,1)S(1)} %shard_map.116.refs_0_), channel_id=1, source_target_pairs={{0,1},{1,0},{2,3},{3,2},{4,5},{5,4},{6,7},{7,6},{8,9},{9,8},{10,11... | collective-permute-start | bytes 3145736 | tf_op jit(solution)/shard_map/ppermute | solution.py:135
  55.1 23.7 %collective-permute-start.15 = (bf16[128,2048]{1,0:T(8,128)(2,1)S(1)}, bf16[128,2048]{1,0:T(8,128)(2,1)S(1)}, u32[]{:S(2)}, u32[]{:S(2)}) collective-permute-start(bf16[128,2048]{1,0:T(8,128)(2,1)S(1)} %get-tuple-element.64), channel_id=1, source_target_pairs={{0,2},{1,3},{2,0},{3,1},{4,6},{5,7},{6,4},{7,5},{8,10},{9,11},{10,... | collective-permute-start | bytes 1572872 | tf_op jit(solution)/shard_map/ppermute | solution.py:135
  57.8 24.8 %collective-permute-start.17 = (bf16[128,2048]{1,0:T(8,128)(2,1)S(1)}, bf16[128,2048]{1,0:T(8,128)(2,1)S(1)}, u32[]{:S(2)}, u32[]{:S(2)}) collective-permute-start(bf16[128,2048]{1,0:T(8,128)(2,1)S(1)} %shard_map.118), channel_id=1, source_target_pairs={{0,4},{1,5},{2,6},{3,7},{4,0},{5,1},{6,2},{7,3},{8,12},{9,13},{10,... | collective-permute-start | bytes 1572872 | tf_op jit(solution)/shard_map/ppermute | solution.py:135
  60.8 24.0 %collective-permute-start.14 = (bf16[512,1024]{1,0:T(8,128)(2,1)S(1)}, bf16[512,1024]{1,0:T(8,128)(2,1)S(1)}, u32[]{:S(2)}, u32[]{:S(2)}) collective-permute-start(bf16[512,1024]{1,0:T(8,128)(2,1)S(1)} %shard_map.117.refs_1_), channel_id=1, source_target_pairs={{0,8},{1,9},{2,10},{3,11},{4,12},{5,13},{6,14},{7,15},{8,0},{9,1},... | collective-permute-start | bytes 3145736 | tf_op jit(solution)/shard_map/ppermute | solution.py:135
  78.8 6.0 %collective-permute-start.13 = (bf16[512,1024]{1,0:T(8,128)(2,1)S(1)}, bf16[512,1024]{1,0:T(8,128)(2,1)S(1)}, u32[]{:S(2)}, u32[]{:S(2)}) collective-permute-start(bf16[512,1024]{1,0:T(8,128)(2,1)S(1)} %shard_map.116.refs_0_), channel_id=1, source_target_pairs={{0,8},{1,9},{2,10},{3,11},{4,12},{5,13},{6,14},{7,15},{8,0},{9,1},... | collective-permute-start | bytes 3145736 | tf_op jit(solution)/shard_map/ppermute | solution.py:135
  82.6 2.7 %collective-permute-start.19 = (bf16[512,1024]{1,0:T(8,128)(2,1)S(1)}, bf16[512,1024]{1,0:T(8,128)(2,1)S(1)}, u32[]{:S(2)}, u32[]{:S(2)}) collective-permute-start(bf16[512,1024]{1,0:T(8,128)(2,1)S(1)} %collective-permute-done.12.refs_3_), channel_id=1, source_target_pairs={{0,8},{1,9},{2,10},{3,11},{4,12},{5,13},{6,14},{7,15},{8,0},{9,1},... | collective-permute-start | bytes 3145736 | tf_op jit(solution)/shard_map/ppermute | solution.py:135
  82.6 4.2 %collective-permute-start.18 = (bf16[512,1024]{1,0:T(8,128)(2,1)S(1)}, bf16[512,1024]{1,0:T(8,128)(2,1)S(1)}, u32[]{:S(2)}, u32[]{:S(2)}) collective-permute-start(bf16[512,1024]{1,0:T(8,128)(2,1)S(1)} %collective-permute-done.11.refs_2_), channel_id=1, source_target_pairs={{0,8},{1,9},{2,10},{3,11},{4,12},{5,13},{6,14},{7,15},{8,0},{9,1},... | collective-permute-start | bytes 3145736 | tf_op jit(solution)/shard_map/ppermute | solution.py:135
  83.1 3.6 %copy-start.3 = (bf16[128,2048]{1,0:T(8,128)(2,1)S(1)}, bf16[128,2048]{1,0:T(8,128)(2,1)}, u32[]{:S(2)}) copy-start(bf16[128,2048]{1,0:T(8,128)(2,1)} %refs_10_.1) | copy-start | bytes 1572868
  91.8 16.3 %collective-permute-start.20 = (bf16[128,1152]{1,0:T(8,128)(2,1)S(1)}, bf16[128,1152]{1,0:T(8,128)(2,1)S(1)}, u32[]{:S(2)}, u32[]{:S(2)}) collective-permute-start(bf16[128,1152]{1,0:T(8,128)(2,1)S(1)} %get-tuple-element.77.refs_0_.refs_2_), channel_id=1, source_target_pairs={{0,4},{1,5},{2,6},{3,7},{4,0},{5,1},{6,2},{7,3},{8,12},{9,13},{10,... | collective-permute-start | bytes 884744 | tf_op jit(solution)/shard_map/ppermute | solution.py:135
  91.9 16.2 %collective-permute-start.23 = (bf16[128,1024]{1,0:T(8,128)(2,1)S(1)}, bf16[128,1024]{1,0:T(8,128)(2,1)S(1)}, u32[]{:S(2)}, u32[]{:S(2)}) collective-permute-start(bf16[128,1024]{1,0:T(8,128)(2,1)S(1)} %get-tuple-element.80), channel_id=1, source_target_pairs={{0,16},{1,17},{2,18},{3,19},{4,20},{5,21},{6,22},{7,23},{8,24},{9,... | collective-permute-start | bytes 786440 | tf_op jit(solution)/shard_map/ppermute | solution.py:135
  93.6 14.5 %collective-permute-start.22 = (bf16[128,1024]{1,0:T(8,128)(2,1)S(1)}, bf16[128,1024]{1,0:T(8,128)(2,1)S(1)}, u32[]{:S(2)}, u32[]{:S(2)}) collective-permute-start(bf16[128,1024]{1,0:T(8,128)(2,1)S(1)} %get-tuple-element.83.refs_0_), channel_id=1, source_target_pairs={{0,16},{1,17},{2,18},{3,19},{4,20},{5,21},{6,22},{7,23},{8,24},{9,... | collective-permute-start | bytes 786440 | tf_op jit(solution)/shard_map/ppermute | solution.py:135
  94.0 17.7 %collective-permute-start.24 = (bf16[128,1024]{1,0:T(8,128)(2,1)S(1)}, bf16[128,1024]{1,0:T(8,128)(2,1)S(1)}, u32[]{:S(2)}, u32[]{:S(2)}) collective-permute-start(bf16[128,1024]{1,0:T(8,128)(2,1)S(1)} %get-tuple-element.85.refs_0_), channel_id=1, source_target_pairs={{0,1},{1,0},{2,3},{3,2},{4,5},{5,4},{6,7},{7,6},{8,9},{9,8},{10,11... | collective-permute-start | bytes 786440 | tf_op jit(solution)/shard_map/ppermute | solution.py:135
  108.2 21.0 %collective-permute-start.26 = (bf16[256,1536]{1,0:T(8,128)(2,1)S(1)}, bf16[256,1536]{1,0:T(8,128)(2,1)S(1)}, u32[]{:S(2)}, u32[]{:S(2)}) collective-permute-start(bf16[256,1536]{1,0:T(8,128)(2,1)S(1)} %shard_map.123), channel_id=1, source_target_pairs={{0,1},{1,0},{2,3},{3,2},{4,5},{5,4},{6,7},{7,6},{8,9},{9,8},{10,11... | collective-permute-start | bytes 2359304 | tf_op jit(solution)/shard_map/ppermute | solution.py:135
  109.9 19.2 %collective-permute-start.21 = (bf16[256,1152]{1,0:T(8,128)(2,1)S(1)}, bf16[256,1152]{1,0:T(8,128)(2,1)S(1)}, u32[]{:S(2)}, u32[]{:S(2)}) collective-permute-start(bf16[256,1152]{1,0:T(8,128)(2,1)S(1)} %shard_map.121), channel_id=1, source_target_pairs={{0,2},{1,3},{2,0},{3,1},{4,6},{5,7},{6,4},{7,5},{8,10},{9,11},{10,... | collective-permute-start | bytes 1769480 | tf_op jit(solution)/shard_map/ppermute | solution.py:135
  111.7 16.3 %collective-permute-start.27 = (bf16[256,1024]{1,0:T(8,128)(2,1)S(1)}, bf16[256,1024]{1,0:T(8,128)(2,1)S(1)}, u32[]{:S(2)}, u32[]{:S(2)}) collective-permute-start(bf16[256,1024]{1,0:T(8,128)(2,1)S(1)} %shard_map.124.refs_1_), channel_id=1, source_target_pairs={{0,16},{1,17},{2,18},{3,19},{4,20},{5,21},{6,22},{7,23},{8,24},{9,... | collective-permute-start | bytes 1572872 | tf_op jit(solution)/shard_map/ppermute | solution.py:135
  113.3 14.8 %collective-permute-start.25 = (bf16[128,896]{1,0:T(8,128)(2,1)S(1)}, bf16[128,896]{1,0:T(8,128)(2,1)S(1)}, u32[]{:S(2)}, u32[]{:S(2)}) collective-permute-start(bf16[128,896]{1,0:T(8,128)(2,1)S(1)} %get-tuple-element.82.refs_0_.refs_2_), channel_id=1, source_target_pairs={{0,4},{1,5},{2,6},{3,7},{4,0},{5,1},{6,2},{7,3},{8,12},{9,13},{10,... | collective-permute-start | bytes 688136 | tf_op jit(solution)/shard_map/ppermute | solution.py:135
  130.0 2.9 %collective-permute-start.28 = (bf16[512,1152]{1,0:T(8,128)(2,1)S(1)}, bf16[512,1152]{1,0:T(8,128)(2,1)S(1)}, u32[]{:S(2)}, u32[]{:S(2)}) collective-permute-start(bf16[512,1152]{1,0:T(8,128)(2,1)S(1)} %shard_map.125), channel_id=1, source_target_pairs={{0,8},{1,9},{2,10},{3,11},{4,12},{5,13},{6,14},{7,15},{8,0},{9,1},... | collective-permute-start | bytes 3538952 | tf_op jit(solution)/shard_map/ppermute | solution.py:135
  131.5 5.9 %collective-permute-start.29 = (bf16[256,2176]{1,0:T(8,128)(2,1)S(1)}, bf16[256,2176]{1,0:T(8,128)(2,1)S(1)}, u32[]{:S(2)}, u32[]{:S(2)}) collective-permute-start(bf16[256,2176]{1,0:T(8,128)(2,1)S(1)} %shard_map.128), channel_id=1, source_target_pairs={{0,8},{1,9},{2,10},{3,11},{4,12},{5,13},{6,14},{7,15},{8,0},{9,1},... | collective-permute-start | bytes 3342344 | tf_op jit(solution)/shard_map/ppermute | solution.py:135
  132.1 18.7 %collective-permute-start.33 = (bf16[256,896]{1,0:T(8,128)(2,1)S(1)}, bf16[256,896]{1,0:T(8,128)(2,1)S(1)}, u32[]{:S(2)}, u32[]{:S(2)}) collective-permute-start(bf16[256,896]{1,0:T(8,128)(2,1)S(1)} %shard_map.130), channel_id=1, source_target_pairs={{0,2},{1,3},{2,0},{3,1},{4,6},{5,7},{6,4},{7,5},{8,10},{9,11},{10,... | collective-permute-start | bytes 1376264 | tf_op jit(solution)/shard_map/ppermute | solution.py:135
  133.8 16.9 %collective-permute-start.30 = (bf16[128,1152]{1,0:T(8,128)(2,1)S(1)}, bf16[128,1152]{1,0:T(8,128)(2,1)S(1)}, u32[]{:S(2)}, u32[]{:S(2)}) collective-permute-start(bf16[128,1152]{1,0:T(8,128)(2,1)S(1)} %get-tuple-element.90), channel_id=1, source_target_pairs={{0,16},{1,17},{2,18},{3,19},{4,20},{5,21},{6,22},{7,23},{8,24},{9,... | collective-permute-start | bytes 884744 | tf_op jit(solution)/shard_map/ppermute | solution.py:135
  135.4 15.3 %collective-permute-start.31 = (bf16[128,1152]{1,0:T(8,128)(2,1)S(1)}, bf16[128,1152]{1,0:T(8,128)(2,1)S(1)}, u32[]{:S(2)}, u32[]{:S(2)}) collective-permute-start(bf16[128,1152]{1,0:T(8,128)(2,1)S(1)} %get-tuple-element.91), channel_id=1, source_target_pairs={{0,1},{1,0},{2,3},{3,2},{4,5},{5,4},{6,7},{7,6},{8,9},{9,8},{10,11... | collective-permute-start | bytes 884744 | tf_op jit(solution)/shard_map/ppermute | solution.py:135
  135.9 14.9 %collective-permute-start.32 = (bf16[128,1152]{1,0:T(8,128)(2,1)S(1)}, bf16[128,1152]{1,0:T(8,128)(2,1)S(1)}, u32[]{:S(2)}, u32[]{:S(2)}) collective-permute-start(bf16[128,1152]{1,0:T(8,128)(2,1)S(1)} %get-tuple-element.92), channel_id=1, source_target_pairs={{0,17},{1,16},{2,19},{3,18},{4,21},{5,20},{6,23},{7,22},{8,25},{9,... | collective-permute-start | bytes 884744 | tf_op jit(solution)/shard_map/ppermute | solution.py:135
  139.3 11.2 %collective-permute-start.34 = (bf16[64,2176]{1,0:T(8,128)(2,1)S(1)}, bf16[64,2176]{1,0:T(8,128)(2,1)S(1)}, u32[]{:S(2)}, u32[]{:S(2)}) collective-permute-start(bf16[64,2176]{1,0:T(8,128)(2,1)S(1)} %get-tuple-element.88), channel_id=1, source_target_pairs={{0,2},{1,3},{2,0},{3,1},{4,6},{5,7},{6,4},{7,5},{8,10},{9,11},{10,... | collective-permute-start | bytes 835592 | tf_op jit(solution)/shard_map/ppermute | solution.py:135
  151.5 3.0 %collective-permute-start.35 = (bf16[512,896]{1,0:T(8,128)(2,1)S(1)}, bf16[512,896]{1,0:T(8,128)(2,1)S(1)}, u32[]{:S(2)}, u32[]{:S(2)}) collective-permute-start(bf16[512,896]{1,0:T(8,128)(2,1)S(1)} %shard_map.132), channel_id=1, source_target_pairs={{0,8},{1,9},{2,10},{3,11},{4,12},{5,13},{6,14},{7,15},{8,0},{9,1},... | collective-permute-start | bytes 2752520 | tf_op jit(solution)/shard_map/ppermute | solution.py:135
  151.6 15.7 %collective-permute-start.39 = (bf16[64,2304]{1,0:T(8,128)(2,1)S(1)}, bf16[64,2304]{1,0:T(8,128)(2,1)S(1)}, u32[]{:S(2)}, u32[]{:S(2)}) collective-permute-start(bf16[64,2304]{1,0:T(8,128)(2,1)S(1)} %get-tuple-element.100), channel_id=1, source_target_pairs={{0,2},{1,3},{2,0},{3,1},{4,6},{5,7},{6,4},{7,5},{8,10},{9,11},{10,... | collective-permute-start | bytes 884744 | tf_op jit(solution)/shard_map/ppermute | solution.py:135
  152.4 14.9 %collective-permute-start.40 = (bf16[64,2304]{1,0:T(8,128)(2,1)S(1)}, bf16[64,2304]{1,0:T(8,128)(2,1)S(1)}, u32[]{:S(2)}, u32[]{:S(2)}) collective-permute-start(bf16[64,2304]{1,0:T(8,128)(2,1)S(1)} %shard_map.131), channel_id=1, source_target_pairs={{0,4},{1,5},{2,6},{3,7},{4,0},{5,1},{6,2},{7,3},{8,12},{9,13},{10,... | collective-permute-start | bytes 884744 | tf_op jit(solution)/shard_map/ppermute | solution.py:135
  155.2 13.1 %collective-permute-start.36 = (bf16[128,896]{1,0:T(8,128)(2,1)S(1)}, bf16[128,896]{1,0:T(8,128)(2,1)S(1)}, u32[]{:S(2)}, u32[]{:S(2)}) collective-permute-start(bf16[128,896]{1,0:T(8,128)(2,1)S(1)} %get-tuple-element.96), channel_id=1, source_target_pairs={{0,16},{1,17},{2,18},{3,19},{4,20},{5,21},{6,22},{7,23},{8,24},{9,... | collective-permute-start | bytes 688136 | tf_op jit(solution)/shard_map/ppermute | solution.py:135
  156.6 12.1 %collective-permute-start.37 = (bf16[128,896]{1,0:T(8,128)(2,1)S(1)}, bf16[128,896]{1,0:T(8,128)(2,1)S(1)}, u32[]{:S(2)}, u32[]{:S(2)}) collective-permute-start(bf16[128,896]{1,0:T(8,128)(2,1)S(1)} %get-tuple-element.97), channel_id=1, source_target_pairs={{0,1},{1,0},{2,3},{3,2},{4,5},{5,4},{6,7},{7,6},{8,9},{9,8},{10,11... | collective-permute-start | bytes 688136 | tf_op jit(solution)/shard_map/ppermute | solution.py:135
  157.1 11.6 %collective-permute-start.38 = (bf16[128,896]{1,0:T(8,128)(2,1)S(1)}, bf16[128,896]{1,0:T(8,128)(2,1)S(1)}, u32[]{:S(2)}, u32[]{:S(2)}) collective-permute-start(bf16[128,896]{1,0:T(8,128)(2,1)S(1)} %get-tuple-element.98), channel_id=1, source_target_pairs={{0,17},{1,16},{2,19},{3,18},{4,21},{5,20},{6,23},{7,22},{8,25},{9,... | collective-permute-start | bytes 688136 | tf_op jit(solution)/shard_map/ppermute | solution.py:135
  (2 other events, 1.3 us)

commit v6 on v5

--- a/solution.py
+++ b/solution.py
@@ -16,21 +16,21 @@
 CUTS = (0, 9, 16)
 CHUNKS = len(CUTS) - 1
 PINS = {
-    "weight_core1": ("operator",),
     "features_join": ("operator", "weight_near", "weight_last"),
     "weight_halves": ("features", "operator", "weight_near"),
     "weight_join1": ("sums",),
     "weight_join2": ("sums",),
     "weight_core2": ("sum_near", "sum_far", "sum_last"),
-    "pick": ("far0",),
-    "join_right": ("far0",),
+    "pick": ("far0", "right"),
     "far1": ("far0", "left", "rows", "right"),
     "across0": ("far1", "left2", "right2"),
-    "grad_far": ("left2",),
     "across1": ("grad_fold", "feat0"),
+    "grad_far": ("left2", "grad_fold"),
     "add": ("grad",),
+    "weight_core1": ("operator",),
+    "operator": ("weight_far",),
 }
-NEAR_PAD, FAR_PAD, LAST_PAD = 256, 256, 128
+NEAR_PAD, FAR_PAD, LAST_PAD = 256, 128, 128
 LOW = jnp.bfloat16
 F32 = jnp.float32
 

time: 170 us -> 170 us (level)
  transfers between devices with their start and end apart: 41 -> 41, of which waited for: 16 -> 17; matrix products, arithmetic and copies ran while one was open for 0% -> 0% of each run, Pallas kernels for 7% -> 7%
where the time goes in v6:
time: 170 us
  waiting for transfers between devices  97.1 us (57%)
  starting transfers between devices  47.1 us (28%)
  Pallas kernels  22.8 us (13%)
    ppermute x41, waiting for transfers between devices, send(): return lax.ppermute(value, AXES, pairs)  97.1 us
    ppermute x41, starting transfers between devices, send(): return lax.ppermute(value, AXES, pairs)  47.1 us
    pallas_call x25, Pallas kernels, call(): pl.pallas_call(kernel, out_shape=outs, in_specs=specs, out_specs=[whole]...  22.8 us
  transfers between devices with their start and end apart: 41, of which 17 were waited for; matrix products, arithmetic and copies ran while one was open for 0% of the time, Pallas kernels for 7%

profile of v6, /device:TPU:0, one launch (start us, length us, event | category | flops | bytes accessed | tf_op | source)
XLA Modules:
  0.0 169.9 jit_solution(11930932791600257577)
XLA Ops:
  1.2 2.8 %shard_map.112 = (bf16[512,256]{1,0:T(8,128)(2,1)}, bf16[512,256]{1,0:T(8,128)(2,1)}, bf16[528,256]{1,0:T(8,128)(2,1)}) custom-call(s32[4]{0:T(128)} %pad_add_fusion.place, s32[2,8]{1,0:T(2,128)} %refs_0_.1, s32[1,8]{1,0:T(1,128)} %refs_1_.1, bf16[1024,256]{1,0:T(8,128)(2,1)} %refs_2_.1, f32[8,128]{1,0:T(8,128)} %bitcast.7), custom_call_target="tpu_custom_call" | custom-call | flops 1 | bytes 1 | tf_op jit(solution)/shard_map/pallas_call | solution.py:57
  4.0 3.0 %collective-permute-start.6 = (bf16[528,256]{1,0:T(8,128)(2,1)}, bf16[528,256]{1,0:T(8,128)(2,1)S(1)}, u32[]{:S(2)}, u32[]{:S(2)}) collective-permute-start(bf16[528,256]{1,0:T(8,128)(2,1)} %get-tuple-element.55), channel_id=1, source_target_pairs={{0,1},{1,0},{2,3},{3,2},{4,5},{5,4},{6,7},{7,6},{8,9},{9,8},{10,11... | collective-permute-start | bytes 811016 | tf_op jit(solution)/shard_map/ppermute | solution.py:135
  7.1 2.6 %collective-permute-start = (bf16[64,2048]{1,0:T(8,128)(2,1)}, bf16[64,2048]{1,0:T(8,128)(2,1)S(1)}, u32[]{:S(2)}, u32[]{:S(2)}) collective-permute-start(bf16[64,2048]{1,0:T(8,128)(2,1)} %weight.1), channel_id=1, source_target_pairs={{0,4},{1,5},{2,6},{3,7},{4,0},{5,1},{6,2},{7,3},{8,12},{9,13},{10,... | collective-permute-start | bytes 786440 | tf_op jit(solution)/shard_map/ppermute | solution.py:135
  9.7 1.5 collective-permute-start.3
  11.7 1.5 collective-permute-start.5
  13.2 8.4 %collective-permute-done.far = bf16[64,2048]{1,0:T(8,128)(2,1)S(1)} collective-permute-done((bf16[64,2048]{1,0:T(8,128)(2,1)}, bf16[64,2048]{1,0:T(8,128)(2,1)S(1)}, u32[]{:S(2)}, u32[]{:S(2)}) %collective-permute-start) | collective-permute-done | bytes 262176 | tf_op jit(solution)/shard_map/ppermute | solution.py:135
  22.4 1.2 collective-permute-start.2
  25.7 5.4 %collective-permute-done.1.near = bf16[64,2048]{1,0:T(8,128)(2,1)S(1)} collective-permute-done((bf16[64,2048]{1,0:T(8,128)(2,1)}, bf16[64,2048]{1,0:T(8,128)(2,1)S(1)}, u32[]{:S(2)}, u32[]{:S(2)}) %collective-permute-start.1) | collective-permute-done | bytes 262176 | tf_op jit(solution)/shard_map/ppermute | solution.py:135
  31.0 3.6 %collective-permute-done.2.last = bf16[64,2048]{1,0:T(8,128)(2,1)S(1)} collective-permute-done((bf16[64,2048]{1,0:T(8,128)(2,1)S(1)}, bf16[64,2048]{1,0:T(8,128)(2,1)S(1)}, u32[]{:S(2)}, u32[]{:S(2)}) %collective-permute-start.2) | collective-permute-done | bytes 262176 | tf_op jit(solution)/shard_map/ppermute | solution.py:135
  34.7 1.6 collective-permute-done.4.refs_1_.refs_6_
  37.6 1.8 %collective-permute-start.10 = (bf16[256,1024]{1,0:T(8,128)(2,1)S(1)}, bf16[256,1024]{1,0:T(8,128)(2,1)S(1)}, u32[]{:S(2)}, u32[]{:S(2)}) collective-permute-start(bf16[256,1024]{1,0:T(8,128)(2,1)S(1)} %get-tuple-element.70.refs_0_), channel_id=1, source_target_pairs={{0,1},{1,0},{2,3},{3,2},{4,5},{5,4},{6,7},{7,6},{8,9},{9,8},{10,11... | collective-permute-start | bytes 1572872 | tf_op jit(solution)/shard_map/ppermute | solution.py:135
  39.4 1.5 collective-permute-start.9
  40.9 2.4 %shard_map.115 = (f32[128,2048]{1,0:T(8,128)S(1)}, f32[128,2048]{1,0:T(8,128)S(1)}, bf16[128,2048]{1,0:T(8,128)(2,1)S(1)}, bf16[128,2048]{1,0:T(8,128)(2,1)S(1)}) custom-call(bf16[512,256]{1,0:T(8,128)(2,1)S(1)} %copy-done, bf16[512,256]{1,0:T(8,128)(2,1)S(1)} %copy-done.1, bf16[512,256]{1,0:T(8,128)(2,1)S(1)} %get-tuple-element.57.refs_2_.refs_1_, ...), custom_call_target="tpu_custom_call" | custom-call | flops 1 | bytes 1 | tf_op jit(solution)/shard_map/pallas_call | solution.py:57
  43.3 1.6 collective-permute-start.16
  44.9 6.7 %collective-permute-done.10.refs_1_ = bf16[256,1024]{1,0:T(8,128)(2,1)S(1)} collective-permute-done((bf16[256,1024]{1,0:T(8,128)(2,1)S(1)}, bf16[256,1024]{1,0:T(8,128)(2,1)S(1)}, u32[]{:S(2)}, u32[]{:S(2)}) %collective-permute-start.10) | collective-permute-done | bytes 524320 | tf_op jit(solution)/shard_map/ppermute | solution.py:135
  51.6 1.8 %collective-permute-start.12 = (bf16[512,1024]{1,0:T(8,128)(2,1)S(1)}, bf16[512,1024]{1,0:T(8,128)(2,1)S(1)}, u32[]{:S(2)}, u32[]{:S(2)}) collective-permute-start(bf16[512,1024]{1,0:T(8,128)(2,1)S(1)} %shard_map.117.refs_1_), channel_id=1, source_target_pairs={{0,16},{1,17},{2,18},{3,19},{4,20},{5,21},{6,22},{7,23},{8,24},{9,... | collective-permute-start | bytes 3145736 | tf_op jit(solution)/shard_map/ppermute | solution.py:135
  53.5 1.6 collective-permute-start.11
  55.1 1.6 collective-permute-start.15
  56.7 1.0 collective-permute-done.16.got
  57.8 3.0 %collective-permute-start.17 = (bf16[128,2048]{1,0:T(8,128)(2,1)S(1)}, bf16[128,2048]{1,0:T(8,128)(2,1)S(1)}, u32[]{:S(2)}, u32[]{:S(2)}) collective-permute-start(bf16[128,2048]{1,0:T(8,128)(2,1)S(1)} %shard_map.118), channel_id=1, source_target_pairs={{0,4},{1,5},{2,6},{3,7},{4,0},{5,1},{6,2},{7,3},{8,12},{9,13},{10,... | collective-permute-start | bytes 1572872 | tf_op jit(solution)/shard_map/ppermute | solution.py:135
  60.8 18.0 %collective-permute-done.15.refs_5_ = bf16[128,2048]{1,0:T(8,128)(2,1)S(1)} collective-permute-done((bf16[128,2048]{1,0:T(8,128)(2,1)S(1)}, bf16[128,2048]{1,0:T(8,128)(2,1)S(1)}, u32[]{:S(2)}, u32[]{:S(2)}) %collective-permute-start.15) | collective-permute-done | bytes 524320 | tf_op jit(solution)/shard_map/ppermute | solution.py:135
  78.8 3.8 %collective-permute-done.17.refs_6_ = bf16[128,2048]{1,0:T(8,128)(2,1)S(1)} collective-permute-done((bf16[128,2048]{1,0:T(8,128)(2,1)S(1)}, bf16[128,2048]{1,0:T(8,128)(2,1)S(1)}, u32[]{:S(2)}, u32[]{:S(2)}) %collective-permute-start.17) | collective-permute-done | bytes 524320 | tf_op jit(solution)/shard_map/ppermute | solution.py:135
  83.1 1.7 shard_map.119
  85.2 1.5 collective-permute-done.18.refs_6_
  86.7 5.1 %shard_map.120 = (bf16[128,2048]{1,0:T(8,128)(2,1)}, bf16[128,1024]{1,0:T(8,128)(2,1)S(1)}, bf16[128,1024]{1,0:T(8,128)(2,1)S(1)}, bf16[128,1152]{1,0:T(8,128)(2,1)S(1)}, bf16[128,896]{1,0:T(8,128)(2,1)S(1)}) custom-call(s32[4]{0:T(128)S(1)} %copy-done.6, bf16[512,1024]{1,0:T(8,128)(2,1)S(1)} %shard_map.116.refs_0_, ...), custom_call_target="tpu_custom_call" | custom-call | flops 1 | bytes 1 | tf_op jit(solution)/shard_map/pallas_call | solution.py:57
  91.8 1.6 collective-permute-start.24
  93.5 1.6 collective-permute-start.23
  95.6 4.6 %collective-permute-done.24.refs_1_ = bf16[128,1024]{1,0:T(8,128)(2,1)S(1)} collective-permute-done((bf16[128,1024]{1,0:T(8,128)(2,1)S(1)}, bf16[128,1024]{1,0:T(8,128)(2,1)S(1)}, u32[]{:S(2)}, u32[]{:S(2)}) %collective-permute-start.24) | collective-permute-done | bytes 262176 | tf_op jit(solution)/shard_map/ppermute | solution.py:135
  100.2 7.9 %collective-permute-done.20.refs_1_.refs_3_ = bf16[128,1152]{1,0:T(8,128)(2,1)S(1)} collective-permute-done((bf16[128,1152]{1,0:T(8,128)(2,1)S(1)}, bf16[128,1152]{1,0:T(8,128)(2,1)S(1)}, u32[]{:S(2)}, u32[]{:S(2)}) %collective-permute-start.20) | collective-permute-done | bytes 294944 | tf_op jit(solution)/shard_map/ppermute | solution.py:135
  108.2 1.7 %collective-permute-start.26 = (bf16[256,1536]{1,0:T(8,128)(2,1)S(1)}, bf16[256,1536]{1,0:T(8,128)(2,1)S(1)}, u32[]{:S(2)}, u32[]{:S(2)}) collective-permute-start(bf16[256,1536]{1,0:T(8,128)(2,1)S(1)} %shard_map.123), channel_id=1, source_target_pairs={{0,1},{1,0},{2,3},{3,2},{4,5},{5,4},{6,7},{7,6},{8,9},{9,8},{10,11... | collective-permute-start | bytes 2359304 | tf_op jit(solution)/shard_map/ppermute | solution.py:135
  109.9 1.9 %collective-permute-start.21 = (bf16[256,1152]{1,0:T(8,128)(2,1)S(1)}, bf16[256,1152]{1,0:T(8,128)(2,1)S(1)}, u32[]{:S(2)}, u32[]{:S(2)}) collective-permute-start(bf16[256,1152]{1,0:T(8,128)(2,1)S(1)} %shard_map.121), channel_id=1, source_target_pairs={{0,2},{1,3},{2,0},{3,1},{4,6},{5,7},{6,4},{7,5},{8,10},{9,11},{10,... | collective-permute-start | bytes 1769480 | tf_op jit(solution)/shard_map/ppermute | solution.py:135
  111.9 1.6 collective-permute-start.27
  113.8 14.1 %collective-permute-done.25.refs_1_.refs_3_ = bf16[128,896]{1,0:T(8,128)(2,1)S(1)} collective-permute-done((bf16[128,896]{1,0:T(8,128)(2,1)S(1)}, bf16[128,896]{1,0:T(8,128)(2,1)S(1)}, u32[]{:S(2)}, u32[]{:S(2)}) %collective-permute-start.25) | collective-permute-done | bytes 229408 | tf_op jit(solution)/shard_map/ppermute | solution.py:135
  127.9 1.3 collective-permute-done.21.refs_4_
  130.2 1.3 shard_map.128
  132.9 0.9 shard_map.126
  133.8 1.6 collective-permute-start.30
  135.4 1.1 collective-permute-start.31
  136.5 0.9 collective-permute-start.32
  137.4 1.9 %shard_map.129 = (f32[64,2176]{1,0:T(8,128)S(1)}, f32[64,2176]{1,0:T(8,128)S(1)}, bf16[64,2304]{1,0:T(8,128)(2,1)S(1)}, bf16[64,2176]{1,0:T(8,128)(2,1)S(1)}) custom-call(s32[4]{0:T(128)S(1)} %copy-done.6, bf16[256,1536]{1,0:T(8,128)(2,1)S(1)} %shard_map.127.refs_0_, bf16[256,1024]{1,0:T(8,128)(2,1)S(1)} %shard_map.124.refs_1_, ...), custom_call_target="tpu_custom_call" | custom-call | flops 1 | bytes 1 | tf_op jit(solution)/shard_map/pallas_call | solution.py:57
  139.3 1.3 collective-permute-start.34
  140.6 9.9 %collective-permute-done.34.got = bf16[64,2176]{1,0:T(8,128)(2,1)S(1)} collective-permute-done((bf16[64,2176]{1,0:T(8,128)(2,1)S(1)}, bf16[64,2176]{1,0:T(8,128)(2,1)S(1)}, u32[]{:S(2)}, u32[]{:S(2)}) %collective-permute-start.34) | collective-permute-done | bytes 278560 | tf_op jit(solution)/shard_map/ppermute | solution.py:135
  152.4 2.0 %collective-permute-start.40 = (bf16[64,2176]{1,0:T(8,128)(2,1)S(1)}, bf16[64,2176]{1,0:T(8,128)(2,1)S(1)}, u32[]{:S(2)}, u32[]{:S(2)}) collective-permute-start(bf16[64,2176]{1,0:T(8,128)(2,1)S(1)} %shard_map.131), channel_id=1, source_target_pairs={{0,4},{1,5},{2,6},{3,7},{4,0},{5,1},{6,2},{7,3},{8,12},{9,13},{10,... | collective-permute-start | bytes 835592 | tf_op jit(solution)/shard_map/ppermute | solution.py:135
  155.2 1.3 collective-permute-start.36
  156.5 1.5 collective-permute-start.37
  158.7 8.2 %collective-permute-done.39.refs_0_ = bf16[64,2304]{1,0:T(8,128)(2,1)S(1)} collective-permute-done((bf16[64,2304]{1,0:T(8,128)(2,1)S(1)}, bf16[64,2304]{1,0:T(8,128)(2,1)S(1)}, u32[]{:S(2)}, u32[]{:S(2)}) %collective-permute-start.39) | collective-permute-done | bytes 294944 | tf_op jit(solution)/shard_map/ppermute | solution.py:135
  167.0 1.0 shard_map.135
  168.7 1.2 shard_map.134
  (78 shorter events, 13.8 us)
Async XLA Ops:
  4.0 18.3 %collective-permute-start.6 = (bf16[528,256]{1,0:T(8,128)(2,1)}, bf16[528,256]{1,0:T(8,128)(2,1)S(1)}, u32[]{:S(2)}, u32[]{:S(2)}) collective-permute-start(bf16[528,256]{1,0:T(8,128)(2,1)} %get-tuple-element.55), channel_id=1, source_target_pairs={{0,1},{1,0},{2,3},{3,2},{4,5},{5,4},{6,7},{7,6},{8,9},{9,8},{10,11... | collective-permute-start | bytes 811016 | tf_op jit(solution)/shard_map/ppermute | solution.py:135
  7.1 14.5 %collective-permute-start = (bf16[64,2048]{1,0:T(8,128)(2,1)}, bf16[64,2048]{1,0:T(8,128)(2,1)S(1)}, u32[]{:S(2)}, u32[]{:S(2)}) collective-permute-start(bf16[64,2048]{1,0:T(8,128)(2,1)} %weight.1), channel_id=1, source_target_pairs={{0,4},{1,5},{2,6},{3,7},{4,0},{5,1},{6,2},{7,3},{8,12},{9,13},{10,... | collective-permute-start | bytes 786440 | tf_op jit(solution)/shard_map/ppermute | solution.py:135
  9.7 25.0 %collective-permute-start.3 = (bf16[128,2048]{1,0:T(8,128)(2,1)}, bf16[128,2048]{1,0:T(8,128)(2,1)S(1)}, u32[]{:S(2)}, u32[]{:S(2)}) collective-permute-start(bf16[128,2048]{1,0:T(8,128)(2,1)} %refs_4_.1), channel_id=1, source_target_pairs={{0,16},{1,17},{2,18},{3,19},{4,20},{5,21},{6,22},{7,23},{8,24},{9,... | collective-permute-start | bytes 1572872 | tf_op jit(solution)/shard_map/ppermute | solution.py:135
  11.2 25.1 %collective-permute-start.4 = (bf16[128,2048]{1,0:T(8,128)(2,1)}, bf16[128,2048]{1,0:T(8,128)(2,1)S(1)}, u32[]{:S(2)}, u32[]{:S(2)}) collective-permute-start(bf16[128,2048]{1,0:T(8,128)(2,1)} %refs_4_.1), channel_id=1, source_target_pairs={{0,1},{1,0},{2,3},{3,2},{4,5},{5,4},{6,7},{7,6},{8,9},{9,8},{10,11... | collective-permute-start | bytes 1572872 | tf_op jit(solution)/shard_map/ppermute | solution.py:135
  11.7 24.6 %collective-permute-start.5 = (bf16[128,2048]{1,0:T(8,128)(2,1)}, bf16[128,2048]{1,0:T(8,128)(2,1)S(1)}, u32[]{:S(2)}, u32[]{:S(2)}) collective-permute-start(bf16[128,2048]{1,0:T(8,128)(2,1)} %refs_4_.1), channel_id=1, source_target_pairs={{0,17},{1,16},{2,19},{3,18},{4,21},{5,20},{6,23},{7,22},{8,25},{9,... | collective-permute-start | bytes 1572872 | tf_op jit(solution)/shard_map/ppermute | solution.py:135
  21.6 9.5 %collective-permute-start.1 = (bf16[64,2048]{1,0:T(8,128)(2,1)}, bf16[64,2048]{1,0:T(8,128)(2,1)S(1)}, u32[]{:S(2)}, u32[]{:S(2)}) collective-permute-start(bf16[64,2048]{1,0:T(8,128)(2,1)} %weight.1), channel_id=1, source_target_pairs={{0,2},{1,3},{2,0},{3,1},{4,6},{5,7},{6,4},{7,5},{8,10},{9,11},{10,... | collective-permute-start | bytes 786440 | tf_op jit(solution)/shard_map/ppermute | solution.py:135
  22.4 12.3 %collective-permute-start.2 = (bf16[64,2048]{1,0:T(8,128)(2,1)S(1)}, bf16[64,2048]{1,0:T(8,128)(2,1)S(1)}, u32[]{:S(2)}, u32[]{:S(2)}) collective-permute-start(bf16[64,2048]{1,0:T(8,128)(2,1)S(1)} %collective-permute-done.far), channel_id=1, source_target_pairs={{0,2},{1,3},{2,0},{3,1},{4,6},{5,7},{6,4},{7,5},{8,10},{9,11},{10,... | collective-permute-start | bytes 786440 | tf_op jit(solution)/shard_map/ppermute | solution.py:135
  34.7 1.8 %copy-start.2 = (bf16[128,2048]{1,0:T(8,128)(2,1)S(1)}, bf16[128,2048]{1,0:T(8,128)(2,1)}, u32[]{:S(2)}) copy-start(bf16[128,2048]{1,0:T(8,128)(2,1)} %refs_4_.1) | copy-start | bytes 1572868
  34.7 2.3 %copy-start.4 = (bf16[64,2048]{1,0:T(8,128)(2,1)S(1)}, bf16[64,2048]{1,0:T(8,128)(2,1)}, u32[]{:S(2)}) copy-start(bf16[64,2048]{1,0:T(8,128)(2,1)} %weight.1) | copy-start | bytes 786436
  34.7 2.3 %copy-start.6 = (s32[4]{0:T(128)S(1)}, s32[4]{0:T(128)}, u32[]{:S(2)}) copy-start(s32[4]{0:T(128)} %pad_add_fusion.place) | copy-start | bytes 52
  36.4 4.5 %copy-start = (bf16[512,256]{1,0:T(8,128)(2,1)S(1)}, bf16[512,256]{1,0:T(8,128)(2,1)}, u32[]{:S(2)}) copy-start(bf16[512,256]{1,0:T(8,128)(2,1)} %get-tuple-element.60.refs_0_) | copy-start | bytes 786436
  36.4 4.5 %copy-start.1 = (bf16[512,256]{1,0:T(8,128)(2,1)S(1)}, bf16[512,256]{1,0:T(8,128)(2,1)}, u32[]{:S(2)}) copy-start(bf16[512,256]{1,0:T(8,128)(2,1)} %get-tuple-element.61.refs_1_.refs_0_) | copy-start | bytes 786436
  36.4 4.5 %collective-permute-start.8 = (bf16[384,2048]{1,0:T(8,128)(2,1)S(1)}, bf16[384,2048]{1,0:T(8,128)(2,1)S(1)}, u32[]{:S(2)}, u32[]{:S(2)}) collective-permute-start(bf16[384,2048]{1,0:T(8,128)(2,1)S(1)} %shard_map.114), channel_id=1, source_target_pairs={{0,8},{1,9},{2,10},{3,11},{4,12},{5,13},{6,14},{7,15},{8,0},{9,1},... | collective-permute-start | bytes 4718600 | tf_op jit(solution)/shard_map/ppermute | solution.py:135
  36.5 4.4 %collective-permute-start.7 = (bf16[128,2048]{1,0:T(8,128)(2,1)S(1)}, bf16[128,2048]{1,0:T(8,128)(2,1)S(1)}, u32[]{:S(2)}, u32[]{:S(2)}) collective-permute-start(bf16[128,2048]{1,0:T(8,128)(2,1)S(1)} %copy-done.2), channel_id=1, source_target_pairs={{0,8},{1,9},{2,10},{3,11},{4,12},{5,13},{6,14},{7,15},{8,0},{9,1},... | collective-permute-start | bytes 1572872 | tf_op jit(solution)/shard_map/ppermute | solution.py:135
  37.6 14.0 %collective-permute-start.10 = (bf16[256,1024]{1,0:T(8,128)(2,1)S(1)}, bf16[256,1024]{1,0:T(8,128)(2,1)S(1)}, u32[]{:S(2)}, u32[]{:S(2)}) collective-permute-start(bf16[256,1024]{1,0:T(8,128)(2,1)S(1)} %get-tuple-element.70.refs_0_), channel_id=1, source_target_pairs={{0,1},{1,0},{2,3},{3,2},{4,5},{5,4},{6,7},{7,6},{8,9},{9,8},{10,11... | collective-permute-start | bytes 1572872 | tf_op jit(solution)/shard_map/ppermute | solution.py:135
  39.4 14.0 %collective-permute-start.9 = (bf16[256,1024]{1,0:T(8,128)(2,1)S(1)}, bf16[256,1024]{1,0:T(8,128)(2,1)S(1)}, u32[]{:S(2)}, u32[]{:S(2)}) collective-permute-start(bf16[256,1024]{1,0:T(8,128)(2,1)S(1)} %get-tuple-element.67.refs_0_), channel_id=1, source_target_pairs={{0,16},{1,17},{2,18},{3,19},{4,20},{5,21},{6,22},{7,23},{8,24},{9,... | collective-permute-start | bytes 1572872 | tf_op jit(solution)/shard_map/ppermute | solution.py:135
  43.3 14.4 %collective-permute-start.16 = (bf16[128,2048]{1,0:T(8,128)(2,1)S(1)}, bf16[128,2048]{1,0:T(8,128)(2,1)S(1)}, u32[]{:S(2)}, u32[]{:S(2)}) collective-permute-start(bf16[128,2048]{1,0:T(8,128)(2,1)S(1)} %get-tuple-element.66), channel_id=1, source_target_pairs={{0,2},{1,3},{2,0},{3,1},{4,6},{5,7},{6,4},{7,5},{8,10},{9,11},{10,... | collective-permute-start | bytes 1572872 | tf_op jit(solution)/shard_map/ppermute | solution.py:135
  51.6 27.2 %collective-permute-start.12 = (bf16[512,1024]{1,0:T(8,128)(2,1)S(1)}, bf16[512,1024]{1,0:T(8,128)(2,1)S(1)}, u32[]{:S(2)}, u32[]{:S(2)}) collective-permute-start(bf16[512,1024]{1,0:T(8,128)(2,1)S(1)} %shard_map.117.refs_1_), channel_id=1, source_target_pairs={{0,16},{1,17},{2,18},{3,19},{4,20},{5,21},{6,22},{7,23},{8,24},{9,... | collective-permute-start | bytes 3145736 | tf_op jit(solution)/shard_map/ppermute | solution.py:135
  53.5 29.6 %copy-start.8 = (f32[2048]{0:T(1024)S(1)}, f32[2048]{0:T(1024)}, u32[]{:S(2)}) copy-start(f32[2048]{0:T(1024)} %param.14) | copy-start | bytes 24580
  53.5 29.1 %collective-permute-start.11 = (bf16[512,1024]{1,0:T(8,128)(2,1)S(1)}, bf16[512,1024]{1,0:T(8,128)(2,1)S(1)}, u32[]{:S(2)}, u32[]{:S(2)}) collective-permute-start(bf16[512,1024]{1,0:T(8,128)(2,1)S(1)} %shard_map.116.refs_0_), channel_id=1, source_target_pairs={{0,1},{1,0},{2,3},{3,2},{4,5},{5,4},{6,7},{7,6},{8,9},{9,8},{10,11... | collective-permute-start | bytes 3145736 | tf_op jit(solution)/shard_map/ppermute | solution.py:135
  55.1 23.7 %collective-permute-start.15 = (bf16[128,2048]{1,0:T(8,128)(2,1)S(1)}, bf16[128,2048]{1,0:T(8,128)(2,1)S(1)}, u32[]{:S(2)}, u32[]{:S(2)}) collective-permute-start(bf16[128,2048]{1,0:T(8,128)(2,1)S(1)} %get-tuple-element.65), channel_id=1, source_target_pairs={{0,2},{1,3},{2,0},{3,1},{4,6},{5,7},{6,4},{7,5},{8,10},{9,11},{10,... | collective-permute-start | bytes 1572872 | tf_op jit(solution)/shard_map/ppermute | solution.py:135
  57.8 24.8 %collective-permute-start.17 = (bf16[128,2048]{1,0:T(8,128)(2,1)S(1)}, bf16[128,2048]{1,0:T(8,128)(2,1)S(1)}, u32[]{:S(2)}, u32[]{:S(2)}) collective-permute-start(bf16[128,2048]{1,0:T(8,128)(2,1)S(1)} %shard_map.118), channel_id=1, source_target_pairs={{0,4},{1,5},{2,6},{3,7},{4,0},{5,1},{6,2},{7,3},{8,12},{9,13},{10,... | collective-permute-start | bytes 1572872 | tf_op jit(solution)/shard_map/ppermute | solution.py:135
  60.8 24.0 %collective-permute-start.14 = (bf16[512,1024]{1,0:T(8,128)(2,1)S(1)}, bf16[512,1024]{1,0:T(8,128)(2,1)S(1)}, u32[]{:S(2)}, u32[]{:S(2)}) collective-permute-start(bf16[512,1024]{1,0:T(8,128)(2,1)S(1)} %shard_map.117.refs_1_), channel_id=1, source_target_pairs={{0,8},{1,9},{2,10},{3,11},{4,12},{5,13},{6,14},{7,15},{8,0},{9,1},... | collective-permute-start | bytes 3145736 | tf_op jit(solution)/shard_map/ppermute | solution.py:135
  78.8 6.0 %collective-permute-start.13 = (bf16[512,1024]{1,0:T(8,128)(2,1)S(1)}, bf16[512,1024]{1,0:T(8,128)(2,1)S(1)}, u32[]{:S(2)}, u32[]{:S(2)}) collective-permute-start(bf16[512,1024]{1,0:T(8,128)(2,1)S(1)} %shard_map.116.refs_0_), channel_id=1, source_target_pairs={{0,8},{1,9},{2,10},{3,11},{4,12},{5,13},{6,14},{7,15},{8,0},{9,1},... | collective-permute-start | bytes 3145736 | tf_op jit(solution)/shard_map/ppermute | solution.py:135
  82.6 2.7 %collective-permute-start.19 = (bf16[512,1024]{1,0:T(8,128)(2,1)S(1)}, bf16[512,1024]{1,0:T(8,128)(2,1)S(1)}, u32[]{:S(2)}, u32[]{:S(2)}) collective-permute-start(bf16[512,1024]{1,0:T(8,128)(2,1)S(1)} %collective-permute-done.12.refs_3_), channel_id=1, source_target_pairs={{0,8},{1,9},{2,10},{3,11},{4,12},{5,13},{6,14},{7,15},{8,0},{9,1},... | collective-permute-start | bytes 3145736 | tf_op jit(solution)/shard_map/ppermute | solution.py:135
  82.6 4.2 %collective-permute-start.18 = (bf16[512,1024]{1,0:T(8,128)(2,1)S(1)}, bf16[512,1024]{1,0:T(8,128)(2,1)S(1)}, u32[]{:S(2)}, u32[]{:S(2)}) collective-permute-start(bf16[512,1024]{1,0:T(8,128)(2,1)S(1)} %collective-permute-done.11.refs_2_), channel_id=1, source_target_pairs={{0,8},{1,9},{2,10},{3,11},{4,12},{5,13},{6,14},{7,15},{8,0},{9,1},... | collective-permute-start | bytes 3145736 | tf_op jit(solution)/shard_map/ppermute | solution.py:135
  83.1 3.6 %copy-start.3 = (bf16[128,2048]{1,0:T(8,128)(2,1)S(1)}, bf16[128,2048]{1,0:T(8,128)(2,1)}, u32[]{:S(2)}) copy-start(bf16[128,2048]{1,0:T(8,128)(2,1)} %refs_10_.1) | copy-start | bytes 1572868
  91.8 16.3 %collective-permute-start.20 = (bf16[128,1152]{1,0:T(8,128)(2,1)S(1)}, bf16[128,1152]{1,0:T(8,128)(2,1)S(1)}, u32[]{:S(2)}, u32[]{:S(2)}) collective-permute-start(bf16[128,1152]{1,0:T(8,128)(2,1)S(1)} %get-tuple-element.78.refs_0_.refs_2_), channel_id=1, source_target_pairs={{0,4},{1,5},{2,6},{3,7},{4,0},{5,1},{6,2},{7,3},{8,12},{9,13},{10,... | collective-permute-start | bytes 884744 | tf_op jit(solution)/shard_map/ppermute | solution.py:135
  91.8 8.3 %collective-permute-start.24 = (bf16[128,1024]{1,0:T(8,128)(2,1)S(1)}, bf16[128,1024]{1,0:T(8,128)(2,1)S(1)}, u32[]{:S(2)}, u32[]{:S(2)}) collective-permute-start(bf16[128,1024]{1,0:T(8,128)(2,1)S(1)} %get-tuple-element.82.refs_0_), channel_id=1, source_target_pairs={{0,1},{1,0},{2,3},{3,2},{4,5},{5,4},{6,7},{7,6},{8,9},{9,8},{10,11... | collective-permute-start | bytes 786440 | tf_op jit(solution)/shard_map/ppermute | solution.py:135
  93.5 14.6 %collective-permute-start.23 = (bf16[128,1024]{1,0:T(8,128)(2,1)S(1)}, bf16[128,1024]{1,0:T(8,128)(2,1)S(1)}, u32[]{:S(2)}, u32[]{:S(2)}) collective-permute-start(bf16[128,1024]{1,0:T(8,128)(2,1)S(1)} %get-tuple-element.81), channel_id=1, source_target_pairs={{0,16},{1,17},{2,18},{3,19},{4,20},{5,21},{6,22},{7,23},{8,24},{9,... | collective-permute-start | bytes 786440 | tf_op jit(solution)/shard_map/ppermute | solution.py:135
  95.1 13.0 %collective-permute-start.22 = (bf16[128,1024]{1,0:T(8,128)(2,1)S(1)}, bf16[128,1024]{1,0:T(8,128)(2,1)S(1)}, u32[]{:S(2)}, u32[]{:S(2)}) collective-permute-start(bf16[128,1024]{1,0:T(8,128)(2,1)S(1)} %get-tuple-element.84.refs_0_), channel_id=1, source_target_pairs={{0,16},{1,17},{2,18},{3,19},{4,20},{5,21},{6,22},{7,23},{8,24},{9,... | collective-permute-start | bytes 786440 | tf_op jit(solution)/shard_map/ppermute | solution.py:135
  108.2 21.0 %collective-permute-start.26 = (bf16[256,1536]{1,0:T(8,128)(2,1)S(1)}, bf16[256,1536]{1,0:T(8,128)(2,1)S(1)}, u32[]{:S(2)}, u32[]{:S(2)}) collective-permute-start(bf16[256,1536]{1,0:T(8,128)(2,1)S(1)} %shard_map.123), channel_id=1, source_target_pairs={{0,1},{1,0},{2,3},{3,2},{4,5},{5,4},{6,7},{7,6},{8,9},{9,8},{10,11... | collective-permute-start | bytes 2359304 | tf_op jit(solution)/shard_map/ppermute | solution.py:135
  109.9 19.2 %collective-permute-start.21 = (bf16[256,1152]{1,0:T(8,128)(2,1)S(1)}, bf16[256,1152]{1,0:T(8,128)(2,1)S(1)}, u32[]{:S(2)}, u32[]{:S(2)}) collective-permute-start(bf16[256,1152]{1,0:T(8,128)(2,1)S(1)} %shard_map.121), channel_id=1, source_target_pairs={{0,2},{1,3},{2,0},{3,1},{4,6},{5,7},{6,4},{7,5},{8,10},{9,11},{10,... | collective-permute-start | bytes 1769480 | tf_op jit(solution)/shard_map/ppermute | solution.py:135
  111.9 16.0 %collective-permute-start.27 = (bf16[256,1024]{1,0:T(8,128)(2,1)S(1)}, bf16[256,1024]{1,0:T(8,128)(2,1)S(1)}, u32[]{:S(2)}, u32[]{:S(2)}) collective-permute-start(bf16[256,1024]{1,0:T(8,128)(2,1)S(1)} %shard_map.124.refs_1_), channel_id=1, source_target_pairs={{0,16},{1,17},{2,18},{3,19},{4,20},{5,21},{6,22},{7,23},{8,24},{9,... | collective-permute-start | bytes 1572872 | tf_op jit(solution)/shard_map/ppermute | solution.py:135
  113.5 14.4 %collective-permute-start.25 = (bf16[128,896]{1,0:T(8,128)(2,1)S(1)}, bf16[128,896]{1,0:T(8,128)(2,1)S(1)}, u32[]{:S(2)}, u32[]{:S(2)}) collective-permute-start(bf16[128,896]{1,0:T(8,128)(2,1)S(1)} %get-tuple-element.83.refs_0_.refs_2_), channel_id=1, source_target_pairs={{0,4},{1,5},{2,6},{3,7},{4,0},{5,1},{6,2},{7,3},{8,12},{9,13},{10,... | collective-permute-start | bytes 688136 | tf_op jit(solution)/shard_map/ppermute | solution.py:135
  130.0 2.9 %collective-permute-start.28 = (bf16[512,1152]{1,0:T(8,128)(2,1)S(1)}, bf16[512,1152]{1,0:T(8,128)(2,1)S(1)}, u32[]{:S(2)}, u32[]{:S(2)}) collective-permute-start(bf16[512,1152]{1,0:T(8,128)(2,1)S(1)} %shard_map.125), channel_id=1, source_target_pairs={{0,8},{1,9},{2,10},{3,11},{4,12},{5,13},{6,14},{7,15},{8,0},{9,1},... | collective-permute-start | bytes 3538952 | tf_op jit(solution)/shard_map/ppermute | solution.py:135
  131.5 5.9 %collective-permute-start.29 = (bf16[256,2176]{1,0:T(8,128)(2,1)S(1)}, bf16[256,2176]{1,0:T(8,128)(2,1)S(1)}, u32[]{:S(2)}, u32[]{:S(2)}) collective-permute-start(bf16[256,2176]{1,0:T(8,128)(2,1)S(1)} %shard_map.128), channel_id=1, source_target_pairs={{0,8},{1,9},{2,10},{3,11},{4,12},{5,13},{6,14},{7,15},{8,0},{9,1},... | collective-permute-start | bytes 3342344 | tf_op jit(solution)/shard_map/ppermute | solution.py:135
  132.1 18.7 %collective-permute-start.33 = (bf16[256,896]{1,0:T(8,128)(2,1)S(1)}, bf16[256,896]{1,0:T(8,128)(2,1)S(1)}, u32[]{:S(2)}, u32[]{:S(2)}) collective-permute-start(bf16[256,896]{1,0:T(8,128)(2,1)S(1)} %shard_map.130), channel_id=1, source_target_pairs={{0,2},{1,3},{2,0},{3,1},{4,6},{5,7},{6,4},{7,5},{8,10},{9,11},{10,... | collective-permute-start | bytes 1376264 | tf_op jit(solution)/shard_map/ppermute | solution.py:135
  133.8 16.9 %collective-permute-start.30 = (bf16[128,1152]{1,0:T(8,128)(2,1)S(1)}, bf16[128,1152]{1,0:T(8,128)(2,1)S(1)}, u32[]{:S(2)}, u32[]{:S(2)}) collective-permute-start(bf16[128,1152]{1,0:T(8,128)(2,1)S(1)} %get-tuple-element.90), channel_id=1, source_target_pairs={{0,16},{1,17},{2,18},{3,19},{4,20},{5,21},{6,22},{7,23},{8,24},{9,... | collective-permute-start | bytes 884744 | tf_op jit(solution)/shard_map/ppermute | solution.py:135
  135.4 15.3 %collective-permute-start.31 = (bf16[128,1152]{1,0:T(8,128)(2,1)S(1)}, bf16[128,1152]{1,0:T(8,128)(2,1)S(1)}, u32[]{:S(2)}, u32[]{:S(2)}) collective-permute-start(bf16[128,1152]{1,0:T(8,128)(2,1)S(1)} %get-tuple-element.91), channel_id=1, source_target_pairs={{0,1},{1,0},{2,3},{3,2},{4,5},{5,4},{6,7},{7,6},{8,9},{9,8},{10,11... | collective-permute-start | bytes 884744 | tf_op jit(solution)/shard_map/ppermute | solution.py:135
  136.5 14.3 %collective-permute-start.32 = (bf16[128,1152]{1,0:T(8,128)(2,1)S(1)}, bf16[128,1152]{1,0:T(8,128)(2,1)S(1)}, u32[]{:S(2)}, u32[]{:S(2)}) collective-permute-start(bf16[128,1152]{1,0:T(8,128)(2,1)S(1)} %get-tuple-element.92), channel_id=1, source_target_pairs={{0,17},{1,16},{2,19},{3,18},{4,21},{5,20},{6,23},{7,22},{8,25},{9,... | collective-permute-start | bytes 884744 | tf_op jit(solution)/shard_map/ppermute | solution.py:135
  139.3 11.2 %collective-permute-start.34 = (bf16[64,2176]{1,0:T(8,128)(2,1)S(1)}, bf16[64,2176]{1,0:T(8,128)(2,1)S(1)}, u32[]{:S(2)}, u32[]{:S(2)}) collective-permute-start(bf16[64,2176]{1,0:T(8,128)(2,1)S(1)} %get-tuple-element.88), channel_id=1, source_target_pairs={{0,2},{1,3},{2,0},{3,1},{4,6},{5,7},{6,4},{7,5},{8,10},{9,11},{10,... | collective-permute-start | bytes 835592 | tf_op jit(solution)/shard_map/ppermute | solution.py:135
  151.5 2.9 %collective-permute-start.35 = (bf16[512,896]{1,0:T(8,128)(2,1)S(1)}, bf16[512,896]{1,0:T(8,128)(2,1)S(1)}, u32[]{:S(2)}, u32[]{:S(2)}) collective-permute-start(bf16[512,896]{1,0:T(8,128)(2,1)S(1)} %shard_map.132), channel_id=1, source_target_pairs={{0,8},{1,9},{2,10},{3,11},{4,12},{5,13},{6,14},{7,15},{8,0},{9,1},... | collective-permute-start | bytes 2752520 | tf_op jit(solution)/shard_map/ppermute | solution.py:135
  151.6 15.4 %collective-permute-start.39 = (bf16[64,2304]{1,0:T(8,128)(2,1)S(1)}, bf16[64,2304]{1,0:T(8,128)(2,1)S(1)}, u32[]{:S(2)}, u32[]{:S(2)}) collective-permute-start(bf16[64,2304]{1,0:T(8,128)(2,1)S(1)} %get-tuple-element.100), channel_id=1, source_target_pairs={{0,2},{1,3},{2,0},{3,1},{4,6},{5,7},{6,4},{7,5},{8,10},{9,11},{10,... | collective-permute-start | bytes 884744 | tf_op jit(solution)/shard_map/ppermute | solution.py:135
  152.4 14.5 %collective-permute-start.40 = (bf16[64,2176]{1,0:T(8,128)(2,1)S(1)}, bf16[64,2176]{1,0:T(8,128)(2,1)S(1)}, u32[]{:S(2)}, u32[]{:S(2)}) collective-permute-start(bf16[64,2176]{1,0:T(8,128)(2,1)S(1)} %shard_map.131), channel_id=1, source_target_pairs={{0,4},{1,5},{2,6},{3,7},{4,0},{5,1},{6,2},{7,3},{8,12},{9,13},{10,... | collective-permute-start | bytes 835592 | tf_op jit(solution)/shard_map/ppermute | solution.py:135
  155.2 12.9 %collective-permute-start.36 = (bf16[128,896]{1,0:T(8,128)(2,1)S(1)}, bf16[128,896]{1,0:T(8,128)(2,1)S(1)}, u32[]{:S(2)}, u32[]{:S(2)}) collective-permute-start(bf16[128,896]{1,0:T(8,128)(2,1)S(1)} %get-tuple-element.96), channel_id=1, source_target_pairs={{0,16},{1,17},{2,18},{3,19},{4,20},{5,21},{6,22},{7,23},{8,24},{9,... | collective-permute-start | bytes 688136 | tf_op jit(solution)/shard_map/ppermute | solution.py:135
  156.5 12.2 %collective-permute-start.37 = (bf16[128,896]{1,0:T(8,128)(2,1)S(1)}, bf16[128,896]{1,0:T(8,128)(2,1)S(1)}, u32[]{:S(2)}, u32[]{:S(2)}) collective-permute-start(bf16[128,896]{1,0:T(8,128)(2,1)S(1)} %get-tuple-element.97), channel_id=1, source_target_pairs={{0,1},{1,0},{2,3},{3,2},{4,5},{5,4},{6,7},{7,6},{8,9},{9,8},{10,11... | collective-permute-start | bytes 688136 | tf_op jit(solution)/shard_map/ppermute | solution.py:135
  158.0 10.7 %collective-permute-start.38 = (bf16[128,896]{1,0:T(8,128)(2,1)S(1)}, bf16[128,896]{1,0:T(8,128)(2,1)S(1)}, u32[]{:S(2)}, u32[]{:S(2)}) collective-permute-start(bf16[128,896]{1,0:T(8,128)(2,1)S(1)} %get-tuple-element.98), channel_id=1, source_target_pairs={{0,17},{1,16},{2,19},{3,18},{4,21},{5,20},{6,23},{7,22},{8,25},{9,... | collective-permute-start | bytes 688136 | tf_op jit(solution)/shard_map/ppermute | solution.py:135
  (2 other events, 1.3 us)

commit v7 on v5

--- a/solution.py
+++ b/solution.py
@@ -296,6 +296,24 @@
         k = i % per * size
         total = parts[i // per][k : k + size] + got[i * size : (i + 1) * size, :].astype(F32)
         out[...] = total.astype(out.dtype)
+
+
+def sum_kernel(first, *refs):
+    *parts, out = refs
+    total = first[...]
+    for part in parts:
+        total = total + part[...].astype(F32)
+    out[...] = total
+
+
+def last_sum_kernel(first, *refs):
+    *parts, out = refs
+    done = first.shape[1]
+    out[:, :done] = first[...]
+    total = parts[0][...]
+    for part in parts[1:]:
+        total = total + part[...].astype(F32)
+    out[:, done:] = total
 
 
 def add_up_kernel(n_keeps, *refs):
@@ -678,8 +696,9 @@
         across1 = feat_across(at, ops, "1", backs[k], fars[k], nears[k])
         feat = feat + feat_own(at, ops, "1", across1, backs[k], fars[k], nears[k])
     near = at.token("grad_near", at.send(at.gate("grad_near", to_near), flip=1))
-    feat[0] = at.gate("add", feat[0])
-    [feat_grad] = call(functools.partial(add_up_kernel, CHUNKS), [like(size, width, kind=F32)], [], *feat)
+    per = len(at.chips)
+    [done] = call(sum_kernel, [like(size, widths[0], kind=F32)], [], at.gate("add", feat[0]), *feat[1:per])
+    [feat_grad] = call(last_sum_kernel, [like(size, width, kind=F32)], [], done, *feat[per:])
     at.token("add", feat_grad)
     outs = [like(own_rows, width, kind=F32), like(1, own_rows, kind=F32)]
     weight_grad, bias_grad = call(last_fold_kernel, outs, [], at.gate("last", total), near, far)

time: 170 us -> 170 us (level)
    pallas_call x25 -> x26, Pallas kernels: 22.8 us -> 22.9 us  [call(): pl.pallas_call(kernel, out_shape=outs, in_specs=specs, out_specs=[whole]...]
where the time goes in v7:
time: 170 us
  waiting for transfers between devices  97.1 us (57%)
  starting transfers between devices  47 us (28%)
  Pallas kernels  22.9 us (13%)
    ppermute x41, waiting for transfers between devices, send(): return lax.ppermute(value, AXES, pairs)  97.1 us
    ppermute x41, starting transfers between devices, send(): return lax.ppermute(value, AXES, pairs)  47 us
    pallas_call x26, Pallas kernels, call(): pl.pallas_call(kernel, out_shape=outs, in_specs=specs, out_specs=[whole]...  22.9 us
  transfers between devices with their start and end apart: 41, of which 16 were waited for; matrix products, arithmetic and copies ran while one was open for 0% of the time, Pallas kernels for 7%

profile of v7, /device:TPU:0, one launch (start us, length us, event | category | flops | bytes accessed | tf_op | source)
XLA Modules:
  0.0 169.8 jit_solution(2343955174348443660)
XLA Ops:
  1.2 2.8 %shard_map.112 = (bf16[512,256]{1,0:T(8,128)(2,1)}, bf16[512,256]{1,0:T(8,128)(2,1)}, bf16[528,256]{1,0:T(8,128)(2,1)}) custom-call(s32[4]{0:T(128)} %pad_add_fusion.place, s32[2,8]{1,0:T(2,128)} %refs_0_.1, s32[1,8]{1,0:T(1,128)} %refs_1_.1, bf16[1024,256]{1,0:T(8,128)(2,1)} %refs_2_.1, f32[8,128]{1,0:T(8,128)} %bitcast.7), custom_call_target="tpu_custom_call" | custom-call | flops 1 | bytes 1 | tf_op jit(solution)/shard_map/pallas_call | solution.py:57
  4.0 3.0 %collective-permute-start.6 = (bf16[528,256]{1,0:T(8,128)(2,1)}, bf16[528,256]{1,0:T(8,128)(2,1)S(1)}, u32[]{:S(2)}, u32[]{:S(2)}) collective-permute-start(bf16[528,256]{1,0:T(8,128)(2,1)} %get-tuple-element.55), channel_id=1, source_target_pairs={{0,1},{1,0},{2,3},{3,2},{4,5},{5,4},{6,7},{7,6},{8,9},{9,8},{10,11... | collective-permute-start | bytes 811016 | tf_op jit(solution)/shard_map/ppermute | solution.py:135
  7.1 2.6 %collective-permute-start = (bf16[64,2048]{1,0:T(8,128)(2,1)}, bf16[64,2048]{1,0:T(8,128)(2,1)S(1)}, u32[]{:S(2)}, u32[]{:S(2)}) collective-permute-start(bf16[64,2048]{1,0:T(8,128)(2,1)} %weight.1), channel_id=1, source_target_pairs={{0,4},{1,5},{2,6},{3,7},{4,0},{5,1},{6,2},{7,3},{8,12},{9,13},{10,... | collective-permute-start | bytes 786440 | tf_op jit(solution)/shard_map/ppermute | solution.py:135
  9.7 1.5 collective-permute-start.3
  11.7 1.5 collective-permute-start.5
  13.2 8.4 %collective-permute-done.far = bf16[64,2048]{1,0:T(8,128)(2,1)S(1)} collective-permute-done((bf16[64,2048]{1,0:T(8,128)(2,1)}, bf16[64,2048]{1,0:T(8,128)(2,1)S(1)}, u32[]{:S(2)}, u32[]{:S(2)}) %collective-permute-start) | collective-permute-done | bytes 262176 | tf_op jit(solution)/shard_map/ppermute | solution.py:135
  22.4 1.2 collective-permute-start.2
  25.7 5.4 %collective-permute-done.1.near = bf16[64,2048]{1,0:T(8,128)(2,1)S(1)} collective-permute-done((bf16[64,2048]{1,0:T(8,128)(2,1)}, bf16[64,2048]{1,0:T(8,128)(2,1)S(1)}, u32[]{:S(2)}, u32[]{:S(2)}) %collective-permute-start.1) | collective-permute-done | bytes 262176 | tf_op jit(solution)/shard_map/ppermute | solution.py:135
  31.0 3.6 %collective-permute-done.2.last = bf16[64,2048]{1,0:T(8,128)(2,1)S(1)} collective-permute-done((bf16[64,2048]{1,0:T(8,128)(2,1)S(1)}, bf16[64,2048]{1,0:T(8,128)(2,1)S(1)}, u32[]{:S(2)}, u32[]{:S(2)}) %collective-permute-start.2) | collective-permute-done | bytes 262176 | tf_op jit(solution)/shard_map/ppermute | solution.py:135
  34.7 1.6 collective-permute-done.4.refs_1_.refs_6_
  37.6 1.8 %collective-permute-start.10 = (bf16[256,1024]{1,0:T(8,128)(2,1)S(1)}, bf16[256,1024]{1,0:T(8,128)(2,1)S(1)}, u32[]{:S(2)}, u32[]{:S(2)}) collective-permute-start(bf16[256,1024]{1,0:T(8,128)(2,1)S(1)} %get-tuple-element.69.refs_0_), channel_id=1, source_target_pairs={{0,1},{1,0},{2,3},{3,2},{4,5},{5,4},{6,7},{7,6},{8,9},{9,8},{10,11... | collective-permute-start | bytes 1572872 | tf_op jit(solution)/shard_map/ppermute | solution.py:135
  39.4 1.5 collective-permute-start.9
  40.9 2.4 %shard_map.115 = (f32[128,2048]{1,0:T(8,128)S(1)}, f32[128,2048]{1,0:T(8,128)S(1)}, bf16[128,2048]{1,0:T(8,128)(2,1)S(1)}, bf16[128,2048]{1,0:T(8,128)(2,1)S(1)}) custom-call(bf16[512,256]{1,0:T(8,128)(2,1)S(1)} %copy-done, bf16[512,256]{1,0:T(8,128)(2,1)S(1)} %copy-done.1, bf16[512,256]{1,0:T(8,128)(2,1)S(1)} %get-tuple-element.56.refs_2_.refs_1_, ...), custom_call_target="tpu_custom_call" | custom-call | flops 1 | bytes 1 | tf_op jit(solution)/shard_map/pallas_call | solution.py:57
  43.3 1.6 collective-permute-start.16
  44.9 6.7 %collective-permute-done.10.refs_1_ = bf16[256,1024]{1,0:T(8,128)(2,1)S(1)} collective-permute-done((bf16[256,1024]{1,0:T(8,128)(2,1)S(1)}, bf16[256,1024]{1,0:T(8,128)(2,1)S(1)}, u32[]{:S(2)}, u32[]{:S(2)}) %collective-permute-start.10) | collective-permute-done | bytes 524320 | tf_op jit(solution)/shard_map/ppermute | solution.py:135
  51.6 1.8 %collective-permute-start.12 = (bf16[512,1024]{1,0:T(8,128)(2,1)S(1)}, bf16[512,1024]{1,0:T(8,128)(2,1)S(1)}, u32[]{:S(2)}, u32[]{:S(2)}) collective-permute-start(bf16[512,1024]{1,0:T(8,128)(2,1)S(1)} %shard_map.117.refs_1_), channel_id=1, source_target_pairs={{0,16},{1,17},{2,18},{3,19},{4,20},{5,21},{6,22},{7,23},{8,24},{9,... | collective-permute-start | bytes 3145736 | tf_op jit(solution)/shard_map/ppermute | solution.py:135
  53.5 1.6 collective-permute-start.11
  55.1 1.6 collective-permute-start.15
  56.7 1.0 collective-permute-done.16.got
  57.8 3.0 %collective-permute-start.17 = (bf16[128,2048]{1,0:T(8,128)(2,1)S(1)}, bf16[128,2048]{1,0:T(8,128)(2,1)S(1)}, u32[]{:S(2)}, u32[]{:S(2)}) collective-permute-start(bf16[128,2048]{1,0:T(8,128)(2,1)S(1)} %shard_map.118), channel_id=1, source_target_pairs={{0,4},{1,5},{2,6},{3,7},{4,0},{5,1},{6,2},{7,3},{8,12},{9,13},{10,... | collective-permute-start | bytes 1572872 | tf_op jit(solution)/shard_map/ppermute | solution.py:135
  60.8 18.0 %collective-permute-done.15.refs_5_ = bf16[128,2048]{1,0:T(8,128)(2,1)S(1)} collective-permute-done((bf16[128,2048]{1,0:T(8,128)(2,1)S(1)}, bf16[128,2048]{1,0:T(8,128)(2,1)S(1)}, u32[]{:S(2)}, u32[]{:S(2)}) %collective-permute-start.15) | collective-permute-done | bytes 524320 | tf_op jit(solution)/shard_map/ppermute | solution.py:135
  78.8 3.8 %collective-permute-done.17.refs_6_ = bf16[128,2048]{1,0:T(8,128)(2,1)S(1)} collective-permute-done((bf16[128,2048]{1,0:T(8,128)(2,1)S(1)}, bf16[128,2048]{1,0:T(8,128)(2,1)S(1)}, u32[]{:S(2)}, u32[]{:S(2)}) %collective-permute-start.17) | collective-permute-done | bytes 524320 | tf_op jit(solution)/shard_map/ppermute | solution.py:135
  83.1 1.7 shard_map.119
  85.2 1.5 collective-permute-done.18.refs_6_
  86.7 5.1 %shard_map.120 = (bf16[128,2048]{1,0:T(8,128)(2,1)}, bf16[128,1024]{1,0:T(8,128)(2,1)S(1)}, bf16[128,1024]{1,0:T(8,128)(2,1)S(1)}, bf16[128,1152]{1,0:T(8,128)(2,1)S(1)}, bf16[128,896]{1,0:T(8,128)(2,1)S(1)}) custom-call(s32[4]{0:T(128)S(1)} %copy-done.6, bf16[512,1024]{1,0:T(8,128)(2,1)S(1)} %shard_map.116.refs_0_, ...), custom_call_target="tpu_custom_call" | custom-call | flops 1 | bytes 1 | tf_op jit(solution)/shard_map/pallas_call | solution.py:57
  91.9 1.7 collective-permute-start.23
  94.0 1.6 collective-permute-start.24
  95.6 12.5 %collective-permute-done.20.refs_1_.refs_3_ = bf16[128,1152]{1,0:T(8,128)(2,1)S(1)} collective-permute-done((bf16[128,1152]{1,0:T(8,128)(2,1)S(1)}, bf16[128,1152]{1,0:T(8,128)(2,1)S(1)}, u32[]{:S(2)}, u32[]{:S(2)}) %collective-permute-start.20) | collective-permute-done | bytes 294944 | tf_op jit(solution)/shard_map/ppermute | solution.py:135
  108.2 1.7 %collective-permute-start.26 = (bf16[256,1536]{1,0:T(8,128)(2,1)S(1)}, bf16[256,1536]{1,0:T(8,128)(2,1)S(1)}, u32[]{:S(2)}, u32[]{:S(2)}) collective-permute-start(bf16[256,1536]{1,0:T(8,128)(2,1)S(1)} %shard_map.123), channel_id=1, source_target_pairs={{0,1},{1,0},{2,3},{3,2},{4,5},{5,4},{6,7},{7,6},{8,9},{9,8},{10,11... | collective-permute-start | bytes 2359304 | tf_op jit(solution)/shard_map/ppermute | solution.py:135
  109.9 1.8 %collective-permute-start.21 = (bf16[256,1152]{1,0:T(8,128)(2,1)S(1)}, bf16[256,1152]{1,0:T(8,128)(2,1)S(1)}, u32[]{:S(2)}, u32[]{:S(2)}) collective-permute-start(bf16[256,1152]{1,0:T(8,128)(2,1)S(1)} %shard_map.121), channel_id=1, source_target_pairs={{0,2},{1,3},{2,0},{3,1},{4,6},{5,7},{6,4},{7,5},{8,10},{9,11},{10,... | collective-permute-start | bytes 1769480 | tf_op jit(solution)/shard_map/ppermute | solution.py:135
  111.7 1.6 collective-permute-start.27
  113.6 14.5 %collective-permute-done.25.refs_1_.refs_3_ = bf16[128,896]{1,0:T(8,128)(2,1)S(1)} collective-permute-done((bf16[128,896]{1,0:T(8,128)(2,1)S(1)}, bf16[128,896]{1,0:T(8,128)(2,1)S(1)}, u32[]{:S(2)}, u32[]{:S(2)}) %collective-permute-start.25) | collective-permute-done | bytes 229408 | tf_op jit(solution)/shard_map/ppermute | solution.py:135
  128.1 1.1 collective-permute-done.21.refs_4_
  129.1 0.9 shard_map.125
  130.2 1.3 shard_map.128
  132.9 0.9 shard_map.126
  133.8 1.6 collective-permute-start.30
  135.9 1.5 collective-permute-start.32
  137.4 1.9 %shard_map.129 = (f32[64,2176]{1,0:T(8,128)S(1)}, f32[64,2176]{1,0:T(8,128)S(1)}, bf16[64,2304]{1,0:T(8,128)(2,1)S(1)}, bf16[64,2176]{1,0:T(8,128)(2,1)S(1)}) custom-call(s32[4]{0:T(128)S(1)} %copy-done.6, bf16[256,1536]{1,0:T(8,128)(2,1)S(1)} %shard_map.127.refs_0_, bf16[256,1024]{1,0:T(8,128)(2,1)S(1)} %shard_map.124.refs_1_, ...), custom_call_target="tpu_custom_call" | custom-call | flops 1 | bytes 1 | tf_op jit(solution)/shard_map/pallas_call | solution.py:57
  139.3 1.3 collective-permute-start.34
  140.6 9.9 %collective-permute-done.34.got = bf16[64,2176]{1,0:T(8,128)(2,1)S(1)} collective-permute-done((bf16[64,2176]{1,0:T(8,128)(2,1)S(1)}, bf16[64,2176]{1,0:T(8,128)(2,1)S(1)}, u32[]{:S(2)}, u32[]{:S(2)}) %collective-permute-start.34) | collective-permute-done | bytes 278560 | tf_op jit(solution)/shard_map/ppermute | solution.py:135
  151.6 0.8 collective-permute-start.39
  152.4 2.1 %collective-permute-start.40 = (bf16[64,2304]{1,0:T(8,128)(2,1)S(1)}, bf16[64,2304]{1,0:T(8,128)(2,1)S(1)}, u32[]{:S(2)}, u32[]{:S(2)}) collective-permute-start(bf16[64,2304]{1,0:T(8,128)(2,1)S(1)} %shard_map.132), channel_id=1, source_target_pairs={{0,4},{1,5},{2,6},{3,7},{4,0},{5,1},{6,2},{7,3},{8,12},{9,13},{10,... | collective-permute-start | bytes 884744 | tf_op jit(solution)/shard_map/ppermute | solution.py:135
  155.2 1.3 collective-permute-start.36
  157.1 1.7 %collective-permute-start.38 = (bf16[128,896]{1,0:T(8,128)(2,1)S(1)}, bf16[128,896]{1,0:T(8,128)(2,1)S(1)}, u32[]{:S(2)}, u32[]{:S(2)}) collective-permute-start(bf16[128,896]{1,0:T(8,128)(2,1)S(1)} %get-tuple-element.98), channel_id=1, source_target_pairs={{0,17},{1,16},{2,19},{3,18},{4,21},{5,20},{6,23},{7,22},{8,25},{9,... | collective-permute-start | bytes 688136 | tf_op jit(solution)/shard_map/ppermute | solution.py:135
  158.9 8.4 %collective-permute-done.39.refs_0_ = bf16[64,2304]{1,0:T(8,128)(2,1)S(1)} collective-permute-done((bf16[64,2304]{1,0:T(8,128)(2,1)S(1)}, bf16[64,2304]{1,0:T(8,128)(2,1)S(1)}, u32[]{:S(2)}, u32[]{:S(2)}) %collective-permute-start.39) | collective-permute-done | bytes 294944 | tf_op jit(solution)/shard_map/ppermute | solution.py:135
  167.3 1.1 shard_map.136
  168.7 1.1 shard_map.135
  (79 shorter events, 12.0 us)
Async XLA Ops:
  4.0 18.3 %collective-permute-start.6 = (bf16[528,256]{1,0:T(8,128)(2,1)}, bf16[528,256]{1,0:T(8,128)(2,1)S(1)}, u32[]{:S(2)}, u32[]{:S(2)}) collective-permute-start(bf16[528,256]{1,0:T(8,128)(2,1)} %get-tuple-element.55), channel_id=1, source_target_pairs={{0,1},{1,0},{2,3},{3,2},{4,5},{5,4},{6,7},{7,6},{8,9},{9,8},{10,11... | collective-permute-start | bytes 811016 | tf_op jit(solution)/shard_map/ppermute | solution.py:135
  7.1 14.5 %collective-permute-start = (bf16[64,2048]{1,0:T(8,128)(2,1)}, bf16[64,2048]{1,0:T(8,128)(2,1)S(1)}, u32[]{:S(2)}, u32[]{:S(2)}) collective-permute-start(bf16[64,2048]{1,0:T(8,128)(2,1)} %weight.1), channel_id=1, source_target_pairs={{0,4},{1,5},{2,6},{3,7},{4,0},{5,1},{6,2},{7,3},{8,12},{9,13},{10,... | collective-permute-start | bytes 786440 | tf_op jit(solution)/shard_map/ppermute | solution.py:135
  9.7 21.4 %collective-permute-start.3 = (bf16[128,2048]{1,0:T(8,128)(2,1)}, bf16[128,2048]{1,0:T(8,128)(2,1)S(1)}, u32[]{:S(2)}, u32[]{:S(2)}) collective-permute-start(bf16[128,2048]{1,0:T(8,128)(2,1)} %refs_4_.1), channel_id=1, source_target_pairs={{0,16},{1,17},{2,18},{3,19},{4,20},{5,21},{6,22},{7,23},{8,24},{9,... | collective-permute-start | bytes 1572872 | tf_op jit(solution)/shard_map/ppermute | solution.py:135
  11.2 25.1 %collective-permute-start.4 = (bf16[128,2048]{1,0:T(8,128)(2,1)}, bf16[128,2048]{1,0:T(8,128)(2,1)S(1)}, u32[]{:S(2)}, u32[]{:S(2)}) collective-permute-start(bf16[128,2048]{1,0:T(8,128)(2,1)} %refs_4_.1), channel_id=1, source_target_pairs={{0,1},{1,0},{2,3},{3,2},{4,5},{5,4},{6,7},{7,6},{8,9},{9,8},{10,11... | collective-permute-start | bytes 1572872 | tf_op jit(solution)/shard_map/ppermute | solution.py:135
  11.7 24.6 %collective-permute-start.5 = (bf16[128,2048]{1,0:T(8,128)(2,1)}, bf16[128,2048]{1,0:T(8,128)(2,1)S(1)}, u32[]{:S(2)}, u32[]{:S(2)}) collective-permute-start(bf16[128,2048]{1,0:T(8,128)(2,1)} %refs_4_.1), channel_id=1, source_target_pairs={{0,17},{1,16},{2,19},{3,18},{4,21},{5,20},{6,23},{7,22},{8,25},{9,... | collective-permute-start | bytes 1572872 | tf_op jit(solution)/shard_map/ppermute | solution.py:135
  21.6 9.5 %collective-permute-start.1 = (bf16[64,2048]{1,0:T(8,128)(2,1)}, bf16[64,2048]{1,0:T(8,128)(2,1)S(1)}, u32[]{:S(2)}, u32[]{:S(2)}) collective-permute-start(bf16[64,2048]{1,0:T(8,128)(2,1)} %weight.1), channel_id=1, source_target_pairs={{0,2},{1,3},{2,0},{3,1},{4,6},{5,7},{6,4},{7,5},{8,10},{9,11},{10,... | collective-permute-start | bytes 786440 | tf_op jit(solution)/shard_map/ppermute | solution.py:135
  22.4 12.3 %collective-permute-start.2 = (bf16[64,2048]{1,0:T(8,128)(2,1)S(1)}, bf16[64,2048]{1,0:T(8,128)(2,1)S(1)}, u32[]{:S(2)}, u32[]{:S(2)}) collective-permute-start(bf16[64,2048]{1,0:T(8,128)(2,1)S(1)} %collective-permute-done.far), channel_id=1, source_target_pairs={{0,2},{1,3},{2,0},{3,1},{4,6},{5,7},{6,4},{7,5},{8,10},{9,11},{10,... | collective-permute-start | bytes 786440 | tf_op jit(solution)/shard_map/ppermute | solution.py:135
  34.7 1.8 %copy-start.2 = (bf16[128,2048]{1,0:T(8,128)(2,1)S(1)}, bf16[128,2048]{1,0:T(8,128)(2,1)}, u32[]{:S(2)}) copy-start(bf16[128,2048]{1,0:T(8,128)(2,1)} %refs_4_.1) | copy-start | bytes 1572868
  34.7 2.3 %copy-start.4 = (bf16[64,2048]{1,0:T(8,128)(2,1)S(1)}, bf16[64,2048]{1,0:T(8,128)(2,1)}, u32[]{:S(2)}) copy-start(bf16[64,2048]{1,0:T(8,128)(2,1)} %weight.1) | copy-start | bytes 786436
  34.7 2.3 %copy-start.6 = (s32[4]{0:T(128)S(1)}, s32[4]{0:T(128)}, u32[]{:S(2)}) copy-start(s32[4]{0:T(128)} %pad_add_fusion.place) | copy-start | bytes 52
  36.4 4.5 %copy-start = (bf16[512,256]{1,0:T(8,128)(2,1)S(1)}, bf16[512,256]{1,0:T(8,128)(2,1)}, u32[]{:S(2)}) copy-start(bf16[512,256]{1,0:T(8,128)(2,1)} %get-tuple-element.59.refs_0_) | copy-start | bytes 786436
  36.4 4.5 %copy-start.1 = (bf16[512,256]{1,0:T(8,128)(2,1)S(1)}, bf16[512,256]{1,0:T(8,128)(2,1)}, u32[]{:S(2)}) copy-start(bf16[512,256]{1,0:T(8,128)(2,1)} %get-tuple-element.60.refs_1_.refs_0_) | copy-start | bytes 786436
  36.4 4.5 %collective-permute-start.8 = (bf16[384,2048]{1,0:T(8,128)(2,1)S(1)}, bf16[384,2048]{1,0:T(8,128)(2,1)S(1)}, u32[]{:S(2)}, u32[]{:S(2)}) collective-permute-start(bf16[384,2048]{1,0:T(8,128)(2,1)S(1)} %shard_map.114), channel_id=1, source_target_pairs={{0,8},{1,9},{2,10},{3,11},{4,12},{5,13},{6,14},{7,15},{8,0},{9,1},... | collective-permute-start | bytes 4718600 | tf_op jit(solution)/shard_map/ppermute | solution.py:135
  36.5 4.4 %collective-permute-start.7 = (bf16[128,2048]{1,0:T(8,128)(2,1)S(1)}, bf16[128,2048]{1,0:T(8,128)(2,1)S(1)}, u32[]{:S(2)}, u32[]{:S(2)}) collective-permute-start(bf16[128,2048]{1,0:T(8,128)(2,1)S(1)} %copy-done.2), channel_id=1, source_target_pairs={{0,8},{1,9},{2,10},{3,11},{4,12},{5,13},{6,14},{7,15},{8,0},{9,1},... | collective-permute-start | bytes 1572872 | tf_op jit(solution)/shard_map/ppermute | solution.py:135
  37.6 14.0 %collective-permute-start.10 = (bf16[256,1024]{1,0:T(8,128)(2,1)S(1)}, bf16[256,1024]{1,0:T(8,128)(2,1)S(1)}, u32[]{:S(2)}, u32[]{:S(2)}) collective-permute-start(bf16[256,1024]{1,0:T(8,128)(2,1)S(1)} %get-tuple-element.69.refs_0_), channel_id=1, source_target_pairs={{0,1},{1,0},{2,3},{3,2},{4,5},{5,4},{6,7},{7,6},{8,9},{9,8},{10,11... | collective-permute-start | bytes 1572872 | tf_op jit(solution)/shard_map/ppermute | solution.py:135
  39.4 14.0 %collective-permute-start.9 = (bf16[256,1024]{1,0:T(8,128)(2,1)S(1)}, bf16[256,1024]{1,0:T(8,128)(2,1)S(1)}, u32[]{:S(2)}, u32[]{:S(2)}) collective-permute-start(bf16[256,1024]{1,0:T(8,128)(2,1)S(1)} %get-tuple-element.66.refs_0_), channel_id=1, source_target_pairs={{0,16},{1,17},{2,18},{3,19},{4,20},{5,21},{6,22},{7,23},{8,24},{9,... | collective-permute-start | bytes 1572872 | tf_op jit(solution)/shard_map/ppermute | solution.py:135
  43.3 14.4 %collective-permute-start.16 = (bf16[128,2048]{1,0:T(8,128)(2,1)S(1)}, bf16[128,2048]{1,0:T(8,128)(2,1)S(1)}, u32[]{:S(2)}, u32[]{:S(2)}) collective-permute-start(bf16[128,2048]{1,0:T(8,128)(2,1)S(1)} %get-tuple-element.65), channel_id=1, source_target_pairs={{0,2},{1,3},{2,0},{3,1},{4,6},{5,7},{6,4},{7,5},{8,10},{9,11},{10,... | collective-permute-start | bytes 1572872 | tf_op jit(solution)/shard_map/ppermute | solution.py:135
  51.6 27.2 %collective-permute-start.12 = (bf16[512,1024]{1,0:T(8,128)(2,1)S(1)}, bf16[512,1024]{1,0:T(8,128)(2,1)S(1)}, u32[]{:S(2)}, u32[]{:S(2)}) collective-permute-start(bf16[512,1024]{1,0:T(8,128)(2,1)S(1)} %shard_map.117.refs_1_), channel_id=1, source_target_pairs={{0,16},{1,17},{2,18},{3,19},{4,20},{5,21},{6,22},{7,23},{8,24},{9,... | collective-permute-start | bytes 3145736 | tf_op jit(solution)/shard_map/ppermute | solution.py:135
  53.5 29.6 %copy-start.8 = (f32[2048]{0:T(1024)S(1)}, f32[2048]{0:T(1024)}, u32[]{:S(2)}) copy-start(f32[2048]{0:T(1024)} %param.14) | copy-start | bytes 24580
  53.5 29.1 %collective-permute-start.11 = (bf16[512,1024]{1,0:T(8,128)(2,1)S(1)}, bf16[512,1024]{1,0:T(8,128)(2,1)S(1)}, u32[]{:S(2)}, u32[]{:S(2)}) collective-permute-start(bf16[512,1024]{1,0:T(8,128)(2,1)S(1)} %shard_map.116.refs_0_), channel_id=1, source_target_pairs={{0,1},{1,0},{2,3},{3,2},{4,5},{5,4},{6,7},{7,6},{8,9},{9,8},{10,11... | collective-permute-start | bytes 3145736 | tf_op jit(solution)/shard_map/ppermute | solution.py:135
  55.1 23.7 %collective-permute-start.15 = (bf16[128,2048]{1,0:T(8,128)(2,1)S(1)}, bf16[128,2048]{1,0:T(8,128)(2,1)S(1)}, u32[]{:S(2)}, u32[]{:S(2)}) collective-permute-start(bf16[128,2048]{1,0:T(8,128)(2,1)S(1)} %get-tuple-element.64), channel_id=1, source_target_pairs={{0,2},{1,3},{2,0},{3,1},{4,6},{5,7},{6,4},{7,5},{8,10},{9,11},{10,... | collective-permute-start | bytes 1572872 | tf_op jit(solution)/shard_map/ppermute | solution.py:135
  57.8 24.8 %collective-permute-start.17 = (bf16[128,2048]{1,0:T(8,128)(2,1)S(1)}, bf16[128,2048]{1,0:T(8,128)(2,1)S(1)}, u32[]{:S(2)}, u32[]{:S(2)}) collective-permute-start(bf16[128,2048]{1,0:T(8,128)(2,1)S(1)} %shard_map.118), channel_id=1, source_target_pairs={{0,4},{1,5},{2,6},{3,7},{4,0},{5,1},{6,2},{7,3},{8,12},{9,13},{10,... | collective-permute-start | bytes 1572872 | tf_op jit(solution)/shard_map/ppermute | solution.py:135
  60.8 24.0 %collective-permute-start.14 = (bf16[512,1024]{1,0:T(8,128)(2,1)S(1)}, bf16[512,1024]{1,0:T(8,128)(2,1)S(1)}, u32[]{:S(2)}, u32[]{:S(2)}) collective-permute-start(bf16[512,1024]{1,0:T(8,128)(2,1)S(1)} %shard_map.117.refs_1_), channel_id=1, source_target_pairs={{0,8},{1,9},{2,10},{3,11},{4,12},{5,13},{6,14},{7,15},{8,0},{9,1},... | collective-permute-start | bytes 3145736 | tf_op jit(solution)/shard_map/ppermute | solution.py:135
  78.8 6.0 %collective-permute-start.13 = (bf16[512,1024]{1,0:T(8,128)(2,1)S(1)}, bf16[512,1024]{1,0:T(8,128)(2,1)S(1)}, u32[]{:S(2)}, u32[]{:S(2)}) collective-permute-start(bf16[512,1024]{1,0:T(8,128)(2,1)S(1)} %shard_map.116.refs_0_), channel_id=1, source_target_pairs={{0,8},{1,9},{2,10},{3,11},{4,12},{5,13},{6,14},{7,15},{8,0},{9,1},... | collective-permute-start | bytes 3145736 | tf_op jit(solution)/shard_map/ppermute | solution.py:135
  82.6 2.7 %collective-permute-start.19 = (bf16[512,1024]{1,0:T(8,128)(2,1)S(1)}, bf16[512,1024]{1,0:T(8,128)(2,1)S(1)}, u32[]{:S(2)}, u32[]{:S(2)}) collective-permute-start(bf16[512,1024]{1,0:T(8,128)(2,1)S(1)} %collective-permute-done.12.refs_3_), channel_id=1, source_target_pairs={{0,8},{1,9},{2,10},{3,11},{4,12},{5,13},{6,14},{7,15},{8,0},{9,1},... | collective-permute-start | bytes 3145736 | tf_op jit(solution)/shard_map/ppermute | solution.py:135
  82.6 4.2 %collective-permute-start.18 = (bf16[512,1024]{1,0:T(8,128)(2,1)S(1)}, bf16[512,1024]{1,0:T(8,128)(2,1)S(1)}, u32[]{:S(2)}, u32[]{:S(2)}) collective-permute-start(bf16[512,1024]{1,0:T(8,128)(2,1)S(1)} %collective-permute-done.11.refs_2_), channel_id=1, source_target_pairs={{0,8},{1,9},{2,10},{3,11},{4,12},{5,13},{6,14},{7,15},{8,0},{9,1},... | collective-permute-start | bytes 3145736 | tf_op jit(solution)/shard_map/ppermute | solution.py:135
  83.1 3.6 %copy-start.3 = (bf16[128,2048]{1,0:T(8,128)(2,1)S(1)}, bf16[128,2048]{1,0:T(8,128)(2,1)}, u32[]{:S(2)}) copy-start(bf16[128,2048]{1,0:T(8,128)(2,1)} %refs_10_.1) | copy-start | bytes 1572868
  91.8 16.3 %collective-permute-start.20 = (bf16[128,1152]{1,0:T(8,128)(2,1)S(1)}, bf16[128,1152]{1,0:T(8,128)(2,1)S(1)}, u32[]{:S(2)}, u32[]{:S(2)}) collective-permute-start(bf16[128,1152]{1,0:T(8,128)(2,1)S(1)} %get-tuple-element.77.refs_0_.refs_2_), channel_id=1, source_target_pairs={{0,4},{1,5},{2,6},{3,7},{4,0},{5,1},{6,2},{7,3},{8,12},{9,13},{10,... | collective-permute-start | bytes 884744 | tf_op jit(solution)/shard_map/ppermute | solution.py:135
  91.9 16.2 %collective-permute-start.23 = (bf16[128,1024]{1,0:T(8,128)(2,1)S(1)}, bf16[128,1024]{1,0:T(8,128)(2,1)S(1)}, u32[]{:S(2)}, u32[]{:S(2)}) collective-permute-start(bf16[128,1024]{1,0:T(8,128)(2,1)S(1)} %get-tuple-element.80), channel_id=1, source_target_pairs={{0,16},{1,17},{2,18},{3,19},{4,20},{5,21},{6,22},{7,23},{8,24},{9,... | collective-permute-start | bytes 786440 | tf_op jit(solution)/shard_map/ppermute | solution.py:135
  93.6 14.5 %collective-permute-start.22 = (bf16[128,1024]{1,0:T(8,128)(2,1)S(1)}, bf16[128,1024]{1,0:T(8,128)(2,1)S(1)}, u32[]{:S(2)}, u32[]{:S(2)}) collective-permute-start(bf16[128,1024]{1,0:T(8,128)(2,1)S(1)} %get-tuple-element.83.refs_0_), channel_id=1, source_target_pairs={{0,16},{1,17},{2,18},{3,19},{4,20},{5,21},{6,22},{7,23},{8,24},{9,... | collective-permute-start | bytes 786440 | tf_op jit(solution)/shard_map/ppermute | solution.py:135
  94.0 17.7 %collective-permute-start.24 = (bf16[128,1024]{1,0:T(8,128)(2,1)S(1)}, bf16[128,1024]{1,0:T(8,128)(2,1)S(1)}, u32[]{:S(2)}, u32[]{:S(2)}) collective-permute-start(bf16[128,1024]{1,0:T(8,128)(2,1)S(1)} %get-tuple-element.85.refs_0_), channel_id=1, source_target_pairs={{0,1},{1,0},{2,3},{3,2},{4,5},{5,4},{6,7},{7,6},{8,9},{9,8},{10,11... | collective-permute-start | bytes 786440 | tf_op jit(solution)/shard_map/ppermute | solution.py:135
  108.2 21.0 %collective-permute-start.26 = (bf16[256,1536]{1,0:T(8,128)(2,1)S(1)}, bf16[256,1536]{1,0:T(8,128)(2,1)S(1)}, u32[]{:S(2)}, u32[]{:S(2)}) collective-permute-start(bf16[256,1536]{1,0:T(8,128)(2,1)S(1)} %shard_map.123), channel_id=1, source_target_pairs={{0,1},{1,0},{2,3},{3,2},{4,5},{5,4},{6,7},{7,6},{8,9},{9,8},{10,11... | collective-permute-start | bytes 2359304 | tf_op jit(solution)/shard_map/ppermute | solution.py:135
  109.9 19.2 %collective-permute-start.21 = (bf16[256,1152]{1,0:T(8,128)(2,1)S(1)}, bf16[256,1152]{1,0:T(8,128)(2,1)S(1)}, u32[]{:S(2)}, u32[]{:S(2)}) collective-permute-start(bf16[256,1152]{1,0:T(8,128)(2,1)S(1)} %shard_map.121), channel_id=1, source_target_pairs={{0,2},{1,3},{2,0},{3,1},{4,6},{5,7},{6,4},{7,5},{8,10},{9,11},{10,... | collective-permute-start | bytes 1769480 | tf_op jit(solution)/shard_map/ppermute | solution.py:135
  111.7 16.3 %collective-permute-start.27 = (bf16[256,1024]{1,0:T(8,128)(2,1)S(1)}, bf16[256,1024]{1,0:T(8,128)(2,1)S(1)}, u32[]{:S(2)}, u32[]{:S(2)}) collective-permute-start(bf16[256,1024]{1,0:T(8,128)(2,1)S(1)} %shard_map.124.refs_1_), channel_id=1, source_target_pairs={{0,16},{1,17},{2,18},{3,19},{4,20},{5,21},{6,22},{7,23},{8,24},{9,... | collective-permute-start | bytes 1572872 | tf_op jit(solution)/shard_map/ppermute | solution.py:135
  113.3 14.8 %collective-permute-start.25 = (bf16[128,896]{1,0:T(8,128)(2,1)S(1)}, bf16[128,896]{1,0:T(8,128)(2,1)S(1)}, u32[]{:S(2)}, u32[]{:S(2)}) collective-permute-start(bf16[128,896]{1,0:T(8,128)(2,1)S(1)} %get-tuple-element.82.refs_0_.refs_2_), channel_id=1, source_target_pairs={{0,4},{1,5},{2,6},{3,7},{4,0},{5,1},{6,2},{7,3},{8,12},{9,13},{10,... | collective-permute-start | bytes 688136 | tf_op jit(solution)/shard_map/ppermute | solution.py:135
  130.0 2.9 %collective-permute-start.28 = (bf16[512,1152]{1,0:T(8,128)(2,1)S(1)}, bf16[512,1152]{1,0:T(8,128)(2,1)S(1)}, u32[]{:S(2)}, u32[]{:S(2)}) collective-permute-start(bf16[512,1152]{1,0:T(8,128)(2,1)S(1)} %shard_map.125), channel_id=1, source_target_pairs={{0,8},{1,9},{2,10},{3,11},{4,12},{5,13},{6,14},{7,15},{8,0},{9,1},... | collective-permute-start | bytes 3538952 | tf_op jit(solution)/shard_map/ppermute | solution.py:135
  131.5 5.9 %collective-permute-start.29 = (bf16[256,2176]{1,0:T(8,128)(2,1)S(1)}, bf16[256,2176]{1,0:T(8,128)(2,1)S(1)}, u32[]{:S(2)}, u32[]{:S(2)}) collective-permute-start(bf16[256,2176]{1,0:T(8,128)(2,1)S(1)} %shard_map.128), channel_id=1, source_target_pairs={{0,8},{1,9},{2,10},{3,11},{4,12},{5,13},{6,14},{7,15},{8,0},{9,1},... | collective-permute-start | bytes 3342344 | tf_op jit(solution)/shard_map/ppermute | solution.py:135
  132.1 18.7 %collective-permute-start.33 = (bf16[256,896]{1,0:T(8,128)(2,1)S(1)}, bf16[256,896]{1,0:T(8,128)(2,1)S(1)}, u32[]{:S(2)}, u32[]{:S(2)}) collective-permute-start(bf16[256,896]{1,0:T(8,128)(2,1)S(1)} %shard_map.131), channel_id=1, source_target_pairs={{0,2},{1,3},{2,0},{3,1},{4,6},{5,7},{6,4},{7,5},{8,10},{9,11},{10,... | collective-permute-start | bytes 1376264 | tf_op jit(solution)/shard_map/ppermute | solution.py:135
  133.8 16.9 %collective-permute-start.30 = (bf16[128,1152]{1,0:T(8,128)(2,1)S(1)}, bf16[128,1152]{1,0:T(8,128)(2,1)S(1)}, u32[]{:S(2)}, u32[]{:S(2)}) collective-permute-start(bf16[128,1152]{1,0:T(8,128)(2,1)S(1)} %get-tuple-element.90), channel_id=1, source_target_pairs={{0,16},{1,17},{2,18},{3,19},{4,20},{5,21},{6,22},{7,23},{8,24},{9,... | collective-permute-start | bytes 884744 | tf_op jit(solution)/shard_map/ppermute | solution.py:135
  135.4 15.3 %collective-permute-start.31 = (bf16[128,1152]{1,0:T(8,128)(2,1)S(1)}, bf16[128,1152]{1,0:T(8,128)(2,1)S(1)}, u32[]{:S(2)}, u32[]{:S(2)}) collective-permute-start(bf16[128,1152]{1,0:T(8,128)(2,1)S(1)} %get-tuple-element.91), channel_id=1, source_target_pairs={{0,1},{1,0},{2,3},{3,2},{4,5},{5,4},{6,7},{7,6},{8,9},{9,8},{10,11... | collective-permute-start | bytes 884744 | tf_op jit(solution)/shard_map/ppermute | solution.py:135
  135.9 14.9 %collective-permute-start.32 = (bf16[128,1152]{1,0:T(8,128)(2,1)S(1)}, bf16[128,1152]{1,0:T(8,128)(2,1)S(1)}, u32[]{:S(2)}, u32[]{:S(2)}) collective-permute-start(bf16[128,1152]{1,0:T(8,128)(2,1)S(1)} %get-tuple-element.92), channel_id=1, source_target_pairs={{0,17},{1,16},{2,19},{3,18},{4,21},{5,20},{6,23},{7,22},{8,25},{9,... | collective-permute-start | bytes 884744 | tf_op jit(solution)/shard_map/ppermute | solution.py:135
  139.3 11.2 %collective-permute-start.34 = (bf16[64,2176]{1,0:T(8,128)(2,1)S(1)}, bf16[64,2176]{1,0:T(8,128)(2,1)S(1)}, u32[]{:S(2)}, u32[]{:S(2)}) collective-permute-start(bf16[64,2176]{1,0:T(8,128)(2,1)S(1)} %get-tuple-element.88), channel_id=1, source_target_pairs={{0,2},{1,3},{2,0},{3,1},{4,6},{5,7},{6,4},{7,5},{8,10},{9,11},{10,... | collective-permute-start | bytes 835592 | tf_op jit(solution)/shard_map/ppermute | solution.py:135
  151.5 3.0 %collective-permute-start.35 = (bf16[512,896]{1,0:T(8,128)(2,1)S(1)}, bf16[512,896]{1,0:T(8,128)(2,1)S(1)}, u32[]{:S(2)}, u32[]{:S(2)}) collective-permute-start(bf16[512,896]{1,0:T(8,128)(2,1)S(1)} %shard_map.133), channel_id=1, source_target_pairs={{0,8},{1,9},{2,10},{3,11},{4,12},{5,13},{6,14},{7,15},{8,0},{9,1},... | collective-permute-start | bytes 2752520 | tf_op jit(solution)/shard_map/ppermute | solution.py:135
  151.6 15.7 %collective-permute-start.39 = (bf16[64,2304]{1,0:T(8,128)(2,1)S(1)}, bf16[64,2304]{1,0:T(8,128)(2,1)S(1)}, u32[]{:S(2)}, u32[]{:S(2)}) collective-permute-start(bf16[64,2304]{1,0:T(8,128)(2,1)S(1)} %get-tuple-element.100), channel_id=1, source_target_pairs={{0,2},{1,3},{2,0},{3,1},{4,6},{5,7},{6,4},{7,5},{8,10},{9,11},{10,... | collective-permute-start | bytes 884744 | tf_op jit(solution)/shard_map/ppermute | solution.py:135
  152.4 14.9 %collective-permute-start.40 = (bf16[64,2304]{1,0:T(8,128)(2,1)S(1)}, bf16[64,2304]{1,0:T(8,128)(2,1)S(1)}, u32[]{:S(2)}, u32[]{:S(2)}) collective-permute-start(bf16[64,2304]{1,0:T(8,128)(2,1)S(1)} %shard_map.132), channel_id=1, source_target_pairs={{0,4},{1,5},{2,6},{3,7},{4,0},{5,1},{6,2},{7,3},{8,12},{9,13},{10,... | collective-permute-start | bytes 884744 | tf_op jit(solution)/shard_map/ppermute | solution.py:135
  155.2 13.1 %collective-permute-start.36 = (bf16[128,896]{1,0:T(8,128)(2,1)S(1)}, bf16[128,896]{1,0:T(8,128)(2,1)S(1)}, u32[]{:S(2)}, u32[]{:S(2)}) collective-permute-start(bf16[128,896]{1,0:T(8,128)(2,1)S(1)} %get-tuple-element.96), channel_id=1, source_target_pairs={{0,16},{1,17},{2,18},{3,19},{4,20},{5,21},{6,22},{7,23},{8,24},{9,... | collective-permute-start | bytes 688136 | tf_op jit(solution)/shard_map/ppermute | solution.py:135
  156.6 12.1 %collective-permute-start.37 = (bf16[128,896]{1,0:T(8,128)(2,1)S(1)}, bf16[128,896]{1,0:T(8,128)(2,1)S(1)}, u32[]{:S(2)}, u32[]{:S(2)}) collective-permute-start(bf16[128,896]{1,0:T(8,128)(2,1)S(1)} %get-tuple-element.97), channel_id=1, source_target_pairs={{0,1},{1,0},{2,3},{3,2},{4,5},{5,4},{6,7},{7,6},{8,9},{9,8},{10,11... | collective-permute-start | bytes 688136 | tf_op jit(solution)/shard_map/ppermute | solution.py:135
  157.1 11.6 %collective-permute-start.38 = (bf16[128,896]{1,0:T(8,128)(2,1)S(1)}, bf16[128,896]{1,0:T(8,128)(2,1)S(1)}, u32[]{:S(2)}, u32[]{:S(2)}) collective-permute-start(bf16[128,896]{1,0:T(8,128)(2,1)S(1)} %get-tuple-element.98), channel_id=1, source_target_pairs={{0,17},{1,16},{2,19},{3,18},{4,21},{5,20},{6,23},{7,22},{8,25},{9,... | collective-permute-start | bytes 688136 | tf_op jit(solution)/shard_map/ppermute | solution.py:135
  (2 other events, 1.3 us)
